TPU v7x, 128 devices: a whole 4x4x4 slice. The times are simulated.
128 devices in a mesh: node: 8 (over x, core), local: 16 (over z, y).
Axes of the slice: x: 4, y: 4, z: 4, core: 2. Of those that a mesh axis runs over, the one named last changes fastest.
Arguments:
- tokens: bfloat16 [8192, 7168], P('node', 'local'), may hold values from -6 to 6
- norm_gain: float32 [7168], replicated, may hold values from 0.5 to 1.5
- dense_gate: bfloat16 [7168, 4096], P(None, 'local'), may hold values from -0.0625 to 0.0625
- dense_up: bfloat16 [7168, 4096], P(None, 'local'), may hold values from -0.0625 to 0.0625
- dense_down: bfloat16 [4096, 7168], P('local'), may hold values from -0.09375 to 0.09375
- expert_gate: bfloat16 [8, 7168, 4096], P('node', None, 'local'), may hold values from -0.0625 to 0.0625
- expert_up: bfloat16 [8, 7168, 4096], P('node', None, 'local'), may hold values from -0.0625 to 0.0625
- expert_down: bfloat16 [8, 4096, 7168], P('node', 'local'), may hold values from -0.09375 to 0.09375
- expert_ids: int32 [8192, 2], P('node'), may hold values from 0 to 127, all different within a row
- route_gates: float32 [8192, 2], P('node'), may hold values from 0.1 to 0.9
Outputs:
- layer_out: bfloat16 [8192, 7168], P('node', 'local')
Inputs may be any that keep to these rules, and one draw needn't show every extreme that they name: `expert_ids`: each row names two different experts.
All inputs are finite; a program needn't handle non-finite values.
Results may differ from a plain program's by a relative error of at most 0.014.
Values may be sent and summed in bfloat16 or wider, within the bound.
No kernel may reach another device: no remote copies, remote signals or barrier semaphores. Data moves between devices by JAX's collectives and lax.ppermute only.
A program may use at most 128 MiB of HBM per device.

v0:
```python
import jax
import jax.numpy as jnp
from jax import lax
from jax.sharding import PartitionSpec as P

CAP = 1


EPSILON = 1e-05


def rms_normed(rows_in, gain_vec):
    as_float = rows_in.astype(jnp.float32)
    inv_scale = lax.rsqrt(jnp.mean(as_float * as_float, axis=-1, keepdims=True) + EPSILON)
    return (as_float * inv_scale * gain_vec).astype(jnp.bfloat16)


def route_ranks(ids_block, window):
    flat_ids = ids_block.reshape(-1)
    expert_range = jnp.arange(window, dtype=jnp.int32)
    member = (flat_ids[:, None] == expert_range[None, :]).astype(jnp.int32)
    before = jnp.cumsum(member, axis=0) - member
    route_rank = jnp.sum(before * member, axis=1)
    in_window = jnp.sum(member, axis=1) > 0
    return (route_rank.reshape(ids_block.shape), in_window.reshape(ids_block.shape))


def swiglu_rows(normed_rows, gate_weight, up_weight):
    gate_value = jnp.dot(normed_rows, gate_weight, preferred_element_type=jnp.float32)
    up_value = jnp.dot(normed_rows, up_weight, preferred_element_type=jnp.float32)
    return (jax.nn.silu(gate_value) * up_value).astype(jnp.bfloat16)


def shards(
    tokens,
    norm_gain,
    dense_gate,
    dense_up,
    dense_down,
    expert_gate,
    expert_up,
    expert_down,
    expert_ids,
    route_gates,
):
    local_count = lax.axis_size("local")
    node_count = lax.axis_size("node")
    local_index = lax.axis_index("local")
    tok_node = tokens.shape[0]
    slice_width = tokens.shape[1]
    whole_rows = lax.all_gather(tokens, "local", axis=1, tiled=True)
    normed = rms_normed(whole_rows, norm_gain)
    width = normed.shape[1]
    dense_hidden = swiglu_rows(normed, dense_gate, dense_up)
    partial_sum = jnp.dot(dense_hidden, dense_down, preferred_element_type=jnp.float32)
    summed_rows = lax.psum(partial_sum.astype(jnp.bfloat16), "local").astype(jnp.float32)
    dense_part = lax.dynamic_slice_in_dim(summed_rows, local_index * slice_width, slice_width, 1)
    route_rank, in_window = route_ranks(expert_ids, node_count)
    owned = in_window & (route_rank < CAP * local_count) & (route_rank // CAP == local_index)
    slot_index = expert_ids * CAP + route_rank % CAP
    slot_count = node_count * CAP
    slot_range = jnp.arange(slot_count, dtype=jnp.int32)
    matched = owned[None, :, :] & (slot_index[None, :, :] == slot_range[:, None, None])
    match_float = matched.astype(jnp.float32)
    chosen = jnp.sum(match_float, axis=2).astype(jnp.bfloat16)
    send_rows = jnp.dot(chosen, normed, preferred_element_type=jnp.float32).astype(jnp.bfloat16)
    slot_gate = jnp.sum(match_float * route_gates[None, :, :], axis=(1, 2))
    token_range = jnp.arange(tok_node, dtype=jnp.int32)
    slot_token = jnp.where(
        jnp.any(matched, axis=(1, 2)),
        jnp.sum(matched.astype(jnp.int32) * token_range[None, :, None], axis=(1, 2)),
        -1,
    )
    outgoing = send_rows.reshape(node_count, CAP, width)
    arrived = lax.all_to_all(outgoing, "node", split_axis=0, concat_axis=0, tiled=True)
    pooled = lax.all_gather(arrived[None], "local", axis=0, tiled=True).reshape(-1, width)
    expert_hidden = swiglu_rows(pooled, expert_gate[0], expert_up[0])
    expert_partial = jnp.dot(expert_hidden, expert_down[0], preferred_element_type=jnp.float32)
    expert_out = lax.psum_scatter(
        expert_partial.astype(jnp.bfloat16), "local", scatter_dimension=0, tiled=True
    )
    returned = lax.all_to_all(
        expert_out.reshape(node_count, CAP, width), "node", split_axis=0, concat_axis=0, tiled=True
    ).reshape(slot_count, width)
    route_term = (slot_gate[:, None] * returned.astype(jnp.float32)).astype(jnp.bfloat16)
    all_terms, all_tokens = (
        lax.all_gather(route_term, "local", axis=0, tiled=True),
        lax.all_gather(slot_token, "local", axis=0, tiled=True),
    )
    my_terms = lax.dynamic_slice_in_dim(all_terms, local_index * slice_width, slice_width, 1)
    placement = (all_tokens[None, :] == token_range[:, None]).astype(jnp.bfloat16)
    expert_part = jnp.dot(placement, my_terms, preferred_element_type=jnp.float32)
    return (tokens.astype(jnp.float32) + dense_part + expert_part).astype(jnp.bfloat16)


def solution(mesh):
    return jax.shard_map(
        shards,
        mesh=mesh,
        in_specs=(
            P("node", "local"),
            P(),
            P(None, "local"),
            P(None, "local"),
            P("local", None),
            P("node", None, "local"),
            P("node", None, "local"),
            P("node", "local", None),
            P("node", None),
            P("node", None),
        ),
        out_specs=P("node", "local"),
        check_vma=False,
    )
```

profile of v0, /device:TPU:0, one launch (start us, length us, event | category | flops | bytes accessed | tf_op | source)
XLA Modules:
  0.0 491.2 jit_solution(12541032613631263034)
XLA Ops:
  6.5 0.7 all-gather.5.cloned.1.call-update
  7.3 0.0 all-gather.9.cloned.1.call-start
  7.3 0.9 copy.30
  8.2 0.3 eq.68
  8.5 0.3 eq.64
  8.8 2.3 reduce-window.6
  11.1 0.3 slice_reduce_fusion
  11.4 0.2 reduce-window.9
  11.5 0.1 add_bitcast_fusion
  11.6 0.1 convert_reduce_fusion
  11.7 0.5 and.37
  12.3 0.2 copy.32
  12.5 0.9 select_reduce_fusion
  13.3 99.5 %all-gather.5.cloned.1.call-done = bf16[1024,7168]{0,1:T(8,128)(2,1)} async-done(((bf16[1024,448]{0,1:T(8,128)(2,1)}), bf16[1024,7168]{0,1:T(8,128)(2,1)}) %all-gather.5.cloned.1.call-update) | async-done | bytes 14680080 | tf_op jit(solution)/shard_map/all_gather | solution.py:51
  112.8 8.1 %fusion = f32[1024]{0:T(1024)S(1)} fusion(bf16[1024,7168]{0,1:T(8,128)(2,1)} %all-gather.5.cloned.1.call-done), kind=kLoop, calls=%fused_computation.2 | loop fusion | flops 22019072 | bytes 14684160 | tf_op jit(solution)/shard_map/reduce_sum | solution.py:14
  120.9 14.4 %fusion.2 = bf16[1024,7168]{0,1:T(8,128)(2,1)} fusion(bf16[1024,7168]{0,1:T(8,128)(2,1)} %all-gather.5.cloned.1.call-done, f32[7168]{0:T(1024)S(1)} %copy-done.3, f32[1024]{0:T(1024)S(1)} %add_rsqrt_fusion), kind=kLoop, calls=%fused_computation.4 | loop fusion | flops 29360128 | bytes 29392896 | tf_op jit(solution)/shard_map/convert_element_type | solution.py:15
  135.3 9.1 %fusion.3 = bf16[8,1,7168]{2,0,1:T(8,128)(2,1)S(1)} fusion(bf16[1024,7168]{0,1:T(8,128)(2,1)} %fusion.2, bf16[8,1024]{1,0:T(8,128)(2,1)S(1)} %get-tuple-element.6), kind=kOutput, calls=%fused_computation.8 | convolution fusion | flops 117497856 | bytes 14811136 | tf_op jit(solution)/shard_map/dot_general | solution.py:66
  144.4 0.5 broadcast.91
  144.9 0.6 reduce.2
  145.5 0.1 reshape.83
  145.6 10.0 %all_to_all.10 = bf16[8,2,3584]{2,1,0:T(2,128)(2,1)S(1)} all-to-all(bf16[8,2,3584]{2,1,0:T(2,128)(2,1)S(1)} %reshape.83), channel_id=1, replica_groups=mesh['node'=8,'local'=16] {'node'}, dimensions={0} | all-to-all | bytes 229376 | tf_op jit(solution)/shard_map/all_to_all | solution.py:75
  155.6 0.1 reshape.84
  155.7 0.7 copy.34
  156.3 0.0 all-gather.9.cloned.1.call-update
  156.4 0.2 all-reduce.5.cloned.1.call-start
  156.6 8.5 %fusion.44 = f32[1024,256]{1,0:T(8,128)S(1)} fusion(bf16[1024,7168]{0,1:T(8,128)(2,1)} %fusion.2, bf16[7168,256]{1,0:T(8,128)(2,1)} %param.12), kind=kOutput, calls=%fused_computation.56 | convolution fusion | flops 3758096384 | bytes 19398656 | tf_op jit(solution)/shard_map/dot_general | solution.py:29
  165.1 7.6 %fusion.11 = bf16[1024,256]{1,0:T(8,128)(2,1)S(1)} fusion(bf16[1024,7168]{0,1:T(8,128)(2,1)} %fusion.2, bf16[7168,256]{1,0:T(8,128)(2,1)S(1)} %copy-done.5, f32[1024,256]{1,0:T(8,128)S(1)} %fusion.44), kind=kOutput, calls=%fused_computation.18 | convolution fusion | flops 3759669248 | bytes 19922944 | tf_op jit(solution)/shard_map/dot_general | solution.py:30
  172.8 9.5 %convolution_convert_fusion = bf16[1024,7168]{0,1:T(8,128)(2,1)} fusion(bf16[1024,256]{1,0:T(8,128)(2,1)S(1)} %fusion.11, bf16[256,7168]{1,0:T(8,128)(2,1)} %param.14), kind=kOutput, calls=%fused_computation.5 | convolution fusion | flops 3765436416 | bytes 18874368 | tf_op jit(solution)/shard_map/dot_general | solution.py:55
  182.3 16.8 %all-gather.9.cloned.1.call-done = bf16[128,1,7168]{2,0,1:T(8,128)(2,1)} async-done(((bf16[8,1,7168]{2,0,1:T(8,128)(2,1)}), bf16[128,1,7168]{2,0,1:T(8,128)(2,1)}) %all-gather.9.cloned.1.call-update) | async-done | bytes 1835024 | tf_op jit(solution)/shard_map/all_gather | solution.py:76
  199.1 3.4 fusion.7
  202.5 6.6 %convolution_convert_fusion.1 = bf16[128,7168]{1,0:T(8,128)(2,1)} fusion(bf16[1,256,7168]{2,1,0:T(8,128)(2,1)} %param.17, bf16[1,7168,256]{2,1,0:T(8,128)(2,1)} %param.16, bf16[128,1,7168]{2,0,1:T(8,128)(2,1)S(1)} %copy-done, f32[128,256]{1,0:T(8,128)S(1)} %fusion.7), kind=kOutput, calls=%fused_computation.6 | convolution fusion | flops 940638208 | bytes 11141120 | tf_op jit(solution)/shard_map/dot_general | solution.py:78
  209.1 0.0 all-gather.7.cloned.1.call-start
  209.1 0.6 copy-done.4
  209.7 0.6 fusion.43
  210.9 215.5 %all-reduce.5.cloned.1.call-done = (bf16[1024,7168]{0,1:T(8,128)(2,1)}, bf16[128,7168]{1,0:T(8,128)(2,1)}) async-done(((bf16[1024,7168]{0,1:T(8,128)(2,1)}, bf16[128,7168]{1,0:T(8,128)(2,1)}), (bf16[1024,7168]{0,1:T(8,128)(2,1)}, bf16[128,7168]{1,0:T(8,128)(2,1)})) %all-reduce.5.cloned.1.call-update) | async-done | bytes 16515088 | tf_op jit(solution)/shard_map/psum | solution.py:56
  426.4 0.9 dynamic-slice_bitcast_fusion
  427.3 0.6 reduce.3
  427.9 0.1 reshape.85
  428.0 10.0 %all_to_all.11 = bf16[8,2,3584]{2,1,0:T(2,128)(2,1)S(1)} all-to-all(bf16[8,2,3584]{2,1,0:T(2,128)(2,1)S(1)} %reshape.85), channel_id=1, replica_groups=mesh['node'=8,'local'=16] {'node'}, dimensions={0} | all-to-all | bytes 229376 | tf_op jit(solution)/shard_map/all_to_all | solution.py:82
  438.0 0.1 reshape.86
  438.1 0.2 convert_element_type.71
  438.3 0.7 fusion.27
  439.7 0.1 fusion.39
  439.9 0.1 select_reduce_fusion.1
  440.0 0.1 select_dynamic-update-slice_fusion
  440.1 14.6 %all-reduce = s32[128]{0:T(128)S(1)} all-reduce(s32[128]{0:T(128)S(1)} %select_dynamic-update-slice_fusion), channel_id=1, replica_groups=mesh['node'=8,'local'=16] {'local'}, use_global_device_ids=true, to_apply=%add | all-reduce | flops 128 | bytes 1024
  454.7 27.2 %all-gather.7.cloned.1.call-done = bf16[128,7168]{1,0:T(8,128)(2,1)} async-done(((bf16[8,7168]{1,0:T(8,128)(2,1)}), bf16[128,7168]{1,0:T(8,128)(2,1)}) %all-gather.7.cloned.1.call-update) | async-done | bytes 1835024 | tf_op jit(solution)/shard_map/all_gather | solution.py:87
  481.9 2.7 add_convert_fusion
  (18 shorter events, 0.1 us)
Async XLA Ops:
  6.5 106.3 %all-gather.5.cloned.1.call-start = ((), (), s32[]{:S(2)}) async-start(), calls=%async_computation.2 | async-start | bytes 15597568 | tf_op jit(solution)/shard_map/all_gather | solution.py:51
  7.3 191.8 %all-gather.9.cloned.1.call-start = ((), (), s32[]{:S(2)}) async-start(), calls=%async_computation.4 | async-start | bytes 1949696 | tf_op jit(solution)/shard_map/all_gather | solution.py:76
  13.3 107.6 %copy-start.3 = (f32[7168]{0:T(1024)S(1)}, f32[7168]{0:T(1024)}, u32[]{:S(2)}) copy-start(f32[7168]{0:T(1024)} %param.11) | copy-start | bytes 86020
  156.4 270.1 %all-reduce.5.cloned.1.call-start = ((), (), s32[]{:S(2)}) async-start(), calls=%async_computation.5 | async-start | bytes 33030144 | tf_op jit(solution)/shard_map/psum | solution.py:56
  156.6 8.5 %copy-start.5 = (bf16[7168,256]{1,0:T(8,128)(2,1)S(1)}, bf16[7168,256]{1,0:T(8,128)(2,1)}, u32[]{:S(2)}) copy-start(bf16[7168,256]{1,0:T(8,128)(2,1)} %param.13) | copy-start | bytes 11010052
  199.1 3.4 copy-start
  209.0 0.7 copy-start.4
  209.0 230.7 %copy-start.2 = (s32[1024,2]{0,1:T(2,128)S(1)}, s32[1024,2]{0,1:T(2,128)}, u32[]{:S(2)}) copy-start(s32[1024,2]{0,1:T(2,128)} %param.18) | copy-start | bytes 24580
  209.0 272.9 %copy-start.1 = (bf16[1024,448]{0,1:T(8,128)(2,1)S(1)}, bf16[1024,448]{0,1:T(8,128)(2,1)}, u32[]{:S(2)}) copy-start(bf16[1024,448]{0,1:T(8,128)(2,1)} %param.10) | copy-start | bytes 2752516
  209.1 272.9 %all-gather.7.cloned.1.call-start = ((), (), s32[]{:S(2)}) async-start(), calls=%async_computation.3 | async-start | bytes 1949696 | tf_op jit(solution)/shard_map/all_gather | solution.py:87
Sparse Core Ops, SparseCore 0:
  9.5 103.2 all-gather.4
  156.5 42.5 all-gather.8
  209.2 217.1 all-reduce.4
  439.2 42.6 all-gather.6
where the time goes:
time: 492 us; the launch traced here: 491 us
  waiting for transfers between devices  360 us (73%)
  matrix products  47.3 us (10%)
  blocking collectives  34.6 us (7%)
  other arithmetic  28.5 us (6%)
  between operations  14.6 us (3%)
  local copies, waits for them, and re-layouts  6.08 us (1%)
    psum x1, waiting for transfers between devices, shards(): lax.psum(partial_sum.astype(jnp.bfloat16), 'local').astype(jnp.float32)  215 us
    all_gather x1, waiting for transfers between devices, shards(): whole_rows = lax.all_gather(tokens, 'local', axis=1, tiled=True)  99.5 us
    all_gather x1, waiting for transfers between devices, shards(): lax.all_gather(route_term, 'local', axis=0, tiled=True)  27.2 us
    all_gather x1, waiting for transfers between devices, shards(): lax.all_gather(arrived[None], 'local', axis=0, tiled=True)  16.8 us
    unnamed x1, blocking collectives  14.6 us
    convert_element_type x1, other arithmetic, rms_normed(): return (as_float * inv_scale * gain_vec).astype(jnp.bfloat16)  14.4 us
    dot_general x2, matrix products, swiglu_rows(): jnp.dot(normed_rows, gate_weight, preferred_element_type=jnp.float32)  11.9 us
    all_to_all x1, blocking collectives, shards(): lax.all_to_all(outgoing, 'node', split_axis=0, concat_axis=0, tiled=True)  10 us
  transfers between devices with their start and end apart: 4, of which 4 were waited for; matrix products, arithmetic and copies ran while one was open for 7% of the time, Pallas kernels for 0%

commit v1 on v0

v1 whole, which is shorter than its diff:
```python
import jax
import jax.numpy as jnp
from jax import lax
from jax.sharding import PartitionSpec as P

EPSILON = 1e-05
NODE_CAP = 16


def route_slots(ids_block, window):
    flat_ids = ids_block.reshape(-1)
    expert_range = jnp.arange(window, dtype=jnp.int32)
    member = (flat_ids[:, None] == expert_range[None, :]).astype(jnp.int32)
    before = jnp.cumsum(member, axis=0) - member
    route_rank = jnp.sum(before * member, axis=1)
    kept = (jnp.sum(member, axis=1) > 0) & (route_rank < NODE_CAP)
    slot = jnp.where(kept, flat_ids * NODE_CAP + route_rank, -1)
    return slot.reshape(ids_block.shape)


def shards(
    tokens,
    norm_gain,
    dense_gate,
    dense_up,
    dense_down,
    expert_gate,
    expert_up,
    expert_down,
    expert_ids,
    route_gates,
):
    local_count = lax.axis_size("local")
    node_count = lax.axis_size("node")
    slice_width = tokens.shape[1]
    width = slice_width * local_count
    hidden = dense_gate.shape[1]
    slot_count = node_count * NODE_CAP

    whole_rows = lax.all_gather(tokens, "local", axis=1, tiled=True)

    slot = route_slots(expert_ids, node_count)
    slot_range = jnp.arange(slot_count, dtype=jnp.int32)
    matched = slot[:, :, None] == slot_range[None, None, :]
    match_float = matched.astype(jnp.float32)
    chosen = jnp.sum(match_float, axis=1).astype(jnp.bfloat16)
    slot_gate = jnp.sum(match_float * route_gates[:, :, None], axis=(0, 1))
    send_rows = lax.dot_general(
        chosen, tokens, (((0,), (0,)), ((), ())), preferred_element_type=jnp.float32
    ).astype(jnp.bfloat16)
    arrived = lax.all_to_all(
        send_rows.reshape(node_count, NODE_CAP, slice_width), "node", split_axis=0, concat_axis=0, tiled=True
    ).reshape(slot_count, slice_width)
    spread = jnp.broadcast_to(arrived[None], (local_count, slot_count, slice_width))
    pooled = lax.all_to_all(spread, "local", split_axis=0, concat_axis=0, tiled=True)
    pooled = pooled.transpose(1, 0, 2).reshape(slot_count, width)

    as_float = tokens.astype(jnp.float32)
    square_sum = lax.psum(jnp.sum(as_float * as_float, axis=-1), "local")
    inv_scale = lax.rsqrt(square_sum / width + EPSILON)[:, None]
    pooled_float = pooled.astype(jnp.float32)
    pooled_scale = lax.rsqrt(jnp.mean(pooled_float * pooled_float, axis=-1, keepdims=True) + EPSILON)
    pooled_normed = (pooled_float * pooled_scale * norm_gain).astype(jnp.bfloat16)

    gain_column = norm_gain[:, None]
    both = jnp.concatenate(
        [
            (dense_gate.astype(jnp.float32) * gain_column).astype(jnp.bfloat16),
            (dense_up.astype(jnp.float32) * gain_column).astype(jnp.bfloat16),
        ],
        axis=1,
    )

    expert_gate_value = jnp.dot(pooled_normed, expert_gate[0], preferred_element_type=jnp.float32)
    expert_up_value = jnp.dot(pooled_normed, expert_up[0], preferred_element_type=jnp.float32)
    expert_hidden = (jax.nn.silu(expert_gate_value) * expert_up_value).astype(jnp.bfloat16)
    expert_partial = jnp.dot(expert_hidden, expert_down[0], preferred_element_type=jnp.float32).astype(jnp.bfloat16)
    partial_blocks = expert_partial.reshape(slot_count, local_count, slice_width).transpose(1, 0, 2)
    partial_blocks = lax.all_to_all(partial_blocks, "local", split_axis=0, concat_axis=0, tiled=True)
    expert_out = jnp.sum(partial_blocks.astype(jnp.float32), axis=0).astype(jnp.bfloat16)
    returned = lax.all_to_all(
        expert_out.reshape(node_count, NODE_CAP, slice_width), "node", split_axis=0, concat_axis=0, tiled=True
    ).reshape(slot_count, slice_width)
    route_term = (slot_gate[:, None] * returned.astype(jnp.float32)).astype(jnp.bfloat16)
    expert_part = jnp.dot(chosen, route_term, preferred_element_type=jnp.float32)

    gate_up = jnp.dot(whole_rows, both, preferred_element_type=jnp.float32) * inv_scale
    dense_hidden = (jax.nn.silu(gate_up[:, :hidden]) * gate_up[:, hidden:]).astype(jnp.bfloat16)
    partial_sum = jnp.dot(dense_hidden, dense_down, preferred_element_type=jnp.float32).astype(jnp.bfloat16)
    dense_part = lax.psum_scatter(partial_sum, "local", scatter_dimension=1, tiled=True).astype(jnp.float32)
    return (tokens.astype(jnp.float32) + dense_part + expert_part).astype(jnp.bfloat16)


def solution(mesh):
    return jax.shard_map(
        shards,
        mesh=mesh,
        in_specs=(
            P("node", "local"),
            P(),
            P(None, "local"),
            P(None, "local"),
            P("local", None),
            P("node", None, "local"),
            P("node", None, "local"),
            P("node", "local", None),
            P("node", None),
            P("node", None),
        ),
        out_specs=P("node", "local"),
        check_vma=False,
    )
```

time: 492 us -> 287 us (0.58)
  waiting for transfers between devices: 360 us -> 109 us
  blocking collectives: 34.6 us -> 99 us
  matrix products: 47.3 us -> 33.9 us
  other arithmetic: 28.5 us -> 15.5 us
  starting transfers between devices: 0.31 us -> 5.34 us
    psum x1 -> x0, waiting for transfers between devices: 215 us -> none  [shards(): lax.psum(partial_sum.astype(jnp.bfloat16), 'local').astype(jnp.float32)]
    all_gather x1, waiting for transfers between devices: 99.5 us -> 54.9 us  [shards(): whole_rows = lax.all_gather(tokens, 'local', axis=1, tiled=True)]
    all_gather x2 -> x0, waiting for transfers between devices: 44 us -> none  [the longest x1 27.2 us: shards(): lax.all_gather(route_term, 'local', axis=0, tiled=True)]
    psum x0 -> x1, blocking collectives: none -> 42.4 us  [shards(): square_sum = lax.psum(jnp.sum(as_float * as_float, axis=-1), 'local')]
    all_to_all x0 -> x1, waiting for transfers between devices: none -> 39.5 us  [shards(): lax.all_to_all(spread, 'local', split_axis=0, concat_axis=0, tiled=True)]
    all_to_all x2 -> x3, blocking collectives: 20 us -> 56.6 us  [the longest x1 36.1 us: shards(): lax.all_to_all(partial_blocks, 'local', split_axis=0, concat_axis=0, tile...]
    unnamed x1 -> x0, blocking collectives: 14.6 us -> none
    dot_general x5 -> x4, matrix products: 31.3 us -> 17.1 us  [the longest x1 13.3 us: shards(): jnp.dot(whole_rows, both, preferred_element_type=jnp.float32) * inv_scale]
  transfers between devices with their start and end apart: 4 -> 3, of which waited for: 4 -> 3; matrix products, arithmetic and copies ran while one was open for 7% -> 11% of each run, Pallas kernels for 0% -> 0%
where the time goes in v1:
time: 287 us; the launch traced here: 286 us
  waiting for transfers between devices  109 us (38%)
  blocking collectives  99 us (34%)
  matrix products  33.9 us (12%)
  other arithmetic  15.5 us (5%)
  between operations  13.6 us (5%)
  local copies, waits for them, and re-layouts  9.71 us (3%)
  starting transfers between devices  5.34 us (2%)
    all_gather x1, waiting for transfers between devices, shards(): whole_rows = lax.all_gather(tokens, 'local', axis=1, tiled=True)  54.9 us
    psum x1, blocking collectives, shards(): square_sum = lax.psum(jnp.sum(as_float * as_float, axis=-1), 'local')  42.4 us
    all_to_all x1, waiting for transfers between devices, shards(): lax.all_to_all(spread, 'local', split_axis=0, concat_axis=0, tiled=True)  39.5 us
    all_to_all x1, blocking collectives, shards(): lax.all_to_all(partial_blocks, 'local', split_axis=0, concat_axis=0, tile...  36.1 us
    reduce_scatter x1, waiting for transfers between devices, shards(): lax.psum_scatter(partial_sum, 'local', scatter_dimension=1, tiled=True)  13.9 us
    dot_general x1, matrix products, shards(): jnp.dot(whole_rows, both, preferred_element_type=jnp.float32) * inv_scale  13.3 us
    all_to_all x1, blocking collectives, shards(): lax.all_to_all(expert_out.reshape(node_count, NODE_CAP, slice_width), 'no...  10.3 us
    all_to_all x1, blocking collectives, shards(): lax.all_to_all(send_rows.reshape(node_count, NODE_CAP, slice_width), 'nod...  10.2 us
  transfers between devices with their start and end apart: 3, of which 3 were waited for; matrix products, arithmetic and copies ran while one was open for 11% of the time, Pallas kernels for 0%

profile of v1, /device:TPU:0, one launch (start us, length us, event | category | flops | bytes accessed | tf_op | source)
XLA Modules:
  0.0 286.1 jit_solution(8103634839476610198)
XLA Ops:
  6.5 0.0 all-gather.2.cloned.1.call-start
  6.5 0.7 all-gather.2.cloned.1.call-update
  7.3 0.0 reduce-scatter.2.cloned.1.call-start
  7.3 1.4 fusion.12
  8.7 42.4 %psum.7 = f32[1024]{0:T(1024)S(1)} all-reduce(f32[1024]{0:T(1024)S(1)} %fusion.12), channel_id=1, replica_groups=mesh['node'=8,'local'=16] {'local'}, use_global_device_ids=true, to_apply=%region_1.2 | all-reduce | flops 1024 | bytes 8192 | tf_op jit(solution)/shard_map/psum | solution.py:59
  51.1 6.8 %multiply_convert_fusion.1 = (bf16[7168,256]{1,0:T(8,128)(2,1)}, bf16[7168,256]{1,0:T(8,128)(2,1)}) fusion(bf16[7168,256]{1,0:T(8,128)(2,1)} %param.12, f32[7168]{0:T(1024)} %param.11, bf16[7168,256]{1,0:T(8,128)(2,1)} %param.13), kind=kLoop, calls=%fused_computation.7 | loop fusion | flops 11010048 | bytes 14708736 | tf_op jit(solution)/shard_map/convert_element_type | solution.py:68
  57.9 54.9 %all-gather.2.cloned.1.call-done = bf16[1024,7168]{0,1:T(8,128)(2,1)} async-done(((bf16[1024,448]{0,1:T(8,128)(2,1)}), bf16[1024,7168]{0,1:T(8,128)(2,1)}) %all-gather.2.cloned.1.call-update) | async-done | bytes 14680080 | tf_op jit(solution)/shard_map/all_gather | solution.py:40
  112.8 13.3 %multiply_bitcast_fusion = f32[1024,512]{0,1:T(8,128)S(1)} fusion(bf16[1024,7168]{0,1:T(8,128)(2,1)} %all-gather.2.cloned.1.call-done, bf16[7168,256]{1,0:T(8,128)(2,1)} %get-tuple-element.10, bf16[7168,256]{1,0:T(8,128)(2,1)} %get-tuple-element.9, f32[1024]{0:T(1024)S(1)} %add_rsqrt_fusion), kind=kOutput, calls=%fused_computation.20 | convolution fusion | flops 7531397120 | bytes 24121344 | tf_op jit(solution)/shard_map/dot_general | solution.py:87
  126.1 9.5 %convolution_convert_fusion = bf16[1024,7168]{0,1:T(8,128)(2,1)} fusion(bf16[256,7168]{1,0:T(8,128)(2,1)} %param.14, f32[1024,512]{0,1:T(8,128)S(1)} %multiply_bitcast_fusion), kind=kOutput, calls=%fused_computation | convolution fusion | flops 3767009280 | bytes 20447232 | tf_op jit(solution)/shard_map/dot_general | solution.py:89
  135.6 0.0 reduce-scatter.2.cloned.1.call-update
  135.7 0.7 copy-done.4
  136.3 0.2 copy.39
  136.6 0.3 eq.38
  136.8 0.3 eq.42
  137.1 0.2 copy.42
  137.4 2.3 reduce-window.6
  139.6 0.3 slice_reduce_fusion
  139.9 0.2 reduce-window.9
  140.1 0.1 add_bitcast_fusion
  140.2 0.1 convert_reduce_fusion.1
  140.3 0.5 reduce_sum.71
  140.8 0.5 gt.13
  141.3 0.1 add_select_fusion
  141.4 0.2 copy.43
  141.6 0.0 copy-done.5
  141.6 0.8 select_reduce_fusion
  142.4 0.0 copy-start.3
  142.4 0.4 convolution_convert_fusion.2
  142.8 0.1 copy.44
  143.0 10.2 %all_to_all.20 = bf16[8,16,448]{2,1,0:T(8,128)(2,1)S(1)} all-to-all(bf16[8,16,448]{2,1,0:T(8,128)(2,1)S(1)} %bitcast.49), channel_id=1, replica_groups=mesh['node'=8,'local'=16] {'node'}, dimensions={0} | all-to-all | bytes 229376 | tf_op jit(solution)/shard_map/all_to_all | solution.py:51
  153.2 0.1 copy.45
  153.3 1.6 broadcast_in_dim.10
  154.9 5.3 %all-to-all-start.1 = ((bf16[16,128,448]{1,2,0:T(8,128)(2,1)}), bf16[16,128,448]{1,2,0:T(8,128)(2,1)S(1)}, u32[]{:S(2)}, u32[]{:S(2)}) async-start(bf16[16,128,448]{1,2,0:T(8,128)(2,1)} %broadcast_in_dim.10), calls=%async_computation.2 | async-start | bytes 3670016 | tf_op jit(solution)/shard_map/all_to_all | solution.py:55
  160.2 0.1 mul.112
  160.3 39.5 %all-to-all-done.1 = bf16[16,128,448]{1,2,0:T(8,128)(2,1)S(1)} async-done(((bf16[16,128,448]{1,2,0:T(8,128)(2,1)}), bf16[16,128,448]{1,2,0:T(8,128)(2,1)S(1)}, u32[]{:S(2)}, u32[]{:S(2)}) %all-to-all-start.1) | async-done | bytes 1835040 | tf_op jit(solution)/shard_map/all_to_all | solution.py:55
  199.7 1.0 fusion.4
  200.7 1.1 fusion.6
  201.8 0.0 copy-start
  201.8 1.2 copy-done
  203.1 0.8 fusion.10
  203.8 7.3 %convolution_convert_fusion.1 = bf16[128,7168]{1,0:T(8,128)(2,1)} fusion(bf16[1,256,7168]{2,1,0:T(8,128)(2,1)} %param.17, bf16[128,7168]{0,1:T(8,128)(2,1)} %bitcast.47, bf16[1,7168,256]{2,1,0:T(8,128)(2,1)} %param.16, f32[128,256]{1,0:T(8,128)S(1)} %fusion.10), kind=kOutput, calls=%fused_computation.1 | convolution fusion | flops 940638208 | bytes 11141120 | tf_op jit(solution)/shard_map/dot_general | solution.py:77
  211.1 3.3 %copy.46 = bf16[128,7168]{0,1:T(8,128)(2,1)S(1)} copy(bf16[128,7168]{1,0:T(8,128)(2,1)} %convolution_convert_fusion.1) | data formatting | bytes 3670016 | tf_op jit(solution)/shard_map/convert_element_type | solution.py:77
  214.4 36.1 %all_to_all.21 = bf16[16,128,448]{1,2,0:T(8,128)(2,1)} all-to-all(bf16[16,128,448]{1,2,0:T(8,128)(2,1)S(1)} %bitcast.48), channel_id=1, replica_groups=mesh['node'=8,'local'=16] {'local'}, dimensions={0} | all-to-all | bytes 3670016 | tf_op jit(solution)/shard_map/all_to_all | solution.py:79
  250.6 1.8 reduce_sum.75
  252.3 0.1 copy.47
  252.4 10.3 %all_to_all.22 = bf16[8,16,448]{2,1,0:T(8,128)(2,1)S(1)} all-to-all(bf16[8,16,448]{2,1,0:T(8,128)(2,1)S(1)} %bitcast.51), channel_id=1, replica_groups=mesh['node'=8,'local'=16] {'node'}, dimensions={0} | all-to-all | bytes 229376 | tf_op jit(solution)/shard_map/all_to_all | solution.py:81
  262.8 13.9 %reduce-scatter.2.cloned.1.call-done = bf16[1024,448]{0,1:T(8,128)(2,1)} async-done(((bf16[1024,7168]{0,1:T(8,128)(2,1)}), bf16[1024,448]{0,1:T(8,128)(2,1)}) %reduce-scatter.2.cloned.1.call-update) | async-done | bytes 917520 | tf_op jit(solution)/shard_map/reduce_scatter | solution.py:90
  276.7 2.6 fusion.14
  (12 shorter events, 0.0 us)
Async XLA Ops:
  6.5 106.3 %all-gather.2.cloned.1.call-start = ((), (), s32[]{:S(2)}) async-start(), calls=%async_computation.5 | async-start | bytes 15597568 | tf_op jit(solution)/shard_map/all_gather | solution.py:40
  7.3 269.4 %reduce-scatter.2.cloned.1.call-start = ((), (), s32[]{:S(2)}) async-start(), calls=%async_computation.6 | async-start | bytes 15597568 | tf_op jit(solution)/shard_map/reduce_scatter | solution.py:90
  135.6 0.7 copy-start.4
  136.3 5.3 %copy-start.5 = (f32[1024,2]{0,1:T(2,128)S(1)}, f32[1024,2]{0,1:T(2,128)}, u32[]{:S(2)}) copy-start(f32[1024,2]{0,1:T(2,128)} %param.19) | copy-start | bytes 24580
  136.3 6.1 %copy-start.1 = (bf16[1024,448]{0,1:T(8,128)(2,1)S(1)}, bf16[1024,448]{0,1:T(8,128)(2,1)}, u32[]{:S(2)}) copy-start(bf16[1024,448]{0,1:T(8,128)(2,1)} %param.10) | copy-start | bytes 2752516
  142.4 17.8 %copy-start.3 = (f32[7168]{0:T(1024)S(1)}, f32[7168]{0:T(1024)}, u32[]{:S(2)}) copy-start(f32[7168]{0:T(1024)} %param.11) | copy-start | bytes 86020
  154.9 44.8 %all-to-all-start.1 = ((bf16[16,128,448]{1,2,0:T(8,128)(2,1)}), bf16[16,128,448]{1,2,0:T(8,128)(2,1)S(1)}, u32[]{:S(2)}, u32[]{:S(2)}) async-start(bf16[16,128,448]{1,2,0:T(8,128)(2,1)} %broadcast_in_dim.10), calls=%async_computation.2 | async-start | bytes 3670016 | tf_op jit(solution)/shard_map/all_to_all | solution.py:55
  199.7 3.3 %copy-start.2 = (bf16[1,7168,256]{2,1,0:T(8,128)(2,1)S(1)}, bf16[1,7168,256]{2,1,0:T(8,128)(2,1)}, u32[]{:S(2)}) copy-start(bf16[1,7168,256]{2,1,0:T(8,128)(2,1)} %param.15) | copy-start | bytes 11010052
  201.8 1.2 copy-start
Sparse Core Ops, SparseCore 0:
  9.5 103.2 all-gather.1
  135.8 140.8 reduce-scatter.1

commit v2 on v1

v2 whole, which is shorter than its diff:
```python
import functools

import jax
import jax.numpy as jnp
from jax import lax
from jax.experimental import pallas as pl
from jax.experimental.pallas import tpu as pltpu
from jax.sharding import PartitionSpec as P

EPSILON = 1e-05
NODE_CAP = 16
GRAY = (0, 1, 3, 2)

LOCAL_LABEL = [GRAY[i % 4] | GRAY[i // 4] << 2 for i in range(16)]
LOCAL_AT = {label: i for i, label in enumerate(LOCAL_LABEL)}
NODE_LABEL = [i % 2 | GRAY[i // 2] << 1 for i in range(8)]
NODE_AT = {label: i for i, label in enumerate(NODE_LABEL)}

STREAMS = ((0, 1, 2), (1, 2, 0), (2, 0, 1))


def stream_rows(rows):
    third = -(-rows // 48) * 16
    return (0, third), (third, 2 * third), (2 * third, rows)


def flip_local(array, bit):
    return lax.ppermute(array, "local", [(i, LOCAL_AT[LOCAL_LABEL[i] ^ (1 << bit)]) for i in range(16)])


def flip_node(array, bit):
    return lax.ppermute(array, "node", [(i, NODE_AT[NODE_LABEL[i] ^ (1 << bit)]) for i in range(8)])


def route_slots(ids_block, window):
    flat_ids = ids_block.reshape(-1)
    expert_range = jnp.arange(window, dtype=jnp.int32)
    member = (flat_ids[:, None] == expert_range[None, :]).astype(jnp.int32)
    before = jnp.cumsum(member, axis=0) - member
    route_rank = jnp.sum(before * member, axis=1)
    kept = (jnp.sum(member, axis=1) > 0) & (route_rank < NODE_CAP)
    slot = jnp.where(kept, flat_ids * NODE_CAP + route_rank, -1)
    return slot.reshape(ids_block.shape)


def transposed_dot(weight, rows):
    return lax.dot_general(weight, rows, (((0,), (0,)), ((), ())), preferred_element_type=jnp.float32)


def silu(value):
    return value / (1.0 + jnp.exp(-value))


def gate_up_kernel(blocks, features, with_scale, pair_ref, *refs):
    if with_scale:
        x0, x1, x2, weight, scale_in, hidden_ref, total = refs
    else:
        x0, x1, x2, weight, hidden_ref, scale_out, total, squares = refs
    step = pl.program_id(0)

    @pl.when(step == 0)
    def _():
        total[...] = jnp.zeros_like(total)
        if not with_scale:
            squares[...] = jnp.zeros_like(squares)

    rows = jnp.concatenate([x0[0], x1[0], x2[0]], axis=0)
    total[...] += transposed_dot(weight[0], rows)
    if not with_scale:
        as_float = rows.astype(jnp.float32)
        squares[...] += jnp.sum(as_float * as_float, axis=0, keepdims=True)

    @pl.when(step == blocks - 1)
    def _():
        if with_scale:
            scale = scale_in[...]
        else:
            scale = lax.rsqrt(squares[...] / features + EPSILON)
            scale_out[...] = scale
        half = total.shape[0] // 2
        hidden_ref[...] = (silu(total[:half] * scale) * (total[half:] * scale)).astype(jnp.bfloat16)


def gate_up(pair_of, streams, weight, scale=None):
    blocks, _, columns = streams[0].shape
    rows = sum(s.shape[1] for s in streams)
    both = weight.shape[-1]

    def stream_spec(s):
        a, b, c = STREAMS[s]

        def index(m, pair):
            return (((m >> a) & 1) | ((m >> b) & 1) << 1 | ((m >> c) & 1) << 2, 0, 0)

        return pl.BlockSpec((1, streams[s].shape[1], columns), index)

    in_specs = [stream_spec(s) for s in range(3)]
    in_specs.append(pl.BlockSpec((1, rows, both), lambda m, pair: (pair[m], 0, 0)))
    operands = [*streams, weight.reshape(blocks, rows, both)]
    out_shape = [jax.ShapeDtypeStruct((both // 2, columns), jnp.bfloat16)]
    out_specs = [pl.BlockSpec((both // 2, columns), lambda m, pair: (0, 0))]
    scratch = [pltpu.VMEM((both, columns), jnp.float32)]
    whole_scale = pl.BlockSpec((1, columns), lambda m, pair: (0, 0))
    if scale is None:
        out_shape.append(jax.ShapeDtypeStruct((1, columns), jnp.float32))
        out_specs.append(whole_scale)
        scratch.append(pltpu.VMEM((1, columns), jnp.float32))
    else:
        in_specs.append(whole_scale)
        operands.append(scale)
    return pl.pallas_call(
        functools.partial(gate_up_kernel, blocks, blocks * rows, scale is not None),
        grid_spec=pltpu.PrefetchScalarGridSpec(
            num_scalar_prefetch=1, grid=(blocks,), in_specs=in_specs, out_specs=out_specs, scratch_shapes=scratch
        ),
        out_shape=out_shape,
        compiler_params=pltpu.CompilerParams(vmem_limit_bytes=24 << 20),
        cost_estimate=pl.CostEstimate(
            flops=2 * blocks * rows * columns * both, bytes_accessed=2 * blocks * rows * (columns + both), transcendentals=0
        ),
    )(pair_of, *operands)


def down_kernel(spans, own_pair, other_pair, *refs):
    own, other = refs[0:3], refs[3:6]
    own_hidden, other_hidden = refs[6], refs[7]
    outs = refs[8:11]
    for s, (low, high) in enumerate(spans):
        part = jnp.dot(own[s][0, low:high], own_hidden[...], preferred_element_type=jnp.float32)
        part += jnp.dot(other[s][0, low:high], other_hidden[...], preferred_element_type=jnp.float32)
        outs[s][0] = part.astype(jnp.bfloat16)


def down(own_pair, other_pair, own_weight, other_weight, own_hidden, other_hidden, sent):
    blocks, rows, hidden = own_weight.shape
    columns = own_hidden.shape[1]
    spans = stream_rows(rows)

    def mask(s, j):
        a, b, c = STREAMS[s]
        return sent << a | ((j >> 1) & 1) << b | (j & 1) << c

    def own_spec(s):
        return pl.BlockSpec((1, rows, hidden), lambda j, p, q: (p[mask(s, j)], 0, 0))

    def other_spec(s):
        return pl.BlockSpec((1, rows, hidden), lambda j, p, q: (q[mask(s, j)], 0, 0))

    hidden_spec = pl.BlockSpec((hidden, columns), lambda j, p, q: (0, 0))
    half = blocks // 2
    return pl.pallas_call(
        functools.partial(down_kernel, spans),
        grid_spec=pltpu.PrefetchScalarGridSpec(
            num_scalar_prefetch=2,
            grid=(half,),
            in_specs=[own_spec(s) for s in range(3)] + [other_spec(s) for s in range(3)] + [hidden_spec] * 2,
            out_specs=[pl.BlockSpec((1, high - low, columns), lambda j, p, q: (j, 0, 0)) for low, high in spans],
        ),
        out_shape=[jax.ShapeDtypeStruct((half, high - low, columns), jnp.bfloat16) for low, high in spans],
        compiler_params=pltpu.CompilerParams(vmem_limit_bytes=24 << 20),
        cost_estimate=pl.CostEstimate(
            flops=4 * half * rows * hidden * columns,
            bytes_accessed=2 * half * rows * (6 * hidden + columns),
            transcendentals=0,
        ),
    )(own_pair, other_pair, *[own_weight] * 3, *[other_weight] * 3, own_hidden, other_hidden)


def expert_kernel(blocks, features, at_ref, x_ref, gate_ref, up_ref, gain_ref, hidden_ref, gate_total, up_total, squares):
    step = pl.program_id(0)

    @pl.when(step == 0)
    def _():
        gate_total[...] = jnp.zeros_like(gate_total)
        up_total[...] = jnp.zeros_like(up_total)
        squares[...] = jnp.zeros_like(squares)

    as_float = x_ref[0].astype(jnp.float32)
    squares[...] += jnp.sum(as_float * as_float, axis=0, keepdims=True)
    rows = (as_float * gain_ref[...]).astype(jnp.bfloat16)
    gate_total[...] += transposed_dot(gate_ref[0], rows)
    up_total[...] += transposed_dot(up_ref[0], rows)

    @pl.when(step == blocks - 1)
    def _():
        scale = lax.rsqrt(squares[...] / features + EPSILON)
        hidden_ref[...] = (silu(gate_total[...] * scale) * (up_total[...] * scale)).astype(jnp.bfloat16)


def expert_gate_up(slice_of, pooled, gate_weight, up_weight, gain_column):
    blocks, rows, columns = pooled.shape
    hidden = gate_weight.shape[-1]
    weight_spec = pl.BlockSpec((1, rows, hidden), lambda m, at: (0, at[m], 0))
    return pl.pallas_call(
        functools.partial(expert_kernel, blocks, blocks * rows),
        grid_spec=pltpu.PrefetchScalarGridSpec(
            num_scalar_prefetch=1,
            grid=(blocks,),
            in_specs=[
                pl.BlockSpec((1, rows, columns), lambda m, at: (m, 0, 0)),
                weight_spec,
                weight_spec,
                pl.BlockSpec((rows, 1), lambda m, at: (at[m], 0)),
            ],
            out_specs=pl.BlockSpec((hidden, columns), lambda m, at: (0, 0)),
            scratch_shapes=[
                pltpu.VMEM((hidden, columns), jnp.float32),
                pltpu.VMEM((hidden, columns), jnp.float32),
                pltpu.VMEM((1, columns), jnp.float32),
            ],
        ),
        out_shape=jax.ShapeDtypeStruct((hidden, columns), jnp.bfloat16),
        compiler_params=pltpu.CompilerParams(vmem_limit_bytes=24 << 20),
        cost_estimate=pl.CostEstimate(
            flops=4 * blocks * rows * columns * hidden,
            bytes_accessed=2 * blocks * rows * (columns + 2 * hidden),
            transcendentals=0,
        ),
    )(slice_of, pooled, gate_weight, up_weight, gain_column)


def add_pair(kept, got):
    return (kept.astype(jnp.float32) + got.astype(jnp.float32)).astype(jnp.bfloat16)


def shards(
    tokens,
    norm_gain,
    dense_gate,
    dense_up,
    dense_down,
    expert_gate,
    expert_up,
    expert_down,
    expert_ids,
    route_gates,
):
    node_count = lax.axis_size("node")
    node_index = lax.axis_index("node")
    local_index = lax.axis_index("local")
    tok_node, slice_width = tokens.shape
    width = slice_width * 16
    pair_width = 2 * slice_width
    half_tokens = tok_node // 2
    slot_count = node_count * NODE_CAP
    spans = stream_rows(pair_width)

    label = jnp.asarray(LOCAL_LABEL, jnp.int32)[local_index]
    own_half = label & 1
    odd = (local_index & 1) == 1
    pair_table = [[LOCAL_AT[LOCAL_LABEL[i] ^ (2 * m)] // 2 for m in range(8)] for i in range(16)]
    pair_of = jnp.asarray(pair_table, jnp.int32)[local_index]
    slice_table = [[LOCAL_AT[LOCAL_LABEL[i] ^ m] for m in range(16)] for i in range(16)]
    slice_of = jnp.asarray(slice_table, jnp.int32)[local_index]
    place_table = [[0] * 8 for _ in range(8)]
    for i in range(8):
        for j in range(8):
            diff = NODE_LABEL[i] ^ NODE_LABEL[j]
            place_table[i][j] = ((diff >> 1) & 1) | ((diff >> 2) & 1) << 1 | (diff & 1) << 2
    other_of = jnp.asarray(place_table, jnp.int32)[node_index][pair_of]

    columns = tokens.T
    mine = lax.dynamic_slice_in_dim(columns, own_half * half_tokens, half_tokens, 1)
    give = lax.dynamic_slice_in_dim(columns, (1 - own_half) * half_tokens, half_tokens, 1)
    got = flip_local(give, 0)

    block_start = node_index * pair_width

    def folded(gate_rows, up_rows, gain_rows):
        gain_rows = gain_rows[:, None]
        return jnp.concatenate(
            [
                (gate_rows.astype(jnp.float32) * gain_rows).astype(jnp.bfloat16),
                (up_rows.astype(jnp.float32) * gain_rows).astype(jnp.bfloat16),
            ],
            axis=1,
        )

    piece = folded(
        lax.dynamic_slice_in_dim(dense_gate, block_start, pair_width, 0),
        lax.dynamic_slice_in_dim(dense_up, block_start, pair_width, 0),
        lax.dynamic_slice_in_dim(norm_gain, block_start, pair_width, 0),
    )
    piece = flip_local(piece, 0)
    other_both = lax.all_gather(piece, "node", axis=0, tiled=True)
    down_piece = flip_local(lax.dynamic_slice_in_dim(dense_down, block_start, pair_width, 1).T, 0)[None]
    for bit in (1, 2, 0):
        down_piece = jnp.concatenate([down_piece, flip_node(down_piece, bit)], axis=0)

    pair_block = jnp.where(odd, jnp.concatenate([got, mine], axis=0), jnp.concatenate([mine, got], axis=0))
    streams = [pair_block[None, low:high] for low, high in spans]
    for step in range(3):
        arrived = [flip_local(streams[s], 1 + STREAMS[s][step]) for s in range(3)]
        streams = [jnp.concatenate([streams[s], arrived[s]], axis=0) for s in range(3)]

    own_both = folded(dense_gate, dense_up, norm_gain)
    own_down = dense_down.T.reshape(8, pair_width, dense_down.shape[0])

    slot = route_slots(expert_ids, node_count)
    slot_range = jnp.arange(slot_count, dtype=jnp.int32)
    match_float = (slot[:, :, None] == slot_range[None, None, :]).astype(jnp.float32)
    chosen = jnp.sum(match_float, axis=1).astype(jnp.bfloat16)
    slot_gate = jnp.sum(match_float * route_gates[:, :, None], axis=(0, 1))
    send_rows = lax.dot_general(
        chosen, tokens, (((0,), (0,)), ((), ())), preferred_element_type=jnp.float32
    ).astype(jnp.bfloat16)
    pooled = lax.all_to_all(
        send_rows.reshape(node_count, NODE_CAP, slice_width), "node", split_axis=0, concat_axis=0, tiled=True
    )
    pooled = pooled.reshape(slot_count, slice_width).T[None]
    for bit in range(4):
        pooled = jnp.concatenate([pooled, flip_local(pooled, bit)], axis=0)
    expert_hidden = expert_gate_up(slice_of, pooled, expert_gate, expert_up, norm_gain[:, None])
    expert_partial = transposed_dot(expert_down[0], expert_hidden).astype(jnp.bfloat16)
    expert_partial = expert_partial.reshape(16, slice_width, slot_count)
    position = local_index
    for bit in (3, 2, 1, 0):
        half = 1 << bit
        upper = position // half
        keep = lax.dynamic_slice_in_dim(expert_partial, upper * half, half, 0)
        send = lax.dynamic_slice_in_dim(expert_partial, (1 - upper) * half, half, 0)
        expert_partial = add_pair(keep, flip_local(send, bit))
        position = position - upper * half
    expert_out = expert_partial[0].T
    returned = lax.all_to_all(
        expert_out.reshape(node_count, NODE_CAP, slice_width), "node", split_axis=0, concat_axis=0, tiled=True
    ).reshape(slot_count, slice_width)
    route_term = (slot_gate[:, None] * returned.astype(jnp.float32)).astype(jnp.bfloat16)
    expert_part = lax.dot_general(
        route_term, chosen, (((0,), (1,)), ((), ())), preferred_element_type=jnp.float32
    )

    own_hidden, scale = gate_up(pair_of, streams, own_both)
    (other_hidden,) = gate_up(pair_of, streams, other_both, scale)
    sent = down(pair_of, other_of, own_down, down_piece, own_hidden, other_hidden, 1)
    arrived = [flip_local(sent[s], 1 + STREAMS[s][0]) for s in range(3)]
    kept = down(pair_of, other_of, own_down, down_piece, own_hidden, other_hidden, 0)
    sums = [add_pair(kept[s], arrived[s]) for s in range(3)]
    for step in (1, 2):
        half = sums[0].shape[0] // 2
        arrived = [flip_local(sums[s][half:], 1 + STREAMS[s][step]) for s in range(3)]
        sums = [add_pair(sums[s][:half], arrived[s]) for s in range(3)]
    pair_sum = jnp.concatenate([sums[s][0] for s in range(3)], axis=0)
    even_rows, odd_rows = pair_sum[:slice_width], pair_sum[slice_width:]
    mine = jnp.where(odd, odd_rows, even_rows)
    got = flip_local(jnp.where(odd, even_rows, odd_rows), 0)
    dense_part = jnp.where(
        own_half == 1, jnp.concatenate([got, mine], axis=1), jnp.concatenate([mine, got], axis=1)
    ).astype(jnp.float32)
    return (columns.astype(jnp.float32) + dense_part + expert_part).astype(jnp.bfloat16).T


def solution(mesh):
    return jax.shard_map(
        shards,
        mesh=mesh,
        in_specs=(
            P("node", "local"),
            P(),
            P(None, "local"),
            P(None, "local"),
            P("local", None),
            P("node", None, "local"),
            P("node", None, "local"),
            P("node", "local", None),
            P("node", None),
            P("node", None),
        ),
        out_specs=P("node", "local"),
        check_vma=False,
    )
```

time: 287 us -> 283 us (0.986)
  blocking collectives: 99 us -> 0 us
  starting transfers between devices: 5.34 us -> 58 us
  matrix products: 33.9 us -> 3.87 us
  other arithmetic: 15.5 us -> 44.5 us
  Pallas kernels: 0 us -> 28.4 us
  local copies, waits for them, and re-layouts: 9.71 us -> 35.9 us
  waiting for transfers between devices: 109 us -> 95.7 us
    ppermute x0 -> x33, waiting for transfers between devices: none -> 89.5 us  [the longest x30 88.4 us: flip_local(): lax.ppermute(array, 'local', [(i, LOCAL_AT[LOCAL_LABEL[i] ^ 1 << bit]) fo...]
    all_to_all x3 -> x0, blocking collectives: 56.6 us -> none  [the longest x1 36.1 us: shards(): lax.all_to_all(partial_blocks, 'local', split_axis=0, concat_axis=0, tile...]
    all_gather x1, waiting for transfers between devices: 54.9 us -> 0.01 us  [shards(): other_both = lax.all_gather(piece, 'node', axis=0, tiled=True)]
    ppermute x0 -> x33, starting transfers between devices: none -> 49.3 us  [the longest x30 44.3 us: flip_local(): lax.ppermute(array, 'local', [(i, LOCAL_AT[LOCAL_LABEL[i] ^ 1 << bit]) fo...]
    psum x1 -> x0, blocking collectives: 42.4 us -> none  [shards(): square_sum = lax.psum(jnp.sum(as_float * as_float, axis=-1), 'local')]
    all_to_all x1 -> x2, waiting for transfers between devices: 39.5 us -> 6.14 us  [the longest x1 6.14 us: shards(): lax.all_to_all(expert_out.reshape(node_count, NODE_CAP, slice_width), 'no...]
    dot_general x5 -> x2, matrix products: 33.5 us -> 3.46 us  [the longest x1 1.96 us: transposed_dot(): lax.dot_general(weight, rows, (((0,), (0,)), ((), ())), preferred_element...]
    pallas_call x0 -> x5, Pallas kernels: none -> 28.4 us  [the longest x2 13.9 us: gate_up(): pl.pallas_call(functools.partial(gate_up_kernel, blocks, blocks * rows, s...]
  transfers between devices with their start and end apart: 3 -> 36, of which waited for: 3 -> 19; matrix products, arithmetic and copies ran while one was open for 11% -> 24% of each run, Pallas kernels for 0% -> 10%
where the time goes in v2:
time: 283 us; the launch traced here: 281 us
  waiting for transfers between devices  95.7 us (34%)
  starting transfers between devices  58 us (20%)
  other arithmetic  44.5 us (16%)
  local copies, waits for them, and re-layouts  35.9 us (13%)
  Pallas kernels  28.4 us (10%)
  between operations  14.8 us (5%)
  matrix products  3.87 us (1%)
    ppermute x30, waiting for transfers between devices, flip_local(): lax.ppermute(array, 'local', [(i, LOCAL_AT[LOCAL_LABEL[i] ^ 1 << bit]) fo...  88.4 us
    ppermute x30, starting transfers between devices, flip_local(): lax.ppermute(array, 'local', [(i, LOCAL_AT[LOCAL_LABEL[i] ^ 1 << bit]) fo...  44.3 us
    pallas_call x2, Pallas kernels, gate_up(): pl.pallas_call(functools.partial(gate_up_kernel, blocks, blocks * rows, s...  13.9 us
    unnamed x92, local copies, waits for them, and re-layouts  13.7 us
    concatenate x9, other arithmetic, shards(): jnp.concatenate([streams[s], arrived[s]], axis=0)  9.35 us
    convert_element_type x9, other arithmetic, add_pair(): (kept.astype(jnp.float32) + got.astype(jnp.float32)).astype(jnp.bfloat16)  8.11 us
    convert_element_type x2, other arithmetic, folded(): (gate_rows.astype(jnp.float32) * gain_rows).astype(jnp.bfloat16)  7.7 us
    pallas_call x1, Pallas kernels, expert_gate_up(): pl.pallas_call(functools.partial(expert_kernel, blocks, blocks * rows), g...  7.45 us
  transfers between devices with their start and end apart: 36, of which 19 were waited for; matrix products, arithmetic and copies ran while one was open for 24% of the time, Pallas kernels for 10%

profile of v2, /device:TPU:0, one launch (start us, length us, event | category | flops | bytes accessed | tf_op | source)
XLA Modules:
  0.0 281.3 jit_solution(676089900897018978)
XLA Ops:
  10.6 20.3 %collective-permute-done.14 = bf16[896,512]{1,0:T(8,128)(2,1)S(1)} collective-permute-done((bf16[896,512]{1,0:T(8,128)(2,1)S(1)}, bf16[896,512]{1,0:T(8,128)(2,1)S(1)}, u32[]{:S(2)}, u32[]{:S(2)}) %collective-permute-start.14) | collective-permute-done | bytes 917536 | tf_op jit(solution)/shard_map/ppermute | solution.py:28
  32.7 2.3 reduce-window.6
  39.9 4.5 %all-to-all-start = ((bf16[8,16,448]{2,1,0:T(8,128)(2,1)}), bf16[8,16,448]{2,1,0:T(8,128)(2,1)S(1)}, u32[]{:S(2)}, u32[]{:S(2)}) async-start(bf16[8,16,448]{2,1,0:T(8,128)(2,1)} %bitcast.24), calls=%async_computation | async-start | bytes 262144 | tf_op jit(solution)/shard_map/all_to_all | solution.py:307
  50.6 6.3 %multiply_convert_fusion.1 = (bf16[7168,256]{1,0:T(8,128)(2,1)S(1)}, bf16[7168,256]{1,0:T(8,128)(2,1)}) fusion(bf16[7168,256]{1,0:T(8,128)(2,1)} %param.16, f32[7168]{0:T(1024)S(1)} %copy-done.37, bf16[7168,256]{1,0:T(8,128)(2,1)} %param.17), kind=kLoop, calls=%fused_computation.5 | loop fusion | flops 11010048 | bytes 14708736 | tf_op jit(solution)/shard_map/convert_element_type | solution.py:273
  56.9 5.5 %pad_maximum_fusion = bf16[7168,512]{1,0:T(8,128)(2,1)} fusion(bf16[7168,256]{1,0:T(8,128)(2,1)} %get-tuple-element.32, bf16[7168,256]{1,0:T(8,128)(2,1)S(1)} %get-tuple-element.31), kind=kLoop, calls=%fused_computation.3 | loop fusion | flops 14680064 | bytes 14680064 | tf_op jit(solution)/shard_map/concatenate | solution.py:271
  65.6 2.4 copy.51.gain_ref
  68.0 5.9 %copy.42 = bf16[7168,256]{1,0:T(8,128)(2,1)} copy(bf16[7168,256]{0,1:T(8,128)(2,1)} %bitcast.92) | data formatting | bytes 7340032 | tf_op jit(solution)/shard_map/transpose | solution.py:297
  75.3 2.3 collective-permute-start.26
  79.1 4.1 %collective-permute-start.11 = (bf16[1,288,512]{2,1,0:T(8,128)(2,1)S(1)}, bf16[1,288,512]{2,1,0:T(8,128)(2,1)S(1)}, u32[]{:S(2)}, u32[]{:S(2)}) collective-permute-start(bf16[1,288,512]{2,1,0:T(8,128)(2,1)S(1)} %slice_bitcast_fusion.2), channel_id=1, source_target_pairs={{0,12},{1,13},{2,14},{3,15},{4,8},{5,9},{6,10},{7,11},{8,4},{9,5},... | collective-permute-start | bytes 884744 | tf_op jit(solution)/shard_map/ppermute | solution.py:28
  83.4 2.1 collective-permute-start.1
  85.5 2.0 collective-permute-start.27
  91.0 2.7 collective-permute-done.8
  96.5 3.0 %collective-permute-start.2 = (bf16[2,896,256]{2,1,0:T(8,128)(2,1)S(1)}, bf16[2,896,256]{2,1,0:T(8,128)(2,1)S(1)}, u32[]{:S(2)}, u32[]{:S(2)}) collective-permute-start(bf16[2,896,256]{2,1,0:T(8,128)(2,1)S(1)} %pad_maximum_fusion.9), channel_id=1, source_target_pairs={{0,96},{16,112},{32,64},{48,80},{64,32},{80,48},{96,0},{112,16},{1... | collective-permute-start | bytes 2752520 | tf_op jit(solution)/shard_map/ppermute | solution.py:32
  101.2 2.0 collective-permute-done.27
  103.9 4.5 %collective-permute-done.12 = bf16[2,288,512]{2,1,0:T(8,128)(2,1)S(1)} collective-permute-done((bf16[2,288,512]{2,1,0:T(8,128)(2,1)S(1)}, bf16[2,288,512]{2,1,0:T(8,128)(2,1)S(1)}, u32[]{:S(2)}, u32[]{:S(2)}) %collective-permute-start.12) | collective-permute-done | bytes 589856 | tf_op jit(solution)/shard_map/ppermute | solution.py:28
  111.6 2.5 collective-permute-start.10
  114.1 2.5 collective-permute-done.6
  119.6 2.8 %pad_maximum_fusion.5 = bf16[4,896,256]{2,1,0:T(8,128)(2,1)} fusion(bf16[2,896,256]{2,1,0:T(8,128)(2,1)S(1)} %collective-permute-done.2, bf16[1,896,256]{2,1,0:T(8,128)(2,1)S(1)} %collective-permute-done.1, bf16[1,896,256]{2,1,0:T(8,128)(2,1)} %bitcast.9), kind=kLoop, calls=%fused_computation.14 | loop fusion | flops 1835008 | bytes 3670016 | tf_op jit(solution)/shard_map/concatenate | solution.py:288
  122.5 7.6 %collective-permute-done.28 = bf16[8,448,128]{2,1,0:T(8,128)(2,1)S(1)} collective-permute-done((bf16[8,448,128]{2,1,0:T(8,128)(2,1)S(1)}, bf16[8,448,128]{2,1,0:T(8,128)(2,1)S(1)}, u32[]{:S(2)}, u32[]{:S(2)}) %collective-permute-start.28) | collective-permute-done | bytes 917536 | tf_op jit(solution)/shard_map/ppermute | solution.py:28
  130.3 7.4 %shard_map.140 = bf16[256,128]{1,0:T(8,128)(2,1)S(1)} custom-call(s32[16]{0:T(128)S(1)} %fusion.22.at_ref, bf16[16,448,128]{2,1,0:T(8,128)(2,1)S(1)} %constant_dynamic-update-slice_fusion.x_ref, bf16[1,7168,256]{2,1,0:T(8,128)(2,1)S(1)} %copy-done.10, bf16[1,7168,256]{2,1,0:T(8,128)(2,1)S(1)} %copy-done.11, f32[7168,1]{1,0:T(8,128)S(1)} %copy-done.8), custom_call_target="tpu_custom_call" | custom-call | flops 939524096 | bytes 9175040 | tf_op jit(solution)/shard_map/pallas_call | solution.py:194
  137.7 2.0 fusion
  139.7 3.3 %copy.52 = bf16[7168,128]{1,0:T(8,128)(2,1)S(1)} copy(bf16[7168,128]{0,1:T(8,128)(2,1)} %fusion) | data formatting | bytes 3670016 | tf_op jit(solution)/shard_map/convert_element_type | solution.py:314
  147.6 2.4 pad_maximum_fusion.3.refs_1_
  150.1 6.8 %collective-permute-done.7 = bf16[4,304,512]{2,1,0:T(8,128)(2,1)} collective-permute-done((bf16[4,304,512]{2,1,0:T(8,128)(2,1)}, bf16[4,304,512]{2,1,0:T(8,128)(2,1)}, u32[]{:S(2)}, u32[]{:S(2)}) %collective-permute-start.7) | collective-permute-done | bytes 1245216 | tf_op jit(solution)/shard_map/ppermute | solution.py:28
  158.5 6.9 %shard_map.136 = (bf16[256,512]{1,0:T(8,128)(2,1)S(1)}, f32[1,512]{1,0:T(1,128)S(1)}) custom-call(s32[8]{0:T(128)S(1)} %fusion.23.pair_ref.own_pair, bf16[8,304,512]{2,1,0:T(8,128)(2,1)S(1)} %pad_maximum_fusion.2.refs_0_, bf16[8,304,512]{2,1,0:T(8,128)(2,1)S(1)} %pad_maximum_fusion.3.refs_1_, bf16[8,288,512]{2,1,0:T(8,128)(2,1)S(1)} %pad_maximum_fusion.4.refs_2_, ...), custom_call_target="tpu_custom_call" | custom-call | flops 3758096384 | bytes 14680064 | tf_op jit(solution)/shard_map/pallas_call | solution.py:111
  165.5 3.3 %pad_maximum_fusion.1.refs_3_.refs_4_.refs_5_ = bf16[8,896,256]{2,1,0:T(8,128)(2,1)} fusion(bf16[4,896,256]{2,1,0:T(8,128)(2,1)} %collective-permute-done.3, bf16[2,896,256]{2,1,0:T(8,128)(2,1)S(1)} %copy-done.17, bf16[1,896,256]{2,1,0:T(8,128)(2,1)S(1)} %copy-done.15, bf16[1,896,256]{2,1,0:T(8,128)(2,1)} %bitcast.9), kind=kLoop, calls=%fused_computation.6 | loop fusion | flops 5505024 | bytes 7340032 | tf_op jit(solution)/shard_map/concatenate | solution.py:288
  172.1 3.1 %copy-done.9 = bf16[7168,512]{1,0:T(8,128)(2,1)S(1)} copy-done((bf16[7168,512]{1,0:T(8,128)(2,1)S(1)}, bf16[7168,512]{1,0:T(8,128)(2,1)}, u32[]{:S(2)}) %copy-start.9) | copy-done | bytes 7340056
  175.2 6.9 %shard_map.137.refs_7_ = bf16[256,512]{1,0:T(8,128)(2,1)S(1)} custom-call(s32[8]{0:T(128)S(1)} %fusion.23.pair_ref.own_pair, bf16[8,304,512]{2,1,0:T(8,128)(2,1)S(1)} %copy-done.5, bf16[8,304,512]{2,1,0:T(8,128)(2,1)S(1)} %pad_maximum_fusion.3.refs_1_, bf16[8,288,512]{2,1,0:T(8,128)(2,1)S(1)} %copy-done.7, bf16[8,896,512]{2,1,0:T(8,128)(2,1)S(1)} %bitcast.89, ...), custom_call_target="tpu_custom_call" | custom-call | flops 3758096384 | bytes 14680064 | tf_op jit(solution)/shard_map/pallas_call | solution.py:111
  182.2 4.0 %shard_map.139 = (bf16[4,304,512]{2,1,0:T(8,128)(2,1)S(1)}, bf16[4,304,512]{2,1,0:T(8,128)(2,1)S(1)}, bf16[4,288,512]{2,1,0:T(8,128)(2,1)}) custom-call(s32[8]{0:T(128)S(1)} %fusion.23.pair_ref.own_pair, s32[8]{0:T(128)S(1)} %gather_fusion, bf16[8,896,256]{2,1,0:T(8,128)(2,1)S(1)} %bitcast.80, bf16[8,896,256]{2,1,0:T(8,128)(2,1)S(1)} %bitcast.81, ...), custom_call_target="tpu_custom_call" | custom-call | flops 1879048192 | bytes 14680064 | tf_op jit(solution)/shard_map/pallas_call | solution.py:151
  186.2 1.8 collective-permute-start.21
  189.6 2.3 collective-permute-start.15
  191.9 1.9 collective-permute-start.18
  193.8 9.3 %collective-permute-done.30 = bf16[4,448,128]{2,1,0:T(8,128)(2,1)} collective-permute-done((bf16[4,448,128]{2,1,0:T(8,128)(2,1)S(1)}, bf16[4,448,128]{2,1,0:T(8,128)(2,1)}, u32[]{:S(2)}, u32[]{:S(2)}) %collective-permute-start.30) | collective-permute-done | bytes 458784 | tf_op jit(solution)/shard_map/ppermute | solution.py:28
  204.5 2.3 collective-permute-start.31
  206.7 2.0 copy-done.1
  208.8 2.0 copy-done.3
  210.8 3.1 %shard_map.138 = (bf16[4,304,512]{2,1,0:T(8,128)(2,1)S(1)}, bf16[4,304,512]{2,1,0:T(8,128)(2,1)S(1)}, bf16[4,288,512]{2,1,0:T(8,128)(2,1)S(1)}) custom-call(s32[8]{0:T(128)S(1)} %fusion.23.pair_ref.own_pair, s32[8]{0:T(128)S(1)} %gather_fusion, bf16[8,896,256]{2,1,0:T(8,128)(2,1)S(1)} %bitcast.83, bf16[8,896,256]{2,1,0:T(8,128)(2,1)S(1)} %bitcast.84, ...), custom_call_target="tpu_custom_call" | custom-call | flops 1879048192 | bytes 14680064 | tf_op jit(solution)/shard_map/pallas_call | solution.py:151
  216.7 4.6 %collective-permute-done.15 = bf16[4,304,512]{2,1,0:T(8,128)(2,1)} collective-permute-done((bf16[4,304,512]{2,1,0:T(8,128)(2,1)S(1)}, bf16[4,304,512]{2,1,0:T(8,128)(2,1)}, u32[]{:S(2)}, u32[]{:S(2)}) %collective-permute-start.15) | collective-permute-done | bytes 1245216 | tf_op jit(solution)/shard_map/ppermute | solution.py:28
  223.0 2.0 collective-permute-start.16
  225.0 4.8 %collective-permute-done.18 = bf16[4,304,512]{2,1,0:T(8,128)(2,1)} collective-permute-done((bf16[4,304,512]{2,1,0:T(8,128)(2,1)S(1)}, bf16[4,304,512]{2,1,0:T(8,128)(2,1)}, u32[]{:S(2)}, u32[]{:S(2)}) %collective-permute-start.18) | collective-permute-done | bytes 1245216 | tf_op jit(solution)/shard_map/ppermute | solution.py:28
  233.9 5.3 %collective-permute-done.16 = bf16[2,304,512]{2,1,0:T(8,128)(2,1)S(1)} collective-permute-done((bf16[2,304,512]{2,1,0:T(8,128)(2,1)S(1)}, bf16[2,304,512]{2,1,0:T(8,128)(2,1)S(1)}, u32[]{:S(2)}, u32[]{:S(2)}) %collective-permute-start.16) | collective-permute-done | bytes 622624 | tf_op jit(solution)/shard_map/ppermute | solution.py:28
  240.2 3.1 %collective-permute-done.19 = bf16[2,304,512]{2,1,0:T(8,128)(2,1)S(1)} collective-permute-done((bf16[2,304,512]{2,1,0:T(8,128)(2,1)S(1)}, bf16[2,304,512]{2,1,0:T(8,128)(2,1)S(1)}, u32[]{:S(2)}, u32[]{:S(2)}) %collective-permute-start.19) | collective-permute-done | bytes 622624 | tf_op jit(solution)/shard_map/ppermute | solution.py:28
  243.5 2.5 collective-permute-start.20
  247.7 4.0 %collective-permute-done.20 = bf16[1,304,512]{2,1,0:T(8,128)(2,1)S(1)} collective-permute-done((bf16[1,304,512]{2,1,0:T(8,128)(2,1)S(1)}, bf16[1,304,512]{2,1,0:T(8,128)(2,1)S(1)}, u32[]{:S(2)}, u32[]{:S(2)}) %collective-permute-start.20) | collective-permute-done | bytes 311328 | tf_op jit(solution)/shard_map/ppermute | solution.py:28
  252.1 2.1 collective-permute-start.32
  254.2 7.6 %collective-permute-done.32 = bf16[1,448,128]{2,1,0:T(8,128)(2,1)S(1)} collective-permute-done((bf16[1,448,128]{2,1,0:T(8,128)(2,1)S(1)}, bf16[1,448,128]{2,1,0:T(8,128)(2,1)S(1)}, u32[]{:S(2)}, u32[]{:S(2)}) %collective-permute-start.32) | collective-permute-done | bytes 114720 | tf_op jit(solution)/shard_map/ppermute | solution.py:28
  262.6 4.2 %all-to-all-start.1 = ((bf16[8,16,448]{2,1,0:T(8,128)(2,1)}), bf16[8,16,448]{2,1,0:T(8,128)(2,1)S(1)}, u32[]{:S(2)}, u32[]{:S(2)}) async-start(bf16[8,16,448]{2,1,0:T(8,128)(2,1)} %bitcast.35), calls=%async_computation.1 | async-start | bytes 262144 | tf_op jit(solution)/shard_map/all_to_all | solution.py:325
  266.8 6.1 %all-to-all-done.1 = bf16[8,16,448]{2,1,0:T(8,128)(2,1)S(1)} async-done(((bf16[8,16,448]{2,1,0:T(8,128)(2,1)}), bf16[8,16,448]{2,1,0:T(8,128)(2,1)S(1)}, u32[]{:S(2)}, u32[]{:S(2)}) %all-to-all-start.1) | async-done | bytes 114720 | tf_op jit(solution)/shard_map/all_to_all | solution.py:325
  (205 shorter events, 63.8 us)
Async XLA Ops:
  6.5 162.2 %all-gather.2.cloned.1.call-start = ((), (), s32[]{:S(2)}) async-start(), calls=%async_computation.2 | async-start | bytes 8257536 | tf_op jit(solution)/shard_map/all_gather | solution.py:285
  8.7 23.2 %copy-start.38 = (s32[1024,2]{0,1:T(2,128)S(1)}, s32[1024,2]{0,1:T(2,128)}, u32[]{:S(2)}) copy-start(s32[1024,2]{0,1:T(2,128)} %param.22) | copy-start | bytes 24580
  8.8 22.1 %collective-permute-start.14 = (bf16[896,512]{1,0:T(8,128)(2,1)S(1)}, bf16[896,512]{1,0:T(8,128)(2,1)S(1)}, u32[]{:S(2)}, u32[]{:S(2)}) collective-permute-start(bf16[896,512]{1,0:T(8,128)(2,1)S(1)} %pad_maximum_fusion.10), channel_id=1, source_target_pairs={{0,1},{1,0},{2,3},{3,2},{4,5},{5,4},{6,7},{7,6},{8,9},{9,8},{10,11... | collective-permute-start | bytes 2752520 | tf_op jit(solution)/shard_map/ppermute | solution.py:28
  39.9 23.9 %all-to-all-start = ((bf16[8,16,448]{2,1,0:T(8,128)(2,1)}), bf16[8,16,448]{2,1,0:T(8,128)(2,1)S(1)}, u32[]{:S(2)}, u32[]{:S(2)}) async-start(bf16[8,16,448]{2,1,0:T(8,128)(2,1)} %bitcast.24), calls=%async_computation | async-start | bytes 262144 | tf_op jit(solution)/shard_map/all_to_all | solution.py:307
  45.8 31.8 %collective-permute-start.4 = (bf16[448,512]{1,0:T(8,128)(2,1)S(1)}, bf16[448,512]{1,0:T(8,128)(2,1)}, u32[]{:S(2)}, u32[]{:S(2)}) collective-permute-start(bf16[448,512]{1,0:T(8,128)(2,1)S(1)} %get-tuple-element.29), channel_id=1, source_target_pairs={{0,1},{1,0},{2,3},{3,2},{4,5},{5,4},{6,7},{7,6},{8,9},{9,8},{10,11... | collective-permute-start | bytes 1376264 | tf_op jit(solution)/shard_map/ppermute | solution.py:28
  49.5 33.9 %collective-permute-start = (bf16[896,256]{1,0:T(8,128)(2,1)}, bf16[896,256]{1,0:T(8,128)(2,1)}, u32[]{:S(2)}, u32[]{:S(2)}) collective-permute-start(bf16[896,256]{1,0:T(8,128)(2,1)} %bitcast.8), channel_id=1, source_target_pairs={{0,1},{1,0},{2,3},{3,2},{4,5},{5,4},{6,7},{7,6},{8,9},{9,8},{10,11... | collective-permute-start | bytes 1376264 | tf_op jit(solution)/shard_map/ppermute | solution.py:28
  64.0 11.2 %collective-permute-start.25 = (bf16[1,448,128]{2,1,0:T(8,128)(2,1)S(1)}, bf16[1,448,128]{2,1,0:T(8,128)(2,1)S(1)}, u32[]{:S(2)}, u32[]{:S(2)}) collective-permute-start(bf16[1,448,128]{2,1,0:T(8,128)(2,1)S(1)} %bitcast.93), channel_id=1, source_target_pairs={{0,1},{1,0},{2,3},{3,2},{4,5},{5,4},{6,7},{7,6},{8,9},{9,8},{10,11... | collective-permute-start | bytes 344072 | tf_op jit(solution)/shard_map/ppermute | solution.py:28
  75.3 10.2 %collective-permute-start.26 = (bf16[2,448,128]{2,1,0:T(8,128)(2,1)S(1)}, bf16[2,448,128]{2,1,0:T(8,128)(2,1)S(1)}, u32[]{:S(2)}, u32[]{:S(2)}) collective-permute-start(bf16[2,448,128]{2,1,0:T(8,128)(2,1)S(1)} %pad_maximum_fusion.18), channel_id=1, source_target_pairs={{0,3},{1,2},{2,1},{3,0},{4,7},{5,6},{6,5},{7,4},{8,11},{9,10},{10,... | collective-permute-start | bytes 688136 | tf_op jit(solution)/shard_map/ppermute | solution.py:28
  79.1 10.7 %collective-permute-start.11 = (bf16[1,288,512]{2,1,0:T(8,128)(2,1)S(1)}, bf16[1,288,512]{2,1,0:T(8,128)(2,1)S(1)}, u32[]{:S(2)}, u32[]{:S(2)}) collective-permute-start(bf16[1,288,512]{2,1,0:T(8,128)(2,1)S(1)} %slice_bitcast_fusion.2), channel_id=1, source_target_pairs={{0,12},{1,13},{2,14},{3,15},{4,8},{5,9},{6,10},{7,11},{8,4},{9,5},... | collective-permute-start | bytes 884744 | tf_op jit(solution)/shard_map/ppermute | solution.py:28
  83.3 10.4 %collective-permute-start.8 = (bf16[1,304,512]{2,1,0:T(8,128)(2,1)S(1)}, bf16[1,304,512]{2,1,0:T(8,128)(2,1)S(1)}, u32[]{:S(2)}, u32[]{:S(2)}) collective-permute-start(bf16[1,304,512]{2,1,0:T(8,128)(2,1)S(1)} %get-tuple-element.27), channel_id=1, source_target_pairs={{0,4},{1,5},{2,6},{3,7},{4,0},{5,1},{6,2},{7,3},{8,12},{9,13},{10,... | collective-permute-start | bytes 933896 | tf_op jit(solution)/shard_map/ppermute | solution.py:28
  83.4 11.8 %collective-permute-start.1 = (bf16[1,896,256]{2,1,0:T(8,128)(2,1)}, bf16[1,896,256]{2,1,0:T(8,128)(2,1)S(1)}, u32[]{:S(2)}, u32[]{:S(2)}) collective-permute-start(bf16[1,896,256]{2,1,0:T(8,128)(2,1)} %bitcast.9), channel_id=1, source_target_pairs={{0,32},{16,48},{32,0},{48,16},{64,96},{80,112},{96,64},{112,80},{1... | collective-permute-start | bytes 1376264 | tf_op jit(solution)/shard_map/ppermute | solution.py:32
  85.5 17.7 %collective-permute-start.27 = (bf16[4,448,128]{2,1,0:T(8,128)(2,1)S(1)}, bf16[4,448,128]{2,1,0:T(8,128)(2,1)S(1)}, u32[]{:S(2)}, u32[]{:S(2)}) collective-permute-start(bf16[4,448,128]{2,1,0:T(8,128)(2,1)S(1)} %pad_maximum_fusion.17), channel_id=1, source_target_pairs={{0,4},{1,5},{2,6},{3,7},{4,0},{5,1},{6,2},{7,3},{8,12},{9,13},{10,... | collective-permute-start | bytes 1376264 | tf_op jit(solution)/shard_map/ppermute | solution.py:28
  87.5 11.9 %collective-permute-start.5 = (bf16[1,304,512]{2,1,0:T(8,128)(2,1)S(1)}, bf16[1,304,512]{2,1,0:T(8,128)(2,1)S(1)}, u32[]{:S(2)}, u32[]{:S(2)}) collective-permute-start(bf16[1,304,512]{2,1,0:T(8,128)(2,1)S(1)} %get-tuple-element.28), channel_id=1, source_target_pairs={{0,3},{1,2},{2,1},{3,0},{4,7},{5,6},{6,5},{7,4},{8,11},{9,10},{10,... | collective-permute-start | bytes 933896 | tf_op jit(solution)/shard_map/ppermute | solution.py:28
  89.8 18.7 %copy-start.26 = (bf16[1,288,512]{2,1,0:T(8,128)(2,1)}, bf16[1,288,512]{2,1,0:T(8,128)(2,1)S(1)}, u32[]{:S(2)}) copy-start(bf16[1,288,512]{2,1,0:T(8,128)(2,1)S(1)} %collective-permute-done.11) | copy-start | bytes 884740
  89.9 18.6 %collective-permute-start.12 = (bf16[2,288,512]{2,1,0:T(8,128)(2,1)S(1)}, bf16[2,288,512]{2,1,0:T(8,128)(2,1)S(1)}, u32[]{:S(2)}, u32[]{:S(2)}) collective-permute-start(bf16[2,288,512]{2,1,0:T(8,128)(2,1)S(1)} %pad_maximum_fusion.14), channel_id=1, source_target_pairs={{0,3},{1,2},{2,1},{3,0},{4,7},{5,6},{6,5},{7,4},{8,11},{9,10},{10,... | collective-permute-start | bytes 1769480 | tf_op jit(solution)/shard_map/ppermute | solution.py:28
  93.7 16.8 %copy-start.22 = (bf16[1,304,512]{2,1,0:T(8,128)(2,1)}, bf16[1,304,512]{2,1,0:T(8,128)(2,1)S(1)}, u32[]{:S(2)}) copy-start(bf16[1,304,512]{2,1,0:T(8,128)(2,1)S(1)} %collective-permute-done.8) | copy-start | bytes 933892
  93.7 16.7 %collective-permute-start.9 = (bf16[2,304,512]{2,1,0:T(8,128)(2,1)S(1)}, bf16[2,304,512]{2,1,0:T(8,128)(2,1)S(1)}, u32[]{:S(2)}, u32[]{:S(2)}) collective-permute-start(bf16[2,304,512]{2,1,0:T(8,128)(2,1)S(1)} %pad_maximum_fusion.13), channel_id=1, source_target_pairs={{0,12},{1,13},{2,14},{3,15},{4,8},{5,9},{6,10},{7,11},{8,4},{9,5},... | collective-permute-start | bytes 1867784 | tf_op jit(solution)/shard_map/ppermute | solution.py:28
  95.2 24.3 %copy-start.14 = (bf16[1,896,256]{2,1,0:T(8,128)(2,1)}, bf16[1,896,256]{2,1,0:T(8,128)(2,1)S(1)}, u32[]{:S(2)}) copy-start(bf16[1,896,256]{2,1,0:T(8,128)(2,1)S(1)} %collective-permute-done.1) | copy-start | bytes 1376260
  96.5 23.1 %collective-permute-start.2 = (bf16[2,896,256]{2,1,0:T(8,128)(2,1)S(1)}, bf16[2,896,256]{2,1,0:T(8,128)(2,1)S(1)}, u32[]{:S(2)}, u32[]{:S(2)}) collective-permute-start(bf16[2,896,256]{2,1,0:T(8,128)(2,1)S(1)} %pad_maximum_fusion.9), channel_id=1, source_target_pairs={{0,96},{16,112},{32,64},{48,80},{64,32},{80,48},{96,0},{112,16},{1... | collective-permute-start | bytes 2752520 | tf_op jit(solution)/shard_map/ppermute | solution.py:32
  99.4 17.2 %copy-start.24 = (bf16[1,304,512]{2,1,0:T(8,128)(2,1)}, bf16[1,304,512]{2,1,0:T(8,128)(2,1)S(1)}, u32[]{:S(2)}) copy-start(bf16[1,304,512]{2,1,0:T(8,128)(2,1)S(1)} %collective-permute-done.5) | copy-start | bytes 933892
  99.5 17.1 %collective-permute-start.6 = (bf16[2,304,512]{2,1,0:T(8,128)(2,1)S(1)}, bf16[2,304,512]{2,1,0:T(8,128)(2,1)S(1)}, u32[]{:S(2)}, u32[]{:S(2)}) collective-permute-start(bf16[2,304,512]{2,1,0:T(8,128)(2,1)S(1)} %pad_maximum_fusion.12), channel_id=1, source_target_pairs={{0,4},{1,5},{2,6},{3,7},{4,0},{5,1},{6,2},{7,3},{8,12},{9,13},{10,... | collective-permute-start | bytes 1867784 | tf_op jit(solution)/shard_map/ppermute | solution.py:28
  103.4 26.7 %collective-permute-start.28 = (bf16[8,448,128]{2,1,0:T(8,128)(2,1)S(1)}, bf16[8,448,128]{2,1,0:T(8,128)(2,1)S(1)}, u32[]{:S(2)}, u32[]{:S(2)}) collective-permute-start(bf16[8,448,128]{2,1,0:T(8,128)(2,1)S(1)} %pad_maximum_fusion.11), channel_id=1, source_target_pairs={{0,12},{1,13},{2,14},{3,15},{4,8},{5,9},{6,10},{7,11},{8,4},{9,5},... | collective-permute-start | bytes 2752520 | tf_op jit(solution)/shard_map/ppermute | solution.py:28
  109.7 36.2 %collective-permute-start.13 = (bf16[4,288,512]{2,1,0:T(8,128)(2,1)}, bf16[4,288,512]{2,1,0:T(8,128)(2,1)}, u32[]{:S(2)}, u32[]{:S(2)}) collective-permute-start(bf16[4,288,512]{2,1,0:T(8,128)(2,1)} %pad_maximum_fusion.8), channel_id=1, source_target_pairs={{0,4},{1,5},{2,6},{3,7},{4,0},{5,1},{6,2},{7,3},{8,12},{9,13},{10,... | collective-permute-start | bytes 3538952 | tf_op jit(solution)/shard_map/ppermute | solution.py:28
  110.4 19.8 %copy-start.11 = (bf16[1,7168,256]{2,1,0:T(8,128)(2,1)S(1)}, bf16[1,7168,256]{2,1,0:T(8,128)(2,1)}, u32[]{:S(2)}) copy-start(bf16[1,7168,256]{2,1,0:T(8,128)(2,1)} %up_ref.1) | copy-start | bytes 11010052
  111.6 36.0 %collective-permute-start.10 = (bf16[4,304,512]{2,1,0:T(8,128)(2,1)}, bf16[4,304,512]{2,1,0:T(8,128)(2,1)}, u32[]{:S(2)}, u32[]{:S(2)}) collective-permute-start(bf16[4,304,512]{2,1,0:T(8,128)(2,1)} %pad_maximum_fusion.7), channel_id=1, source_target_pairs={{0,3},{1,2},{2,1},{3,0},{4,7},{5,6},{6,5},{7,4},{8,11},{9,10},{10,... | collective-permute-start | bytes 3735560 | tf_op jit(solution)/shard_map/ppermute | solution.py:28
  116.6 13.6 %copy-start.10 = (bf16[1,7168,256]{2,1,0:T(8,128)(2,1)S(1)}, bf16[1,7168,256]{2,1,0:T(8,128)(2,1)}, u32[]{:S(2)}) copy-start(bf16[1,7168,256]{2,1,0:T(8,128)(2,1)} %gate_ref.1) | copy-start | bytes 11010052
  117.8 39.1 %collective-permute-start.7 = (bf16[4,304,512]{2,1,0:T(8,128)(2,1)}, bf16[4,304,512]{2,1,0:T(8,128)(2,1)}, u32[]{:S(2)}, u32[]{:S(2)}) collective-permute-start(bf16[4,304,512]{2,1,0:T(8,128)(2,1)} %pad_maximum_fusion.6), channel_id=1, source_target_pairs={{0,12},{1,13},{2,14},{3,15},{4,8},{5,9},{6,10},{7,11},{8,4},{9,5},... | collective-permute-start | bytes 3735560 | tf_op jit(solution)/shard_map/ppermute | solution.py:28
  122.4 43.0 %collective-permute-start.3 = (bf16[4,896,256]{2,1,0:T(8,128)(2,1)}, bf16[4,896,256]{2,1,0:T(8,128)(2,1)}, u32[]{:S(2)}, u32[]{:S(2)}) collective-permute-start(bf16[4,896,256]{2,1,0:T(8,128)(2,1)} %pad_maximum_fusion.5), channel_id=1, source_target_pairs={{0,16},{16,0},{32,48},{48,32},{64,80},{80,64},{96,112},{112,96},{1... | collective-permute-start | bytes 5505032 | tf_op jit(solution)/shard_map/ppermute | solution.py:32
  144.0 44.0 %collective-permute-start.29 = (bf16[8,448,128]{2,1,0:T(8,128)(2,1)}, bf16[8,448,128]{2,1,0:T(8,128)(2,1)}, u32[]{:S(2)}, u32[]{:S(2)}) collective-permute-start(bf16[8,448,128]{2,1,0:T(8,128)(2,1)} %constant_dynamic-slice_fusion.3), channel_id=1, source_target_pairs={{0,12},{1,13},{2,14},{3,15},{4,8},{5,9},{6,10},{7,11},{8,4},{9,5},... | collective-permute-start | bytes 2752520 | tf_op jit(solution)/shard_map/ppermute | solution.py:28
  145.9 12.6 %slice-start = ((s8[7340032]{0:T(1024)(128)(4,1)}), s8[4194304]{0:T(1024)(128)(4,1)S(1)}, s32[]{:S(2)}) async-start(s8[7340032]{0:T(1024)(128)(4,1)} %bitcast.86), calls=%async_computation.3 | async-start | bytes 8388608
  147.6 10.9 %copy-start.6 = (bf16[8,288,512]{2,1,0:T(8,128)(2,1)}, bf16[8,288,512]{2,1,0:T(8,128)(2,1)S(1)}, u32[]{:S(2)}) copy-start(bf16[8,288,512]{2,1,0:T(8,128)(2,1)S(1)} %pad_maximum_fusion.4.refs_2_) | copy-start | bytes 7077892
  147.6 10.9 %slice-start.1 = ((s8[7340032]{0:T(1024)(128)(4,1)}), s8[3145728]{0:T(1024)(128)(4,1)S(1)}, s32[]{:S(2)}) async-start(s8[7340032]{0:T(1024)(128)(4,1)} %bitcast.86), calls=%async_computation.4 | async-start | bytes 6291456
  186.2 27.8 %collective-permute-start.21 = (bf16[4,288,512]{2,1,0:T(8,128)(2,1)}, bf16[4,288,512]{2,1,0:T(8,128)(2,1)}, u32[]{:S(2)}, u32[]{:S(2)}) collective-permute-start(bf16[4,288,512]{2,1,0:T(8,128)(2,1)} %get-tuple-element.20), channel_id=1, source_target_pairs={{0,12},{1,13},{2,14},{3,15},{4,8},{5,9},{6,10},{7,11},{8,4},{9,5},... | collective-permute-start | bytes 3538952 | tf_op jit(solution)/shard_map/ppermute | solution.py:28
  189.5 13.6 %collective-permute-start.30 = (bf16[4,448,128]{2,1,0:T(8,128)(2,1)S(1)}, bf16[4,448,128]{2,1,0:T(8,128)(2,1)}, u32[]{:S(2)}, u32[]{:S(2)}) collective-permute-start(bf16[4,448,128]{2,1,0:T(8,128)(2,1)S(1)} %constant_dynamic-slice_fusion.2), channel_id=1, source_target_pairs={{0,4},{1,5},{2,6},{3,7},{4,0},{5,1},{6,2},{7,3},{8,12},{9,13},{10,... | collective-permute-start | bytes 1376264 | tf_op jit(solution)/shard_map/ppermute | solution.py:28
  189.6 31.7 %collective-permute-start.15 = (bf16[4,304,512]{2,1,0:T(8,128)(2,1)S(1)}, bf16[4,304,512]{2,1,0:T(8,128)(2,1)}, u32[]{:S(2)}, u32[]{:S(2)}) collective-permute-start(bf16[4,304,512]{2,1,0:T(8,128)(2,1)S(1)} %get-tuple-element.16), channel_id=1, source_target_pairs={{0,3},{1,2},{2,1},{3,0},{4,7},{5,6},{6,5},{7,4},{8,11},{9,10},{10,... | collective-permute-start | bytes 3735560 | tf_op jit(solution)/shard_map/ppermute | solution.py:28
  191.9 38.0 %collective-permute-start.18 = (bf16[4,304,512]{2,1,0:T(8,128)(2,1)S(1)}, bf16[4,304,512]{2,1,0:T(8,128)(2,1)}, u32[]{:S(2)}, u32[]{:S(2)}) collective-permute-start(bf16[4,304,512]{2,1,0:T(8,128)(2,1)S(1)} %get-tuple-element.18), channel_id=1, source_target_pairs={{0,4},{1,5},{2,6},{3,7},{4,0},{5,1},{6,2},{7,3},{8,12},{9,13},{10,... | collective-permute-start | bytes 3735560 | tf_op jit(solution)/shard_map/ppermute | solution.py:28
  204.5 28.5 %collective-permute-start.31 = (bf16[2,448,128]{2,1,0:T(8,128)(2,1)S(1)}, bf16[2,448,128]{2,1,0:T(8,128)(2,1)S(1)}, u32[]{:S(2)}, u32[]{:S(2)}) collective-permute-start(bf16[2,448,128]{2,1,0:T(8,128)(2,1)S(1)} %constant_dynamic-slice_fusion.1), channel_id=1, source_target_pairs={{0,3},{1,2},{2,1},{3,0},{4,7},{5,6},{6,5},{7,4},{8,11},{9,10},{10,... | collective-permute-start | bytes 688136 | tf_op jit(solution)/shard_map/ppermute | solution.py:28
  215.6 17.5 %collective-permute-start.22 = (bf16[2,288,512]{2,1,0:T(8,128)(2,1)S(1)}, bf16[2,288,512]{2,1,0:T(8,128)(2,1)S(1)}, u32[]{:S(2)}, u32[]{:S(2)}) collective-permute-start(bf16[2,288,512]{2,1,0:T(8,128)(2,1)S(1)} %slice.92), channel_id=1, source_target_pairs={{0,3},{1,2},{2,1},{3,0},{4,7},{5,6},{6,5},{7,4},{8,11},{9,10},{10,... | collective-permute-start | bytes 1769480 | tf_op jit(solution)/shard_map/ppermute | solution.py:28
  223.0 16.2 %collective-permute-start.16 = (bf16[2,304,512]{2,1,0:T(8,128)(2,1)S(1)}, bf16[2,304,512]{2,1,0:T(8,128)(2,1)S(1)}, u32[]{:S(2)}, u32[]{:S(2)}) collective-permute-start(bf16[2,304,512]{2,1,0:T(8,128)(2,1)S(1)} %slice.84), channel_id=1, source_target_pairs={{0,4},{1,5},{2,6},{3,7},{4,0},{5,1},{6,2},{7,3},{8,12},{9,13},{10,... | collective-permute-start | bytes 1867784 | tf_op jit(solution)/shard_map/ppermute | solution.py:28
  231.5 11.8 %collective-permute-start.19 = (bf16[2,304,512]{2,1,0:T(8,128)(2,1)S(1)}, bf16[2,304,512]{2,1,0:T(8,128)(2,1)S(1)}, u32[]{:S(2)}, u32[]{:S(2)}) collective-permute-start(bf16[2,304,512]{2,1,0:T(8,128)(2,1)S(1)} %slice.88), channel_id=1, source_target_pairs={{0,12},{1,13},{2,14},{3,15},{4,8},{5,9},{6,10},{7,11},{8,4},{9,5},... | collective-permute-start | bytes 1867784 | tf_op jit(solution)/shard_map/ppermute | solution.py:28
  233.3 12.7 %collective-permute-start.23 = (bf16[1,288,512]{2,1,0:T(8,128)(2,1)S(1)}, bf16[1,288,512]{2,1,0:T(8,128)(2,1)S(1)}, u32[]{:S(2)}, u32[]{:S(2)}) collective-permute-start(bf16[1,288,512]{2,1,0:T(8,128)(2,1)S(1)} %slice.94), channel_id=1, source_target_pairs={{0,4},{1,5},{2,6},{3,7},{4,0},{5,1},{6,2},{7,3},{8,12},{9,13},{10,... | collective-permute-start | bytes 884744 | tf_op jit(solution)/shard_map/ppermute | solution.py:28
  239.4 8.2 %collective-permute-start.17 = (bf16[1,304,512]{2,1,0:T(8,128)(2,1)S(1)}, bf16[1,304,512]{2,1,0:T(8,128)(2,1)S(1)}, u32[]{:S(2)}, u32[]{:S(2)}) collective-permute-start(bf16[1,304,512]{2,1,0:T(8,128)(2,1)S(1)} %slice.86), channel_id=1, source_target_pairs={{0,12},{1,13},{2,14},{3,15},{4,8},{5,9},{6,10},{7,11},{8,4},{9,5},... | collective-permute-start | bytes 933896 | tf_op jit(solution)/shard_map/ppermute | solution.py:28
  243.5 8.2 %collective-permute-start.20 = (bf16[1,304,512]{2,1,0:T(8,128)(2,1)S(1)}, bf16[1,304,512]{2,1,0:T(8,128)(2,1)S(1)}, u32[]{:S(2)}, u32[]{:S(2)}) collective-permute-start(bf16[1,304,512]{2,1,0:T(8,128)(2,1)S(1)} %slice.90), channel_id=1, source_target_pairs={{0,3},{1,2},{2,1},{3,0},{4,7},{5,6},{6,5},{7,4},{8,11},{9,10},{10,... | collective-permute-start | bytes 933896 | tf_op jit(solution)/shard_map/ppermute | solution.py:28
  247.7 25.2 %copy-start.19 = (bf16[1024,448]{0,1:T(8,128)(2,1)S(1)}, bf16[1024,448]{0,1:T(8,128)(2,1)}, u32[]{:S(2)}) copy-start(bf16[1024,448]{0,1:T(8,128)(2,1)} %param.14) | copy-start | bytes 2752516
  247.7 25.2 %copy-start.35 = (bf16[1024,128]{1,0:T(8,128)(2,1)S(1)}, bf16[1024,128]{1,0:T(8,128)(2,1)}, u32[]{:S(2)}) copy-start(bf16[1024,128]{1,0:T(8,128)(2,1)} %copy-done.34) | copy-start | bytes 786436
  252.0 21.0 %collective-permute-start.24 = (bf16[448,512]{1,0:T(8,128)(2,1)S(1)}, bf16[448,512]{1,0:T(8,128)(2,1)S(1)}, u32[]{:S(2)}, u32[]{:S(2)}) collective-permute-start(bf16[448,512]{1,0:T(8,128)(2,1)S(1)} %get-tuple-element.25), channel_id=1, source_target_pairs={{0,1},{1,0},{2,3},{3,2},{4,5},{5,4},{6,7},{7,6},{8,9},{9,8},{10,11... | collective-permute-start | bytes 1376264 | tf_op jit(solution)/shard_map/ppermute | solution.py:28
  252.1 9.7 %collective-permute-start.32 = (bf16[1,448,128]{2,1,0:T(8,128)(2,1)S(1)}, bf16[1,448,128]{2,1,0:T(8,128)(2,1)S(1)}, u32[]{:S(2)}, u32[]{:S(2)}) collective-permute-start(bf16[1,448,128]{2,1,0:T(8,128)(2,1)S(1)} %constant_dynamic-slice_fusion), channel_id=1, source_target_pairs={{0,1},{1,0},{2,3},{3,2},{4,5},{5,4},{6,7},{7,6},{8,9},{9,8},{10,11... | collective-permute-start | bytes 344072 | tf_op jit(solution)/shard_map/ppermute | solution.py:28
  262.6 10.4 %all-to-all-start.1 = ((bf16[8,16,448]{2,1,0:T(8,128)(2,1)}), bf16[8,16,448]{2,1,0:T(8,128)(2,1)S(1)}, u32[]{:S(2)}, u32[]{:S(2)}) async-start(bf16[8,16,448]{2,1,0:T(8,128)(2,1)} %bitcast.35), calls=%async_computation.1 | async-start | bytes 262144 | tf_op jit(solution)/shard_map/all_to_all | solution.py:325
  (31 other events, 146.2 us)
Sparse Core Ops, SparseCore 0:
  32.1 49.2 all-gather.1

commit v3 on v2

v3 whole, which is shorter than its diff:
```python
import functools

import jax
import jax.numpy as jnp
from jax import lax
from jax.experimental import pallas as pl
from jax.experimental.pallas import tpu as pltpu
from jax.sharding import PartitionSpec as P

EPSILON = 1e-05
NODE_CAP = 16
GRAY = (0, 1, 3, 2)

LOCAL_LABEL = [GRAY[i % 4] | GRAY[i // 4] << 2 for i in range(16)]
LOCAL_AT = {label: i for i, label in enumerate(LOCAL_LABEL)}
NODE_LABEL = [i % 2 | GRAY[i // 2] << 1 for i in range(8)]
NODE_AT = {label: i for i, label in enumerate(NODE_LABEL)}

STREAMS = ((0, 1, 2), (1, 2, 0), (2, 0, 1))
ROW_BITS = (1, 2, 3, 0)


def stream_rows(rows):
    third = -(-rows // 48) * 16
    return (0, third), (third, 2 * third), (2 * third, rows)


def flip_local(array, bit):
    return lax.ppermute(array, "local", [(i, LOCAL_AT[LOCAL_LABEL[i] ^ (1 << bit)]) for i in range(16)])


def flip_node(array, bit):
    return lax.ppermute(array, "node", [(i, NODE_AT[NODE_LABEL[i] ^ (1 << bit)]) for i in range(8)])


def route_slots(ids_block, window):
    flat_ids = ids_block.reshape(-1)
    expert_range = jnp.arange(window, dtype=jnp.int32)
    member = (flat_ids[:, None] == expert_range[None, :]).astype(jnp.int32)
    before = jnp.cumsum(member, axis=0) - member
    route_rank = jnp.sum(before * member, axis=1)
    kept = (jnp.sum(member, axis=1) > 0) & (route_rank < NODE_CAP)
    slot = jnp.where(kept, flat_ids * NODE_CAP + route_rank, -1)
    return slot.reshape(ids_block.shape)


def transposed_dot(weight, rows):
    return lax.dot_general(weight, rows, (((0,), (0,)), ((), ())), preferred_element_type=jnp.float32)


def silu(value):
    return value / (1.0 + jnp.exp(-value))


def gate_up_kernel(last, features, count, *refs):
    refs = refs[1:]
    x, gains, refs = refs[0:3], refs[3:6], refs[6:]
    weights, refs = [refs[s * count : (s + 1) * count] for s in range(3)], refs[3 * count :]
    if last:
        total_in, squares_in, result, squares_out, total, squares = refs
    else:
        result, squares_out, total, squares = refs
    step = pl.program_id(0)

    @pl.when(step == 0)
    def _():
        total[...] = total_in[...] if last else jnp.zeros_like(total)
        squares[...] = squares_in[...] if last else jnp.zeros_like(squares)

    wide = total.shape[0] // count
    for s in range(3):
        as_float = x[s][0].astype(jnp.float32)
        squares[...] += jnp.sum(as_float * as_float, axis=0, keepdims=True)
        rows = (as_float * gains[s][...]).astype(jnp.bfloat16)
        for i in range(count):
            total[i * wide : (i + 1) * wide] += transposed_dot(weights[s][i][...], rows)

    @pl.when(step == pl.num_programs(0) - 1)
    def _():
        squares_out[...] = squares[...]
        if last:
            scale = lax.rsqrt(squares[...] / features + EPSILON)
            half = total.shape[0] // 2
            result[...] = (silu(total[:half] * scale) * (total[half:] * scale)).astype(jnp.bfloat16)
        else:
            result[...] = total[...]


def gate_up(pair_of, streams, gain_column, weights, before=None):
    last = int(before is not None)
    blocks, _, columns = streams[0].shape
    features = weights[0].shape[0]
    pair_rows = features // (2 * blocks)
    spans = stream_rows(pair_rows)
    both = sum(w.shape[1] for w in weights)

    def row_spec(s, wide):
        a, b, c = STREAMS[s]
        low, high = spans[s]

        def index(j, pair):
            mask = (j & 1) << a | ((j >> 1) & 1) << b | last << c
            return pl.multiple_of(pair[mask] * pair_rows + low, 16), 0

        return pl.BlockSpec((pl.Element(high - low), pl.Element(wide)), index)

    def whole(rows):
        return pl.BlockSpec((rows, columns), lambda j, pair: (0, 0))

    in_specs = [pl.BlockSpec((1, high - low, columns), lambda j, pair: (j, 0, 0)) for low, high in spans]
    in_specs += [row_spec(s, 1) for s in range(3)]
    in_specs += [row_spec(s, w.shape[1]) for s in range(3) for w in weights]
    operands = [*streams, *[gain_column] * 3, *[w for _ in range(3) for w in weights]]
    if last:
        in_specs += [whole(both), whole(1)]
        operands += before
        result = jax.ShapeDtypeStruct((both // 2, columns), jnp.bfloat16)
    else:
        result = jax.ShapeDtypeStruct((both, columns), jnp.float32)
    return pl.pallas_call(
        functools.partial(gate_up_kernel, last, features, len(weights)),
        grid_spec=pltpu.PrefetchScalarGridSpec(
            num_scalar_prefetch=1,
            grid=(blocks,),
            in_specs=in_specs,
            out_specs=[whole(result.shape[0]), whole(1)],
            scratch_shapes=[pltpu.VMEM((both, columns), jnp.float32), pltpu.VMEM((1, columns), jnp.float32)],
        ),
        out_shape=[result, jax.ShapeDtypeStruct((1, columns), jnp.float32)],
        compiler_params=pltpu.CompilerParams(vmem_limit_bytes=24 << 20),
        cost_estimate=pl.CostEstimate(
            flops=features * columns * both, bytes_accessed=features * (columns + both), transcendentals=0
        ),
    )(pair_of, *operands)


def down_kernel(spans, own_pair, other_pair, own, other, own_hidden, other_hidden, *outs):
    step = pl.program_id(0)
    part = transposed_dot(own[...], own_hidden[...]) + transposed_dot(other[0], other_hidden[...])
    for s, (low, high) in enumerate(spans):
        rows = part[low:high].astype(jnp.bfloat16)
        is_sent = ((step >> STREAMS[s][0]) & 1) == 1

        @pl.when(is_sent)
        def _():
            outs[s][0] = rows

        @pl.when(jnp.logical_not(is_sent))
        def _():
            outs[3 + s][0] = rows


def down(own_pair, other_pair, own_weight, other_weight, own_hidden, other_hidden):
    blocks, hidden, rows = other_weight.shape
    columns = own_hidden.shape[1]
    spans = stream_rows(rows)

    def out_spec(s, sent):
        a, b, c = STREAMS[s]
        low, high = spans[s]

        def index(m, p, q):
            if sent:
                here = jnp.where((m >> a) & 1 == 1, m, ((m >> a) | 1) << a)
            else:
                here = jnp.where((m >> a) & 1 == 0, m, jnp.minimum(((m >> a) + 1) << a, (blocks - 1) ^ (1 << a)))
            return ((here >> b) & 1) << 1 | ((here >> c) & 1), 0, 0

        return pl.BlockSpec((1, high - low, columns), index)

    hidden_spec = pl.BlockSpec((hidden, columns), lambda m, p, q: (0, 0))
    return pl.pallas_call(
        functools.partial(down_kernel, spans),
        grid_spec=pltpu.PrefetchScalarGridSpec(
            num_scalar_prefetch=2,
            grid=(blocks,),
            in_specs=[
                pl.BlockSpec((hidden, rows), lambda m, p, q: (0, p[m])),
                pl.BlockSpec((1, hidden, rows), lambda m, p, q: (q[m], 0, 0)),
                hidden_spec,
                hidden_spec,
            ],
            out_specs=[out_spec(s, sent) for sent in (1, 0) for s in range(3)],
        ),
        out_shape=[jax.ShapeDtypeStruct((blocks // 2, high - low, columns), jnp.bfloat16) for low, high in spans] * 2,
        compiler_params=pltpu.CompilerParams(vmem_limit_bytes=24 << 20),
        cost_estimate=pl.CostEstimate(
            flops=4 * blocks * rows * hidden * columns,
            bytes_accessed=2 * blocks * rows * (2 * hidden + columns),
            transcendentals=0,
        ),
    )(own_pair, other_pair, own_weight, other_weight, own_hidden, other_hidden)


def expert_kernel(blocks, features, at_ref, x_ref, gate_ref, up_ref, gain_ref, hidden_ref, gate_total, up_total, squares):
    step = pl.program_id(0)

    @pl.when(step == 0)
    def _():
        gate_total[...] = jnp.zeros_like(gate_total)
        up_total[...] = jnp.zeros_like(up_total)
        squares[...] = jnp.zeros_like(squares)

    as_float = x_ref[0].astype(jnp.float32)
    squares[...] += jnp.sum(as_float * as_float, axis=0, keepdims=True)
    rows = (as_float * gain_ref[...]).astype(jnp.bfloat16)
    gate_total[...] += transposed_dot(gate_ref[0], rows)
    up_total[...] += transposed_dot(up_ref[0], rows)

    @pl.when(step == blocks - 1)
    def _():
        scale = lax.rsqrt(squares[...] / features + EPSILON)
        hidden_ref[...] = (silu(gate_total[...] * scale) * (up_total[...] * scale)).astype(jnp.bfloat16)


def expert_gate_up(slice_of, pooled, gate_weight, up_weight, gain_column):
    blocks, rows, columns = pooled.shape
    hidden = gate_weight.shape[-1]
    weight_spec = pl.BlockSpec((1, rows, hidden), lambda m, at: (0, at[m], 0))
    return pl.pallas_call(
        functools.partial(expert_kernel, blocks, blocks * rows),
        grid_spec=pltpu.PrefetchScalarGridSpec(
            num_scalar_prefetch=1,
            grid=(blocks,),
            in_specs=[
                pl.BlockSpec((1, rows, columns), lambda m, at: (m, 0, 0)),
                weight_spec,
                weight_spec,
                pl.BlockSpec((rows, 1), lambda m, at: (at[m], 0)),
            ],
            out_specs=pl.BlockSpec((hidden, columns), lambda m, at: (0, 0)),
            scratch_shapes=[
                pltpu.VMEM((hidden, columns), jnp.float32),
                pltpu.VMEM((hidden, columns), jnp.float32),
                pltpu.VMEM((1, columns), jnp.float32),
            ],
        ),
        out_shape=jax.ShapeDtypeStruct((hidden, columns), jnp.bfloat16),
        compiler_params=pltpu.CompilerParams(vmem_limit_bytes=24 << 20),
        cost_estimate=pl.CostEstimate(
            flops=4 * blocks * rows * columns * hidden,
            bytes_accessed=2 * blocks * rows * (columns + 2 * hidden),
            transcendentals=0,
        ),
    )(slice_of, pooled, gate_weight, up_weight, gain_column)


def add_pair(kept, got):
    return (kept.astype(jnp.float32) + got.astype(jnp.float32)).astype(jnp.bfloat16)


def shards(
    tokens,
    norm_gain,
    dense_gate,
    dense_up,
    dense_down,
    expert_gate,
    expert_up,
    expert_down,
    expert_ids,
    route_gates,
):
    node_count = lax.axis_size("node")
    node_index = lax.axis_index("node")
    local_index = lax.axis_index("local")
    tok_node, slice_width = tokens.shape
    width = slice_width * 16
    pair_width = 2 * slice_width
    half_tokens = tok_node // 2
    slot_count = node_count * NODE_CAP
    spans = stream_rows(pair_width)

    label = jnp.asarray(LOCAL_LABEL, jnp.int32)[local_index]
    own_half = label & 1
    odd = (local_index & 1) == 1
    pair_table = [[LOCAL_AT[LOCAL_LABEL[i] ^ (2 * m)] // 2 for m in range(8)] for i in range(16)]
    pair_of = jnp.asarray(pair_table, jnp.int32)[local_index]
    slice_table = [
        [LOCAL_AT[LOCAL_LABEL[i] ^ sum(((q >> t) & 1) << bit for t, bit in enumerate(ROW_BITS))] for q in range(16)]
        for i in range(16)
    ]
    slice_of = jnp.asarray(slice_table, jnp.int32)[local_index]
    place_table = [[0] * 8 for _ in range(8)]
    for i in range(8):
        for j in range(8):
            diff = NODE_LABEL[i] ^ NODE_LABEL[j]
            place_table[i][j] = ((diff >> 1) & 1) | ((diff >> 2) & 1) << 1 | (diff & 1) << 2
    other_of = jnp.asarray(place_table, jnp.int32)[node_index][pair_of]
    block_start = node_index * pair_width

    columns = tokens.T
    mine = lax.dynamic_slice_in_dim(columns, own_half * half_tokens, half_tokens, 1)
    give = lax.dynamic_slice_in_dim(columns, (1 - own_half) * half_tokens, half_tokens, 1)
    got = flip_local(give, 0)

    slot = route_slots(expert_ids, node_count)
    slot_range = jnp.arange(slot_count, dtype=jnp.int32)
    match_float = (slot[:, :, None] == slot_range[None, None, :]).astype(jnp.float32)
    chosen = jnp.sum(match_float, axis=1).astype(jnp.bfloat16)
    slot_gate = jnp.sum(match_float * route_gates[:, :, None], axis=(0, 1))
    send_rows = lax.dot_general(
        chosen, tokens, (((0,), (0,)), ((), ())), preferred_element_type=jnp.float32
    ).astype(jnp.bfloat16)
    got, send_rows = lax.optimization_barrier((got, send_rows))
    pooled = lax.all_to_all(
        send_rows.reshape(node_count, NODE_CAP, slice_width), "node", split_axis=0, concat_axis=0, tiled=True
    )

    piece = jnp.concatenate(
        [lax.dynamic_slice_in_dim(w, block_start, pair_width, 0) for w in (dense_gate, dense_up)], axis=1
    )
    piece, _ = lax.optimization_barrier((piece, got))
    piece = flip_local(piece, 0)

    pair_block = jnp.where(odd, jnp.concatenate([got, mine], axis=0), jnp.concatenate([mine, got], axis=0))
    streams = [pair_block[None, low:high] for low, high in spans]
    arrived = [flip_local(streams[s], 1 + STREAMS[s][0]) for s in range(3)]
    pooled = pooled.reshape(slot_count, slice_width).T[None]
    gain_column = norm_gain[:, None]
    arrived, pooled, gain_column = lax.optimization_barrier((arrived, pooled, gain_column))
    streams = [jnp.concatenate([streams[s], arrived[s]], axis=0) for s in range(3)]
    arrived = [flip_local(streams[s], 1 + STREAMS[s][1]) for s in range(3)]
    for bit in ROW_BITS[:2]:
        pooled = jnp.concatenate([pooled, flip_local(pooled, bit)], axis=0)
    pooled, arrived, piece = lax.optimization_barrier((pooled, arrived, piece))
    other_both = lax.all_gather(piece, "node", axis=0, tiled=True)
    down_piece = lax.dynamic_slice_in_dim(dense_down, block_start, pair_width, 1)
    down_piece, _ = lax.optimization_barrier((down_piece, arrived[0]))
    down_piece = flip_local(down_piece, 0)[None]
    streams = [jnp.concatenate([streams[s], arrived[s]], axis=0) for s in range(3)]
    arrived = [flip_local(streams[s], 1 + STREAMS[s][2]) for s in range(3)]
    own_weights = (dense_gate, dense_up)
    own_before = gate_up(pair_of, streams, gain_column, own_weights)
    pooled = jnp.concatenate([pooled, flip_local(pooled, ROW_BITS[2])], axis=0)
    own_before, down_piece, pooled = lax.optimization_barrier((own_before, down_piece, pooled))
    pooled_other = flip_local(pooled, ROW_BITS[3])
    down_piece = jnp.concatenate([down_piece, flip_node(down_piece, 1)], axis=0)
    down_piece, own_before, arrived = lax.optimization_barrier((down_piece, own_before, arrived))
    down_other = flip_node(down_piece, 2)
    own_hidden, _ = gate_up(pair_of, arrived, gain_column, own_weights, own_before)

    own_hidden, pooled_other = lax.optimization_barrier((own_hidden, pooled_other))
    pooled = jnp.concatenate([pooled, pooled_other], axis=0)
    expert_hidden = expert_gate_up(slice_of, pooled, expert_gate, expert_up, gain_column)
    expert_hidden, down_other = lax.optimization_barrier((expert_hidden, down_other))
    down_piece = jnp.concatenate([down_piece, down_other], axis=0)
    down_other = flip_node(down_piece, 0)
    expert_partial = transposed_dot(expert_down[0], expert_hidden).astype(jnp.bfloat16)
    expert_partial = expert_partial.reshape(2, 2, 2, 2, slice_width, slot_count)

    def halve(array, bit):
        axis = 3 - bit
        upper = (local_index >> bit) & 1
        keep = lax.dynamic_slice_in_dim(array, upper, 1, axis)
        return keep, lax.dynamic_slice_in_dim(array, 1 - upper, 1, axis)

    halves = [lax.slice_in_dim(expert_partial, i, i + 1, axis=2) for i in (0, 1)]
    keep, send = [
        jnp.concatenate([lax.dynamic_slice_in_dim(h, bit ^ i, 1, 3) for i, h in enumerate(halves)], axis=2)
        for bit in (own_half, 1 - own_half)
    ]
    keep, send, other_both = lax.optimization_barrier((keep, send, other_both))
    expert_got = flip_local(send, 0)

    other_before = gate_up(pair_of, streams, gain_column, (other_both,))
    other_hidden, _ = gate_up(pair_of, arrived, gain_column, (other_both,), other_before)
    down_piece = jnp.concatenate([down_piece, down_other], axis=0)
    parts = down(pair_of, other_of, dense_down, down_piece, own_hidden, other_hidden)
    sent, sums = parts[:3], parts[3:]
    arrived = [flip_local(sent[s], 1 + STREAMS[s][0]) for s in range(3)]
    expert_got, _ = lax.optimization_barrier((expert_got, sums))
    for step in (1, 2):
        keep, send = halve(add_pair(keep, expert_got), 4 - step)
        expert_got = flip_local(send, 4 - step)
        if step == 2:
            arrived, expert_got = lax.optimization_barrier((arrived, expert_got))
        half = sums[0].shape[0] // 2
        came = [flip_local(add_pair(sums[s][half:], arrived[s][half:]), 1 + STREAMS[s][step]) for s in range(3)]
        sums = [add_pair(sums[s][:half], arrived[s][:half]) for s in range(3)]
        arrived = came
    keep, send = halve(add_pair(keep, expert_got), 1)
    expert_got = flip_local(send, 1)
    sums = [add_pair(sums[s], arrived[s]) for s in range(3)]
    pair_sum = jnp.concatenate([sums[s][0] for s in range(3)], axis=0)
    even_rows, odd_rows = pair_sum[:slice_width], pair_sum[slice_width:]
    mine = jnp.where(odd, odd_rows, even_rows)
    got = flip_local(jnp.where(odd, even_rows, odd_rows), 0)
    expert_out = add_pair(keep, expert_got).reshape(slice_width, slot_count).T
    returned = lax.all_to_all(
        expert_out.reshape(node_count, NODE_CAP, slice_width), "node", split_axis=0, concat_axis=0, tiled=True
    ).reshape(slot_count, slice_width)
    route_term = (slot_gate[:, None] * returned.astype(jnp.float32)).astype(jnp.bfloat16)
    expert_part = lax.dot_general(
        route_term, chosen, (((0,), (1,)), ((), ())), preferred_element_type=jnp.float32
    )
    dense_part = jnp.where(
        own_half == 1, jnp.concatenate([got, mine], axis=1), jnp.concatenate([mine, got], axis=1)
    ).astype(jnp.float32)
    return (columns.astype(jnp.float32) + dense_part + expert_part).astype(jnp.bfloat16).T


def solution(mesh):
    return jax.shard_map(
        shards,
        mesh=mesh,
        in_specs=(
            P("node", "local"),
            P(),
            P(None, "local"),
            P(None, "local"),
            P("local", None),
            P("node", None, "local"),
            P("node", None, "local"),
            P("node", "local", None),
            P("node", None),
            P("node", None),
        ),
        out_specs=P("node", "local"),
        check_vma=False,
    )
```

time: 283 us -> 289 us (1.021)
  Pallas kernels: 28.4 us -> 43.3 us
  other arithmetic: 44.5 us -> 37.1 us
  starting transfers between devices: 58 us -> 53.9 us
    ppermute x30, waiting for transfers between devices: 88.4 us -> 64.4 us  [flip_local(): lax.ppermute(array, 'local', [(i, LOCAL_AT[LOCAL_LABEL[i] ^ 1 << bit]) fo...]
    ppermute x3, waiting for transfers between devices: 1.14 us -> 19.2 us  [flip_node(): lax.ppermute(array, 'node', [(i, NODE_AT[NODE_LABEL[i] ^ 1 << bit]) for i...]
    pallas_call x2 -> x4, Pallas kernels: 13.9 us -> 27.2 us  [gate_up(): pl.pallas_call(functools.partial(gate_up_kernel, last, features, len(weig...]
    convert_element_type x2 -> x0, other arithmetic: 7.7 us -> none  [folded(): (gate_rows.astype(jnp.float32) * gain_rows).astype(jnp.bfloat16)]
    transpose x2 -> x1, local copies, waits for them, and re-layouts: 6.63 us -> 0.77 us  [shards(): expert_out = add_pair(keep, expert_got).reshape(slice_width, slot_count).T]
    all_to_all x1, waiting for transfers between devices: 0.01 us -> 4.96 us  [shards(): lax.all_to_all(send_rows.reshape(node_count, NODE_CAP, slice_width), 'nod...]
    convert_element_type x9, other arithmetic: 8.11 us -> 12.3 us  [add_pair(): (kept.astype(jnp.float32) + got.astype(jnp.float32)).astype(jnp.bfloat16)]
    optimization_barrier x0 -> x2, local copies, waits for them, and re-layouts: none -> 3.88 us  [the longest x1 3.12 us: shards(): lax.optimization_barrier((arrived, pooled, gain_column))]
  transfers between devices with their start and end apart: 36 -> 36, of which waited for: 19 -> 13; matrix products, arithmetic and copies ran while one was open for 24% -> 20% of each run, Pallas kernels for 10% -> 13%
where the time goes in v3:
time: 289 us; the launch traced here: 287 us
  waiting for transfers between devices  94.6 us (33%)
  starting transfers between devices  53.9 us (19%)
  Pallas kernels  43.3 us (15%)
  local copies, waits for them, and re-layouts  37.9 us (13%)
  other arithmetic  37.1 us (13%)
  between operations  14.7 us (5%)
  matrix products  5.87 us (2%)
    ppermute x30, waiting for transfers between devices, flip_local(): lax.ppermute(array, 'local', [(i, LOCAL_AT[LOCAL_LABEL[i] ^ 1 << bit]) fo...  64.4 us
    ppermute x30, starting transfers between devices, flip_local(): lax.ppermute(array, 'local', [(i, LOCAL_AT[LOCAL_LABEL[i] ^ 1 << bit]) fo...  43.7 us
    pallas_call x4, Pallas kernels, gate_up(): pl.pallas_call(functools.partial(gate_up_kernel, last, features, len(weig...  27.2 us
    ppermute x3, waiting for transfers between devices, flip_node(): lax.ppermute(array, 'node', [(i, NODE_AT[NODE_LABEL[i] ^ 1 << bit]) for i...  19.2 us
    unnamed x69, local copies, waits for them, and re-layouts  15.4 us
    convert_element_type x9, other arithmetic, add_pair(): (kept.astype(jnp.float32) + got.astype(jnp.float32)).astype(jnp.bfloat16)  12.3 us
    pallas_call x1, Pallas kernels, down(): pl.pallas_call(functools.partial(down_kernel, spans), grid_spec=pltpu.Pre...  8.65 us
    pallas_call x1, Pallas kernels, expert_gate_up(): pl.pallas_call(functools.partial(expert_kernel, blocks, blocks * rows), g...  7.45 us
  transfers between devices with their start and end apart: 36, of which 13 were waited for; matrix products, arithmetic and copies ran while one was open for 20% of the time, Pallas kernels for 13%

profile of v3, /device:TPU:0, one launch (start us, length us, event | category | flops | bytes accessed | tf_op | source)
XLA Modules:
  0.0 287.2 jit_solution(16794140223722012530)
XLA Ops:
  8.4 2.0 dynamic-slice_bitcast_fusion.1
  12.9 2.3 reduce-window.6
  19.1 3.8 %collective-permute-done = bf16[448,512]{1,0:T(8,128)(2,1)} collective-permute-done((bf16[448,512]{1,0:T(8,128)(2,1)}, bf16[448,512]{1,0:T(8,128)(2,1)}, u32[]{:S(2)}, u32[]{:S(2)}) %collective-permute-start) | collective-permute-done | bytes 458784 | tf_op jit(solution)/shard_map/ppermute | solution.py:29
  24.4 3.3 %collective-permute-start.1 = (bf16[1,304,512]{2,1,0:T(8,128)(2,1)S(1)}, bf16[1,304,512]{2,1,0:T(8,128)(2,1)S(1)}, u32[]{:S(2)}, u32[]{:S(2)}) collective-permute-start(bf16[1,304,512]{2,1,0:T(8,128)(2,1)S(1)} %get-tuple-element.120), channel_id=1, source_target_pairs={{0,3},{1,2},{2,1},{3,0},{4,7},{5,6},{6,5},{7,4},{8,11},{9,10},{10,... | collective-permute-start | bytes 933896 | tf_op jit(solution)/shard_map/ppermute | solution.py:29
  27.7 1.9 collective-permute-start.2
  29.7 2.6 collective-permute-start.3
  34.2 4.3 %all-to-all-start = ((bf16[8,16,448]{2,1,0:T(8,128)(2,1)}), bf16[8,16,448]{2,1,0:T(8,128)(2,1)S(1)}, u32[]{:S(2)}, u32[]{:S(2)}) async-start(bf16[8,16,448]{2,1,0:T(8,128)(2,1)} %bitcast.12), calls=%async_computation | async-start | bytes 262144 | tf_op jit(solution)/shard_map/all_to_all | solution.py:306
  39.7 5.0 %all-to-all-done = bf16[8,16,448]{2,1,0:T(8,128)(2,1)S(1)} async-done(((bf16[8,16,448]{2,1,0:T(8,128)(2,1)}), bf16[8,16,448]{2,1,0:T(8,128)(2,1)S(1)}, u32[]{:S(2)}, u32[]{:S(2)}) %all-to-all-start) | async-done | bytes 114720 | tf_op jit(solution)/shard_map/all_to_all | solution.py:306
  48.2 3.0 %collective-permute-start.4 = (bf16[1,448,128]{2,1,0:T(8,128)(2,1)S(1)}, bf16[1,448,128]{2,1,0:T(8,128)(2,1)S(1)}, u32[]{:S(2)}, u32[]{:S(2)}) collective-permute-start(bf16[1,448,128]{2,1,0:T(8,128)(2,1)S(1)} %bitcast.73), channel_id=1, source_target_pairs={{0,3},{1,2},{2,1},{3,0},{4,7},{5,6},{6,5},{7,4},{8,11},{9,10},{10,... | collective-permute-start | bytes 344072 | tf_op jit(solution)/shard_map/ppermute | solution.py:29
  51.2 15.0 %collective-permute-done.4 = bf16[1,448,128]{2,1,0:T(8,128)(2,1)S(1)} collective-permute-done((bf16[1,448,128]{2,1,0:T(8,128)(2,1)S(1)}, bf16[1,448,128]{2,1,0:T(8,128)(2,1)S(1)}, u32[]{:S(2)}, u32[]{:S(2)}) %collective-permute-start.4) | collective-permute-done | bytes 114720 | tf_op jit(solution)/shard_map/ppermute | solution.py:29
  67.8 4.6 %collective-permute-done.5 = bf16[2,448,128]{2,1,0:T(8,128)(2,1)S(1)} collective-permute-done((bf16[2,448,128]{2,1,0:T(8,128)(2,1)S(1)}, bf16[2,448,128]{2,1,0:T(8,128)(2,1)S(1)}, u32[]{:S(2)}, u32[]{:S(2)}) %collective-permute-start.5) | collective-permute-done | bytes 229408 | tf_op jit(solution)/shard_map/ppermute | solution.py:29
  73.3 2.4 collective-permute-start.11
  81.0 1.9 constant_dynamic-slice_fusion.8
  83.6 3.1 %copy.67.refs_4_.refs_5_.refs_6_.gain_ref = f32[7168,1]{1,0:T(8,128)} copy(f32[7168,1]{0,1:T(1,128)} %bitcast.80) | data formatting | bytes 57344 | tf_op jit(solution)/shard_map/optimization_barrier | solution.py:321
  86.7 2.0 copy-done
  88.7 2.1 copy-done.5
  90.8 2.1 copy-done.6
  92.9 6.2 %shard_map.136 = (f32[512,512]{1,0:T(8,128)S(1)}, f32[1,512]{1,0:T(1,128)S(1)}) custom-call(s32[8]{0:T(128)S(1)} %fusion.23.refs_0_.own_pair, bf16[4,304,512]{2,1,0:T(8,128)(2,1)S(1)} %pad_maximum_fusion.3.refs_1_, bf16[4,304,512]{2,1,0:T(8,128)(2,1)S(1)} %pad_maximum_fusion.4.refs_2_, bf16[4,288,512]{2,1,0:T(8,128)(2,1)} %pad_maximum_fusion.5.refs_3_, ...), custom_call_target="tpu_custom_call" | custom-call | flops 1879048192 | bytes 7340032 | tf_op jit(solution)/shard_map/pallas_call | solution.py:120
  101.1 2.0 collective-permute-start.16
  103.2 18.9 %collective-permute-done.12 = bf16[1,256,896]{2,1,0:T(8,128)(2,1)S(1)} collective-permute-done((bf16[1,256,896]{2,1,0:T(8,128)(2,1)S(1)}, bf16[1,256,896]{2,1,0:T(8,128)(2,1)S(1)}, u32[]{:S(2)}, u32[]{:S(2)}) %collective-permute-start.12) | collective-permute-done | bytes 458784 | tf_op jit(solution)/shard_map/ppermute | solution.py:33
  124.6 7.3 %shard_map.137 = (bf16[256,512]{1,0:T(8,128)(2,1)S(1)}, f32[1,512]{1,0:T(1,128)}) custom-call(s32[8]{0:T(128)S(1)} %fusion.23.refs_0_.own_pair, bf16[4,304,512]{2,1,0:T(8,128)(2,1)} %collective-permute-done.13.refs_1_, bf16[4,304,512]{2,1,0:T(8,128)(2,1)} %collective-permute-done.14.refs_2_, bf16[4,288,512]{2,1,0:T(8,128)(2,1)} %collective-permute-done.15.refs_3_, ...), custom_call_target="tpu_custom_call" | custom-call | flops 1879048192 | bytes 7340032 | tf_op jit(solution)/shard_map/pallas_call | solution.py:120
  132.1 1.9 copy-done.8
  133.9 7.5 %shard_map.138 = bf16[256,128]{1,0:T(8,128)(2,1)S(1)} custom-call(s32[16]{0:T(128)S(1)} %fusion.22.at_ref, bf16[16,448,128]{2,1,0:T(8,128)(2,1)S(1)} %pad_maximum_fusion.1.x_ref, bf16[1,7168,256]{2,1,0:T(8,128)(2,1)S(1)} %copy-done.8, bf16[1,7168,256]{2,1,0:T(8,128)(2,1)S(1)} %copy-done.9, f32[7168,1]{1,0:T(8,128)S(1)} %copy-done.1), custom_call_target="tpu_custom_call" | custom-call | flops 939524096 | bytes 9175040 | tf_op jit(solution)/shard_map/pallas_call | solution.py:220
  145.3 4.0 %fusion = bf16[7168,128]{0,1:T(8,128)(2,1)} fusion(bf16[256,128]{1,0:T(8,128)(2,1)S(1)} %shard_map.138, bf16[1,256,7168]{2,1,0:T(8,128)(2,1)} %param.21), kind=kOutput, calls=%fused_computation.2 | convolution fusion | flops 470679552 | bytes 5570560 | tf_op jit(solution)/shard_map/dot_general | solution.py:48
  149.3 3.9 %copy.74 = bf16[7168,128]{1,0:T(8,128)(2,1)} copy(bf16[7168,128]{0,1:T(8,128)(2,1)} %fusion) | data formatting | bytes 3670016 | tf_op jit(solution)/shard_map/convert_element_type | solution.py:349
  157.0 3.3 %pad_maximum_fusion.other = bf16[8,256,896]{2,1,0:T(8,128)(2,1)} fusion(bf16[4,256,896]{2,1,0:T(8,128)(2,1)} %collective-permute-done.18, bf16[2,256,896]{2,1,0:T(8,128)(2,1)S(1)} %copy-done.16, bf16[2,256,896]{2,1,0:T(8,128)(2,1)S(1)} %copy-done.14), kind=kLoop, calls=%fused_computation.3 | loop fusion | flops 3670016 | bytes 7340032 | tf_op jit(solution)/shard_map/concatenate | solution.py:368
  160.3 2.0 copy-done.2
  162.3 3.1 %copy-done.4 = bf16[7168,512]{1,0:T(8,128)(2,1)S(1)} copy-done((bf16[7168,512]{1,0:T(8,128)(2,1)S(1)}, bf16[7168,512]{1,0:T(8,128)(2,1)}, u32[]{:S(2)}) %copy-start.4) | copy-done | bytes 7340056
  165.4 6.4 %shard_map.139 = (f32[512,512]{1,0:T(8,128)S(1)}, f32[1,512]{1,0:T(1,128)S(1)}) custom-call(s32[8]{0:T(128)S(1)} %fusion.23.refs_0_.own_pair, bf16[4,304,512]{2,1,0:T(8,128)(2,1)S(1)} %pad_maximum_fusion.3.refs_1_, bf16[4,304,512]{2,1,0:T(8,128)(2,1)S(1)} %pad_maximum_fusion.4.refs_2_, bf16[4,288,512]{2,1,0:T(8,128)(2,1)} %pad_maximum_fusion.5.refs_3_, ...), custom_call_target="tpu_custom_call" | custom-call | flops 1879048192 | bytes 7340032 | tf_op jit(solution)/shard_map/pallas_call | solution.py:120
  171.8 2.0 collective-permute-start.25
  173.7 7.3 %shard_map.140 = (bf16[256,512]{1,0:T(8,128)(2,1)S(1)}, f32[1,512]{1,0:T(1,128)}) custom-call(s32[8]{0:T(128)S(1)} %fusion.23.refs_0_.own_pair, bf16[4,304,512]{2,1,0:T(8,128)(2,1)} %collective-permute-done.13.refs_1_, bf16[4,304,512]{2,1,0:T(8,128)(2,1)} %collective-permute-done.14.refs_2_, bf16[4,288,512]{2,1,0:T(8,128)(2,1)} %collective-permute-done.15.refs_3_, ...), custom_call_target="tpu_custom_call" | custom-call | flops 1879048192 | bytes 7340032 | tf_op jit(solution)/shard_map/pallas_call | solution.py:120
  181.0 8.6 %shard_map.141 = (bf16[4,304,512]{2,1,0:T(8,128)(2,1)}, bf16[4,304,512]{2,1,0:T(8,128)(2,1)}, bf16[4,288,512]{2,1,0:T(8,128)(2,1)}, bf16[4,304,512]{2,1,0:T(8,12...) custom-call(s32[8]{0:T(128)S(1)} %fusion.23.refs_0_.own_pair, s32[8]{0:T(128)S(1)} %gather_fusion, ...), custom_call_target="tpu_custom_call" | custom-call | flops 3758096384 | bytes 14680064 | tf_op jit(solution)/shard_map/pallas_call | solution.py:172
  190.7 1.7 collective-permute-start.21
  192.5 2.7 collective-permute-start.19
  195.1 2.2 collective-permute-start.23
  200.2 20.4 %collective-permute-done.21 = bf16[4,304,512]{2,1,0:T(8,128)(2,1)} collective-permute-done((bf16[4,304,512]{2,1,0:T(8,128)(2,1)}, bf16[4,304,512]{2,1,0:T(8,128)(2,1)}, u32[]{:S(2)}, u32[]{:S(2)}) %collective-permute-start.21) | collective-permute-done | bytes 1245216 | tf_op jit(solution)/shard_map/ppermute | solution.py:29
  220.6 2.4 add_convert_fusion.1
  223.0 2.2 collective-permute-start.22
  225.2 2.4 add_convert_fusion.4
  228.8 2.4 add_convert_fusion.6
  231.2 2.6 collective-permute-start.24
  236.1 11.8 %collective-permute-done.27 = bf16[1,1,2,1,448,128]{5,4,3,2,1,0:T(8,128)(2,1)S(1)} collective-permute-done((bf16[1,1,2,1,448,128]{5,4,3,2,1,0:T(8,128)(2,1)}, bf16[1,1,2,1,448,128]{5,4,3,2,1,0:T(8,128)(2,1)S(1)}, u32[]{:S(2)}, u32[]{:S(2)}) %collective-permute-start.27) | collective-permute-done | bytes 229408 | tf_op jit(solution)/shard_map/ppermute | solution.py:29
  252.1 2.6 collective-permute-start.29
  255.7 2.7 collective-permute-done.30
  262.5 1.9 collective-permute-start.32
  264.5 4.1 %collective-permute-done.32 = bf16[1,1,1,1,448,128]{5,4,3,2,1,0:T(8,128)(2,1)S(1)} collective-permute-done((bf16[1,1,1,1,448,128]{5,4,3,2,1,0:T(8,128)(2,1)S(1)}, bf16[1,1,1,1,448,128]{5,4,3,2,1,0:T(8,128)(2,1)S(1)}, u32[]{:S(2)}, u32[]{:S(2)}) %collective-permute-start.32) | collective-permute-done | bytes 114720 | tf_op jit(solution)/shard_map/ppermute | solution.py:29
  269.4 3.4 %all-to-all-start.1 = ((bf16[8,16,448]{2,1,0:T(8,128)(2,1)}), bf16[8,16,448]{2,1,0:T(8,128)(2,1)S(1)}, u32[]{:S(2)}, u32[]{:S(2)}) async-start(bf16[8,16,448]{2,1,0:T(8,128)(2,1)} %bitcast.27), calls=%async_computation.1 | async-start | bytes 262144 | tf_op jit(solution)/shard_map/all_to_all | solution.py:390
  272.8 6.1 %all-to-all-done.1 = bf16[8,16,448]{2,1,0:T(8,128)(2,1)S(1)} async-done(((bf16[8,16,448]{2,1,0:T(8,128)(2,1)}), bf16[8,16,448]{2,1,0:T(8,128)(2,1)S(1)}, u32[]{:S(2)}, u32[]{:S(2)}) %all-to-all-start.1) | async-done | bytes 114720 | tf_op jit(solution)/shard_map/all_to_all | solution.py:390
  (173 shorter events, 55.4 us)
Async XLA Ops:
  10.4 12.5 %collective-permute-start = (bf16[448,512]{1,0:T(8,128)(2,1)}, bf16[448,512]{1,0:T(8,128)(2,1)}, u32[]{:S(2)}, u32[]{:S(2)}) collective-permute-start(bf16[448,512]{1,0:T(8,128)(2,1)} %get-tuple-element.121), channel_id=1, source_target_pairs={{0,1},{1,0},{2,3},{3,2},{4,5},{5,4},{6,7},{7,6},{8,9},{9,8},{10,11... | collective-permute-start | bytes 1376264 | tf_op jit(solution)/shard_map/ppermute | solution.py:29
  24.4 20.4 %collective-permute-start.1 = (bf16[1,304,512]{2,1,0:T(8,128)(2,1)S(1)}, bf16[1,304,512]{2,1,0:T(8,128)(2,1)S(1)}, u32[]{:S(2)}, u32[]{:S(2)}) collective-permute-start(bf16[1,304,512]{2,1,0:T(8,128)(2,1)S(1)} %get-tuple-element.120), channel_id=1, source_target_pairs={{0,3},{1,2},{2,1},{3,0},{4,7},{5,6},{6,5},{7,4},{8,11},{9,10},{10,... | collective-permute-start | bytes 933896 | tf_op jit(solution)/shard_map/ppermute | solution.py:29
  27.7 17.1 %collective-permute-start.2 = (bf16[1,304,512]{2,1,0:T(8,128)(2,1)S(1)}, bf16[1,304,512]{2,1,0:T(8,128)(2,1)S(1)}, u32[]{:S(2)}, u32[]{:S(2)}) collective-permute-start(bf16[1,304,512]{2,1,0:T(8,128)(2,1)S(1)} %get-tuple-element.119), channel_id=1, source_target_pairs={{0,4},{1,5},{2,6},{3,7},{4,0},{5,1},{6,2},{7,3},{8,12},{9,13},{10,... | collective-permute-start | bytes 933896 | tf_op jit(solution)/shard_map/ppermute | solution.py:29
  29.7 15.2 %collective-permute-start.3 = (bf16[1,288,512]{2,1,0:T(8,128)(2,1)S(1)}, bf16[1,288,512]{2,1,0:T(8,128)(2,1)S(1)}, u32[]{:S(2)}, u32[]{:S(2)}) collective-permute-start(bf16[1,288,512]{2,1,0:T(8,128)(2,1)S(1)} %slice_bitcast_fusion.2), channel_id=1, source_target_pairs={{0,12},{1,13},{2,14},{3,15},{4,8},{5,9},{6,10},{7,11},{8,4},{9,5},... | collective-permute-start | bytes 884744 | tf_op jit(solution)/shard_map/ppermute | solution.py:29
  34.2 10.4 %all-to-all-start = ((bf16[8,16,448]{2,1,0:T(8,128)(2,1)}), bf16[8,16,448]{2,1,0:T(8,128)(2,1)S(1)}, u32[]{:S(2)}, u32[]{:S(2)}) async-start(bf16[8,16,448]{2,1,0:T(8,128)(2,1)} %bitcast.12), calls=%async_computation | async-start | bytes 262144 | tf_op jit(solution)/shard_map/all_to_all | solution.py:306
  38.5 121.7 %all-gather.2.cloned.1.call-start = ((), (), s32[]{:S(2)}) async-start(), calls=%async_computation.2 | async-start | bytes 8257536 | tf_op jit(solution)/shard_map/all_gather | solution.py:327
  39.6 33.7 %collective-permute-start.9 = (bf16[896,512]{1,0:T(8,128)(2,1)}, bf16[896,512]{1,0:T(8,128)(2,1)}, u32[]{:S(2)}, u32[]{:S(2)}) collective-permute-start(bf16[896,512]{1,0:T(8,128)(2,1)} %pad_maximum_fusion.6), channel_id=1, source_target_pairs={{0,1},{1,0},{2,3},{3,2},{4,5},{5,4},{6,7},{7,6},{8,9},{9,8},{10,11... | collective-permute-start | bytes 2752520 | tf_op jit(solution)/shard_map/ppermute | solution.py:29
  45.9 27.4 %collective-permute-start.7 = (bf16[2,304,512]{2,1,0:T(8,128)(2,1)}, bf16[2,304,512]{2,1,0:T(8,128)(2,1)}, u32[]{:S(2)}, u32[]{:S(2)}) collective-permute-start(bf16[2,304,512]{2,1,0:T(8,128)(2,1)} %pad_maximum_fusion.12), channel_id=1, source_target_pairs={{0,12},{1,13},{2,14},{3,15},{4,8},{5,9},{6,10},{7,11},{8,4},{9,5},... | collective-permute-start | bytes 1867784 | tf_op jit(solution)/shard_map/ppermute | solution.py:29
  47.5 25.8 %collective-permute-start.6 = (bf16[2,304,512]{2,1,0:T(8,128)(2,1)}, bf16[2,304,512]{2,1,0:T(8,128)(2,1)S(1)}, u32[]{:S(2)}, u32[]{:S(2)}) collective-permute-start(bf16[2,304,512]{2,1,0:T(8,128)(2,1)} %pad_maximum_fusion.11), channel_id=1, source_target_pairs={{0,4},{1,5},{2,6},{3,7},{4,0},{5,1},{6,2},{7,3},{8,12},{9,13},{10,... | collective-permute-start | bytes 1867784 | tf_op jit(solution)/shard_map/ppermute | solution.py:29
  47.9 24.5 %collective-permute-start.8 = (bf16[2,288,512]{2,1,0:T(8,128)(2,1)S(1)}, bf16[2,288,512]{2,1,0:T(8,128)(2,1)S(1)}, u32[]{:S(2)}, u32[]{:S(2)}) collective-permute-start(bf16[2,288,512]{2,1,0:T(8,128)(2,1)S(1)} %pad_maximum_fusion.13), channel_id=1, source_target_pairs={{0,3},{1,2},{2,1},{3,0},{4,7},{5,6},{6,5},{7,4},{8,11},{9,10},{10,... | collective-permute-start | bytes 1769480 | tf_op jit(solution)/shard_map/ppermute | solution.py:29
  48.2 27.5 %copy-start.21 = (bf16[1,304,512]{2,1,0:T(8,128)(2,1)S(1)}, bf16[1,304,512]{2,1,0:T(8,128)(2,1)}, u32[]{:S(2)}) copy-start(bf16[1,304,512]{2,1,0:T(8,128)(2,1)} %copy-done.20) | copy-start | bytes 933892
  48.2 18.0 %collective-permute-start.4 = (bf16[1,448,128]{2,1,0:T(8,128)(2,1)S(1)}, bf16[1,448,128]{2,1,0:T(8,128)(2,1)S(1)}, u32[]{:S(2)}, u32[]{:S(2)}) collective-permute-start(bf16[1,448,128]{2,1,0:T(8,128)(2,1)S(1)} %bitcast.73), channel_id=1, source_target_pairs={{0,3},{1,2},{2,1},{3,0},{4,7},{5,6},{6,5},{7,4},{8,11},{9,10},{10,... | collective-permute-start | bytes 344072 | tf_op jit(solution)/shard_map/ppermute | solution.py:29
  66.3 6.1 %collective-permute-start.5 = (bf16[2,448,128]{2,1,0:T(8,128)(2,1)S(1)}, bf16[2,448,128]{2,1,0:T(8,128)(2,1)S(1)}, u32[]{:S(2)}, u32[]{:S(2)}) collective-permute-start(bf16[2,448,128]{2,1,0:T(8,128)(2,1)S(1)} %pad_maximum_fusion.17), channel_id=1, source_target_pairs={{0,4},{1,5},{2,6},{3,7},{4,0},{5,1},{6,2},{7,3},{8,12},{9,13},{10,... | collective-permute-start | bytes 688136 | tf_op jit(solution)/shard_map/ppermute | solution.py:29
  73.3 25.8 %collective-permute-start.11 = (bf16[4,448,128]{2,1,0:T(8,128)(2,1)S(1)}, bf16[4,448,128]{2,1,0:T(8,128)(2,1)}, u32[]{:S(2)}, u32[]{:S(2)}) collective-permute-start(bf16[4,448,128]{2,1,0:T(8,128)(2,1)S(1)} %pad_maximum_fusion.16), channel_id=1, source_target_pairs={{0,12},{1,13},{2,14},{3,15},{4,8},{5,9},{6,10},{7,11},{8,4},{9,5},... | collective-permute-start | bytes 1376264 | tf_op jit(solution)/shard_map/ppermute | solution.py:29
  77.0 45.2 %collective-permute-start.14 = (bf16[4,304,512]{2,1,0:T(8,128)(2,1)S(1)}, bf16[4,304,512]{2,1,0:T(8,128)(2,1)}, u32[]{:S(2)}, u32[]{:S(2)}) collective-permute-start(bf16[4,304,512]{2,1,0:T(8,128)(2,1)S(1)} %pad_maximum_fusion.4.refs_2_), channel_id=1, source_target_pairs={{0,3},{1,2},{2,1},{3,0},{4,7},{5,6},{6,5},{7,4},{8,11},{9,10},{10,... | collective-permute-start | bytes 3735560 | tf_op jit(solution)/shard_map/ppermute | solution.py:29
  78.6 43.6 %collective-permute-start.13 = (bf16[4,304,512]{2,1,0:T(8,128)(2,1)S(1)}, bf16[4,304,512]{2,1,0:T(8,128)(2,1)}, u32[]{:S(2)}, u32[]{:S(2)}) collective-permute-start(bf16[4,304,512]{2,1,0:T(8,128)(2,1)S(1)} %pad_maximum_fusion.3.refs_1_), channel_id=1, source_target_pairs={{0,12},{1,13},{2,14},{3,15},{4,8},{5,9},{6,10},{7,11},{8,4},{9,5},... | collective-permute-start | bytes 3735560 | tf_op jit(solution)/shard_map/ppermute | solution.py:29
  80.8 41.4 %collective-permute-start.15 = (bf16[4,288,512]{2,1,0:T(8,128)(2,1)}, bf16[4,288,512]{2,1,0:T(8,128)(2,1)}, u32[]{:S(2)}, u32[]{:S(2)}) collective-permute-start(bf16[4,288,512]{2,1,0:T(8,128)(2,1)} %pad_maximum_fusion.5.refs_3_), channel_id=1, source_target_pairs={{0,4},{1,5},{2,6},{3,7},{4,0},{5,1},{6,2},{7,3},{8,12},{9,13},{10,... | collective-permute-start | bytes 3538952 | tf_op jit(solution)/shard_map/ppermute | solution.py:29
  82.9 17.5 %collective-permute-start.10 = (bf16[256,896]{1,0:T(8,128)(2,1)}, bf16[256,896]{1,0:T(8,128)(2,1)S(1)}, u32[]{:S(2)}, u32[]{:S(2)}) collective-permute-start(bf16[256,896]{1,0:T(8,128)(2,1)} %constant_dynamic-slice_fusion.8), channel_id=1, source_target_pairs={{0,1},{1,0},{2,3},{3,2},{4,5},{5,4},{6,7},{7,6},{8,9},{9,8},{10,11... | collective-permute-start | bytes 1376264 | tf_op jit(solution)/shard_map/ppermute | solution.py:29
  99.1 25.5 %copy-start.1 = (f32[7168,1]{1,0:T(8,128)S(1)}, f32[7168,1]{1,0:T(8,128)}, u32[]{:S(2)}) copy-start(f32[7168,1]{1,0:T(8,128)} %copy.67.refs_4_.refs_5_.refs_6_.gain_ref) | copy-start | bytes 86020
  100.4 21.7 %collective-permute-start.12 = (bf16[1,256,896]{2,1,0:T(8,128)(2,1)S(1)}, bf16[1,256,896]{2,1,0:T(8,128)(2,1)S(1)}, u32[]{:S(2)}, u32[]{:S(2)}) collective-permute-start(bf16[1,256,896]{2,1,0:T(8,128)(2,1)S(1)} %bitcast.77), channel_id=1, source_target_pairs={{0,32},{16,48},{32,0},{48,16},{64,96},{80,112},{96,64},{112,80},{1... | collective-permute-start | bytes 1376264 | tf_op jit(solution)/shard_map/ppermute | solution.py:33
  101.1 30.7 %collective-permute-start.16 = (bf16[8,448,128]{2,1,0:T(8,128)(2,1)S(1)}, bf16[8,448,128]{2,1,0:T(8,128)(2,1)S(1)}, u32[]{:S(2)}, u32[]{:S(2)}) collective-permute-start(bf16[8,448,128]{2,1,0:T(8,128)(2,1)S(1)} %pad_maximum_fusion.7), channel_id=1, source_target_pairs={{0,1},{1,0},{2,3},{3,2},{4,5},{5,4},{6,7},{7,6},{8,9},{9,8},{10,11... | collective-permute-start | bytes 2752520 | tf_op jit(solution)/shard_map/ppermute | solution.py:29
  122.2 19.4 %copy-start.13 = (bf16[2,256,896]{2,1,0:T(8,128)(2,1)}, bf16[2,256,896]{2,1,0:T(8,128)(2,1)S(1)}, u32[]{:S(2)}) copy-start(bf16[2,256,896]{2,1,0:T(8,128)(2,1)S(1)} %pad_maximum_fusion.8) | copy-start | bytes 2752516
  122.2 19.4 %collective-permute-start.17 = (bf16[2,256,896]{2,1,0:T(8,128)(2,1)S(1)}, bf16[2,256,896]{2,1,0:T(8,128)(2,1)S(1)}, u32[]{:S(2)}, u32[]{:S(2)}) collective-permute-start(bf16[2,256,896]{2,1,0:T(8,128)(2,1)S(1)} %pad_maximum_fusion.8), channel_id=1, source_target_pairs={{0,96},{16,112},{32,64},{48,80},{64,32},{80,48},{96,0},{112,16},{1... | collective-permute-start | bytes 2752520 | tf_op jit(solution)/shard_map/ppermute | solution.py:33
  124.6 7.5 %copy-start.9 = (bf16[1,7168,256]{2,1,0:T(8,128)(2,1)S(1)}, bf16[1,7168,256]{2,1,0:T(8,128)(2,1)}, u32[]{:S(2)}) copy-start(bf16[1,7168,256]{2,1,0:T(8,128)(2,1)} %up_ref.1) | copy-start | bytes 11010052
  143.3 13.7 %collective-permute-start.18 = (bf16[4,256,896]{2,1,0:T(8,128)(2,1)}, bf16[4,256,896]{2,1,0:T(8,128)(2,1)}, u32[]{:S(2)}, u32[]{:S(2)}) collective-permute-start(bf16[4,256,896]{2,1,0:T(8,128)(2,1)} %pad_maximum_fusion.2), channel_id=1, source_target_pairs={{0,16},{16,0},{32,48},{48,32},{64,80},{80,64},{96,112},{112,96},{1... | collective-permute-start | bytes 5505032 | tf_op jit(solution)/shard_map/ppermute | solution.py:33
  165.4 8.4 %copy-start.3 = (f32[7168,1]{1,0:T(8,128)S(1)}, f32[7168,1]{1,0:T(8,128)}, u32[]{:S(2)}) copy-start(f32[7168,1]{1,0:T(8,128)} %copy.67.refs_4_.refs_5_.refs_6_.gain_ref) | copy-start | bytes 86020
  171.8 25.5 %collective-permute-start.25 = (bf16[2,2,2,1,448,128]{5,4,3,2,1,0:T(8,128)(2,1)}, bf16[2,2,2,1,448,128]{5,4,3,2,1,0:T(8,128)(2,1)}, u32[]{:S(2)}, u32[]{:S(2)}) collective-permute-start(bf16[2,2,2,1,448,128]{5,4,3,2,1,0:T(8,128)(2,1)} %pad_maximum_fusion.10), channel_id=1, source_target_pairs={{0,1},{1,0},{2,3},{3,2},{4,5},{5,4},{6,7},{7,6},{8,9},{9,8},{10,11... | collective-permute-start | bytes 2752520 | tf_op jit(solution)/shard_map/ppermute | solution.py:29
  173.7 7.3 %copy-start.7 = (bf16[8,256,896]{2,1,0:T(8,128)(2,1)S(1)}, bf16[8,256,896]{2,1,0:T(8,128)(2,1)}, u32[]{:S(2)}) copy-start(bf16[8,256,896]{2,1,0:T(8,128)(2,1)} %pad_maximum_fusion.other) | copy-start | bytes 11010052
  173.7 7.3 %copy-start.12 = (bf16[256,7168]{1,0:T(8,128)(2,1)S(1)}, bf16[256,7168]{1,0:T(8,128)(2,1)}, u32[]{:S(2)}) copy-start(bf16[256,7168]{1,0:T(8,128)(2,1)} %own.1) | copy-start | bytes 11010052
  190.7 29.8 %collective-permute-start.21 = (bf16[4,304,512]{2,1,0:T(8,128)(2,1)}, bf16[4,304,512]{2,1,0:T(8,128)(2,1)}, u32[]{:S(2)}, u32[]{:S(2)}) collective-permute-start(bf16[4,304,512]{2,1,0:T(8,128)(2,1)} %get-tuple-element.91), channel_id=1, source_target_pairs={{0,4},{1,5},{2,6},{3,7},{4,0},{5,1},{6,2},{7,3},{8,12},{9,13},{10,... | collective-permute-start | bytes 3735560 | tf_op jit(solution)/shard_map/ppermute | solution.py:29
  192.5 32.8 %collective-permute-start.19 = (bf16[4,304,512]{2,1,0:T(8,128)(2,1)}, bf16[4,304,512]{2,1,0:T(8,128)(2,1)}, u32[]{:S(2)}, u32[]{:S(2)}) collective-permute-start(bf16[4,304,512]{2,1,0:T(8,128)(2,1)} %get-tuple-element.89), channel_id=1, source_target_pairs={{0,3},{1,2},{2,1},{3,0},{4,7},{5,6},{6,5},{7,4},{8,11},{9,10},{10,... | collective-permute-start | bytes 3735560 | tf_op jit(solution)/shard_map/ppermute | solution.py:29
  195.1 33.7 %collective-permute-start.23 = (bf16[4,288,512]{2,1,0:T(8,128)(2,1)}, bf16[4,288,512]{2,1,0:T(8,128)(2,1)}, u32[]{:S(2)}, u32[]{:S(2)}) collective-permute-start(bf16[4,288,512]{2,1,0:T(8,128)(2,1)} %get-tuple-element.93), channel_id=1, source_target_pairs={{0,12},{1,13},{2,14},{3,15},{4,8},{5,9},{6,10},{7,11},{8,4},{9,5},... | collective-permute-start | bytes 3538952 | tf_op jit(solution)/shard_map/ppermute | solution.py:29
  199.0 36.2 %collective-permute-start.26 = (bf16[1,2,2,1,448,128]{5,4,3,2,1,0:T(8,128)(2,1)S(1)}, bf16[1,2,2,1,448,128]{5,4,3,2,1,0:T(8,128)(2,1)S(1)}, u32[]{:S(2)}, u32[]{:S(2)}) collective-permute-start(bf16[1,2,2,1,448,128]{5,4,3,2,1,0:T(8,128)(2,1)S(1)} %constant_dynamic-slice_fusion.2), channel_id=1, source_target_pairs={{0,12},{1,13},{2,14},{3,15},{4,8},{5,9},{6,10},{7,11},{8,4},{9,5},... | collective-permute-start | bytes 1376264 | tf_op jit(solution)/shard_map/ppermute | solution.py:29
  223.0 5.8 %copy-start.11 = (bf16[4,288,512]{2,1,0:T(8,128)(2,1)S(1)}, bf16[4,288,512]{2,1,0:T(8,128)(2,1)}, u32[]{:S(2)}) copy-start(bf16[4,288,512]{2,1,0:T(8,128)(2,1)} %copy-done.10) | copy-start | bytes 3538948
  223.0 24.9 %collective-permute-start.22 = (bf16[2,304,512]{2,1,0:T(8,128)(2,1)}, bf16[2,304,512]{2,1,0:T(8,128)(2,1)}, u32[]{:S(2)}, u32[]{:S(2)}) collective-permute-start(bf16[2,304,512]{2,1,0:T(8,128)(2,1)} %get-tuple-element.108), channel_id=1, source_target_pairs={{0,12},{1,13},{2,14},{3,15},{4,8},{5,9},{6,10},{7,11},{8,4},{9,5},... | collective-permute-start | bytes 1867784 | tf_op jit(solution)/shard_map/ppermute | solution.py:29
  227.7 20.2 %collective-permute-start.20 = (bf16[2,304,512]{2,1,0:T(8,128)(2,1)}, bf16[2,304,512]{2,1,0:T(8,128)(2,1)S(1)}, u32[]{:S(2)}, u32[]{:S(2)}) collective-permute-start(bf16[2,304,512]{2,1,0:T(8,128)(2,1)} %get-tuple-element.106), channel_id=1, source_target_pairs={{0,4},{1,5},{2,6},{3,7},{4,0},{5,1},{6,2},{7,3},{8,12},{9,13},{10,... | collective-permute-start | bytes 1867784 | tf_op jit(solution)/shard_map/ppermute | solution.py:29
  231.2 16.7 %collective-permute-start.24 = (bf16[2,288,512]{2,1,0:T(8,128)(2,1)}, bf16[2,288,512]{2,1,0:T(8,128)(2,1)}, u32[]{:S(2)}, u32[]{:S(2)}) collective-permute-start(bf16[2,288,512]{2,1,0:T(8,128)(2,1)} %get-tuple-element.109), channel_id=1, source_target_pairs={{0,3},{1,2},{2,1},{3,0},{4,7},{5,6},{6,5},{7,4},{8,11},{9,10},{10,... | collective-permute-start | bytes 1769480 | tf_op jit(solution)/shard_map/ppermute | solution.py:29
  236.1 11.8 %collective-permute-start.27 = (bf16[1,1,2,1,448,128]{5,4,3,2,1,0:T(8,128)(2,1)}, bf16[1,1,2,1,448,128]{5,4,3,2,1,0:T(8,128)(2,1)S(1)}, u32[]{:S(2)}, u32[]{:S(2)}) collective-permute-start(bf16[1,1,2,1,448,128]{5,4,3,2,1,0:T(8,128)(2,1)} %constant_dynamic-slice_fusion.1), channel_id=1, source_target_pairs={{0,4},{1,5},{2,6},{3,7},{4,0},{5,1},{6,2},{7,3},{8,12},{9,13},{10,... | collective-permute-start | bytes 688136 | tf_op jit(solution)/shard_map/ppermute | solution.py:29
  247.9 11.6 %copy-start.26 = (bf16[2,304,512]{2,1,0:T(8,128)(2,1)}, bf16[2,304,512]{2,1,0:T(8,128)(2,1)S(1)}, u32[]{:S(2)}) copy-start(bf16[2,304,512]{2,1,0:T(8,128)(2,1)S(1)} %collective-permute-done.20) | copy-start | bytes 1867780
  248.0 11.5 %collective-permute-start.28 = (bf16[1,304,512]{2,1,0:T(8,128)(2,1)S(1)}, bf16[1,304,512]{2,1,0:T(8,128)(2,1)S(1)}, u32[]{:S(2)}, u32[]{:S(2)}) collective-permute-start(bf16[1,304,512]{2,1,0:T(8,128)(2,1)S(1)} %add_convert_fusion.12), channel_id=1, source_target_pairs={{0,12},{1,13},{2,14},{3,15},{4,8},{5,9},{6,10},{7,11},{8,4},{9,5},... | collective-permute-start | bytes 933896 | tf_op jit(solution)/shard_map/ppermute | solution.py:29
  250.7 7.7 %collective-permute-start.30 = (bf16[1,288,512]{2,1,0:T(8,128)(2,1)S(1)}, bf16[1,288,512]{2,1,0:T(8,128)(2,1)S(1)}, u32[]{:S(2)}, u32[]{:S(2)}) collective-permute-start(bf16[1,288,512]{2,1,0:T(8,128)(2,1)S(1)} %add_convert_fusion.15), channel_id=1, source_target_pairs={{0,4},{1,5},{2,6},{3,7},{4,0},{5,1},{6,2},{7,3},{8,12},{9,13},{10,... | collective-permute-start | bytes 884744 | tf_op jit(solution)/shard_map/ppermute | solution.py:29
  252.1 9.1 %collective-permute-start.29 = (bf16[1,304,512]{2,1,0:T(8,128)(2,1)S(1)}, bf16[1,304,512]{2,1,0:T(8,128)(2,1)S(1)}, u32[]{:S(2)}, u32[]{:S(2)}) collective-permute-start(bf16[1,304,512]{2,1,0:T(8,128)(2,1)S(1)} %add_convert_fusion.9), channel_id=1, source_target_pairs={{0,3},{1,2},{2,1},{3,0},{4,7},{5,6},{6,5},{7,4},{8,11},{9,10},{10,... | collective-permute-start | bytes 933896 | tf_op jit(solution)/shard_map/ppermute | solution.py:29
  260.6 18.2 %copy-start.18 = (bf16[1024,448]{0,1:T(8,128)(2,1)S(1)}, bf16[1024,448]{0,1:T(8,128)(2,1)}, u32[]{:S(2)}) copy-start(bf16[1024,448]{0,1:T(8,128)(2,1)} %param.14) | copy-start | bytes 2752516
  260.6 18.2 %copy-start.25 = (bf16[1024,128]{1,0:T(8,128)(2,1)S(1)}, bf16[1024,128]{1,0:T(8,128)(2,1)}, u32[]{:S(2)}) copy-start(bf16[1024,128]{1,0:T(8,128)(2,1)} %copy-done.24) | copy-start | bytes 786436
  260.7 18.2 %copy-start.33 = (f32[128]{0:T(128)S(1)}, f32[128]{0:T(128)}, u32[]{:S(2)}) copy-start(f32[128]{0:T(128)} %get-tuple-element.101) | copy-start | bytes 1540
  262.4 16.4 %collective-permute-start.31 = (bf16[448,512]{1,0:T(8,128)(2,1)S(1)}, bf16[448,512]{1,0:T(8,128)(2,1)S(1)}, u32[]{:S(2)}, u32[]{:S(2)}) collective-permute-start(bf16[448,512]{1,0:T(8,128)(2,1)S(1)} %get-tuple-element.113), channel_id=1, source_target_pairs={{0,1},{1,0},{2,3},{3,2},{4,5},{5,4},{6,7},{7,6},{8,9},{9,8},{10,11... | collective-permute-start | bytes 1376264 | tf_op jit(solution)/shard_map/ppermute | solution.py:29
  262.5 6.1 %collective-permute-start.32 = (bf16[1,1,1,1,448,128]{5,4,3,2,1,0:T(8,128)(2,1)S(1)}, bf16[1,1,1,1,448,128]{5,4,3,2,1,0:T(8,128)(2,1)S(1)}, u32[]{:S(2)}, u32[]{:S(2)}) collective-permute-start(bf16[1,1,1,1,448,128]{5,4,3,2,1,0:T(8,128)(2,1)S(1)} %constant_dynamic-slice_fusion), channel_id=1, source_target_pairs={{0,3},{1,2},{2,1},{3,0},{4,7},{5,6},{6,5},{7,4},{8,11},{9,10},{10,... | collective-permute-start | bytes 344072 | tf_op jit(solution)/shard_map/ppermute | solution.py:29
  269.4 9.4 %all-to-all-start.1 = ((bf16[8,16,448]{2,1,0:T(8,128)(2,1)}), bf16[8,16,448]{2,1,0:T(8,128)(2,1)S(1)}, u32[]{:S(2)}, u32[]{:S(2)}) async-start(bf16[8,16,448]{2,1,0:T(8,128)(2,1)} %bitcast.27), calls=%async_computation.1 | async-start | bytes 262144 | tf_op jit(solution)/shard_map/all_to_all | solution.py:390
  (22 other events, 59.4 us)
Sparse Core Ops, SparseCore 0:
  73.4 51.5 all-gather.1

commit v4 on v1

v4 whole, which is shorter than its diff:
```python
import functools

import jax
import jax.numpy as jnp
from jax import lax
from jax.experimental import pallas as pl
from jax.experimental.pallas import tpu as pltpu
from jax.sharding import PartitionSpec as P

EPSILON = 1e-05
NODE_CAP = 16
GRAY = (0, 1, 3, 2)

LOCAL_LABEL = [GRAY[i % 4] | GRAY[i // 4] << 2 for i in range(16)]
LOCAL_AT = {label: i for i, label in enumerate(LOCAL_LABEL)}

STREAMS = ((0, 1, 2, 3), (1, 2, 3, 0), (2, 3, 0, 1), (3, 0, 1, 2))


def flip_local(array, bit):
    return lax.ppermute(array, "local", [(i, LOCAL_AT[LOCAL_LABEL[i] ^ (1 << bit)]) for i in range(16)])


def route_slots(ids_block, window):
    flat_ids = ids_block.reshape(-1)
    expert_range = jnp.arange(window, dtype=jnp.int32)
    member = (flat_ids[:, None] == expert_range[None, :]).astype(jnp.int32)
    before = jnp.cumsum(member, axis=0) - member
    route_rank = jnp.sum(before * member, axis=1)
    kept = (jnp.sum(member, axis=1) > 0) & (route_rank < NODE_CAP)
    slot = jnp.where(kept, flat_ids * NODE_CAP + route_rank, -1)
    return slot.reshape(ids_block.shape)


def transposed_dot(weight, rows):
    return lax.dot_general(weight, rows, (((0,), (0,)), ((), ())), preferred_element_type=jnp.float32)


def silu(value):
    return value / (1.0 + jnp.exp(-value))


def gate_up_kernel(features, weight_ref, x_ref, hidden_ref, total, squares):
    step = pl.program_id(0)
    as_float = x_ref[...].astype(jnp.float32)
    square_sum = jnp.sum(as_float * as_float, axis=0, keepdims=True)
    part = jnp.dot(weight_ref[...], x_ref[...], preferred_element_type=jnp.float32)

    @pl.when(step == 0)
    def _():
        total[...] = part
        squares[...] = square_sum

    @pl.when(step > 0)
    def _():
        total[...] += part
        squares[...] += square_sum

    @pl.when(step == pl.num_programs(0) - 1)
    def _():
        scale = lax.rsqrt(squares[...] / features + EPSILON)
        half = total.shape[0] // 2
        hidden_ref[...] = (silu(total[:half] * scale) * (total[half:] * scale)).astype(jnp.bfloat16)


def gate_up(weight, rows):
    both, features = weight.shape
    columns = rows.shape[1]
    deep = 1024
    return pl.pallas_call(
        functools.partial(gate_up_kernel, features),
        grid=(features // deep,),
        in_specs=[pl.BlockSpec((both, deep), lambda m: (0, m)), pl.BlockSpec((deep, columns), lambda m: (m, 0))],
        out_specs=pl.BlockSpec((both // 2, columns), lambda m: (0, 0)),
        out_shape=jax.ShapeDtypeStruct((both // 2, columns), jnp.bfloat16),
        scratch_shapes=[pltpu.VMEM((both, columns), jnp.float32), pltpu.VMEM((1, columns), jnp.float32)],
        compiler_params=pltpu.CompilerParams(vmem_limit_bytes=56 << 20),
        cost_estimate=pl.CostEstimate(
            flops=2 * features * columns * both, bytes_accessed=2 * features * (columns + both), transcendentals=0
        ),
    )(weight, rows)


def down_kernel(slice_ref, *refs):
    weights, hidden_ref, outs = refs[:4], refs[4], refs[5:]
    columns = outs[0].shape[-1]
    for s in range(4):
        part = jnp.dot(
            weights[s][0], hidden_ref[:, s * columns : (s + 1) * columns], preferred_element_type=jnp.float32
        )
        outs[s][0] = part.astype(jnp.bfloat16)


def down(slice_of, weight, hidden, sent):
    blocks, rows, deep = weight.shape
    columns = hidden.shape[1] // 4

    def weight_spec(s):
        a, b, c, d = STREAMS[s]

        def index(j, at):
            return at[sent << a | ((j >> 2) & 1) << b | ((j >> 1) & 1) << c | (j & 1) << d], 0, 0

        return pl.BlockSpec((1, rows, deep), index)

    return pl.pallas_call(
        down_kernel,
        grid_spec=pltpu.PrefetchScalarGridSpec(
            num_scalar_prefetch=1,
            grid=(blocks // 2,),
            in_specs=[weight_spec(s) for s in range(4)] + [pl.BlockSpec(hidden.shape, lambda j, at: (0, 0))],
            out_specs=[pl.BlockSpec((1, rows, columns), lambda j, at: (j, 0, 0))] * 4,
        ),
        out_shape=[jax.ShapeDtypeStruct((blocks // 2, rows, columns), jnp.bfloat16)] * 4,
        compiler_params=pltpu.CompilerParams(vmem_limit_bytes=24 << 20),
        cost_estimate=pl.CostEstimate(
            flops=4 * blocks * rows * deep * columns, bytes_accessed=4 * blocks * rows * (deep + columns), transcendentals=0
        ),
    )(slice_of, *[weight] * 4, hidden)


def expert_kernel(blocks, features, at_ref, x_ref, gate_ref, up_ref, gain_ref, hidden_ref, gate_total, up_total, squares):
    step = pl.program_id(0)

    @pl.when(step == 0)
    def _():
        gate_total[...] = jnp.zeros_like(gate_total)
        up_total[...] = jnp.zeros_like(up_total)
        squares[...] = jnp.zeros_like(squares)

    as_float = x_ref[0].astype(jnp.float32)
    squares[...] += jnp.sum(as_float * as_float, axis=0, keepdims=True)
    rows = (as_float * gain_ref[...]).astype(jnp.bfloat16)
    gate_total[...] += transposed_dot(gate_ref[0], rows)
    up_total[...] += transposed_dot(up_ref[0], rows)

    @pl.when(step == blocks - 1)
    def _():
        scale = lax.rsqrt(squares[...] / features + EPSILON)
        hidden_ref[...] = (silu(gate_total[...] * scale) * (up_total[...] * scale)).astype(jnp.bfloat16)


def expert_gate_up(slice_of, pooled, gate_weight, up_weight, gain_column):
    blocks, rows, columns = pooled.shape
    hidden = gate_weight.shape[-1]
    weight_spec = pl.BlockSpec((1, rows, hidden), lambda m, at: (0, at[m], 0))
    return pl.pallas_call(
        functools.partial(expert_kernel, blocks, blocks * rows),
        grid_spec=pltpu.PrefetchScalarGridSpec(
            num_scalar_prefetch=1,
            grid=(blocks,),
            in_specs=[
                pl.BlockSpec((1, rows, columns), lambda m, at: (m, 0, 0)),
                weight_spec,
                weight_spec,
                pl.BlockSpec((rows, 1), lambda m, at: (at[m], 0)),
            ],
            out_specs=pl.BlockSpec((hidden, columns), lambda m, at: (0, 0)),
            scratch_shapes=[
                pltpu.VMEM((hidden, columns), jnp.float32),
                pltpu.VMEM((hidden, columns), jnp.float32),
                pltpu.VMEM((1, columns), jnp.float32),
            ],
        ),
        out_shape=jax.ShapeDtypeStruct((hidden, columns), jnp.bfloat16),
        compiler_params=pltpu.CompilerParams(vmem_limit_bytes=24 << 20),
        cost_estimate=pl.CostEstimate(
            flops=4 * blocks * rows * columns * hidden,
            bytes_accessed=2 * blocks * rows * (columns + 2 * hidden),
            transcendentals=0,
        ),
    )(slice_of, pooled, gate_weight, up_weight, gain_column)


def add_pair(kept, got):
    return (kept.astype(jnp.float32) + got.astype(jnp.float32)).astype(jnp.bfloat16)


def shards(
    tokens,
    norm_gain,
    dense_gate,
    dense_up,
    dense_down,
    expert_gate,
    expert_up,
    expert_down,
    expert_ids,
    route_gates,
):
    node_count = lax.axis_size("node")
    local_index = lax.axis_index("local")
    slice_width = tokens.shape[1]
    slot_count = node_count * NODE_CAP
    slice_table = [[LOCAL_AT[LOCAL_LABEL[i] ^ m] for m in range(16)] for i in range(16)]
    slice_of = jnp.asarray(slice_table, jnp.int32)[local_index]

    columns = tokens.T
    whole_columns = lax.all_gather(columns, "local", axis=0, tiled=True)

    slot = route_slots(expert_ids, node_count)
    slot_range = jnp.arange(slot_count, dtype=jnp.int32)
    match_float = (slot[:, :, None] == slot_range[None, None, :]).astype(jnp.float32)
    chosen = jnp.sum(match_float, axis=1).astype(jnp.bfloat16)
    slot_gate = jnp.sum(match_float * route_gates[:, :, None], axis=(0, 1))
    send_rows = lax.dot_general(
        chosen, tokens, (((0,), (0,)), ((), ())), preferred_element_type=jnp.float32
    ).astype(jnp.bfloat16)
    pooled = lax.all_to_all(
        send_rows.reshape(node_count, NODE_CAP, slice_width), "node", split_axis=0, concat_axis=0, tiled=True
    )
    pooled = pooled.reshape(slot_count, slice_width).T[None]

    gain_column = norm_gain[:, None]
    for bit in range(4):
        got = flip_local(pooled, bit)
        if bit == 1:
            dense_gate, dense_up, _ = lax.optimization_barrier((dense_gate, dense_up, pooled))
            weight = jnp.concatenate(
                [(w.astype(jnp.float32) * gain_column).astype(jnp.bfloat16).T for w in (dense_gate, dense_up)], axis=0
            )
            got, weight = lax.optimization_barrier((got, weight))
        if bit == 2:
            dense_down, _ = lax.optimization_barrier((dense_down, pooled))
            turned_down = dense_down.T.reshape(16, slice_width, dense_down.shape[0])
            got, turned_down = lax.optimization_barrier((got, turned_down))
        pooled = jnp.concatenate([pooled, got], axis=0)
    expert_hidden = expert_gate_up(slice_of, pooled, expert_gate, expert_up, gain_column)
    expert_partial = transposed_dot(expert_down[0], expert_hidden).astype(jnp.bfloat16)
    expert_partial = expert_partial.reshape(16, slice_width, slot_count)

    def halve(array, bit):
        half = 1 << bit
        upper = (local_index >> bit) & 1
        keep = lax.dynamic_slice_in_dim(array, upper * half, half, 0)
        return keep, lax.dynamic_slice_in_dim(array, (1 - upper) * half, half, 0)

    keep, send = halve(expert_partial, 3)
    keep, send, whole_columns = lax.optimization_barrier((keep, send, whole_columns))
    expert_got = flip_local(send, 3)

    hidden = gate_up(weight, whole_columns)
    hidden, expert_got = lax.optimization_barrier((hidden, expert_got))
    keep, send = halve(add_pair(keep, expert_got), 2)
    expert_got = flip_local(send, 2)
    sent = down(slice_of, turned_down, hidden, 1)
    arrived = [flip_local(sent[s], STREAMS[s][0]) for s in range(4)]
    hidden, _ = lax.optimization_barrier((hidden, sent))
    sums = down(slice_of, turned_down, hidden, 0)
    expert_got, sums = lax.optimization_barrier((expert_got, sums))
    for step in (1, 2, 3):
        if step < 3:
            keep, send = halve(add_pair(keep, expert_got), 2 - step)
            expert_got = flip_local(send, 2 - step)
        half = sums[0].shape[0] // 2
        came = [flip_local(add_pair(sums[s][half:], arrived[s][half:]), STREAMS[s][step]) for s in range(4)]
        sums = [add_pair(sums[s][:half], arrived[s][:half]) for s in range(4)]
        arrived = came
        if step == 1:
            sums, expert_got = lax.optimization_barrier((sums, expert_got))
        if step == 2:
            expert_out = add_pair(keep, expert_got)[0].T
            returned = lax.all_to_all(
                expert_out.reshape(node_count, NODE_CAP, slice_width), "node", split_axis=0, concat_axis=0, tiled=True
            ).reshape(slot_count, slice_width)
            route_term = (slot_gate[:, None] * returned.astype(jnp.float32)).astype(jnp.bfloat16)
            arrived[3], route_term = lax.optimization_barrier((arrived[3], route_term))
    expert_part = lax.dot_general(
        route_term, chosen, (((0,), (1,)), ((), ())), preferred_element_type=jnp.float32
    )
    dense_part = jnp.concatenate(
        [sums[s][0].astype(jnp.float32) + arrived[s][0].astype(jnp.float32) for s in range(4)], axis=1
    )
    return (columns.astype(jnp.float32) + dense_part + expert_part).astype(jnp.bfloat16).T


def solution(mesh):
    return jax.shard_map(
        shards,
        mesh=mesh,
        in_specs=(
            P("node", "local"),
            P(),
            P(None, "local"),
            P(None, "local"),
            P("local", None),
            P("node", None, "local"),
            P("node", None, "local"),
            P("node", "local", None),
            P("node", None),
            P("node", None),
        ),
        out_specs=P("node", "local"),
        check_vma=False,
    )
```

time: 287 us -> 316 us (1.10)
  blocking collectives: 99 us -> 10.3 us
  waiting for transfers between devices: 109 us -> 141 us
  Pallas kernels: 0 us -> 31.5 us
  local copies, waits for them, and re-layouts: 9.71 us -> 41.2 us
  matrix products: 33.9 us -> 3.67 us
  starting transfers between devices: 5.34 us -> 34.3 us
  other arithmetic: 15.5 us -> 39 us
    ppermute x0 -> x24, waiting for transfers between devices: none -> 135 us  [flip_local(): lax.ppermute(array, 'local', [(i, LOCAL_AT[LOCAL_LABEL[i] ^ 1 << bit]) fo...]
    all_gather x1, waiting for transfers between devices: 54.9 us -> 0.01 us  [shards(): whole_columns = lax.all_gather(columns, 'local', axis=0, tiled=True)]
    all_to_all x2 -> x0, blocking collectives: 46.5 us -> none  [the longest x1 36.1 us: shards(): lax.all_to_all(partial_blocks, 'local', split_axis=0, concat_axis=0, tile...]
    psum x1 -> x0, blocking collectives: 42.4 us -> none  [shards(): square_sum = lax.psum(jnp.sum(as_float * as_float, axis=-1), 'local')]
    all_to_all x1, waiting for transfers between devices: 39.5 us -> 5.21 us  [shards(): lax.all_to_all(expert_out.reshape(node_count, NODE_CAP, slice_width), 'no...]
    pallas_call x0 -> x4, Pallas kernels: none -> 31.5 us  [the longest x1 14.8 us: gate_up(): pl.pallas_call(functools.partial(gate_up_kernel, features), grid=(feature...]
    ppermute x0 -> x24, starting transfers between devices: none -> 30.8 us  [flip_local(): lax.ppermute(array, 'local', [(i, LOCAL_AT[LOCAL_LABEL[i] ^ 1 << bit]) fo...]
    dot_general x5 -> x2, matrix products: 33.5 us -> 3.27 us  [the longest x1 1.91 us: transposed_dot(): lax.dot_general(weight, rows, (((0,), (0,)), ((), ())), preferred_element...]
  transfers between devices with their start and end apart: 3 -> 26, of which waited for: 3 -> 13; matrix products, arithmetic and copies ran while one was open for 11% -> 23% of each run, Pallas kernels for 0% -> 8%
where the time goes in v4:
time: 316 us; the launch traced here: 315 us
  waiting for transfers between devices  141 us (45%)
  local copies, waits for them, and re-layouts  41.2 us (13%)
  other arithmetic  39 us (12%)
  starting transfers between devices  34.3 us (11%)
  Pallas kernels  31.5 us (10%)
  between operations  13.8 us (4%)
  blocking collectives  10.3 us (3%)
  matrix products  3.67 us (1%)
    ppermute x24, waiting for transfers between devices, flip_local(): lax.ppermute(array, 'local', [(i, LOCAL_AT[LOCAL_LABEL[i] ^ 1 << bit]) fo...  135 us
    ppermute x24, starting transfers between devices, flip_local(): lax.ppermute(array, 'local', [(i, LOCAL_AT[LOCAL_LABEL[i] ^ 1 << bit]) fo...  30.8 us
    convert_element_type x15, other arithmetic, add_pair(): (kept.astype(jnp.float32) + got.astype(jnp.float32)).astype(jnp.bfloat16)  21.1 us
    pallas_call x1, Pallas kernels, gate_up(): pl.pallas_call(functools.partial(gate_up_kernel, features), grid=(feature...  14.8 us
    optimization_barrier x2, local copies, waits for them, and re-layouts, shards(): lax.optimization_barrier((dense_gate, dense_up, pooled))  11.9 us
    unnamed x45, local copies, waits for them, and re-layouts  11.1 us
    all_to_all x1, blocking collectives, shards(): lax.all_to_all(send_rows.reshape(node_count, NODE_CAP, slice_width), 'nod...  10.3 us
    pallas_call x2, Pallas kernels, down(): pl.pallas_call(down_kernel, grid_spec=pltpu.PrefetchScalarGridSpec(num_sc...  9.23 us
  transfers between devices with their start and end apart: 26, of which 13 were waited for; matrix products, arithmetic and copies ran while one was open for 23% of the time, Pallas kernels for 8%

profile of v4, /device:TPU:0, one launch (start us, length us, event | category | flops | bytes accessed | tf_op | source)
XLA Modules:
  0.0 314.8 jit_solution(259141918644249799)
XLA Ops:
  9.0 2.3 reduce-window.6
  15.3 10.3 %all_to_all.10 = bf16[8,16,448]{2,1,0:T(8,128)(2,1)S(1)} all-to-all(bf16[8,16,448]{2,1,0:T(8,128)(2,1)S(1)} %bitcast.72), channel_id=1, replica_groups=mesh['node'=8,'local'=16] {'node'}, dimensions={0} | all-to-all | bytes 229376 | tf_op jit(solution)/shard_map/all_to_all | solution.py:209
  25.8 1.7 collective-permute-start
  27.4 6.4 %collective-permute-done = bf16[1,448,128]{2,1,0:T(8,128)(2,1)S(1)} collective-permute-done((bf16[1,448,128]{2,1,0:T(8,128)(2,1)S(1)}, bf16[1,448,128]{2,1,0:T(8,128)(2,1)S(1)}, u32[]{:S(2)}, u32[]{:S(2)}) %collective-permute-start) | collective-permute-done | bytes 114720 | tf_op jit(solution)/shard_map/ppermute | solution.py:21
  34.5 3.0 collective-permute-start.1
  37.6 6.0 %copy.49 = bf16[7168,256]{0,1:T(8,128)(2,1)} copy(bf16[7168,256]{1,0:T(8,128)(2,1)} %param.13) | data formatting | bytes 7340032 | tf_op jit(solution)/shard_map/optimization_barrier | solution.py:218
  43.5 6.0 %copy.50 = bf16[7168,256]{0,1:T(8,128)(2,1)} copy(bf16[7168,256]{1,0:T(8,128)(2,1)} %param.14) | data formatting | bytes 7340032 | tf_op jit(solution)/shard_map/optimization_barrier | solution.py:218
  49.5 6.7 %fusion.1 = (bf16[256,7168]{1,0:T(8,128)(2,1)S(1)}, bf16[256,7168]{1,0:T(8,128)(2,1)}) fusion(bf16[7168,256]{0,1:T(8,128)(2,1)} %copy.49, f32[7168]{0:T(1024)S(1)} %copy-done.17, bf16[7168,256]{0,1:T(8,128)(2,1)} %copy.50), kind=kLoop, calls=%fused_computation.5 | loop fusion | flops 11010048 | bytes 14708736 | tf_op jit(solution)/shard_map/transpose | solution.py:220
  56.2 5.5 %pad_maximum_fusion.weight_ref = bf16[512,7168]{1,0:T(8,128)(2,1)} fusion(bf16[256,7168]{1,0:T(8,128)(2,1)} %get-tuple-element.94, bf16[256,7168]{1,0:T(8,128)(2,1)S(1)} %get-tuple-element.93), kind=kLoop, calls=%fused_computation.2 | loop fusion | flops 14680064 | bytes 14680064 | tf_op jit(solution)/shard_map/concatenate | solution.py:219
  61.7 1.9 collective-permute-start.2
  63.6 6.0 %copy.51 = bf16[7168,256]{1,0:T(8,128)(2,1)} copy(bf16[7168,256]{0,1:T(8,128)(2,1)} %bitcast.66) | data formatting | bytes 7340032 | tf_op jit(solution)/shard_map/transpose | solution.py:225
  69.6 14.8 %collective-permute-done.2 = bf16[4,448,128]{2,1,0:T(8,128)(2,1)S(1)} collective-permute-done((bf16[4,448,128]{2,1,0:T(8,128)(2,1)S(1)}, bf16[4,448,128]{2,1,0:T(8,128)(2,1)S(1)}, u32[]{:S(2)}, u32[]{:S(2)}) %collective-permute-start.2) | collective-permute-done | bytes 458784 | tf_op jit(solution)/shard_map/ppermute | solution.py:21
  85.4 3.7 %collective-permute-start.3 = (bf16[8,448,128]{2,1,0:T(8,128)(2,1)}, bf16[8,448,128]{2,1,0:T(8,128)(2,1)S(1)}, u32[]{:S(2)}, u32[]{:S(2)}) collective-permute-start(bf16[8,448,128]{2,1,0:T(8,128)(2,1)} %pad_maximum_fusion.1), channel_id=1, source_target_pairs={{0,12},{1,13},{2,14},{3,15},{4,8},{5,9},{6,10},{7,11},{8,4},{9,5},... | collective-permute-start | bytes 2752520 | tf_op jit(solution)/shard_map/ppermute | solution.py:21
  89.1 2.5 copy.52.gain_ref
  92.5 36.8 %collective-permute-done.3 = bf16[8,448,128]{2,1,0:T(8,128)(2,1)S(1)} collective-permute-done((bf16[8,448,128]{2,1,0:T(8,128)(2,1)}, bf16[8,448,128]{2,1,0:T(8,128)(2,1)S(1)}, u32[]{:S(2)}, u32[]{:S(2)}) %collective-permute-start.3) | collective-permute-done | bytes 917536 | tf_op jit(solution)/shard_map/ppermute | solution.py:21
  129.5 2.0 copy-done.3
  131.6 2.0 copy-done.4
  133.6 7.4 %shard_map.109 = bf16[256,128]{1,0:T(8,128)(2,1)S(1)} custom-call(s32[16]{0:T(128)S(1)} %fusion.14.at_ref.slice_ref, bf16[16,448,128]{2,1,0:T(8,128)(2,1)S(1)} %constant_dynamic-update-slice_fusion.x_ref, bf16[1,7168,256]{2,1,0:T(8,128)(2,1)S(1)} %copy-done.3, bf16[1,7168,256]{2,1,0:T(8,128)(2,1)S(1)} %copy-done.4, f32[7168,1]{1,0:T(8,128)S(1)} %copy-done.2), custom_call_target="tpu_custom_call" | custom-call | flops 939524096 | bytes 9175040 | tf_op jit(solution)/shard_map/pallas_call | solution.py:147
  141.1 1.9 fusion
  143.0 3.3 %copy.53 = bf16[7168,128]{1,0:T(8,128)(2,1)S(1)} copy(bf16[7168,128]{0,1:T(8,128)(2,1)} %fusion) | data formatting | bytes 3670016 | tf_op jit(solution)/shard_map/convert_element_type | solution.py:229
  147.6 3.1 collective-permute-start.4
  150.8 14.8 %shard_map.110.refs_4_ = bf16[256,1024]{1,0:T(8,128)(2,1)} custom-call(bf16[512,7168]{1,0:T(8,128)(2,1)} %pad_maximum_fusion.weight_ref, bf16[7168,1024]{1,0:T(8,128)(2,1)} %all-gather.2.cloned.1.call-done.x_ref), custom_call_target="tpu_custom_call" | custom-call | flops 7516192768 | bytes 22020096 | tf_op jit(solution)/shard_map/pallas_call | solution.py:70
  165.6 3.9 %collective-permute-done.4 = bf16[8,448,128]{2,1,0:T(8,128)(2,1)} collective-permute-done((bf16[8,448,128]{2,1,0:T(8,128)(2,1)}, bf16[8,448,128]{2,1,0:T(8,128)(2,1)}, u32[]{:S(2)}, u32[]{:S(2)}) %collective-permute-start.4) | collective-permute-done | bytes 917536 | tf_op jit(solution)/shard_map/ppermute | solution.py:21
  170.5 5.4 %shard_map.111 = (bf16[8,448,256]{2,1,0:T(8,128)(2,1)}, bf16[8,448,256]{2,1,0:T(8,128)(2,1)S(1)}, bf16[8,448,256]{2,1,0:T(8,128)(2,1)S(1)}, bf16[8,448,256]{2,1,0:T(8,128)(2,1)}) custom-call(s32[16]{0:T(128)S(1)} %fusion.14.at_ref.slice_ref, bf16[16,448,256]{2,1,0:T(8,128)(2,1)S(1)} %bitcast.57, bf16[16,448,256]{2,1,0:T(8,128)(2,1)S(1)} %bitcast.58, ...), custom_call_target="tpu_custom_call" | custom-call | flops 1879048192 | bytes 14680064 | tf_op jit(solution)/shard_map/pallas_call | solution.py:106
  177.1 2.8 collective-permute-start.9
  180.5 1.8 add_convert_fusion.8
  184.0 2.0 collective-permute-start.5
  186.0 2.0 copy-done.1
  188.0 3.8 %shard_map.112 = (bf16[8,448,256]{2,1,0:T(8,128)(2,1)S(1)}, bf16[8,448,256]{2,1,0:T(8,128)(2,1)S(1)}, bf16[8,448,256]{2,1,0:T(8,128)(2,1)S(1)}, bf16[8,448,256]{2,1,0:T(8,128)(2,1)S(1)}) custom-call(s32[16]{0:T(128)S(1)} %fusion.14.at_ref.slice_ref, bf16[16,448,256]{2,1,0:T(8,128)(2,1)S(1)} %bitcast.61, bf16[16,448,256]{2,1,0:T(8,128)(2,1)S(1)} %bitcast.62, ...), custom_call_target="tpu_custom_call" | custom-call | flops 1879048192 | bytes 14680064 | tf_op jit(solution)/shard_map/pallas_call | solution.py:106
  191.9 36.7 %collective-permute-done.5 = bf16[4,448,128]{2,1,0:T(8,128)(2,1)} collective-permute-done((bf16[4,448,128]{2,1,0:T(8,128)(2,1)}, bf16[4,448,128]{2,1,0:T(8,128)(2,1)}, u32[]{:S(2)}, u32[]{:S(2)}) %collective-permute-start.5) | collective-permute-done | bytes 458784 | tf_op jit(solution)/shard_map/ppermute | solution.py:21
  229.7 3.0 collective-permute-start.10
  232.7 3.1 add_convert_fusion.4
  236.2 3.1 add_convert_fusion.3
  239.3 3.1 add_convert_fusion.2
  242.4 2.8 add_convert_fusion.1
  245.4 1.8 collective-permute-start.22
  247.9 7.6 %collective-permute-done.22 = bf16[1,448,128]{2,1,0:T(8,128)(2,1)S(1)} collective-permute-done((bf16[1,448,128]{2,1,0:T(8,128)(2,1)S(1)}, bf16[1,448,128]{2,1,0:T(8,128)(2,1)S(1)}, u32[]{:S(2)}, u32[]{:S(2)}) %collective-permute-start.22) | collective-permute-done | bytes 114720 | tf_op jit(solution)/shard_map/ppermute | solution.py:21
  256.3 3.5 %all-to-all-start.1 = ((bf16[8,16,448]{2,1,0:T(8,128)(2,1)}), bf16[8,16,448]{2,1,0:T(8,128)(2,1)S(1)}, u32[]{:S(2)}, u32[]{:S(2)}) async-start(bf16[8,16,448]{2,1,0:T(8,128)(2,1)} %bitcast.21), calls=%async_computation.1 | async-start | bytes 262144 | tf_op jit(solution)/shard_map/all_to_all | solution.py:263
  260.7 5.2 %all-to-all-done.1 = bf16[8,16,448]{2,1,0:T(8,128)(2,1)S(1)} async-done(((bf16[8,16,448]{2,1,0:T(8,128)(2,1)}), bf16[8,16,448]{2,1,0:T(8,128)(2,1)S(1)}, u32[]{:S(2)}, u32[]{:S(2)}) %all-to-all-start.1) | async-done | bytes 114720 | tf_op jit(solution)/shard_map/all_to_all | solution.py:263
  266.1 1.4 add_convert_fusion.10
  268.5 1.4 add_convert_fusion.12
  270.0 1.5 add_convert_fusion.14
  272.4 12.1 %collective-permute-done.11 = bf16[4,448,256]{2,1,0:T(8,128)(2,1)} collective-permute-done((bf16[4,448,256]{2,1,0:T(8,128)(2,1)}, bf16[4,448,256]{2,1,0:T(8,128)(2,1)}, u32[]{:S(2)}, u32[]{:S(2)}) %collective-permute-start.11) | collective-permute-done | bytes 917536 | tf_op jit(solution)/shard_map/ppermute | solution.py:21
  284.5 1.4 add_convert_fusion.16
  286.6 7.3 %collective-permute-done.21 = bf16[2,448,256]{2,1,0:T(8,128)(2,1)S(1)} collective-permute-done((bf16[2,448,256]{2,1,0:T(8,128)(2,1)S(1)}, bf16[2,448,256]{2,1,0:T(8,128)(2,1)S(1)}, u32[]{:S(2)}, u32[]{:S(2)}) %collective-permute-start.21) | collective-permute-done | bytes 458784 | tf_op jit(solution)/shard_map/ppermute | solution.py:21
  295.8 3.4 %collective-permute-done.12 = bf16[2,448,256]{2,1,0:T(8,128)(2,1)S(1)} collective-permute-done((bf16[2,448,256]{2,1,0:T(8,128)(2,1)S(1)}, bf16[2,448,256]{2,1,0:T(8,128)(2,1)S(1)}, u32[]{:S(2)}, u32[]{:S(2)}) %collective-permute-start.12) | collective-permute-done | bytes 458784 | tf_op jit(solution)/shard_map/ppermute | solution.py:21
  300.1 2.6 collective-permute-done.23
  303.0 3.5 %collective-permute-done.13 = bf16[1,448,256]{2,1,0:T(8,128)(2,1)S(1)} collective-permute-done((bf16[1,448,256]{2,1,0:T(8,128)(2,1)S(1)}, bf16[1,448,256]{2,1,0:T(8,128)(2,1)S(1)}, u32[]{:S(2)}, u32[]{:S(2)}) %collective-permute-start.13) | collective-permute-done | bytes 229408 | tf_op jit(solution)/shard_map/ppermute | solution.py:21
  (114 shorter events, 26.8 us)
Async XLA Ops:
  6.5 2.2 copy-start.18
  6.5 141.1 %all-gather.2.cloned.1.call-start = ((), (), s32[]{:S(2)}) async-start(), calls=%async_computation.2 | async-start | bytes 15597568 | tf_op jit(solution)/shard_map/all_gather | solution.py:199
  9.0 4.3 %copy-start.19 = (f32[1024,2]{0,1:T(2,128)S(1)}, f32[1024,2]{0,1:T(2,128)}, u32[]{:S(2)}) copy-start(f32[1024,2]{0,1:T(2,128)} %param.20) | copy-start | bytes 24580
  9.0 5.8 %copy-start.8 = (bf16[1024,448]{0,1:T(8,128)(2,1)S(1)}, bf16[1024,448]{0,1:T(8,128)(2,1)}, u32[]{:S(2)}) copy-start(bf16[1024,448]{0,1:T(8,128)(2,1)} %param.11) | copy-start | bytes 2752516
  14.0 0.7 copy-start.15
  25.8 8.1 %collective-permute-start = (bf16[1,448,128]{2,1,0:T(8,128)(2,1)S(1)}, bf16[1,448,128]{2,1,0:T(8,128)(2,1)S(1)}, u32[]{:S(2)}, u32[]{:S(2)}) collective-permute-start(bf16[1,448,128]{2,1,0:T(8,128)(2,1)S(1)} %bitcast.68), channel_id=1, source_target_pairs={{0,1},{1,0},{2,3},{3,2},{4,5},{5,4},{6,7},{7,6},{8,9},{9,8},{10,11... | collective-permute-start | bytes 344072 | tf_op jit(solution)/shard_map/ppermute | solution.py:21
  34.5 27.1 %collective-permute-start.1 = (bf16[2,448,128]{2,1,0:T(8,128)(2,1)}, bf16[2,448,128]{2,1,0:T(8,128)(2,1)S(1)}, u32[]{:S(2)}, u32[]{:S(2)}) collective-permute-start(bf16[2,448,128]{2,1,0:T(8,128)(2,1)} %pad_maximum_fusion.3), channel_id=1, source_target_pairs={{0,3},{1,2},{2,1},{3,0},{4,7},{5,6},{6,5},{7,4},{8,11},{9,10},{10,... | collective-permute-start | bytes 688136 | tf_op jit(solution)/shard_map/ppermute | solution.py:21
  43.5 6.0 %copy-start.17 = (f32[7168]{0:T(1024)S(1)}, f32[7168]{0:T(1024)}, u32[]{:S(2)}) copy-start(f32[7168]{0:T(1024)} %param.12) | copy-start | bytes 86020
  61.7 22.7 %collective-permute-start.2 = (bf16[4,448,128]{2,1,0:T(8,128)(2,1)S(1)}, bf16[4,448,128]{2,1,0:T(8,128)(2,1)S(1)}, u32[]{:S(2)}, u32[]{:S(2)}) collective-permute-start(bf16[4,448,128]{2,1,0:T(8,128)(2,1)S(1)} %pad_maximum_fusion.2), channel_id=1, source_target_pairs={{0,4},{1,5},{2,6},{3,7},{4,0},{5,1},{6,2},{7,3},{8,12},{9,13},{10,... | collective-permute-start | bytes 1376264 | tf_op jit(solution)/shard_map/ppermute | solution.py:21
  85.4 44.0 %collective-permute-start.3 = (bf16[8,448,128]{2,1,0:T(8,128)(2,1)}, bf16[8,448,128]{2,1,0:T(8,128)(2,1)S(1)}, u32[]{:S(2)}, u32[]{:S(2)}) collective-permute-start(bf16[8,448,128]{2,1,0:T(8,128)(2,1)} %pad_maximum_fusion.1), channel_id=1, source_target_pairs={{0,12},{1,13},{2,14},{3,15},{4,8},{5,9},{6,10},{7,11},{8,4},{9,5},... | collective-permute-start | bytes 2752520 | tf_op jit(solution)/shard_map/ppermute | solution.py:21
  91.5 38.0 %copy-start.2 = (f32[7168,1]{1,0:T(8,128)S(1)}, f32[7168,1]{1,0:T(8,128)}, u32[]{:S(2)}) copy-start(f32[7168,1]{1,0:T(8,128)} %copy.52.gain_ref) | copy-start | bytes 86020
  129.5 2.0 copy-start.3
  131.6 2.0 copy-start.4
  133.6 7.5 %copy-start.9 = (bf16[1,256,7168]{2,1,0:T(8,128)(2,1)S(1)}, bf16[1,256,7168]{2,1,0:T(8,128)(2,1)}, u32[]{:S(2)}) copy-start(bf16[1,256,7168]{2,1,0:T(8,128)(2,1)} %param.18) | copy-start | bytes 11010052
  147.6 21.8 %collective-permute-start.4 = (bf16[8,448,128]{2,1,0:T(8,128)(2,1)}, bf16[8,448,128]{2,1,0:T(8,128)(2,1)}, u32[]{:S(2)}, u32[]{:S(2)}) collective-permute-start(bf16[8,448,128]{2,1,0:T(8,128)(2,1)} %get-tuple-element.46), channel_id=1, source_target_pairs={{0,12},{1,13},{2,14},{3,15},{4,8},{5,9},{6,10},{7,11},{8,4},{9,5},... | collective-permute-start | bytes 2752520 | tf_op jit(solution)/shard_map/ppermute | solution.py:21
  150.8 18.7 %copy-start = (bf16[7168,256]{1,0:T(8,128)(2,1)S(1)}, bf16[7168,256]{1,0:T(8,128)(2,1)}, u32[]{:S(2)}) copy-start(bf16[7168,256]{1,0:T(8,128)(2,1)} %copy.51) | copy-start | bytes 11010052
  169.5 1.0 copy-start.5
  175.9 1.2 copy-start.7
  177.1 55.6 %collective-permute-start.9 = (bf16[8,448,256]{2,1,0:T(8,128)(2,1)}, bf16[8,448,256]{2,1,0:T(8,128)(2,1)}, u32[]{:S(2)}, u32[]{:S(2)}) collective-permute-start(bf16[8,448,256]{2,1,0:T(8,128)(2,1)} %get-tuple-element.53), channel_id=1, source_target_pairs={{0,12},{1,13},{2,14},{3,15},{4,8},{5,9},{6,10},{7,11},{8,4},{9,5},... | collective-permute-start | bytes 5505032 | tf_op jit(solution)/shard_map/ppermute | solution.py:21
  179.9 56.2 %collective-permute-start.6 = (bf16[8,448,256]{2,1,0:T(8,128)(2,1)}, bf16[8,448,256]{2,1,0:T(8,128)(2,1)}, u32[]{:S(2)}, u32[]{:S(2)}) collective-permute-start(bf16[8,448,256]{2,1,0:T(8,128)(2,1)} %get-tuple-element.50), channel_id=1, source_target_pairs={{0,1},{1,0},{2,3},{3,2},{4,5},{5,4},{6,7},{7,6},{8,9},{9,8},{10,11... | collective-permute-start | bytes 5505032 | tf_op jit(solution)/shard_map/ppermute | solution.py:21
  180.5 58.8 %collective-permute-start.7 = (bf16[8,448,256]{2,1,0:T(8,128)(2,1)}, bf16[8,448,256]{2,1,0:T(8,128)(2,1)}, u32[]{:S(2)}, u32[]{:S(2)}) collective-permute-start(bf16[8,448,256]{2,1,0:T(8,128)(2,1)} %copy-done.7), channel_id=1, source_target_pairs={{0,3},{1,2},{2,1},{3,0},{4,7},{5,6},{6,5},{7,4},{8,11},{9,10},{10,... | collective-permute-start | bytes 5505032 | tf_op jit(solution)/shard_map/ppermute | solution.py:21
  180.5 5.5 %copy-start.6 = (bf16[256,1024]{1,0:T(8,128)(2,1)S(1)}, bf16[256,1024]{1,0:T(8,128)(2,1)}, u32[]{:S(2)}) copy-start(bf16[256,1024]{1,0:T(8,128)(2,1)} %shard_map.110.refs_4_) | copy-start | bytes 1572868
  180.5 61.9 %collective-permute-start.8 = (bf16[8,448,256]{2,1,0:T(8,128)(2,1)S(1)}, bf16[8,448,256]{2,1,0:T(8,128)(2,1)}, u32[]{:S(2)}, u32[]{:S(2)}) collective-permute-start(bf16[8,448,256]{2,1,0:T(8,128)(2,1)S(1)} %get-tuple-element.52), channel_id=1, source_target_pairs={{0,4},{1,5},{2,6},{3,7},{4,0},{5,1},{6,2},{7,3},{8,12},{9,13},{10,... | collective-permute-start | bytes 5505032 | tf_op jit(solution)/shard_map/ppermute | solution.py:21
  182.3 0.9 copy-start.10
  184.0 44.5 %collective-permute-start.5 = (bf16[4,448,128]{2,1,0:T(8,128)(2,1)}, bf16[4,448,128]{2,1,0:T(8,128)(2,1)}, u32[]{:S(2)}, u32[]{:S(2)}) collective-permute-start(bf16[4,448,128]{2,1,0:T(8,128)(2,1)} %constant_dynamic-slice_fusion.2), channel_id=1, source_target_pairs={{0,4},{1,5},{2,6},{3,7},{4,0},{5,1},{6,2},{7,3},{8,12},{9,13},{10,... | collective-permute-start | bytes 1376264 | tf_op jit(solution)/shard_map/ppermute | solution.py:21
  186.0 2.0 copy-start.1
  188.0 40.5 %copy-start.11 = (bf16[8,448,128]{2,1,0:T(8,128)(2,1)S(1)}, bf16[8,448,128]{2,1,0:T(8,128)(2,1)}, u32[]{:S(2)}) copy-start(bf16[8,448,128]{2,1,0:T(8,128)(2,1)} %copy-done.10) | copy-start | bytes 2752516
  229.7 15.6 %collective-permute-start.10 = (bf16[2,448,128]{2,1,0:T(8,128)(2,1)S(1)}, bf16[2,448,128]{2,1,0:T(8,128)(2,1)S(1)}, u32[]{:S(2)}, u32[]{:S(2)}) collective-permute-start(bf16[2,448,128]{2,1,0:T(8,128)(2,1)S(1)} %constant_dynamic-slice_fusion.1), channel_id=1, source_target_pairs={{0,3},{1,2},{2,1},{3,0},{4,7},{5,6},{6,5},{7,4},{8,11},{9,10},{10,... | collective-permute-start | bytes 688136 | tf_op jit(solution)/shard_map/ppermute | solution.py:21
  235.9 30.2 %collective-permute-start.20 = (bf16[4,448,256]{2,1,0:T(8,128)(2,1)}, bf16[4,448,256]{2,1,0:T(8,128)(2,1)}, u32[]{:S(2)}, u32[]{:S(2)}) collective-permute-start(bf16[4,448,256]{2,1,0:T(8,128)(2,1)} %get-tuple-element.82), channel_id=1, source_target_pairs={{0,1},{1,0},{2,3},{3,2},{4,5},{5,4},{6,7},{7,6},{8,9},{9,8},{10,11... | collective-permute-start | bytes 2752520 | tf_op jit(solution)/shard_map/ppermute | solution.py:21
  245.3 20.8 %copy-start.14 = (bf16[4,448,256]{2,1,0:T(8,128)(2,1)S(1)}, bf16[4,448,256]{2,1,0:T(8,128)(2,1)}, u32[]{:S(2)}) copy-start(bf16[4,448,256]{2,1,0:T(8,128)(2,1)} %get-tuple-element.67) | copy-start | bytes 2752516
  245.4 10.1 %collective-permute-start.22 = (bf16[1,448,128]{2,1,0:T(8,128)(2,1)S(1)}, bf16[1,448,128]{2,1,0:T(8,128)(2,1)S(1)}, u32[]{:S(2)}, u32[]{:S(2)}) collective-permute-start(bf16[1,448,128]{2,1,0:T(8,128)(2,1)S(1)} %constant_dynamic-slice_fusion), channel_id=1, source_target_pairs={{0,1},{1,0},{2,3},{3,2},{4,5},{5,4},{6,7},{7,6},{8,9},{9,8},{10,11... | collective-permute-start | bytes 344072 | tf_op jit(solution)/shard_map/ppermute | solution.py:21
  247.2 21.3 %collective-permute-start.17 = (bf16[4,448,256]{2,1,0:T(8,128)(2,1)}, bf16[4,448,256]{2,1,0:T(8,128)(2,1)}, u32[]{:S(2)}, u32[]{:S(2)}) collective-permute-start(bf16[4,448,256]{2,1,0:T(8,128)(2,1)} %get-tuple-element.79), channel_id=1, source_target_pairs={{0,12},{1,13},{2,14},{3,15},{4,8},{5,9},{6,10},{7,11},{8,4},{9,5},... | collective-permute-start | bytes 2752520 | tf_op jit(solution)/shard_map/ppermute | solution.py:21
  247.9 22.1 %collective-permute-start.14 = (bf16[4,448,256]{2,1,0:T(8,128)(2,1)}, bf16[4,448,256]{2,1,0:T(8,128)(2,1)}, u32[]{:S(2)}, u32[]{:S(2)}) collective-permute-start(bf16[4,448,256]{2,1,0:T(8,128)(2,1)} %get-tuple-element.77), channel_id=1, source_target_pairs={{0,4},{1,5},{2,6},{3,7},{4,0},{5,1},{6,2},{7,3},{8,12},{9,13},{10,... | collective-permute-start | bytes 2752520 | tf_op jit(solution)/shard_map/ppermute | solution.py:21
  256.3 9.7 %all-to-all-start.1 = ((bf16[8,16,448]{2,1,0:T(8,128)(2,1)}), bf16[8,16,448]{2,1,0:T(8,128)(2,1)S(1)}, u32[]{:S(2)}, u32[]{:S(2)}) async-start(bf16[8,16,448]{2,1,0:T(8,128)(2,1)} %bitcast.21), calls=%async_computation.1 | async-start | bytes 262144 | tf_op jit(solution)/shard_map/all_to_all | solution.py:263
  259.8 24.7 %collective-permute-start.11 = (bf16[4,448,256]{2,1,0:T(8,128)(2,1)}, bf16[4,448,256]{2,1,0:T(8,128)(2,1)}, u32[]{:S(2)}, u32[]{:S(2)}) collective-permute-start(bf16[4,448,256]{2,1,0:T(8,128)(2,1)} %get-tuple-element.75), channel_id=1, source_target_pairs={{0,3},{1,2},{2,1},{3,0},{4,7},{5,6},{6,5},{7,4},{8,11},{9,10},{10,... | collective-permute-start | bytes 2752520 | tf_op jit(solution)/shard_map/ppermute | solution.py:21
  267.4 2.5 copy-start.13
  267.5 26.4 %collective-permute-start.21 = (bf16[2,448,256]{2,1,0:T(8,128)(2,1)S(1)}, bf16[2,448,256]{2,1,0:T(8,128)(2,1)S(1)}, u32[]{:S(2)}, u32[]{:S(2)}) collective-permute-start(bf16[2,448,256]{2,1,0:T(8,128)(2,1)S(1)} %get-tuple-element.90), channel_id=1, source_target_pairs={{0,3},{1,2},{2,1},{3,0},{4,7},{5,6},{6,5},{7,4},{8,11},{9,10},{10,... | collective-permute-start | bytes 1376264 | tf_op jit(solution)/shard_map/ppermute | solution.py:21
  269.8 14.7 %copy-start.12 = (bf16[4,448,256]{2,1,0:T(8,128)(2,1)S(1)}, bf16[4,448,256]{2,1,0:T(8,128)(2,1)}, u32[]{:S(2)}) copy-start(bf16[4,448,256]{2,1,0:T(8,128)(2,1)} %get-tuple-element.64) | copy-start | bytes 2752516
  269.8 24.7 %collective-permute-start.18 = (bf16[2,448,256]{2,1,0:T(8,128)(2,1)S(1)}, bf16[2,448,256]{2,1,0:T(8,128)(2,1)S(1)}, u32[]{:S(2)}, u32[]{:S(2)}) collective-permute-start(bf16[2,448,256]{2,1,0:T(8,128)(2,1)S(1)} %get-tuple-element.88), channel_id=1, source_target_pairs={{0,1},{1,0},{2,3},{3,2},{4,5},{5,4},{6,7},{7,6},{8,9},{9,8},{10,11... | collective-permute-start | bytes 1376264 | tf_op jit(solution)/shard_map/ppermute | solution.py:21
  271.4 24.2 %collective-permute-start.15 = (bf16[2,448,256]{2,1,0:T(8,128)(2,1)S(1)}, bf16[2,448,256]{2,1,0:T(8,128)(2,1)S(1)}, u32[]{:S(2)}, u32[]{:S(2)}) collective-permute-start(bf16[2,448,256]{2,1,0:T(8,128)(2,1)S(1)} %get-tuple-element.86), channel_id=1, source_target_pairs={{0,12},{1,13},{2,14},{3,15},{4,8},{5,9},{6,10},{7,11},{8,4},{9,5},... | collective-permute-start | bytes 1376264 | tf_op jit(solution)/shard_map/ppermute | solution.py:21
  285.9 13.2 %collective-permute-start.12 = (bf16[2,448,256]{2,1,0:T(8,128)(2,1)S(1)}, bf16[2,448,256]{2,1,0:T(8,128)(2,1)S(1)}, u32[]{:S(2)}, u32[]{:S(2)}) collective-permute-start(bf16[2,448,256]{2,1,0:T(8,128)(2,1)S(1)} %get-tuple-element.84), channel_id=1, source_target_pairs={{0,4},{1,5},{2,6},{3,7},{4,0},{5,1},{6,2},{7,3},{8,12},{9,13},{10,... | collective-permute-start | bytes 1376264 | tf_op jit(solution)/shard_map/ppermute | solution.py:21
  293.9 8.8 %collective-permute-start.23 = (bf16[1,448,256]{2,1,0:T(8,128)(2,1)S(1)}, bf16[1,448,256]{2,1,0:T(8,128)(2,1)S(1)}, u32[]{:S(2)}, u32[]{:S(2)}) collective-permute-start(bf16[1,448,256]{2,1,0:T(8,128)(2,1)S(1)} %add_convert_fusion.18), channel_id=1, source_target_pairs={{0,4},{1,5},{2,6},{3,7},{4,0},{5,1},{6,2},{7,3},{8,12},{9,13},{10,... | collective-permute-start | bytes 688136 | tf_op jit(solution)/shard_map/ppermute | solution.py:21
  294.6 8.2 %collective-permute-start.19 = (bf16[1,448,256]{2,1,0:T(8,128)(2,1)S(1)}, bf16[1,448,256]{2,1,0:T(8,128)(2,1)S(1)}, u32[]{:S(2)}, u32[]{:S(2)}) collective-permute-start(bf16[1,448,256]{2,1,0:T(8,128)(2,1)S(1)} %add_convert_fusion.21), channel_id=1, source_target_pairs={{0,3},{1,2},{2,1},{3,0},{4,7},{5,6},{6,5},{7,4},{8,11},{9,10},{10,... | collective-permute-start | bytes 688136 | tf_op jit(solution)/shard_map/ppermute | solution.py:21
  295.7 7.3 %collective-permute-start.16 = (bf16[1,448,256]{2,1,0:T(8,128)(2,1)S(1)}, bf16[1,448,256]{2,1,0:T(8,128)(2,1)S(1)}, u32[]{:S(2)}, u32[]{:S(2)}) collective-permute-start(bf16[1,448,256]{2,1,0:T(8,128)(2,1)S(1)} %add_convert_fusion.23), channel_id=1, source_target_pairs={{0,1},{1,0},{2,3},{3,2},{4,5},{5,4},{6,7},{7,6},{8,9},{9,8},{10,11... | collective-permute-start | bytes 688136 | tf_op jit(solution)/shard_map/ppermute | solution.py:21
  299.2 7.3 %collective-permute-start.13 = (bf16[1,448,256]{2,1,0:T(8,128)(2,1)S(1)}, bf16[1,448,256]{2,1,0:T(8,128)(2,1)S(1)}, u32[]{:S(2)}, u32[]{:S(2)}) collective-permute-start(bf16[1,448,256]{2,1,0:T(8,128)(2,1)S(1)} %add_convert_fusion.25), channel_id=1, source_target_pairs={{0,12},{1,13},{2,14},{3,15},{4,8},{5,9},{6,10},{7,11},{8,4},{9,5},... | collective-permute-start | bytes 688136 | tf_op jit(solution)/shard_map/ppermute | solution.py:21
  302.8 3.9 %copy-start.16 = (bf16[1024,128]{1,0:T(8,128)(2,1)S(1)}, bf16[1024,128]{1,0:T(8,128)(2,1)}, u32[]{:S(2)}) copy-start(bf16[1024,128]{1,0:T(8,128)(2,1)} %copy-done.15) | copy-start | bytes 786436
Sparse Core Ops, SparseCore 0:
  9.5 127.1 all-gather.1

commit v5 on v4

v5 whole, which is shorter than its diff:
```python
import functools

import jax
import jax.numpy as jnp
from jax import lax
from jax.experimental import pallas as pl
from jax.experimental.pallas import tpu as pltpu
from jax.sharding import PartitionSpec as P

EPSILON = 1e-05
NODE_CAP = 16
GRAY = (0, 1, 3, 2)

LOCAL_LABEL = [GRAY[i % 4] | GRAY[i // 4] << 2 for i in range(16)]
LOCAL_AT = {label: i for i, label in enumerate(LOCAL_LABEL)}

STREAMS = ((0, 1, 2, 3), (1, 2, 3, 0), (2, 3, 0, 1), (3, 0, 1, 2))


def flip_local(array, bit):
    return lax.ppermute(array, "local", [(i, LOCAL_AT[LOCAL_LABEL[i] ^ (1 << bit)]) for i in range(16)])


def route_slots(ids_block, window):
    flat_ids = ids_block.reshape(-1)
    expert_range = jnp.arange(window, dtype=jnp.int32)
    member = (flat_ids[:, None] == expert_range[None, :]).astype(jnp.int32)
    before = jnp.cumsum(member, axis=0) - member
    route_rank = jnp.sum(before * member, axis=1)
    kept = (jnp.sum(member, axis=1) > 0) & (route_rank < NODE_CAP)
    slot = jnp.where(kept, flat_ids * NODE_CAP + route_rank, -1)
    return slot.reshape(ids_block.shape)


def transposed_dot(weight, rows):
    return lax.dot_general(weight, rows, (((0,), (0,)), ((), ())), preferred_element_type=jnp.float32)


def silu(value):
    return value / (1.0 + jnp.exp(-value))


def quarter_kernel(masks, deep, slice_ref, weight_ref, turned_ref, x_ref, scale_ref, hidden_ref, sent_ref, total):
    step = pl.program_id(0)
    here = pl.ds(pl.multiple_of(step * deep, 128), deep)
    part = jnp.dot(weight_ref[:, here], x_ref[...], preferred_element_type=jnp.float32)

    @pl.when(step == 0)
    def _():
        total[...] = part

    @pl.when(step > 0)
    def _():
        total[...] += part

    @pl.when(step == pl.num_programs(0) - 1)
    def _():
        scale = scale_ref[...]
        half = total.shape[0] // 2
        hidden = (silu(total[:half] * scale) * (total[half:] * scale)).astype(jnp.bfloat16)
        hidden_ref[...] = hidden
        for j, mask in enumerate(masks):
            out = jnp.dot(turned_ref[slice_ref[mask]], hidden, preferred_element_type=jnp.float32)
            sent_ref[j] = out.astype(jnp.bfloat16)


def stream_masks(s, sent):
    a, b, c, d = STREAMS[s]
    return [sent << a | ((j >> 2) & 1) << b | ((j >> 1) & 1) << c | (j & 1) << d for j in range(8)]


def quarter(s, slice_of, weight, turned, rows, scale):
    both, features = weight.shape
    columns = rows.shape[1] // 4
    blocks, slice_rows, _ = turned.shape
    deep = features // 4
    return pl.pallas_call(
        functools.partial(quarter_kernel, stream_masks(s, 1), deep),
        grid_spec=pltpu.PrefetchScalarGridSpec(
            num_scalar_prefetch=1,
            grid=(features // deep,),
            in_specs=[
                pl.BlockSpec(memory_space=pltpu.VMEM),
                pl.BlockSpec(memory_space=pltpu.VMEM),
                pl.BlockSpec((deep, columns), lambda m, at: (m, s)),
                pl.BlockSpec((1, columns), lambda m, at: (0, s)),
            ],
            out_specs=[
                pl.BlockSpec((both // 2, columns), lambda m, at: (0, 0)),
                pl.BlockSpec((blocks // 2, slice_rows, columns), lambda m, at: (0, 0, 0)),
            ],
            scratch_shapes=[pltpu.VMEM((both, columns), jnp.float32)],
        ),
        out_shape=[
            jax.ShapeDtypeStruct((both // 2, columns), jnp.bfloat16),
            jax.ShapeDtypeStruct((blocks // 2, slice_rows, columns), jnp.bfloat16),
        ],
        compiler_params=pltpu.CompilerParams(vmem_limit_bytes=36 << 20),
        cost_estimate=pl.CostEstimate(
            flops=3 * features * columns * both, bytes_accessed=2 * features * (columns + both), transcendentals=0
        ),
    )(slice_of, weight, turned, rows, scale)


def keep_kernel(slice_ref, *refs):
    weights, hidden, outs = refs[:4], refs[4:8], refs[8:]
    for s in range(4):
        outs[s][0] = jnp.dot(weights[s][0], hidden[s][...], preferred_element_type=jnp.float32).astype(jnp.bfloat16)


def kept_parts(slice_of, turned, hidden):
    blocks, rows, deep = turned.shape
    columns = hidden[0].shape[1]

    def weight_spec(s):
        a, b, c, d = STREAMS[s]
        return pl.BlockSpec(
            (1, rows, deep), lambda j, at: (at[((j >> 2) & 1) << b | ((j >> 1) & 1) << c | (j & 1) << d], 0, 0)
        )

    return pl.pallas_call(
        keep_kernel,
        grid_spec=pltpu.PrefetchScalarGridSpec(
            num_scalar_prefetch=1,
            grid=(blocks // 2,),
            in_specs=[weight_spec(s) for s in range(4)] + [pl.BlockSpec((deep, columns), lambda j, at: (0, 0))] * 4,
            out_specs=[pl.BlockSpec((1, rows, columns), lambda j, at: (j, 0, 0))] * 4,
        ),
        out_shape=[jax.ShapeDtypeStruct((blocks // 2, rows, columns), jnp.bfloat16)] * 4,
        compiler_params=pltpu.CompilerParams(vmem_limit_bytes=24 << 20),
        cost_estimate=pl.CostEstimate(
            flops=4 * blocks * rows * deep * columns, bytes_accessed=4 * blocks * rows * (deep + columns), transcendentals=0
        ),
    )(slice_of, *[turned] * 4, *hidden)


def expert_kernel(blocks, features, at_ref, x_ref, gate_ref, up_ref, gain_ref, hidden_ref, gate_total, up_total, squares):
    step = pl.program_id(0)

    @pl.when(step == 0)
    def _():
        gate_total[...] = jnp.zeros_like(gate_total)
        up_total[...] = jnp.zeros_like(up_total)
        squares[...] = jnp.zeros_like(squares)

    as_float = x_ref[0].astype(jnp.float32)
    squares[...] += jnp.sum(as_float * as_float, axis=0, keepdims=True)
    rows = (as_float * gain_ref[...]).astype(jnp.bfloat16)
    gate_total[...] += transposed_dot(gate_ref[0], rows)
    up_total[...] += transposed_dot(up_ref[0], rows)

    @pl.when(step == blocks - 1)
    def _():
        scale = lax.rsqrt(squares[...] / features + EPSILON)
        hidden_ref[...] = (silu(gate_total[...] * scale) * (up_total[...] * scale)).astype(jnp.bfloat16)


def expert_gate_up(slice_of, pooled, gate_weight, up_weight, gain_column):
    blocks, rows, columns = pooled.shape
    hidden = gate_weight.shape[-1]
    weight_spec = pl.BlockSpec((1, rows, hidden), lambda m, at: (0, at[m], 0))
    return pl.pallas_call(
        functools.partial(expert_kernel, blocks, blocks * rows),
        grid_spec=pltpu.PrefetchScalarGridSpec(
            num_scalar_prefetch=1,
            grid=(blocks,),
            in_specs=[
                pl.BlockSpec((1, rows, columns), lambda m, at: (m, 0, 0)),
                weight_spec,
                weight_spec,
                pl.BlockSpec((rows, 1), lambda m, at: (at[m], 0)),
            ],
            out_specs=pl.BlockSpec((hidden, columns), lambda m, at: (0, 0)),
            scratch_shapes=[
                pltpu.VMEM((hidden, columns), jnp.float32),
                pltpu.VMEM((hidden, columns), jnp.float32),
                pltpu.VMEM((1, columns), jnp.float32),
            ],
        ),
        out_shape=jax.ShapeDtypeStruct((hidden, columns), jnp.bfloat16),
        compiler_params=pltpu.CompilerParams(vmem_limit_bytes=24 << 20),
        cost_estimate=pl.CostEstimate(
            flops=4 * blocks * rows * columns * hidden,
            bytes_accessed=2 * blocks * rows * (columns + 2 * hidden),
            transcendentals=0,
        ),
    )(slice_of, pooled, gate_weight, up_weight, gain_column)


def add_pair(kept, got):
    return (kept.astype(jnp.float32) + got.astype(jnp.float32)).astype(jnp.bfloat16)


def shards(
    tokens,
    norm_gain,
    dense_gate,
    dense_up,
    dense_down,
    expert_gate,
    expert_up,
    expert_down,
    expert_ids,
    route_gates,
):
    node_count = lax.axis_size("node")
    local_index = lax.axis_index("local")
    slice_width = tokens.shape[1]
    width = slice_width * 16
    slot_count = node_count * NODE_CAP
    slice_table = [[LOCAL_AT[LOCAL_LABEL[i] ^ m] for m in range(16)] for i in range(16)]
    slice_of = jnp.asarray(slice_table, jnp.int32)[local_index]

    columns = tokens.T
    whole_columns = lax.all_gather(columns, "local", axis=0, tiled=True)

    slot = route_slots(expert_ids, node_count)
    slot_range = jnp.arange(slot_count, dtype=jnp.int32)
    match_float = (slot[:, :, None] == slot_range[None, None, :]).astype(jnp.float32)
    chosen = jnp.sum(match_float, axis=1).astype(jnp.bfloat16)
    slot_gate = jnp.sum(match_float * route_gates[:, :, None], axis=(0, 1))
    send_rows = lax.dot_general(
        chosen, tokens, (((0,), (0,)), ((), ())), preferred_element_type=jnp.float32
    ).astype(jnp.bfloat16)
    routed = lax.all_to_all(
        send_rows.reshape(node_count, NODE_CAP, slice_width), "node", split_axis=0, concat_axis=0, tiled=True
    )
    routed = routed.reshape(slot_count, slice_width).T

    as_float = columns.astype(jnp.float32)
    square_sum = lax.psum(jnp.sum(as_float * as_float, axis=0), "local")
    scale = lax.rsqrt(square_sum / width + EPSILON)[None, :]
    gain_column = norm_gain[:, None]
    weight = jnp.concatenate(
        [(w.astype(jnp.float32) * gain_column).astype(jnp.bfloat16).T for w in (dense_gate, dense_up)], axis=0
    )
    turned = dense_down.T.reshape(16, slice_width, dense_down.shape[0])
    weight, turned, scale, routed, whole_columns = lax.optimization_barrier(
        (weight, turned, scale, routed, whole_columns)
    )
    pooled = lax.all_gather(routed, "local", axis=0, tiled=True)

    quarters = [quarter(s, slice_of, weight, turned, whole_columns, scale) for s in range(4)]
    arrived = [flip_local(quarters[s][1], STREAMS[s][0]) for s in range(4)]
    sums = kept_parts(slice_of, turned, [q[0] for q in quarters])

    pooled, sums = lax.optimization_barrier((pooled, sums))
    expert_hidden = expert_gate_up(
        jnp.arange(16, dtype=jnp.int32), pooled.reshape(16, slice_width, slot_count), expert_gate, expert_up, gain_column
    )
    expert_partial = transposed_dot(expert_down[0], expert_hidden).astype(jnp.bfloat16)
    expert_partial, arrived[0] = lax.optimization_barrier((expert_partial, arrived[0]))
    expert_out = lax.psum_scatter(expert_partial, "local", scatter_dimension=0, tiled=True)
    for step in (1, 2, 3):
        half = sums[0].shape[0] // 2
        came = [flip_local(add_pair(sums[s][half:], arrived[s][half:]), STREAMS[s][step]) for s in range(4)]
        sums = [add_pair(sums[s][:half], arrived[s][:half]) for s in range(4)]
        arrived = came
    returned = lax.all_to_all(
        expert_out.T.reshape(node_count, NODE_CAP, slice_width), "node", split_axis=0, concat_axis=0, tiled=True
    ).reshape(slot_count, slice_width)
    route_term = (slot_gate[:, None] * returned.astype(jnp.float32)).astype(jnp.bfloat16)
    expert_part = lax.dot_general(
        route_term, chosen, (((0,), (1,)), ((), ())), preferred_element_type=jnp.float32
    )
    dense_part = jnp.concatenate(
        [sums[s][0].astype(jnp.float32) + arrived[s][0].astype(jnp.float32) for s in range(4)], axis=1
    )
    return (columns.astype(jnp.float32) + dense_part + expert_part).astype(jnp.bfloat16).T


def solution(mesh):
    return jax.shard_map(
        shards,
        mesh=mesh,
        in_specs=(
            P("node", "local"),
            P(),
            P(None, "local"),
            P(None, "local"),
            P("local", None),
            P("node", None, "local"),
            P("node", None, "local"),
            P("node", "local", None),
            P("node", None),
            P("node", None),
        ),
        out_specs=P("node", "local"),
        check_vma=False,
    )
```

time: 316 us -> 289 us (0.915)
  waiting for transfers between devices: 141 us -> 80.2 us
  blocking collectives: 10.3 us -> 42.3 us
  other arithmetic: 39 us -> 30 us
  local copies, waits for them, and re-layouts: 41.2 us -> 50.1 us
  Pallas kernels: 31.5 us -> 39.3 us
  starting transfers between devices: 34.3 us -> 27.3 us
    ppermute x24 -> x16, waiting for transfers between devices: 135 us -> 34.6 us  [flip_local(): lax.ppermute(array, 'local', [(i, LOCAL_AT[LOCAL_LABEL[i] ^ 1 << bit]) fo...]
    psum x0 -> x1, blocking collectives: none -> 42.3 us  [shards(): square_sum = lax.psum(jnp.sum(as_float * as_float, axis=0), 'local')]
    unnamed x45, local copies, waits for them, and re-layouts: 11.1 us -> 37.3 us
    all_gather x1, waiting for transfers between devices: 0.01 us -> 20.8 us  [shards(): whole_columns = lax.all_gather(columns, 'local', axis=0, tiled=True)]
    unnamed x1 -> x4, waiting for transfers between devices: 0.71 us -> 19.7 us
    ppermute x24 -> x16, starting transfers between devices: 30.8 us -> 18.6 us  [flip_local(): lax.ppermute(array, 'local', [(i, LOCAL_AT[LOCAL_LABEL[i] ^ 1 << bit]) fo...]
    optimization_barrier x2 -> x1, local copies, waits for them, and re-layouts: 11.9 us -> 0.76 us  [shards(): lax.optimization_barrier((weight, turned, scale, routed, whole_columns))]
    all_to_all x1 -> x0, blocking collectives: 10.3 us -> none  [shards(): lax.all_to_all(send_rows.reshape(node_count, NODE_CAP, slice_width), 'nod...]
  transfers between devices with their start and end apart: 26 -> 21, of which waited for: 13 -> 10; matrix products, arithmetic and copies ran while one was open for 23% -> 22% of each run, Pallas kernels for 8% -> 14%
where the time goes in v5:
time: 289 us; the launch traced here: 287 us
  waiting for transfers between devices  80.2 us (28%)
  local copies, waits for them, and re-layouts  50.1 us (17%)
  blocking collectives  42.3 us (15%)
  Pallas kernels  39.3 us (14%)
  other arithmetic  30 us (10%)
  starting transfers between devices  27.3 us (9%)
  between operations  13.4 us (5%)
  matrix products  4.67 us (2%)
    psum x1, blocking collectives, shards(): square_sum = lax.psum(jnp.sum(as_float * as_float, axis=0), 'local')  42.3 us
    unnamed x45, local copies, waits for them, and re-layouts  37.3 us
    ppermute x16, waiting for transfers between devices, flip_local(): lax.ppermute(array, 'local', [(i, LOCAL_AT[LOCAL_LABEL[i] ^ 1 << bit]) fo...  34.6 us
    pallas_call x4, Pallas kernels, quarter(): pl.pallas_call(functools.partial(quarter_kernel, stream_masks(s, 1), deep...  28 us
    all_gather x1, waiting for transfers between devices, shards(): whole_columns = lax.all_gather(columns, 'local', axis=0, tiled=True)  20.8 us
    unnamed x4, waiting for transfers between devices  19.7 us
    ppermute x16, starting transfers between devices, flip_local(): lax.ppermute(array, 'local', [(i, LOCAL_AT[LOCAL_LABEL[i] ^ 1 << bit]) fo...  18.6 us
    convert_element_type x12, other arithmetic, add_pair(): (kept.astype(jnp.float32) + got.astype(jnp.float32)).astype(jnp.bfloat16)  12.8 us
  transfers between devices with their start and end apart: 21, of which 10 were waited for; matrix products, arithmetic and copies ran while one was open for 22% of the time, Pallas kernels for 14%

profile of v5, /device:TPU:0, one launch (start us, length us, event | category | flops | bytes accessed | tf_op | source)
XLA Modules:
  0.0 287.4 jit_solution(18000610559879291478)
XLA Ops:
  8.7 2.3 reduce-window.6
  15.2 4.4 %all-to-all-start = ((bf16[8,16,448]{2,1,0:T(8,128)(2,1)}), bf16[8,16,448]{2,1,0:T(8,128)(2,1)S(1)}, u32[]{:S(2)}, u32[]{:S(2)}) async-start(bf16[8,16,448]{2,1,0:T(8,128)(2,1)} %bitcast.7), calls=%async_computation | async-start | bytes 262144 | tf_op jit(solution)/shard_map/all_to_all | solution.py:225
  19.7 6.1 %copy.39 = bf16[7168,256]{0,1:T(8,128)(2,1)} copy(bf16[7168,256]{1,0:T(8,128)(2,1)} %param.13) | data formatting | bytes 7340032 | tf_op args[2]
  25.8 6.0 %copy.40 = bf16[7168,256]{0,1:T(8,128)(2,1)} copy(bf16[7168,256]{1,0:T(8,128)(2,1)} %param.14) | data formatting | bytes 7340032 | tf_op args[3]
  32.0 42.3 %psum.7 = f32[1024]{0:T(1024)S(1)} all-reduce(f32[1024]{0:T(1024)S(1)} %fusion.4), channel_id=1, replica_groups=mesh['node'=8,'local'=16] {'local'}, use_global_device_ids=true, to_apply=%region_1.2 | all-reduce | flops 1024 | bytes 8192 | tf_op jit(solution)/shard_map/psum | solution.py:231
  74.3 6.5 %fusion.1 = (bf16[256,7168]{1,0:T(8,128)(2,1)S(1)}, bf16[256,7168]{1,0:T(8,128)(2,1)}) fusion(bf16[7168,256]{0,1:T(8,128)(2,1)} %copy.39, f32[7168]{0:T(1024)S(1)} %copy-done.16, bf16[7168,256]{0,1:T(8,128)(2,1)} %copy.40), kind=kLoop, calls=%fused_computation.5 | loop fusion | flops 11010048 | bytes 14708736 | tf_op jit(solution)/shard_map/transpose | solution.py:235
  80.9 5.5 %pad_maximum_fusion.weight_ref = bf16[512,7168]{1,0:T(8,128)(2,1)} fusion(bf16[256,7168]{1,0:T(8,128)(2,1)} %get-tuple-element.74, bf16[256,7168]{1,0:T(8,128)(2,1)S(1)} %get-tuple-element.73), kind=kLoop, calls=%fused_computation.2 | loop fusion | flops 14680064 | bytes 14680064 | tf_op jit(solution)/shard_map/concatenate | solution.py:234
  86.4 6.0 %copy.41 = bf16[7168,256]{1,0:T(8,128)(2,1)} copy(bf16[7168,256]{0,1:T(8,128)(2,1)} %bitcast.68) | data formatting | bytes 7340032 | tf_op jit(solution)/shard_map/transpose | solution.py:237
  92.4 20.8 %all-gather.3.cloned.1.call-done.x_ref = bf16[7168,1024]{1,0:T(8,128)(2,1)} async-done(((bf16[448,1024]{1,0:T(8,128)(2,1)}), bf16[7168,1024]{1,0:T(8,128)(2,1)}) %all-gather.3.cloned.1.call-update) | async-done | bytes 14680080 | tf_op jit(solution)/shard_map/all_gather | solution.py:215
  114.7 2.0 copy-done
  116.8 3.1 %copy-done.2 = bf16[512,7168]{1,0:T(8,128)(2,1)S(1)} copy-done((bf16[512,7168]{1,0:T(8,128)(2,1)S(1)}, bf16[512,7168]{1,0:T(8,128)(2,1)}, u32[]{:S(2)}) %copy-start.2) | copy-done | bytes 7340056
  119.9 7.0 %shard_map.109 = (bf16[256,256]{1,0:T(8,128)(2,1)S(1)}, bf16[8,448,256]{2,1,0:T(8,128)(2,1)}) custom-call(s32[16]{0:T(128)S(1)} %dynamic-slice_bitcast_fusion.slice_ref, bf16[512,7168]{1,0:T(8,128)(2,1)S(1)} %copy-done.2, bf16[16,448,256]{2,1,0:T(8,128)(2,1)S(1)} %bitcast.54, bf16[7168,1024]{1,0:T(8,128)(2,1)} %all-gather.3.cloned.1.call-done.x_ref, ...), custom_call_target="tpu_custom_call" | custom-call | flops 2818572288 | bytes 11010048 | tf_op jit(solution)/shard_map/pallas_call | solution.py:77
  127.8 7.0 %shard_map.110 = (bf16[256,256]{1,0:T(8,128)(2,1)S(1)}, bf16[8,448,256]{2,1,0:T(8,128)(2,1)}) custom-call(s32[16]{0:T(128)S(1)} %dynamic-slice_bitcast_fusion.slice_ref, bf16[512,7168]{1,0:T(8,128)(2,1)S(1)} %copy-done.2, bf16[16,448,256]{2,1,0:T(8,128)(2,1)S(1)} %bitcast.55, bf16[7168,1024]{1,0:T(8,128)(2,1)} %all-gather.3.cloned.1.call-done.x_ref, ...), custom_call_target="tpu_custom_call" | custom-call | flops 2818572288 | bytes 11010048 | tf_op jit(solution)/shard_map/pallas_call | solution.py:77
  134.8 2.1 collective-permute-start.4
  136.9 7.0 %shard_map.111 = (bf16[256,256]{1,0:T(8,128)(2,1)S(1)}, bf16[8,448,256]{2,1,0:T(8,128)(2,1)}) custom-call(s32[16]{0:T(128)S(1)} %dynamic-slice_bitcast_fusion.slice_ref, bf16[512,7168]{1,0:T(8,128)(2,1)S(1)} %copy-done.2, bf16[16,448,256]{2,1,0:T(8,128)(2,1)S(1)} %bitcast.56, bf16[7168,1024]{1,0:T(8,128)(2,1)} %all-gather.3.cloned.1.call-done.x_ref, ...), custom_call_target="tpu_custom_call" | custom-call | flops 2818572288 | bytes 11010048 | tf_op jit(solution)/shard_map/pallas_call | solution.py:77
  144.2 7.0 %shard_map.112 = (bf16[256,256]{1,0:T(8,128)(2,1)S(1)}, bf16[8,448,256]{2,1,0:T(8,128)(2,1)}) custom-call(s32[16]{0:T(128)S(1)} %dynamic-slice_bitcast_fusion.slice_ref, bf16[512,7168]{1,0:T(8,128)(2,1)S(1)} %copy-done.2, bf16[16,448,256]{2,1,0:T(8,128)(2,1)S(1)} %bitcast.57, bf16[7168,1024]{1,0:T(8,128)(2,1)} %all-gather.3.cloned.1.call-done.x_ref, ...), custom_call_target="tpu_custom_call" | custom-call | flops 2818572288 | bytes 11010048 | tf_op jit(solution)/shard_map/pallas_call | solution.py:77
  151.1 2.0 collective-permute-start.12
  153.1 2.4 copy.49.gain_ref
  155.5 2.1 copy-done.1
  157.6 3.9 %shard_map.113 = (bf16[8,448,256]{2,1,0:T(8,128)(2,1)S(1)}, bf16[8,448,256]{2,1,0:T(8,128)(2,1)S(1)}, bf16[8,448,256]{2,1,0:T(8,128)(2,1)S(1)}, bf16[8,448,256]{2,1,0:T(8,128)(2,1)S(1)}) custom-call(s32[16]{0:T(128)S(1)} %dynamic-slice_bitcast_fusion.slice_ref, bf16[16,448,256]{2,1,0:T(8,128)(2,1)S(1)} %bitcast.58, bf16[16,448,256]{2,1,0:T(8,128)(2,1)S(1)} %bitcast.59, ...), custom_call_target="tpu_custom_call" | custom-call | flops 1879048192 | bytes 14680064 | tf_op jit(solution)/shard_map/pallas_call | solution.py:121
  165.3 2.0 copy-done.3
  167.4 2.0 copy-done.4
  169.4 2.0 copy-done.5
  171.5 1.5 copy-done.6
  173.0 7.5 %shard_map.114 = bf16[256,128]{1,0:T(8,128)(2,1)S(1)} custom-call(s32[16]{0:T(128)S(1)} %iota.15.at_ref, bf16[16,448,128]{2,1,0:T(8,128)(2,1)S(1)} %bitcast.62, bf16[1,7168,256]{2,1,0:T(8,128)(2,1)S(1)} %copy-done.4, bf16[1,7168,256]{2,1,0:T(8,128)(2,1)S(1)} %copy-done.5, f32[7168,1]{1,0:T(8,128)S(1)} %copy-done.3), custom_call_target="tpu_custom_call" | custom-call | flops 939524096 | bytes 9175040 | tf_op jit(solution)/shard_map/pallas_call | solution.py:162
  180.4 1.9 fusion
  182.4 3.2 %add_convert_fusion.7 = (bf16[4,448,256]{2,1,0:T(8,128)(2,1)}, bf16[4,448,256]{2,1,0:T(8,128)(2,1)}) fusion(bf16[8,448,256]{2,1,0:T(8,128)(2,1)} %collective-permute-done, bf16[8,448,256]{2,1,0:T(8,128)(2,1)S(1)} %copy-done.11), kind=kLoop, calls=%fused_computation.20 | loop fusion | flops 3670016 | bytes 5505024 | tf_op jit(solution)/shard_map/convert_element_type | solution.py:191
  187.0 3.9 %copy.50 = bf16[7168,128]{1,0:T(8,128)(2,1)} copy(bf16[7168,128]{0,1:T(8,128)(2,1)} %fusion) | data formatting | bytes 3670016
  190.9 2.6 add_convert_fusion.5
  194.2 2.0 add_convert_fusion.3
  196.2 1.6 collective-permute-start.9
  197.8 1.9 add_convert_fusion.1
  200.3 9.1 %collective-permute-done.1 = bf16[4,448,256]{2,1,0:T(8,128)(2,1)} collective-permute-done((bf16[4,448,256]{2,1,0:T(8,128)(2,1)}, bf16[4,448,256]{2,1,0:T(8,128)(2,1)}, u32[]{:S(2)}, u32[]{:S(2)}) %collective-permute-start.1) | collective-permute-done | bytes 917536 | tf_op jit(solution)/shard_map/ppermute | solution.py:21
  209.5 1.4 add_convert_fusion.15
  212.0 8.3 %collective-permute-done.5 = bf16[4,448,256]{2,1,0:T(8,128)(2,1)S(1)} collective-permute-done((bf16[4,448,256]{2,1,0:T(8,128)(2,1)S(1)}, bf16[4,448,256]{2,1,0:T(8,128)(2,1)S(1)}, u32[]{:S(2)}, u32[]{:S(2)}) %collective-permute-start.5) | collective-permute-done | bytes 917536 | tf_op jit(solution)/shard_map/ppermute | solution.py:21
  221.7 3.1 %collective-permute-done.9 = bf16[4,448,256]{2,1,0:T(8,128)(2,1)S(1)} collective-permute-done((bf16[4,448,256]{2,1,0:T(8,128)(2,1)S(1)}, bf16[4,448,256]{2,1,0:T(8,128)(2,1)S(1)}, u32[]{:S(2)}, u32[]{:S(2)}) %collective-permute-start.9) | collective-permute-done | bytes 917536 | tf_op jit(solution)/shard_map/ppermute | solution.py:21
  225.2 2.0 collective-permute-done.13
  227.5 2.2 collective-permute-start.14
  229.7 1.7 collective-permute-start.3
  231.4 5.4 %collective-permute-done.6 = bf16[2,448,256]{2,1,0:T(8,128)(2,1)S(1)} collective-permute-done((bf16[2,448,256]{2,1,0:T(8,128)(2,1)S(1)}, bf16[2,448,256]{2,1,0:T(8,128)(2,1)S(1)}, u32[]{:S(2)}, u32[]{:S(2)}) %collective-permute-start.6) | collective-permute-done | bytes 458784 | tf_op jit(solution)/shard_map/ppermute | solution.py:21
  237.1 2.7 collective-permute-done.10
  239.9 2.1 collective-permute-start.11
  243.4 4.0 %collective-permute-done.11 = bf16[1,448,256]{2,1,0:T(8,128)(2,1)S(1)} collective-permute-done((bf16[1,448,256]{2,1,0:T(8,128)(2,1)S(1)}, bf16[1,448,256]{2,1,0:T(8,128)(2,1)S(1)}, u32[]{:S(2)}, u32[]{:S(2)}) %collective-permute-start.11) | collective-permute-done | bytes 229408 | tf_op jit(solution)/shard_map/ppermute | solution.py:21
  247.5 18.9 %reduce-scatter.4.cloned.1.call-done = bf16[448,128]{1,0:T(8,128)(2,1)} async-done(((bf16[7168,128]{1,0:T(8,128)(2,1)}), bf16[448,128]{1,0:T(8,128)(2,1)}) %reduce-scatter.4.cloned.1.call-update) | async-done | bytes 114704
  266.4 1.6 copy.51
  268.1 4.3 %all-to-all-start.1 = ((bf16[8,16,448]{2,1,0:T(8,128)(2,1)}), bf16[8,16,448]{2,1,0:T(8,128)(2,1)}, u32[]{:S(2)}, u32[]{:S(2)}) async-start(bf16[8,16,448]{2,1,0:T(8,128)(2,1)} %bitcast.20), calls=%async_computation.1 | async-start | bytes 262144 | tf_op jit(solution)/shard_map/all_to_all | solution.py:259
  273.4 5.1 %all-to-all-done.1 = bf16[8,16,448]{2,1,0:T(8,128)(2,1)} async-done(((bf16[8,16,448]{2,1,0:T(8,128)(2,1)}), bf16[8,16,448]{2,1,0:T(8,128)(2,1)}, u32[]{:S(2)}, u32[]{:S(2)}) %all-to-all-start.1) | async-done | bytes 114720 | tf_op jit(solution)/shard_map/all_to_all | solution.py:259
  278.5 2.3 fusion.7
  (94 shorter events, 22.1 us)
Async XLA Ops:
  6.5 106.7 %all-gather.3.cloned.1.call-start = ((), (), s32[]{:S(2)}) async-start(), calls=%async_computation.3 | async-start | bytes 15597568 | tf_op jit(solution)/shard_map/all_gather | solution.py:215
  6.5 6.1 %copy-start.18 = (s32[1024,2]{0,1:T(2,128)S(1)}, s32[1024,2]{0,1:T(2,128)}, u32[]{:S(2)}) copy-start(s32[1024,2]{0,1:T(2,128)} %param.19) | copy-start | bytes 24580
  11.5 1.8 copy-start.19
  11.6 2.4 copy-start.12
  15.2 77.2 %all-to-all-start = ((bf16[8,16,448]{2,1,0:T(8,128)(2,1)}), bf16[8,16,448]{2,1,0:T(8,128)(2,1)S(1)}, u32[]{:S(2)}, u32[]{:S(2)}) async-start(bf16[8,16,448]{2,1,0:T(8,128)(2,1)} %bitcast.7), calls=%async_computation | async-start | bytes 262144 | tf_op jit(solution)/shard_map/all_to_all | solution.py:225
  19.6 145.7 %all-gather.5.cloned.1.call-start = ((), (), s32[]{:S(2)}) async-start(), calls=%async_computation.4 | async-start | bytes 1949696 | tf_op jit(solution)/shard_map/all_gather | solution.py:241
  25.8 48.6 %copy-start.16 = (f32[7168]{0:T(1024)S(1)}, f32[7168]{0:T(1024)}, u32[]{:S(2)}) copy-start(f32[7168]{0:T(1024)} %param.12) | copy-start | bytes 86020
  114.0 152.4 %reduce-scatter.4.cloned.1.call-start = ((), (), s32[]{:S(2)}) async-start(), calls=%async_computation.5 | async-start | bytes 1949696
  114.7 2.0 copy-start
  116.8 3.1 %copy-start.2 = (bf16[512,7168]{1,0:T(8,128)(2,1)S(1)}, bf16[512,7168]{1,0:T(8,128)(2,1)}, u32[]{:S(2)}) copy-start(bf16[512,7168]{1,0:T(8,128)(2,1)} %pad_maximum_fusion.weight_ref) | copy-start | bytes 22020100
  126.9 55.5 %collective-permute-start = (bf16[8,448,256]{2,1,0:T(8,128)(2,1)}, bf16[8,448,256]{2,1,0:T(8,128)(2,1)}, u32[]{:S(2)}, u32[]{:S(2)}) collective-permute-start(bf16[8,448,256]{2,1,0:T(8,128)(2,1)} %get-tuple-element.44), channel_id=1, source_target_pairs={{0,1},{1,0},{2,3},{3,2},{4,5},{5,4},{6,7},{7,6},{8,9},{9,8},{10,11... | collective-permute-start | bytes 5505032 | tf_op jit(solution)/shard_map/ppermute | solution.py:21
  134.8 56.1 %collective-permute-start.4 = (bf16[8,448,256]{2,1,0:T(8,128)(2,1)}, bf16[8,448,256]{2,1,0:T(8,128)(2,1)}, u32[]{:S(2)}, u32[]{:S(2)}) collective-permute-start(bf16[8,448,256]{2,1,0:T(8,128)(2,1)} %get-tuple-element.47), channel_id=1, source_target_pairs={{0,3},{1,2},{2,1},{3,0},{4,7},{5,6},{6,5},{7,4},{8,11},{9,10},{10,... | collective-permute-start | bytes 5505032 | tf_op jit(solution)/shard_map/ppermute | solution.py:21
  144.0 9.2 %copy-start.17 = (f32[7168]{0:T(1024)S(1)}, f32[7168]{0:T(1024)}, u32[]{:S(2)}) copy-start(f32[7168]{0:T(1024)} %param.12) | copy-start | bytes 86020
  144.0 50.3 %collective-permute-start.8 = (bf16[8,448,256]{2,1,0:T(8,128)(2,1)}, bf16[8,448,256]{2,1,0:T(8,128)(2,1)}, u32[]{:S(2)}, u32[]{:S(2)}) collective-permute-start(bf16[8,448,256]{2,1,0:T(8,128)(2,1)} %get-tuple-element.49), channel_id=1, source_target_pairs={{0,4},{1,5},{2,6},{3,7},{4,0},{5,1},{6,2},{7,3},{8,12},{9,13},{10,... | collective-permute-start | bytes 5505032 | tf_op jit(solution)/shard_map/ppermute | solution.py:21
  151.1 46.7 %collective-permute-start.12 = (bf16[8,448,256]{2,1,0:T(8,128)(2,1)}, bf16[8,448,256]{2,1,0:T(8,128)(2,1)}, u32[]{:S(2)}, u32[]{:S(2)}) collective-permute-start(bf16[8,448,256]{2,1,0:T(8,128)(2,1)} %get-tuple-element.51), channel_id=1, source_target_pairs={{0,12},{1,13},{2,14},{3,15},{4,8},{5,9},{6,10},{7,11},{8,4},{9,5},... | collective-permute-start | bytes 5505032 | tf_op jit(solution)/shard_map/ppermute | solution.py:21
  155.5 2.1 copy-start.1
  161.5 1.3 copy-start.7
  162.8 1.3 copy-start.9
  164.1 1.3 copy-start.10
  165.3 2.0 copy-start.3
  167.4 2.0 copy-start.4
  169.4 2.0 copy-start.5
  171.5 1.5 copy-start.6
  173.0 7.5 %copy-start.13 = (bf16[1,256,7168]{2,1,0:T(8,128)(2,1)S(1)}, bf16[1,256,7168]{2,1,0:T(8,128)(2,1)}, u32[]{:S(2)}) copy-start(bf16[1,256,7168]{2,1,0:T(8,128)(2,1)} %param.18) | copy-start | bytes 11010052
  180.4 1.9 copy-start.11
  185.6 23.9 %collective-permute-start.1 = (bf16[4,448,256]{2,1,0:T(8,128)(2,1)}, bf16[4,448,256]{2,1,0:T(8,128)(2,1)}, u32[]{:S(2)}, u32[]{:S(2)}) collective-permute-start(bf16[4,448,256]{2,1,0:T(8,128)(2,1)} %get-tuple-element.58), channel_id=1, source_target_pairs={{0,3},{1,2},{2,1},{3,0},{4,7},{5,6},{6,5},{7,4},{8,11},{9,10},{10,... | collective-permute-start | bytes 2752520 | tf_op jit(solution)/shard_map/ppermute | solution.py:21
  190.9 3.3 %copy-start.8 = (bf16[8,448,256]{2,1,0:T(8,128)(2,1)S(1)}, bf16[8,448,256]{2,1,0:T(8,128)(2,1)}, u32[]{:S(2)}) copy-start(bf16[8,448,256]{2,1,0:T(8,128)(2,1)} %copy-done.7) | copy-start | bytes 5505028
  193.5 26.7 %collective-permute-start.5 = (bf16[4,448,256]{2,1,0:T(8,128)(2,1)S(1)}, bf16[4,448,256]{2,1,0:T(8,128)(2,1)S(1)}, u32[]{:S(2)}, u32[]{:S(2)}) collective-permute-start(bf16[4,448,256]{2,1,0:T(8,128)(2,1)S(1)} %get-tuple-element.60), channel_id=1, source_target_pairs={{0,4},{1,5},{2,6},{3,7},{4,0},{5,1},{6,2},{7,3},{8,12},{9,13},{10,... | collective-permute-start | bytes 2752520 | tf_op jit(solution)/shard_map/ppermute | solution.py:21
  196.2 13.3 %copy-start.14 = (bf16[4,448,256]{2,1,0:T(8,128)(2,1)S(1)}, bf16[4,448,256]{2,1,0:T(8,128)(2,1)}, u32[]{:S(2)}) copy-start(bf16[4,448,256]{2,1,0:T(8,128)(2,1)} %get-tuple-element.57) | copy-start | bytes 2752516
  196.2 28.6 %collective-permute-start.9 = (bf16[4,448,256]{2,1,0:T(8,128)(2,1)S(1)}, bf16[4,448,256]{2,1,0:T(8,128)(2,1)S(1)}, u32[]{:S(2)}, u32[]{:S(2)}) collective-permute-start(bf16[4,448,256]{2,1,0:T(8,128)(2,1)S(1)} %get-tuple-element.62), channel_id=1, source_target_pairs={{0,12},{1,13},{2,14},{3,15},{4,8},{5,9},{6,10},{7,11},{8,4},{9,5},... | collective-permute-start | bytes 2752520 | tf_op jit(solution)/shard_map/ppermute | solution.py:21
  199.8 27.4 %collective-permute-start.13 = (bf16[4,448,256]{2,1,0:T(8,128)(2,1)S(1)}, bf16[4,448,256]{2,1,0:T(8,128)(2,1)S(1)}, u32[]{:S(2)}, u32[]{:S(2)}) collective-permute-start(bf16[4,448,256]{2,1,0:T(8,128)(2,1)S(1)} %get-tuple-element.64), channel_id=1, source_target_pairs={{0,1},{1,0},{2,3},{3,2},{4,5},{5,4},{6,7},{7,6},{8,9},{9,8},{10,11... | collective-permute-start | bytes 2752520 | tf_op jit(solution)/shard_map/ppermute | solution.py:21
  210.9 18.7 %collective-permute-start.2 = (bf16[2,448,256]{2,1,0:T(8,128)(2,1)S(1)}, bf16[2,448,256]{2,1,0:T(8,128)(2,1)S(1)}, u32[]{:S(2)}, u32[]{:S(2)}) collective-permute-start(bf16[2,448,256]{2,1,0:T(8,128)(2,1)S(1)} %get-tuple-element.66), channel_id=1, source_target_pairs={{0,4},{1,5},{2,6},{3,7},{4,0},{5,1},{6,2},{7,3},{8,12},{9,13},{10,... | collective-permute-start | bytes 1376264 | tf_op jit(solution)/shard_map/ppermute | solution.py:21
  220.5 16.2 %collective-permute-start.6 = (bf16[2,448,256]{2,1,0:T(8,128)(2,1)S(1)}, bf16[2,448,256]{2,1,0:T(8,128)(2,1)S(1)}, u32[]{:S(2)}, u32[]{:S(2)}) collective-permute-start(bf16[2,448,256]{2,1,0:T(8,128)(2,1)S(1)} %get-tuple-element.68), channel_id=1, source_target_pairs={{0,12},{1,13},{2,14},{3,15},{4,8},{5,9},{6,10},{7,11},{8,4},{9,5},... | collective-permute-start | bytes 1376264 | tf_op jit(solution)/shard_map/ppermute | solution.py:21
  225.0 14.8 %collective-permute-start.10 = (bf16[2,448,256]{2,1,0:T(8,128)(2,1)S(1)}, bf16[2,448,256]{2,1,0:T(8,128)(2,1)S(1)}, u32[]{:S(2)}, u32[]{:S(2)}) collective-permute-start(bf16[2,448,256]{2,1,0:T(8,128)(2,1)S(1)} %get-tuple-element.70), channel_id=1, source_target_pairs={{0,1},{1,0},{2,3},{3,2},{4,5},{5,4},{6,7},{7,6},{8,9},{9,8},{10,11... | collective-permute-start | bytes 1376264 | tf_op jit(solution)/shard_map/ppermute | solution.py:21
  227.5 14.5 %collective-permute-start.14 = (bf16[2,448,256]{2,1,0:T(8,128)(2,1)S(1)}, bf16[2,448,256]{2,1,0:T(8,128)(2,1)S(1)}, u32[]{:S(2)}, u32[]{:S(2)}) collective-permute-start(bf16[2,448,256]{2,1,0:T(8,128)(2,1)S(1)} %get-tuple-element.72), channel_id=1, source_target_pairs={{0,3},{1,2},{2,1},{3,0},{4,7},{5,6},{6,5},{7,4},{8,11},{9,10},{10,... | collective-permute-start | bytes 1376264 | tf_op jit(solution)/shard_map/ppermute | solution.py:21
  229.7 13.5 %collective-permute-start.3 = (bf16[1,448,256]{2,1,0:T(8,128)(2,1)S(1)}, bf16[1,448,256]{2,1,0:T(8,128)(2,1)S(1)}, u32[]{:S(2)}, u32[]{:S(2)}) collective-permute-start(bf16[1,448,256]{2,1,0:T(8,128)(2,1)S(1)} %add_convert_fusion.22), channel_id=1, source_target_pairs={{0,12},{1,13},{2,14},{3,15},{4,8},{5,9},{6,10},{7,11},{8,4},{9,5},... | collective-permute-start | bytes 688136 | tf_op jit(solution)/shard_map/ppermute | solution.py:21
  236.8 6.5 %collective-permute-start.7 = (bf16[1,448,256]{2,1,0:T(8,128)(2,1)S(1)}, bf16[1,448,256]{2,1,0:T(8,128)(2,1)S(1)}, u32[]{:S(2)}, u32[]{:S(2)}) collective-permute-start(bf16[1,448,256]{2,1,0:T(8,128)(2,1)S(1)} %add_convert_fusion.20), channel_id=1, source_target_pairs={{0,1},{1,0},{2,3},{3,2},{4,5},{5,4},{6,7},{7,6},{8,9},{9,8},{10,11... | collective-permute-start | bytes 688136 | tf_op jit(solution)/shard_map/ppermute | solution.py:21
  239.9 7.5 %collective-permute-start.11 = (bf16[1,448,256]{2,1,0:T(8,128)(2,1)S(1)}, bf16[1,448,256]{2,1,0:T(8,128)(2,1)S(1)}, u32[]{:S(2)}, u32[]{:S(2)}) collective-permute-start(bf16[1,448,256]{2,1,0:T(8,128)(2,1)S(1)} %add_convert_fusion.18), channel_id=1, source_target_pairs={{0,3},{1,2},{2,1},{3,0},{4,7},{5,6},{6,5},{7,4},{8,11},{9,10},{10,... | collective-permute-start | bytes 688136 | tf_op jit(solution)/shard_map/ppermute | solution.py:21
  242.0 1.3 copy-start.15
  242.8 29.5 %collective-permute-start.15 = (bf16[1,448,256]{2,1,0:T(8,128)(2,1)}, bf16[1,448,256]{2,1,0:T(8,128)(2,1)}, u32[]{:S(2)}, u32[]{:S(2)}) collective-permute-start(bf16[1,448,256]{2,1,0:T(8,128)(2,1)} %add_convert_fusion.16), channel_id=1, source_target_pairs={{0,4},{1,5},{2,6},{3,7},{4,0},{5,1},{6,2},{7,3},{8,12},{9,13},{10,... | collective-permute-start | bytes 688136 | tf_op jit(solution)/shard_map/ppermute | solution.py:21
  268.1 10.5 %all-to-all-start.1 = ((bf16[8,16,448]{2,1,0:T(8,128)(2,1)}), bf16[8,16,448]{2,1,0:T(8,128)(2,1)}, u32[]{:S(2)}, u32[]{:S(2)}) async-start(bf16[8,16,448]{2,1,0:T(8,128)(2,1)} %bitcast.20), calls=%async_computation.1 | async-start | bytes 262144 | tf_op jit(solution)/shard_map/all_to_all | solution.py:259
Sparse Core Ops, SparseCore 0:
  9.5 103.6 all-gather.2
  115.3 48.5 all-gather.4
  191.1 75.3 reduce-scatter.3

commit v6 on v5

v6 whole, which is shorter than its diff:
```python
import functools

import jax
import jax.numpy as jnp
from jax import lax
from jax.experimental import pallas as pl
from jax.experimental.pallas import tpu as pltpu
from jax.sharding import PartitionSpec as P

EPSILON = 1e-05
NODE_CAP = 16
GRAY = (0, 1, 3, 2)

LOCAL_LABEL = [GRAY[i % 4] | GRAY[i // 4] << 2 for i in range(16)]
LOCAL_AT = {label: i for i, label in enumerate(LOCAL_LABEL)}

STREAMS = ((0, 1, 2, 3), (1, 2, 3, 0), (2, 3, 0, 1), (3, 0, 1, 2))


def flip_local(array, bit):
    return lax.ppermute(array, "local", [(i, LOCAL_AT[LOCAL_LABEL[i] ^ (1 << bit)]) for i in range(16)])


def route_slots(ids_block, window):
    flat_ids = ids_block.reshape(-1)
    expert_range = jnp.arange(window, dtype=jnp.int32)
    member = (flat_ids[:, None] == expert_range[None, :]).astype(jnp.int32)
    before = jnp.cumsum(member, axis=0) - member
    route_rank = jnp.sum(before * member, axis=1)
    kept = (jnp.sum(member, axis=1) > 0) & (route_rank < NODE_CAP)
    slot = jnp.where(kept, flat_ids * NODE_CAP + route_rank, -1)
    return slot.reshape(ids_block.shape)


def transposed_dot(weight, rows):
    return lax.dot_general(weight, rows, (((0,), (0,)), ((), ())), preferred_element_type=jnp.float32)


def silu(value):
    return value / (1.0 + jnp.exp(-value))


def send_kernel(first, slice_ref, gate_up_ref, scale_ref, turned_ref, hidden_ref, *outs):
    step = pl.program_id(0)

    @pl.when(step == 0)
    def _():
        half = gate_up_ref.shape[0] // 2
        scale = scale_ref[...]
        hidden_ref[...] = (silu(gate_up_ref[:half] * scale) * (gate_up_ref[half:] * scale)).astype(jnp.bfloat16)

    columns = outs[0].shape[-1]
    for i, out in enumerate(outs):
        at = slice_ref[stream_mask(first + i, 1, step)]
        hidden = hidden_ref[:, i * columns : (i + 1) * columns]
        out[0] = jnp.dot(turned_ref[at], hidden, preferred_element_type=jnp.float32).astype(jnp.bfloat16)


def stream_mask(s, sent, j):
    a, b, c, d = STREAMS[s]
    return sent << a | ((j >> 2) & 1) << b | ((j >> 1) & 1) << c | (j & 1) << d


def sent_parts(first, slice_of, gate_up, scale, turned):
    both = gate_up.shape[0]
    columns = gate_up.shape[1] // 4
    blocks, slice_rows, deep = turned.shape
    pair = first // 2
    return pl.pallas_call(
        functools.partial(send_kernel, first),
        grid_spec=pltpu.PrefetchScalarGridSpec(
            num_scalar_prefetch=1,
            grid=(blocks // 2,),
            in_specs=[
                pl.BlockSpec((both, 2 * columns), lambda j, at: (0, pair)),
                pl.BlockSpec((1, 2 * columns), lambda j, at: (0, pair)),
                pl.BlockSpec(memory_space=pltpu.VMEM),
            ],
            out_specs=[pl.BlockSpec((deep, 2 * columns), lambda j, at: (0, 0))]
            + [pl.BlockSpec((1, slice_rows, columns), lambda j, at: (j, 0, 0))] * 2,
        ),
        out_shape=[jax.ShapeDtypeStruct((deep, 2 * columns), jnp.bfloat16)]
        + [jax.ShapeDtypeStruct((blocks // 2, slice_rows, columns), jnp.bfloat16)] * 2,
        compiler_params=pltpu.CompilerParams(vmem_limit_bytes=24 << 20),
        cost_estimate=pl.CostEstimate(
            flops=2 * blocks * slice_rows * deep * columns,
            bytes_accessed=2 * blocks * slice_rows * (deep + columns),
            transcendentals=0,
        ),
    )(slice_of, gate_up, scale, turned)


def keep_kernel(slice_ref, *refs):
    weights, hidden, outs = refs[:4], refs[4:6], refs[6:]
    columns = outs[0].shape[-1]
    for s in range(4):
        rows = hidden[s // 2][:, s % 2 * columns : (s % 2 + 1) * columns]
        outs[s][0] = jnp.dot(weights[s][0], rows, preferred_element_type=jnp.float32).astype(jnp.bfloat16)


def kept_parts(slice_of, turned, hidden):
    blocks, rows, deep = turned.shape
    columns = hidden[0].shape[1] // 2

    def weight_spec(s):
        return pl.BlockSpec((1, rows, deep), lambda j, at: (at[stream_mask(s, 0, j)], 0, 0))

    return pl.pallas_call(
        keep_kernel,
        grid_spec=pltpu.PrefetchScalarGridSpec(
            num_scalar_prefetch=1,
            grid=(blocks // 2,),
            in_specs=[weight_spec(s) for s in range(4)] + [pl.BlockSpec((deep, 2 * columns), lambda j, at: (0, 0))] * 2,
            out_specs=[pl.BlockSpec((1, rows, columns), lambda j, at: (j, 0, 0))] * 4,
        ),
        out_shape=[jax.ShapeDtypeStruct((blocks // 2, rows, columns), jnp.bfloat16)] * 4,
        compiler_params=pltpu.CompilerParams(vmem_limit_bytes=24 << 20),
        cost_estimate=pl.CostEstimate(
            flops=4 * blocks * rows * deep * columns, bytes_accessed=4 * blocks * rows * (deep + columns), transcendentals=0
        ),
    )(slice_of, *[turned] * 4, *hidden)


def expert_kernel(blocks, features, at_ref, x0, x1, x2, x3, gate_ref, up_ref, gain_ref, hidden_ref, gate_total, up_total, squares):
    step = pl.program_id(0)

    @pl.when(step == 0)
    def _():
        gate_total[...] = jnp.zeros_like(gate_total)
        up_total[...] = jnp.zeros_like(up_total)
        squares[...] = jnp.zeros_like(squares)

    as_float = jnp.concatenate([x0[0], x1[0], x2[0], x3[0]], axis=0).astype(jnp.float32)
    squares[...] += jnp.sum(as_float * as_float, axis=0, keepdims=True)
    rows = (as_float * gain_ref[...]).astype(jnp.bfloat16)
    gate_total[...] += transposed_dot(gate_ref[0], rows)
    up_total[...] += transposed_dot(up_ref[0], rows)

    @pl.when(step == blocks - 1)
    def _():
        scale = lax.rsqrt(squares[...] / features + EPSILON)
        hidden_ref[...] = (silu(gate_total[...] * scale) * (up_total[...] * scale)).astype(jnp.bfloat16)


def expert_gate_up(slice_of, pooled, gate_weight, up_weight, gain_column):
    blocks, quarter_rows, columns = pooled[0].shape
    rows = 4 * quarter_rows
    hidden = gate_weight.shape[-1]
    weight_spec = pl.BlockSpec((1, rows, hidden), lambda m, at: (0, at[m], 0))

    def stream_spec(s):
        a, b, c, d = STREAMS[s]

        def index(m, at):
            return ((m >> a) & 1) | ((m >> b) & 1) << 1 | ((m >> c) & 1) << 2 | ((m >> d) & 1) << 3, 0, 0

        return pl.BlockSpec((1, quarter_rows, columns), index)

    return pl.pallas_call(
        functools.partial(expert_kernel, blocks, blocks * rows),
        grid_spec=pltpu.PrefetchScalarGridSpec(
            num_scalar_prefetch=1,
            grid=(blocks,),
            in_specs=[stream_spec(s) for s in range(4)]
            + [weight_spec, weight_spec, pl.BlockSpec((rows, 1), lambda m, at: (at[m], 0))],
            out_specs=pl.BlockSpec((hidden, columns), lambda m, at: (0, 0)),
            scratch_shapes=[
                pltpu.VMEM((hidden, columns), jnp.float32),
                pltpu.VMEM((hidden, columns), jnp.float32),
                pltpu.VMEM((1, columns), jnp.float32),
            ],
        ),
        out_shape=jax.ShapeDtypeStruct((hidden, columns), jnp.bfloat16),
        compiler_params=pltpu.CompilerParams(vmem_limit_bytes=24 << 20),
        cost_estimate=pl.CostEstimate(
            flops=4 * blocks * rows * columns * hidden,
            bytes_accessed=2 * blocks * rows * (columns + 2 * hidden),
            transcendentals=0,
        ),
    )(slice_of, *pooled, gate_weight, up_weight, gain_column)


def add_pair(kept, got):
    return (kept.astype(jnp.float32) + got.astype(jnp.float32)).astype(jnp.bfloat16)


def shards(
    tokens,
    norm_gain,
    dense_gate,
    dense_up,
    dense_down,
    expert_gate,
    expert_up,
    expert_down,
    expert_ids,
    route_gates,
):
    node_count = lax.axis_size("node")
    local_index = lax.axis_index("local")
    slice_width = tokens.shape[1]
    width = slice_width * 16
    slot_count = node_count * NODE_CAP
    slice_table = [[LOCAL_AT[LOCAL_LABEL[i] ^ m] for m in range(16)] for i in range(16)]
    slice_of = jnp.asarray(slice_table, jnp.int32)[local_index]

    columns = tokens.T
    whole_columns = lax.all_gather(columns, "local", axis=0, tiled=True)

    slot = route_slots(expert_ids, node_count)
    slot_range = jnp.arange(slot_count, dtype=jnp.int32)
    match_float = (slot[:, :, None] == slot_range[None, None, :]).astype(jnp.float32)
    chosen = jnp.sum(match_float, axis=1).astype(jnp.bfloat16)
    slot_gate = jnp.sum(match_float * route_gates[:, :, None], axis=(0, 1))
    send_rows = lax.dot_general(
        chosen, tokens, (((0,), (0,)), ((), ())), preferred_element_type=jnp.float32
    ).astype(jnp.bfloat16)
    routed = lax.all_to_all(
        send_rows.reshape(node_count, NODE_CAP, slice_width), "node", split_axis=0, concat_axis=0, tiled=True
    )
    routed = routed.reshape(slot_count, slice_width).T

    as_float = columns.astype(jnp.float32)
    square_sum = jnp.sum(as_float * as_float, axis=0, keepdims=True)
    gain_column = norm_gain[:, None]
    part = slice_width // 4
    pooled = [routed[None, s * part : (s + 1) * part] for s in range(4)]
    for step in range(4):
        got = [flip_local(pooled[s], STREAMS[s][step]) for s in range(4)]
        square_sum = square_sum + flip_local(square_sum, step)
        if step == 1:
            dense_gate, dense_up, _ = lax.optimization_barrier((dense_gate, dense_up, pooled))
            weight = jnp.concatenate(
                [(w.astype(jnp.float32) * gain_column).astype(jnp.bfloat16) for w in (dense_gate, dense_up)], axis=1
            )
            got, weight = lax.optimization_barrier((got, weight))
        if step == 2:
            dense_down, _ = lax.optimization_barrier((dense_down, pooled))
            turned = dense_down.T.reshape(16, slice_width, dense_down.shape[0])
            got, turned = lax.optimization_barrier((got, turned))
        pooled = [jnp.concatenate([pooled[s], got[s]], axis=0) for s in range(4)]
    scale = lax.rsqrt(square_sum / width + EPSILON)

    expert_hidden = expert_gate_up(slice_of, pooled, expert_gate, expert_up, gain_column)
    expert_partial = transposed_dot(expert_down[0], expert_hidden).astype(jnp.bfloat16)
    expert_partial, scale, whole_columns = lax.optimization_barrier((expert_partial, scale, whole_columns))
    expert_out = lax.psum_scatter(expert_partial, "local", scatter_dimension=0, tiled=True)

    gate_up = transposed_dot(weight, whole_columns)
    low_hidden, *sent = sent_parts(0, slice_of, gate_up, scale, turned)
    high_hidden, *more = sent_parts(2, slice_of, gate_up, scale, turned)
    sent += more
    arrived = [flip_local(sent[s], STREAMS[s][0]) for s in range(4)]
    sums = kept_parts(slice_of, turned, (low_hidden, high_hidden))
    for step in (1, 2, 3):
        half = sums[0].shape[0] // 2
        came = [flip_local(add_pair(sums[s][half:], arrived[s][half:]), STREAMS[s][step]) for s in range(4)]
        sums = [add_pair(sums[s][:half], arrived[s][:half]) for s in range(4)]
        arrived = came
        if step == 2:
            arrived[3], expert_out = lax.optimization_barrier((arrived[3], expert_out))
    returned = lax.all_to_all(
        expert_out.T.reshape(node_count, NODE_CAP, slice_width), "node", split_axis=0, concat_axis=0, tiled=True
    ).reshape(slot_count, slice_width)
    route_term = (slot_gate[:, None] * returned.astype(jnp.float32)).astype(jnp.bfloat16)
    expert_part = lax.dot_general(
        route_term, chosen, (((0,), (1,)), ((), ())), preferred_element_type=jnp.float32
    )
    dense_part = jnp.concatenate(
        [sums[s][0].astype(jnp.float32) + arrived[s][0].astype(jnp.float32) for s in range(4)], axis=1
    )
    return (columns.astype(jnp.float32) + dense_part + expert_part).astype(jnp.bfloat16).T


def solution(mesh):
    return jax.shard_map(
        shards,
        mesh=mesh,
        in_specs=(
            P("node", "local"),
            P(),
            P(None, "local"),
            P(None, "local"),
            P("local", None),
            P("node", None, "local"),
            P("node", None, "local"),
            P("node", "local", None),
            P("node", None),
            P("node", None),
        ),
        out_specs=P("node", "local"),
        check_vma=False,
    )
```

time: 289 us -> 265 us (0.917)
  blocking collectives: 42.3 us -> 0 us
  starting transfers between devices: 27.3 us -> 56.9 us
  local copies, waits for them, and re-layouts: 50.1 us -> 26.7 us
  Pallas kernels: 39.3 us -> 22.2 us
  matrix products: 4.67 us -> 16.7 us
  other arithmetic: 30 us -> 38.4 us
  waiting for transfers between devices: 80.2 us -> 88.5 us
    psum x1 -> x0, blocking collectives: 42.3 us -> none  [shards(): square_sum = lax.psum(jnp.sum(as_float * as_float, axis=0), 'local')]
    ppermute x16 -> x36, waiting for transfers between devices: 34.6 us -> 69.4 us  [flip_local(): lax.ppermute(array, 'local', [(i, LOCAL_AT[LOCAL_LABEL[i] ^ 1 << bit]) fo...]
    ppermute x16 -> x36, starting transfers between devices: 18.6 us -> 48 us  [flip_local(): lax.ppermute(array, 'local', [(i, LOCAL_AT[LOCAL_LABEL[i] ^ 1 << bit]) fo...]
    unnamed x45 -> x37, local copies, waits for them, and re-layouts: 37.3 us -> 12.6 us
    unnamed x4 -> x3, waiting for transfers between devices: 19.7 us -> 0.75 us
    pallas_call x4 -> x2, Pallas kernels: 28 us -> 10.8 us  [sent_parts(): pl.pallas_call(functools.partial(send_kernel, first), grid_spec=pltpu.Pre...]
    dot_general x1 -> x2, matrix products: 1.93 us -> 14 us  [transposed_dot(): lax.dot_general(weight, rows, (((0,), (0,)), ((), ())), preferred_element...]
    all_gather x1, waiting for transfers between devices: 20.8 us -> 13.1 us  [shards(): whole_columns = lax.all_gather(columns, 'local', axis=0, tiled=True)]
  transfers between devices with their start and end apart: 21 -> 40, of which waited for: 10 -> 22; matrix products, arithmetic and copies ran while one was open for 22% -> 23% of each run, Pallas kernels for 14% -> 6%
where the time goes in v6:
time: 265 us; the launch traced here: 263 us
  waiting for transfers between devices  88.5 us (33%)
  starting transfers between devices  56.9 us (21%)
  other arithmetic  38.4 us (14%)
  local copies, waits for them, and re-layouts  26.7 us (10%)
  Pallas kernels  22.2 us (8%)
  matrix products  16.7 us (6%)
  between operations  13.8 us (5%)
    ppermute x36, waiting for transfers between devices, flip_local(): lax.ppermute(array, 'local', [(i, LOCAL_AT[LOCAL_LABEL[i] ^ 1 << bit]) fo...  69.4 us
    ppermute x36, starting transfers between devices, flip_local(): lax.ppermute(array, 'local', [(i, LOCAL_AT[LOCAL_LABEL[i] ^ 1 << bit]) fo...  48 us
    dot_general x2, matrix products, transposed_dot(): lax.dot_general(weight, rows, (((0,), (0,)), ((), ())), preferred_element...  14 us
    all_gather x1, waiting for transfers between devices, shards(): whole_columns = lax.all_gather(columns, 'local', axis=0, tiled=True)  13.1 us
    unnamed x37, local copies, waits for them, and re-layouts  12.6 us
    convert_element_type x12, other arithmetic, add_pair(): (kept.astype(jnp.float32) + got.astype(jnp.float32)).astype(jnp.bfloat16)  11.1 us
    pallas_call x2, Pallas kernels, sent_parts(): pl.pallas_call(functools.partial(send_kernel, first), grid_spec=pltpu.Pre...  10.8 us
    pallas_call x1, Pallas kernels, expert_gate_up(): pl.pallas_call(functools.partial(expert_kernel, blocks, blocks * rows), g...  7.66 us
  transfers between devices with their start and end apart: 40, of which 22 were waited for; matrix products, arithmetic and copies ran while one was open for 23% of the time, Pallas kernels for 6%

profile of v6, /device:TPU:0, one launch (start us, length us, event | category | flops | bytes accessed | tf_op | source)
XLA Modules:
  0.0 263.4 jit_solution(16827340734765610359)
XLA Ops:
  8.7 1.7 collective-permute-start.16
  11.2 2.3 reduce-window.6
  15.7 2.3 collective-permute-start.17
  18.8 1.9 collective-permute-done.17
  20.6 1.9 collective-permute-start.18
  23.7 4.3 %all-to-all-start = ((bf16[8,16,448]{2,1,0:T(8,128)(2,1)}), bf16[8,16,448]{2,1,0:T(8,128)(2,1)S(1)}, u32[]{:S(2)}, u32[]{:S(2)}) async-start(bf16[8,16,448]{2,1,0:T(8,128)(2,1)} %bitcast.3), calls=%async_computation | async-start | bytes 262144 | tf_op jit(solution)/shard_map/all_to_all | solution.py:218
  28.1 2.6 collective-permute-start.19
  31.4 2.5 copy.41.gain_ref
  34.3 2.6 collective-permute-start.6
  38.0 2.2 collective-permute-start.2
  40.2 2.1 collective-permute-start.7
  44.2 2.3 collective-permute-start.1
  46.5 7.0 %multiply_convert_fusion.1 = (bf16[7168,256]{1,0:T(8,128)(2,1)}, bf16[7168,256]{1,0:T(8,128)(2,1)}) fusion(bf16[7168,256]{1,0:T(8,128)(2,1)} %param.13, f32[7168]{0:T(1024)S(1)} %copy-done.9, bf16[7168,256]{1,0:T(8,128)(2,1)} %param.14), kind=kLoop, calls=%fused_computation.4 | loop fusion | flops 11010048 | bytes 14708736 | tf_op jit(solution)/shard_map/convert_element_type | solution.py:234
  53.5 6.6 %pad_maximum_fusion = bf16[7168,512]{1,0:T(8,128)(2,1)} fusion(bf16[7168,256]{1,0:T(8,128)(2,1)} %get-tuple-element.90, bf16[7168,256]{1,0:T(8,128)(2,1)} %get-tuple-element.89), kind=kLoop, calls=%fused_computation.2 | loop fusion | flops 14680064 | bytes 14680064 | tf_op jit(solution)/shard_map/concatenate | solution.py:233
  63.7 2.2 collective-permute-start.9
  67.3 5.9 %copy.40 = bf16[7168,256]{1,0:T(8,128)(2,1)} copy(bf16[7168,256]{0,1:T(8,128)(2,1)} %bitcast.73) | data formatting | bytes 7340032 | tf_op jit(solution)/shard_map/transpose | solution.py:239
  79.1 1.9 collective-permute-start.13
  87.0 2.9 %collective-permute-done.14 = bf16[8,112,128]{2,1,0:T(8,128)(2,1)S(1)} collective-permute-done((bf16[8,112,128]{2,1,0:T(8,128)(2,1)S(1)}, bf16[8,112,128]{2,1,0:T(8,128)(2,1)S(1)}, u32[]{:S(2)}, u32[]{:S(2)}) %collective-permute-start.14) | collective-permute-done | bytes 229408 | tf_op jit(solution)/shard_map/ppermute | solution.py:21
  91.2 3.9 %collective-permute-done.12 = bf16[8,112,128]{2,1,0:T(8,128)(2,1)S(1)} collective-permute-done((bf16[8,112,128]{2,1,0:T(8,128)(2,1)S(1)}, bf16[8,112,128]{2,1,0:T(8,128)(2,1)S(1)}, u32[]{:S(2)}, u32[]{:S(2)}) %collective-permute-start.12) | collective-permute-done | bytes 229408 | tf_op jit(solution)/shard_map/ppermute | solution.py:21
  95.1 2.0 copy-done.3
  97.1 2.2 copy-done.4
  99.3 7.7 %shard_map.109 = bf16[256,128]{1,0:T(8,128)(2,1)S(1)} custom-call(s32[16]{0:T(128)S(1)} %dynamic-slice_bitcast_fusion.at_ref.slice_ref, bf16[16,112,128]{2,1,0:T(8,128)(2,1)S(1)} %constant_dynamic-update-slice_fusion.x0, bf16[16,112,128]{2,1,0:T(8,128)(2,1)S(1)} %constant_dynamic-update-slice_fusion.5.x1, ...), custom_call_target="tpu_custom_call" | custom-call | flops 939524096 | bytes 9175040 | tf_op jit(solution)/shard_map/pallas_call | solution.py:159
  107.7 13.1 %all-gather.2.cloned.1.call-done = bf16[7168,1024]{1,0:T(8,128)(2,1)} async-done(((bf16[448,1024]{1,0:T(8,128)(2,1)}), bf16[7168,1024]{1,0:T(8,128)(2,1)}) %all-gather.2.cloned.1.call-update) | async-done | bytes 14680080 | tf_op jit(solution)/shard_map/all_gather | solution.py:208
  120.7 13.3 %fusion.14.gate_up_ref = f32[512,1024]{1,0:T(8,128)S(1)} fusion(bf16[7168,512]{1,0:T(8,128)(2,1)} %pad_maximum_fusion, bf16[7168,1024]{1,0:T(8,128)(2,1)} %all-gather.2.cloned.1.call-done), kind=kOutput, calls=%fused_computation.100 | convolution fusion | flops 7516192768 | bytes 24117248 | tf_op jit(solution)/shard_map/dot_general | solution.py:36
  134.1 5.4 %shard_map.110 = (bf16[256,512]{1,0:T(8,128)(2,1)S(1)}, bf16[8,448,256]{2,1,0:T(8,128)(2,1)}, bf16[8,448,256]{2,1,0:T(8,128)(2,1)}) custom-call(s32[16]{0:T(128)S(1)} %dynamic-slice_bitcast_fusion.at_ref.slice_ref, f32[512,1024]{1,0:T(8,128)S(1)} %fusion.14.gate_up_ref, f32[1,1024]{1,0:T(1,128)S(1)} %add_rsqrt_fusion.scale_ref, ...), custom_call_target="tpu_custom_call" | custom-call | flops 939524096 | bytes 7340032 | tf_op jit(solution)/shard_map/pallas_call | solution.py:69
  140.9 2.1 collective-permute-start.24
  143.0 5.4 %shard_map.111 = (bf16[256,512]{1,0:T(8,128)(2,1)S(1)}, bf16[8,448,256]{2,1,0:T(8,128)(2,1)}, bf16[8,448,256]{2,1,0:T(8,128)(2,1)}) custom-call(s32[16]{0:T(128)S(1)} %dynamic-slice_bitcast_fusion.at_ref.slice_ref, f32[512,1024]{1,0:T(8,128)S(1)} %fusion.14.gate_up_ref, f32[1,1024]{1,0:T(1,128)S(1)} %add_rsqrt_fusion.scale_ref, ...), custom_call_target="tpu_custom_call" | custom-call | flops 939524096 | bytes 7340032 | tf_op jit(solution)/shard_map/pallas_call | solution.py:69
  148.6 1.8 collective-permute-start.32
  150.4 2.3 copy.42
  152.7 2.0 copy-done.1
  154.8 3.8 %shard_map.112 = (bf16[8,448,256]{2,1,0:T(8,128)(2,1)S(1)}, bf16[8,448,256]{2,1,0:T(8,128)(2,1)S(1)}, bf16[8,448,256]{2,1,0:T(8,128)(2,1)S(1)}, bf16[8,448,256]{2,1,0:T(8,128)(2,1)S(1)}) custom-call(s32[16]{0:T(128)S(1)} %dynamic-slice_bitcast_fusion.at_ref.slice_ref, bf16[16,448,256]{2,1,0:T(8,128)(2,1)S(1)} %bitcast.68, ...), custom_call_target="tpu_custom_call" | custom-call | flops 1879048192 | bytes 14680064 | tf_op jit(solution)/shard_map/pallas_call | solution.py:108
  158.6 26.9 %collective-permute-done.20 = bf16[8,448,256]{2,1,0:T(8,128)(2,1)} collective-permute-done((bf16[8,448,256]{2,1,0:T(8,128)(2,1)}, bf16[8,448,256]{2,1,0:T(8,128)(2,1)}, u32[]{:S(2)}, u32[]{:S(2)}) %collective-permute-start.20) | collective-permute-done | bytes 1835040 | tf_op jit(solution)/shard_map/ppermute | solution.py:21
  185.5 1.9 add_convert_fusion.7
  187.4 2.9 %collective-permute-start.21 = (bf16[4,448,256]{2,1,0:T(8,128)(2,1)S(1)}, bf16[4,448,256]{2,1,0:T(8,128)(2,1)S(1)}, u32[]{:S(2)}, u32[]{:S(2)}) collective-permute-start(bf16[4,448,256]{2,1,0:T(8,128)(2,1)S(1)} %get-tuple-element.66), channel_id=1, source_target_pairs={{0,3},{1,2},{2,1},{3,0},{4,7},{5,6},{6,5},{7,4},{8,11},{9,10},{10,... | collective-permute-start | bytes 2752520 | tf_op jit(solution)/shard_map/ppermute | solution.py:21
  190.4 1.9 add_convert_fusion.5
  192.4 5.4 %collective-permute-done.28 = bf16[8,448,256]{2,1,0:T(8,128)(2,1)} collective-permute-done((bf16[8,448,256]{2,1,0:T(8,128)(2,1)}, bf16[8,448,256]{2,1,0:T(8,128)(2,1)}, u32[]{:S(2)}, u32[]{:S(2)}) %collective-permute-start.28) | collective-permute-done | bytes 1835040 | tf_op jit(solution)/shard_map/ppermute | solution.py:21
  197.9 1.9 add_convert_fusion.3
  201.0 1.9 add_convert_fusion.1
  203.3 9.3 %collective-permute-done.21 = bf16[4,448,256]{2,1,0:T(8,128)(2,1)S(1)} collective-permute-done((bf16[4,448,256]{2,1,0:T(8,128)(2,1)S(1)}, bf16[4,448,256]{2,1,0:T(8,128)(2,1)S(1)}, u32[]{:S(2)}, u32[]{:S(2)}) %collective-permute-start.21) | collective-permute-done | bytes 917536 | tf_op jit(solution)/shard_map/ppermute | solution.py:21
  214.0 5.2 %collective-permute-done.25 = bf16[4,448,256]{2,1,0:T(8,128)(2,1)S(1)} collective-permute-done((bf16[4,448,256]{2,1,0:T(8,128)(2,1)S(1)}, bf16[4,448,256]{2,1,0:T(8,128)(2,1)S(1)}, u32[]{:S(2)}, u32[]{:S(2)}) %collective-permute-start.25) | collective-permute-done | bytes 917536 | tf_op jit(solution)/shard_map/ppermute | solution.py:21
  220.7 1.9 collective-permute-done.29
  222.9 2.3 collective-permute-done.33
  229.8 3.1 %collective-permute-done.26 = bf16[2,448,256]{2,1,0:T(8,128)(2,1)S(1)} collective-permute-done((bf16[2,448,256]{2,1,0:T(8,128)(2,1)S(1)}, bf16[2,448,256]{2,1,0:T(8,128)(2,1)S(1)}, u32[]{:S(2)}, u32[]{:S(2)}) %collective-permute-start.26) | collective-permute-done | bytes 458784 | tf_op jit(solution)/shard_map/ppermute | solution.py:21
  234.7 2.0 collective-permute-start.31
  236.9 2.2 collective-permute-done.27
  243.3 4.6 %all-to-all-start.1 = ((bf16[8,16,448]{2,1,0:T(8,128)(2,1)}), bf16[8,16,448]{2,1,0:T(8,128)(2,1)}, u32[]{:S(2)}, u32[]{:S(2)}) async-start(bf16[8,16,448]{2,1,0:T(8,128)(2,1)} %bitcast.21), calls=%async_computation.1 | async-start | bytes 262144 | tf_op jit(solution)/shard_map/all_to_all | solution.py:262
  249.1 5.1 %all-to-all-done.1 = bf16[8,16,448]{2,1,0:T(8,128)(2,1)} async-done(((bf16[8,16,448]{2,1,0:T(8,128)(2,1)}), bf16[8,16,448]{2,1,0:T(8,128)(2,1)}, u32[]{:S(2)}, u32[]{:S(2)}) %all-to-all-start.1) | async-done | bytes 114720 | tf_op jit(solution)/shard_map/all_to_all | solution.py:262
  254.2 2.3 fusion.5
  (141 shorter events, 48.5 us)
Async XLA Ops:
  6.5 3.9 %copy-start.10 = (s32[1024,2]{0,1:T(2,128)S(1)}, s32[1024,2]{0,1:T(2,128)}, u32[]{:S(2)}) copy-start(s32[1024,2]{0,1:T(2,128)} %param.19) | copy-start | bytes 24580
  6.5 114.2 %all-gather.2.cloned.1.call-start = ((), (), s32[]{:S(2)}) async-start(), calls=%async_computation.3 | async-start | bytes 15597568 | tf_op jit(solution)/shard_map/all_gather | solution.py:208
  8.7 7.1 %collective-permute-start.16 = (f32[1,1024]{1,0:T(1,128)S(1)}, f32[1,1024]{1,0:T(1,128)S(1)}, u32[]{:S(2)}, u32[]{:S(2)}) collective-permute-start(f32[1,1024]{1,0:T(1,128)S(1)} %bitcast.78), channel_id=1, source_target_pairs={{0,1},{1,0},{2,3},{3,2},{4,5},{5,4},{6,7},{7,6},{8,9},{9,8},{10,11... | collective-permute-start | bytes 12296 | tf_op jit(solution)/shard_map/ppermute | solution.py:21
  13.9 4.1 %copy-start.11 = (f32[1024,2]{0,1:T(2,128)S(1)}, f32[1024,2]{0,1:T(2,128)}, u32[]{:S(2)}) copy-start(f32[1024,2]{0,1:T(2,128)} %param.20) | copy-start | bytes 24580
  14.1 8.5 %copy-start.5 = (bf16[1024,448]{0,1:T(8,128)(2,1)S(1)}, bf16[1024,448]{0,1:T(8,128)(2,1)}, u32[]{:S(2)}) copy-start(bf16[1024,448]{0,1:T(8,128)(2,1)} %param.11) | copy-start | bytes 2752516
  15.4 16.0 %copy-start.9 = (f32[7168]{0:T(1024)S(1)}, f32[7168]{0:T(1024)}, u32[]{:S(2)}) copy-start(f32[7168]{0:T(1024)} %param.12) | copy-start | bytes 86020
  15.7 4.9 %collective-permute-start.17 = (f32[1,1024]{1,0:T(1,128)S(1)}, f32[1,1024]{1,0:T(1,128)S(1)}, u32[]{:S(2)}, u32[]{:S(2)}) collective-permute-start(f32[1,1024]{1,0:T(1,128)S(1)} %add.132), channel_id=1, source_target_pairs={{0,3},{1,2},{2,1},{3,0},{4,7},{5,6},{6,5},{7,4},{8,11},{9,10},{10,... | collective-permute-start | bytes 12296 | tf_op jit(solution)/shard_map/ppermute | solution.py:21
  20.6 7.5 %collective-permute-start.18 = (f32[1,1024]{1,0:T(1,128)S(1)}, f32[1,1024]{1,0:T(1,128)S(1)}, u32[]{:S(2)}, u32[]{:S(2)}) collective-permute-start(f32[1,1024]{1,0:T(1,128)S(1)} %add.133), channel_id=1, source_target_pairs={{0,4},{1,5},{2,6},{3,7},{4,0},{5,1},{6,2},{7,3},{8,12},{9,13},{10,... | collective-permute-start | bytes 12296 | tf_op jit(solution)/shard_map/ppermute | solution.py:21
  23.7 10.4 %all-to-all-start = ((bf16[8,16,448]{2,1,0:T(8,128)(2,1)}), bf16[8,16,448]{2,1,0:T(8,128)(2,1)S(1)}, u32[]{:S(2)}, u32[]{:S(2)}) async-start(bf16[8,16,448]{2,1,0:T(8,128)(2,1)} %bitcast.3), calls=%async_computation | async-start | bytes 262144 | tf_op jit(solution)/shard_map/all_to_all | solution.py:218
  28.0 211.1 %reduce-scatter.4.cloned.1.call-start = ((), (), s32[]{:S(2)}) async-start(), calls=%async_computation.4 | async-start | bytes 1949696
  28.1 5.8 %collective-permute-start.19 = (f32[1,1024]{1,0:T(1,128)S(1)}, f32[1,1024]{1,0:T(1,128)S(1)}, u32[]{:S(2)}, u32[]{:S(2)}) collective-permute-start(f32[1,1024]{1,0:T(1,128)S(1)} %add.134), channel_id=1, source_target_pairs={{0,12},{1,13},{2,14},{3,15},{4,8},{5,9},{6,10},{7,11},{8,4},{9,5},... | collective-permute-start | bytes 12296 | tf_op jit(solution)/shard_map/ppermute | solution.py:21
  34.3 5.9 %collective-permute-start.6 = (bf16[1,112,128]{2,1,0:T(8,128)(2,1)S(1)}, bf16[1,112,128]{2,1,0:T(8,128)(2,1)S(1)}, u32[]{:S(2)}, u32[]{:S(2)}) collective-permute-start(bf16[1,112,128]{2,1,0:T(8,128)(2,1)S(1)} %get-tuple-element.85), channel_id=1, source_target_pairs={{0,12},{1,13},{2,14},{3,15},{4,8},{5,9},{6,10},{7,11},{8,4},{9,5},... | collective-permute-start | bytes 86024 | tf_op jit(solution)/shard_map/ppermute | solution.py:21
  36.9 5.4 %collective-permute-start.4 = (bf16[1,112,128]{2,1,0:T(8,128)(2,1)S(1)}, bf16[1,112,128]{2,1,0:T(8,128)(2,1)S(1)}, u32[]{:S(2)}, u32[]{:S(2)}) collective-permute-start(bf16[1,112,128]{2,1,0:T(8,128)(2,1)S(1)} %get-tuple-element.86), channel_id=1, source_target_pairs={{0,4},{1,5},{2,6},{3,7},{4,0},{5,1},{6,2},{7,3},{8,12},{9,13},{10,... | collective-permute-start | bytes 86024 | tf_op jit(solution)/shard_map/ppermute | solution.py:21
  38.0 5.1 %collective-permute-start.2 = (bf16[1,112,128]{2,1,0:T(8,128)(2,1)S(1)}, bf16[1,112,128]{2,1,0:T(8,128)(2,1)S(1)}, u32[]{:S(2)}, u32[]{:S(2)}) collective-permute-start(bf16[1,112,128]{2,1,0:T(8,128)(2,1)S(1)} %get-tuple-element.87), channel_id=1, source_target_pairs={{0,3},{1,2},{2,1},{3,0},{4,7},{5,6},{6,5},{7,4},{8,11},{9,10},{10,... | collective-permute-start | bytes 86024 | tf_op jit(solution)/shard_map/ppermute | solution.py:21
  40.2 4.0 %collective-permute-start = (bf16[1,112,128]{2,1,0:T(8,128)(2,1)S(1)}, bf16[1,112,128]{2,1,0:T(8,128)(2,1)S(1)}, u32[]{:S(2)}, u32[]{:S(2)}) collective-permute-start(bf16[1,112,128]{2,1,0:T(8,128)(2,1)S(1)} %get-tuple-element.88), channel_id=1, source_target_pairs={{0,1},{1,0},{2,3},{3,2},{4,5},{5,4},{6,7},{7,6},{8,9},{9,8},{10,11... | collective-permute-start | bytes 86024 | tf_op jit(solution)/shard_map/ppermute | solution.py:21
  40.2 20.0 %collective-permute-start.7 = (bf16[2,112,128]{2,1,0:T(8,128)(2,1)S(1)}, bf16[2,112,128]{2,1,0:T(8,128)(2,1)S(1)}, u32[]{:S(2)}, u32[]{:S(2)}) collective-permute-start(bf16[2,112,128]{2,1,0:T(8,128)(2,1)S(1)} %pad_maximum_fusion.12), channel_id=1, source_target_pairs={{0,1},{1,0},{2,3},{3,2},{4,5},{5,4},{6,7},{7,6},{8,9},{9,8},{10,11... | collective-permute-start | bytes 172040 | tf_op jit(solution)/shard_map/ppermute | solution.py:21
  42.3 17.9 %collective-permute-start.5 = (bf16[2,112,128]{2,1,0:T(8,128)(2,1)S(1)}, bf16[2,112,128]{2,1,0:T(8,128)(2,1)S(1)}, u32[]{:S(2)}, u32[]{:S(2)}) collective-permute-start(bf16[2,112,128]{2,1,0:T(8,128)(2,1)S(1)} %pad_maximum_fusion.11), channel_id=1, source_target_pairs={{0,12},{1,13},{2,14},{3,15},{4,8},{5,9},{6,10},{7,11},{8,4},{9,5},... | collective-permute-start | bytes 172040 | tf_op jit(solution)/shard_map/ppermute | solution.py:21
  43.1 17.1 %collective-permute-start.3 = (bf16[2,112,128]{2,1,0:T(8,128)(2,1)S(1)}, bf16[2,112,128]{2,1,0:T(8,128)(2,1)S(1)}, u32[]{:S(2)}, u32[]{:S(2)}) collective-permute-start(bf16[2,112,128]{2,1,0:T(8,128)(2,1)S(1)} %pad_maximum_fusion.10), channel_id=1, source_target_pairs={{0,4},{1,5},{2,6},{3,7},{4,0},{5,1},{6,2},{7,3},{8,12},{9,13},{10,... | collective-permute-start | bytes 172040 | tf_op jit(solution)/shard_map/ppermute | solution.py:21
  44.2 16.0 %collective-permute-start.1 = (bf16[2,112,128]{2,1,0:T(8,128)(2,1)S(1)}, bf16[2,112,128]{2,1,0:T(8,128)(2,1)S(1)}, u32[]{:S(2)}, u32[]{:S(2)}) collective-permute-start(bf16[2,112,128]{2,1,0:T(8,128)(2,1)S(1)} %pad_maximum_fusion.9), channel_id=1, source_target_pairs={{0,3},{1,2},{2,1},{3,0},{4,7},{5,6},{6,5},{7,4},{8,11},{9,10},{10,... | collective-permute-start | bytes 172040 | tf_op jit(solution)/shard_map/ppermute | solution.py:21
  60.9 12.4 %collective-permute-start.11 = (bf16[4,112,128]{2,1,0:T(8,128)(2,1)}, bf16[4,112,128]{2,1,0:T(8,128)(2,1)}, u32[]{:S(2)}, u32[]{:S(2)}) collective-permute-start(bf16[4,112,128]{2,1,0:T(8,128)(2,1)} %pad_maximum_fusion.8), channel_id=1, source_target_pairs={{0,3},{1,2},{2,1},{3,0},{4,7},{5,6},{6,5},{7,4},{8,11},{9,10},{10,... | collective-permute-start | bytes 344072 | tf_op jit(solution)/shard_map/ppermute | solution.py:21
  63.0 10.3 %collective-permute-start.10 = (bf16[4,112,128]{2,1,0:T(8,128)(2,1)}, bf16[4,112,128]{2,1,0:T(8,128)(2,1)}, u32[]{:S(2)}, u32[]{:S(2)}) collective-permute-start(bf16[4,112,128]{2,1,0:T(8,128)(2,1)} %pad_maximum_fusion.7), channel_id=1, source_target_pairs={{0,1},{1,0},{2,3},{3,2},{4,5},{5,4},{6,7},{7,6},{8,9},{9,8},{10,11... | collective-permute-start | bytes 344072 | tf_op jit(solution)/shard_map/ppermute | solution.py:21
  63.7 9.6 %collective-permute-start.9 = (bf16[4,112,128]{2,1,0:T(8,128)(2,1)}, bf16[4,112,128]{2,1,0:T(8,128)(2,1)}, u32[]{:S(2)}, u32[]{:S(2)}) collective-permute-start(bf16[4,112,128]{2,1,0:T(8,128)(2,1)} %pad_maximum_fusion.6), channel_id=1, source_target_pairs={{0,12},{1,13},{2,14},{3,15},{4,8},{5,9},{6,10},{7,11},{8,4},{9,5},... | collective-permute-start | bytes 344072 | tf_op jit(solution)/shard_map/ppermute | solution.py:21
  66.6 7.5 %collective-permute-start.8 = (bf16[4,112,128]{2,1,0:T(8,128)(2,1)}, bf16[4,112,128]{2,1,0:T(8,128)(2,1)}, u32[]{:S(2)}, u32[]{:S(2)}) collective-permute-start(bf16[4,112,128]{2,1,0:T(8,128)(2,1)} %pad_maximum_fusion.5), channel_id=1, source_target_pairs={{0,4},{1,5},{2,6},{3,7},{4,0},{5,1},{6,2},{7,3},{8,12},{9,13},{10,... | collective-permute-start | bytes 344072 | tf_op jit(solution)/shard_map/ppermute | solution.py:21
  75.0 12.0 %collective-permute-start.15 = (bf16[8,112,128]{2,1,0:T(8,128)(2,1)S(1)}, bf16[8,112,128]{2,1,0:T(8,128)(2,1)S(1)}, u32[]{:S(2)}, u32[]{:S(2)}) collective-permute-start(bf16[8,112,128]{2,1,0:T(8,128)(2,1)S(1)} %pad_maximum_fusion.4), channel_id=1, source_target_pairs={{0,4},{1,5},{2,6},{3,7},{4,0},{5,1},{6,2},{7,3},{8,12},{9,13},{10,... | collective-permute-start | bytes 688136 | tf_op jit(solution)/shard_map/ppermute | solution.py:21
  76.8 18.3 %copy-start.2 = (f32[7168,1]{1,0:T(8,128)S(1)}, f32[7168,1]{1,0:T(8,128)}, u32[]{:S(2)}) copy-start(f32[7168,1]{1,0:T(8,128)} %copy.41.gain_ref) | copy-start | bytes 86020
  76.8 13.1 %collective-permute-start.14 = (bf16[8,112,128]{2,1,0:T(8,128)(2,1)S(1)}, bf16[8,112,128]{2,1,0:T(8,128)(2,1)S(1)}, u32[]{:S(2)}, u32[]{:S(2)}) collective-permute-start(bf16[8,112,128]{2,1,0:T(8,128)(2,1)S(1)} %pad_maximum_fusion.3), channel_id=1, source_target_pairs={{0,3},{1,2},{2,1},{3,0},{4,7},{5,6},{6,5},{7,4},{8,11},{9,10},{10,... | collective-permute-start | bytes 688136 | tf_op jit(solution)/shard_map/ppermute | solution.py:21
  79.1 12.0 %collective-permute-start.13 = (bf16[8,112,128]{2,1,0:T(8,128)(2,1)S(1)}, bf16[8,112,128]{2,1,0:T(8,128)(2,1)S(1)}, u32[]{:S(2)}, u32[]{:S(2)}) collective-permute-start(bf16[8,112,128]{2,1,0:T(8,128)(2,1)S(1)} %pad_maximum_fusion.2), channel_id=1, source_target_pairs={{0,1},{1,0},{2,3},{3,2},{4,5},{5,4},{6,7},{7,6},{8,9},{9,8},{10,11... | collective-permute-start | bytes 688136 | tf_op jit(solution)/shard_map/ppermute | solution.py:21
  81.9 13.1 %collective-permute-start.12 = (bf16[8,112,128]{2,1,0:T(8,128)(2,1)S(1)}, bf16[8,112,128]{2,1,0:T(8,128)(2,1)S(1)}, u32[]{:S(2)}, u32[]{:S(2)}) collective-permute-start(bf16[8,112,128]{2,1,0:T(8,128)(2,1)S(1)} %pad_maximum_fusion.1), channel_id=1, source_target_pairs={{0,12},{1,13},{2,14},{3,15},{4,8},{5,9},{6,10},{7,11},{8,4},{9,5},... | collective-permute-start | bytes 688136 | tf_op jit(solution)/shard_map/ppermute | solution.py:21
  99.3 7.7 %copy-start.6 = (bf16[1,256,7168]{2,1,0:T(8,128)(2,1)S(1)}, bf16[1,256,7168]{2,1,0:T(8,128)(2,1)}, u32[]{:S(2)}) copy-start(bf16[1,256,7168]{2,1,0:T(8,128)(2,1)} %param.18) | copy-start | bytes 11010052
  120.7 13.3 %copy-start = (bf16[7168,256]{1,0:T(8,128)(2,1)S(1)}, bf16[7168,256]{1,0:T(8,128)(2,1)}, u32[]{:S(2)}) copy-start(bf16[7168,256]{1,0:T(8,128)(2,1)} %copy.40) | copy-start | bytes 11010052
  139.4 46.1 %collective-permute-start.20 = (bf16[8,448,256]{2,1,0:T(8,128)(2,1)}, bf16[8,448,256]{2,1,0:T(8,128)(2,1)}, u32[]{:S(2)}, u32[]{:S(2)}) collective-permute-start(bf16[8,448,256]{2,1,0:T(8,128)(2,1)} %get-tuple-element.51), channel_id=1, source_target_pairs={{0,1},{1,0},{2,3},{3,2},{4,5},{5,4},{6,7},{7,6},{8,9},{9,8},{10,11... | collective-permute-start | bytes 5505032 | tf_op jit(solution)/shard_map/ppermute | solution.py:21
  140.9 49.5 %collective-permute-start.24 = (bf16[8,448,256]{2,1,0:T(8,128)(2,1)}, bf16[8,448,256]{2,1,0:T(8,128)(2,1)}, u32[]{:S(2)}, u32[]{:S(2)}) collective-permute-start(bf16[8,448,256]{2,1,0:T(8,128)(2,1)} %get-tuple-element.53), channel_id=1, source_target_pairs={{0,3},{1,2},{2,1},{3,0},{4,7},{5,6},{6,5},{7,4},{8,11},{9,10},{10,... | collective-permute-start | bytes 5505032 | tf_op jit(solution)/shard_map/ppermute | solution.py:21
  148.4 49.5 %collective-permute-start.28 = (bf16[8,448,256]{2,1,0:T(8,128)(2,1)}, bf16[8,448,256]{2,1,0:T(8,128)(2,1)}, u32[]{:S(2)}, u32[]{:S(2)}) collective-permute-start(bf16[8,448,256]{2,1,0:T(8,128)(2,1)} %get-tuple-element.55), channel_id=1, source_target_pairs={{0,4},{1,5},{2,6},{3,7},{4,0},{5,1},{6,2},{7,3},{8,12},{9,13},{10,... | collective-permute-start | bytes 5505032 | tf_op jit(solution)/shard_map/ppermute | solution.py:21
  148.6 52.4 %collective-permute-start.32 = (bf16[8,448,256]{2,1,0:T(8,128)(2,1)}, bf16[8,448,256]{2,1,0:T(8,128)(2,1)}, u32[]{:S(2)}, u32[]{:S(2)}) collective-permute-start(bf16[8,448,256]{2,1,0:T(8,128)(2,1)} %get-tuple-element.57), channel_id=1, source_target_pairs={{0,12},{1,13},{2,14},{3,15},{4,8},{5,9},{6,10},{7,11},{8,4},{9,5},... | collective-permute-start | bytes 5505032 | tf_op jit(solution)/shard_map/ppermute | solution.py:21
  187.4 25.1 %collective-permute-start.21 = (bf16[4,448,256]{2,1,0:T(8,128)(2,1)S(1)}, bf16[4,448,256]{2,1,0:T(8,128)(2,1)S(1)}, u32[]{:S(2)}, u32[]{:S(2)}) collective-permute-start(bf16[4,448,256]{2,1,0:T(8,128)(2,1)S(1)} %get-tuple-element.66), channel_id=1, source_target_pairs={{0,3},{1,2},{2,1},{3,0},{4,7},{5,6},{6,5},{7,4},{8,11},{9,10},{10,... | collective-permute-start | bytes 2752520 | tf_op jit(solution)/shard_map/ppermute | solution.py:21
  192.2 26.9 %collective-permute-start.25 = (bf16[4,448,256]{2,1,0:T(8,128)(2,1)S(1)}, bf16[4,448,256]{2,1,0:T(8,128)(2,1)S(1)}, u32[]{:S(2)}, u32[]{:S(2)}) collective-permute-start(bf16[4,448,256]{2,1,0:T(8,128)(2,1)S(1)} %get-tuple-element.68), channel_id=1, source_target_pairs={{0,4},{1,5},{2,6},{3,7},{4,0},{5,1},{6,2},{7,3},{8,12},{9,13},{10,... | collective-permute-start | bytes 2752520 | tf_op jit(solution)/shard_map/ppermute | solution.py:21
  199.8 22.8 %collective-permute-start.29 = (bf16[4,448,256]{2,1,0:T(8,128)(2,1)S(1)}, bf16[4,448,256]{2,1,0:T(8,128)(2,1)S(1)}, u32[]{:S(2)}, u32[]{:S(2)}) collective-permute-start(bf16[4,448,256]{2,1,0:T(8,128)(2,1)S(1)} %get-tuple-element.70), channel_id=1, source_target_pairs={{0,12},{1,13},{2,14},{3,15},{4,8},{5,9},{6,10},{7,11},{8,4},{9,5},... | collective-permute-start | bytes 2752520 | tf_op jit(solution)/shard_map/ppermute | solution.py:21
  202.9 22.3 %collective-permute-start.33 = (bf16[4,448,256]{2,1,0:T(8,128)(2,1)S(1)}, bf16[4,448,256]{2,1,0:T(8,128)(2,1)S(1)}, u32[]{:S(2)}, u32[]{:S(2)}) collective-permute-start(bf16[4,448,256]{2,1,0:T(8,128)(2,1)S(1)} %get-tuple-element.72), channel_id=1, source_target_pairs={{0,1},{1,0},{2,3},{3,2},{4,5},{5,4},{6,7},{7,6},{8,9},{9,8},{10,11... | collective-permute-start | bytes 2752520 | tf_op jit(solution)/shard_map/ppermute | solution.py:21
  212.8 15.7 %collective-permute-start.22 = (bf16[2,448,256]{2,1,0:T(8,128)(2,1)S(1)}, bf16[2,448,256]{2,1,0:T(8,128)(2,1)S(1)}, u32[]{:S(2)}, u32[]{:S(2)}) collective-permute-start(bf16[2,448,256]{2,1,0:T(8,128)(2,1)S(1)} %get-tuple-element.74), channel_id=1, source_target_pairs={{0,4},{1,5},{2,6},{3,7},{4,0},{5,1},{6,2},{7,3},{8,12},{9,13},{10,... | collective-permute-start | bytes 1376264 | tf_op jit(solution)/shard_map/ppermute | solution.py:21
  219.4 13.5 %collective-permute-start.26 = (bf16[2,448,256]{2,1,0:T(8,128)(2,1)S(1)}, bf16[2,448,256]{2,1,0:T(8,128)(2,1)S(1)}, u32[]{:S(2)}, u32[]{:S(2)}) collective-permute-start(bf16[2,448,256]{2,1,0:T(8,128)(2,1)S(1)} %get-tuple-element.76), channel_id=1, source_target_pairs={{0,12},{1,13},{2,14},{3,15},{4,8},{5,9},{6,10},{7,11},{8,4},{9,5},... | collective-permute-start | bytes 1376264 | tf_op jit(solution)/shard_map/ppermute | solution.py:21
  222.8 11.0 %collective-permute-start.30 = (bf16[2,448,256]{2,1,0:T(8,128)(2,1)S(1)}, bf16[2,448,256]{2,1,0:T(8,128)(2,1)S(1)}, u32[]{:S(2)}, u32[]{:S(2)}) collective-permute-start(bf16[2,448,256]{2,1,0:T(8,128)(2,1)S(1)} %get-tuple-element.78), channel_id=1, source_target_pairs={{0,1},{1,0},{2,3},{3,2},{4,5},{5,4},{6,7},{7,6},{8,9},{9,8},{10,11... | collective-permute-start | bytes 1376264 | tf_op jit(solution)/shard_map/ppermute | solution.py:21
  226.2 14.7 %collective-permute-start.34 = (bf16[2,448,256]{2,1,0:T(8,128)(2,1)}, bf16[2,448,256]{2,1,0:T(8,128)(2,1)S(1)}, u32[]{:S(2)}, u32[]{:S(2)}) collective-permute-start(bf16[2,448,256]{2,1,0:T(8,128)(2,1)} %get-tuple-element.79), channel_id=1, source_target_pairs={{0,3},{1,2},{2,1},{3,0},{4,7},{5,6},{6,5},{7,4},{8,11},{9,10},{10,... | collective-permute-start | bytes 1376264 | tf_op jit(solution)/shard_map/ppermute | solution.py:21
  228.5 8.2 %collective-permute-start.23 = (bf16[1,448,256]{2,1,0:T(8,128)(2,1)S(1)}, bf16[1,448,256]{2,1,0:T(8,128)(2,1)S(1)}, u32[]{:S(2)}, u32[]{:S(2)}) collective-permute-start(bf16[1,448,256]{2,1,0:T(8,128)(2,1)S(1)} %add_convert_fusion.22), channel_id=1, source_target_pairs={{0,12},{1,13},{2,14},{3,15},{4,8},{5,9},{6,10},{7,11},{8,4},{9,5},... | collective-permute-start | bytes 688136 | tf_op jit(solution)/shard_map/ppermute | solution.py:21
  232.9 6.1 %collective-permute-start.27 = (bf16[1,448,256]{2,1,0:T(8,128)(2,1)S(1)}, bf16[1,448,256]{2,1,0:T(8,128)(2,1)S(1)}, u32[]{:S(2)}, u32[]{:S(2)}) collective-permute-start(bf16[1,448,256]{2,1,0:T(8,128)(2,1)S(1)} %add_convert_fusion.20), channel_id=1, source_target_pairs={{0,1},{1,0},{2,3},{3,2},{4,5},{5,4},{6,7},{7,6},{8,9},{9,8},{10,11... | collective-permute-start | bytes 688136 | tf_op jit(solution)/shard_map/ppermute | solution.py:21
  233.8 2.9 %copy-start.7 = (bf16[2,448,256]{2,1,0:T(8,128)(2,1)}, bf16[2,448,256]{2,1,0:T(8,128)(2,1)S(1)}, u32[]{:S(2)}) copy-start(bf16[2,448,256]{2,1,0:T(8,128)(2,1)S(1)} %collective-permute-done.30) | copy-start | bytes 1376260
  234.7 7.5 %collective-permute-start.31 = (bf16[1,448,256]{2,1,0:T(8,128)(2,1)}, bf16[1,448,256]{2,1,0:T(8,128)(2,1)}, u32[]{:S(2)}, u32[]{:S(2)}) collective-permute-start(bf16[1,448,256]{2,1,0:T(8,128)(2,1)} %add_convert_fusion.18), channel_id=1, source_target_pairs={{0,3},{1,2},{2,1},{3,0},{4,7},{5,6},{6,5},{7,4},{8,11},{9,10},{10,... | collective-permute-start | bytes 688136 | tf_op jit(solution)/shard_map/ppermute | solution.py:21
  241.7 6.3 %collective-permute-start.35 = (bf16[1,448,256]{2,1,0:T(8,128)(2,1)}, bf16[1,448,256]{2,1,0:T(8,128)(2,1)}, u32[]{:S(2)}, u32[]{:S(2)}) collective-permute-start(bf16[1,448,256]{2,1,0:T(8,128)(2,1)} %add_convert_fusion.16), channel_id=1, source_target_pairs={{0,4},{1,5},{2,6},{3,7},{4,0},{5,1},{6,2},{7,3},{8,12},{9,13},{10,... | collective-permute-start | bytes 688136 | tf_op jit(solution)/shard_map/ppermute | solution.py:21
  243.3 10.9 %all-to-all-start.1 = ((bf16[8,16,448]{2,1,0:T(8,128)(2,1)}), bf16[8,16,448]{2,1,0:T(8,128)(2,1)}, u32[]{:S(2)}, u32[]{:S(2)}) async-start(bf16[8,16,448]{2,1,0:T(8,128)(2,1)} %bitcast.21), calls=%async_computation.1 | async-start | bytes 262144 | tf_op jit(solution)/shard_map/all_to_all | solution.py:262
  (4 other events, 7.1 us)
Sparse Core Ops, SparseCore 0:
  9.5 111.1 all-gather.1
  152.8 75.5 reduce-scatter.3

commit v7 on v6

--- a/solution.py
+++ b/solution.py
@@ -41,19 +41,16 @@
 
 
 def send_kernel(first, slice_ref, gate_up_ref, scale_ref, turned_ref, hidden_ref, *outs):
-    step = pl.program_id(0)
-
-    @pl.when(step == 0)
-    def _():
-        half = gate_up_ref.shape[0] // 2
-        scale = scale_ref[...]
-        hidden_ref[...] = (silu(gate_up_ref[:half] * scale) * (gate_up_ref[half:] * scale)).astype(jnp.bfloat16)
-
+    half = gate_up_ref.shape[0] // 2
     columns = outs[0].shape[-1]
     for i, out in enumerate(outs):
-        at = slice_ref[stream_mask(first + i, 1, step)]
-        hidden = hidden_ref[:, i * columns : (i + 1) * columns]
-        out[0] = jnp.dot(turned_ref[at], hidden, preferred_element_type=jnp.float32).astype(jnp.bfloat16)
+        here = slice((first + i) * columns, (first + i + 1) * columns)
+        scale = scale_ref[:, here]
+        hidden = (silu(gate_up_ref[:half, here] * scale) * (gate_up_ref[half:, here] * scale)).astype(jnp.bfloat16)
+        hidden_ref[:, i * columns : (i + 1) * columns] = hidden
+        for j in range(out.shape[0]):
+            at = slice_ref[stream_mask(first + i, 1, j)]
+            out[j] = jnp.dot(turned_ref[at], hidden, preferred_element_type=jnp.float32).astype(jnp.bfloat16)
 
 
 def stream_mask(s, sent, j):
@@ -65,20 +62,11 @@
     both = gate_up.shape[0]
     columns = gate_up.shape[1] // 4
     blocks, slice_rows, deep = turned.shape
-    pair = first // 2
+    in_vmem = pl.BlockSpec(memory_space=pltpu.VMEM)
     return pl.pallas_call(
         functools.partial(send_kernel, first),
-        grid_spec=pltpu.PrefetchScalarGridSpec(
-            num_scalar_prefetch=1,
-            grid=(blocks // 2,),
-            in_specs=[
-                pl.BlockSpec((both, 2 * columns), lambda j, at: (0, pair)),
-                pl.BlockSpec((1, 2 * columns), lambda j, at: (0, pair)),
-                pl.BlockSpec(memory_space=pltpu.VMEM),
-            ],
-            out_specs=[pl.BlockSpec((deep, 2 * columns), lambda j, at: (0, 0))]
-            + [pl.BlockSpec((1, slice_rows, columns), lambda j, at: (j, 0, 0))] * 2,
-        ),
+        in_specs=[pl.BlockSpec(memory_space=pltpu.SMEM), in_vmem, in_vmem, in_vmem],
+        out_specs=[in_vmem] * 3,
         out_shape=[jax.ShapeDtypeStruct((deep, 2 * columns), jnp.bfloat16)]
         + [jax.ShapeDtypeStruct((blocks // 2, slice_rows, columns), jnp.bfloat16)] * 2,
         compiler_params=pltpu.CompilerParams(vmem_limit_bytes=24 << 20),
@@ -180,8 +168,28 @@
     )(slice_of, *pooled, gate_weight, up_weight, gain_column)
 
 
-def add_pair(kept, got):
-    return (kept.astype(jnp.float32) + got.astype(jnp.float32)).astype(jnp.bfloat16)
+def expert_down_kernel(weight_ref, hidden_ref, out_ref):
+    out_ref[...] = transposed_dot(weight_ref[0], hidden_ref[...]).astype(jnp.bfloat16)
+
+
+def expert_down_parts(weight, hidden):
+    _, deep, features = weight.shape
+    columns = hidden.shape[1]
+    wide = features // 4
+    return pl.pallas_call(
+        expert_down_kernel,
+        grid=(features // wide,),
+        in_specs=[
+            pl.BlockSpec((1, deep, wide), lambda m: (0, 0, m)),
+            pl.BlockSpec((deep, columns), lambda m: (0, 0)),
+        ],
+        out_specs=pl.BlockSpec((wide, columns), lambda m: (m, 0)),
+        out_shape=jax.ShapeDtypeStruct((features, columns), jnp.bfloat16),
+        compiler_params=pltpu.CompilerParams(vmem_limit_bytes=24 << 20),
+        cost_estimate=pl.CostEstimate(
+            flops=2 * features * deep * columns, bytes_accessed=2 * features * (deep + columns), transcendentals=0
+        ),
+    )(weight, hidden)
 
 
 def shards(
@@ -242,7 +250,7 @@
     scale = lax.rsqrt(square_sum / width + EPSILON)
 
     expert_hidden = expert_gate_up(slice_of, pooled, expert_gate, expert_up, gain_column)
-    expert_partial = transposed_dot(expert_down[0], expert_hidden).astype(jnp.bfloat16)
+    expert_partial = expert_down_parts(expert_down, expert_hidden)
     expert_partial, scale, whole_columns = lax.optimization_barrier((expert_partial, scale, whole_columns))
     expert_out = lax.psum_scatter(expert_partial, "local", scatter_dimension=0, tiled=True)
 
@@ -252,23 +260,27 @@
     sent += more
     arrived = [flip_local(sent[s], STREAMS[s][0]) for s in range(4)]
     sums = kept_parts(slice_of, turned, (low_hidden, high_hidden))
+    terms = [[sums[s], arrived[s]] for s in range(4)]
+
+    def added(s, low, high):
+        return sum(term[low:high].astype(jnp.float32) for term in terms[s])
+
     for step in (1, 2, 3):
-        half = sums[0].shape[0] // 2
-        came = [flip_local(add_pair(sums[s][half:], arrived[s][half:]), STREAMS[s][step]) for s in range(4)]
-        sums = [add_pair(sums[s][:half], arrived[s][:half]) for s in range(4)]
-        arrived = came
+        half = 8 >> step
+        for s in range(4):
+            terms[s].append(flip_local(added(s, half, 2 * half).astype(jnp.bfloat16), STREAMS[s][step]))
+        if step == 1:
+            terms[3][-1], expert_out = lax.optimization_barrier((terms[3][-1], expert_out))
+            returned = lax.all_to_all(
+                expert_out.T.reshape(node_count, NODE_CAP, slice_width), "node", split_axis=0, concat_axis=0, tiled=True
+            ).reshape(slot_count, slice_width)
+            route_term = (slot_gate[:, None] * returned.astype(jnp.float32)).astype(jnp.bfloat16)
         if step == 2:
-            arrived[3], expert_out = lax.optimization_barrier((arrived[3], expert_out))
-    returned = lax.all_to_all(
-        expert_out.T.reshape(node_count, NODE_CAP, slice_width), "node", split_axis=0, concat_axis=0, tiled=True
-    ).reshape(slot_count, slice_width)
-    route_term = (slot_gate[:, None] * returned.astype(jnp.float32)).astype(jnp.bfloat16)
+            terms[3][-1], route_term = lax.optimization_barrier((terms[3][-1], route_term))
     expert_part = lax.dot_general(
         route_term, chosen, (((0,), (1,)), ((), ())), preferred_element_type=jnp.float32
     )
-    dense_part = jnp.concatenate(
-        [sums[s][0].astype(jnp.float32) + arrived[s][0].astype(jnp.float32) for s in range(4)], axis=1
-    )
+    dense_part = jnp.concatenate([added(s, 0, 1)[0] for s in range(4)], axis=1)
     return (columns.astype(jnp.float32) + dense_part + expert_part).astype(jnp.bfloat16).T
 
 

time: 265 us -> 277 us (1.045)
  other arithmetic: 38.4 us -> 50.1 us
  waiting for transfers between devices: 88.5 us -> 91.8 us
    ppermute x36, waiting for transfers between devices: 69.4 us -> 80.2 us  [flip_local(): lax.ppermute(array, 'local', [(i, LOCAL_AT[LOCAL_LABEL[i] ^ 1 << bit]) fo...]
    convert_element_type x12 -> x13, other arithmetic: 11.1 us -> 18.3 us  [the longest x12 18.3 us: shards(): added(s, half, 2 * half).astype(jnp.bfloat16)]
    squeeze x0 -> x4, other arithmetic: none -> 6.76 us  [shards(): dense_part = jnp.concatenate([added(s, 0, 1)[0] for s in range(4)], axis=1)]
    all_to_all x1, waiting for transfers between devices: 5.08 us -> 0.01 us  [shards(): lax.all_to_all(expert_out.T.reshape(node_count, NODE_CAP, slice_width), '...]
    ppermute x36, starting transfers between devices: 48 us -> 50.9 us  [flip_local(): lax.ppermute(array, 'local', [(i, LOCAL_AT[LOCAL_LABEL[i] ^ 1 << bit]) fo...]
    unnamed x37 -> x50, local copies, waits for them, and re-layouts: 12.6 us -> 10.3 us
    pallas_call x2 -> x3, Pallas kernels: 10.8 us -> 9.32 us  [the longest x2 6.2 us: sent_parts(): pl.pallas_call(functools.partial(send_kernel, first), in_specs=[pl.BlockS...]
    dot_general x2 -> x1, matrix products: 14 us -> 13.3 us  [transposed_dot(): lax.dot_general(weight, rows, (((0,), (0,)), ((), ())), preferred_element...]
  transfers between devices with their start and end apart: 40 -> 40, of which waited for: 22 -> 16; matrix products, arithmetic and copies ran while one was open for 23% -> 24% of each run, Pallas kernels for 6% -> 6%
where the time goes in v7:
time: 277 us; the launch traced here: 276 us
  waiting for transfers between devices  91.8 us (33%)
  starting transfers between devices  59.5 us (21%)
  other arithmetic  50.1 us (18%)
  local copies, waits for them, and re-layouts  24.5 us (9%)
  Pallas kernels  20.8 us (8%)
  matrix products  15.1 us (5%)
  between operations  13.9 us (5%)
    ppermute x36, waiting for transfers between devices, flip_local(): lax.ppermute(array, 'local', [(i, LOCAL_AT[LOCAL_LABEL[i] ^ 1 << bit]) fo...  80.2 us
    ppermute x36, starting transfers between devices, flip_local(): lax.ppermute(array, 'local', [(i, LOCAL_AT[LOCAL_LABEL[i] ^ 1 << bit]) fo...  50.9 us
    convert_element_type x12, other arithmetic, shards(): added(s, half, 2 * half).astype(jnp.bfloat16)  18.3 us
    dot_general x1, matrix products, transposed_dot(): lax.dot_general(weight, rows, (((0,), (0,)), ((), ())), preferred_element...  13.3 us
    all_gather x1, waiting for transfers between devices, shards(): whole_columns = lax.all_gather(columns, 'local', axis=0, tiled=True)  10.7 us
    unnamed x50, local copies, waits for them, and re-layouts  10.3 us
    pallas_call x1, Pallas kernels, expert_gate_up(): pl.pallas_call(functools.partial(expert_kernel, blocks, blocks * rows), g...  7.67 us
    convert_element_type x1, other arithmetic, shards(): (w.astype(jnp.float32) * gain_column).astype(jnp.bfloat16)  7.04 us
  transfers between devices with their start and end apart: 40, of which 16 were waited for; matrix products, arithmetic and copies ran while one was open for 24% of the time, Pallas kernels for 6%

profile of v7, /device:TPU:0, one launch (start us, length us, event | category | flops | bytes accessed | tf_op | source)
XLA Modules:
  0.0 275.6 jit_solution(6201280032757323791)
XLA Ops:
  8.7 1.7 collective-permute-start.16
  11.2 2.3 reduce-window.6
  15.7 2.3 collective-permute-start.17
  18.8 1.9 collective-permute-done.17
  20.6 1.9 collective-permute-start.18
  23.7 4.3 %all-to-all-start = ((bf16[8,16,448]{2,1,0:T(8,128)(2,1)}), bf16[8,16,448]{2,1,0:T(8,128)(2,1)S(1)}, u32[]{:S(2)}, u32[]{:S(2)}) async-start(bf16[8,16,448]{2,1,0:T(8,128)(2,1)} %bitcast.3), calls=%async_computation | async-start | bytes 262144 | tf_op jit(solution)/shard_map/all_to_all | solution.py:226
  28.1 2.6 collective-permute-start.19
  31.4 2.5 copy.33.gain_ref
  34.3 2.6 collective-permute-start.6
  38.0 2.2 collective-permute-start.2
  40.2 2.1 collective-permute-start.7
  44.2 2.3 collective-permute-start.1
  46.5 7.0 %multiply_convert_fusion.1 = (bf16[7168,256]{1,0:T(8,128)(2,1)}, bf16[7168,256]{1,0:T(8,128)(2,1)}) fusion(bf16[7168,256]{1,0:T(8,128)(2,1)} %param.13, f32[7168]{0:T(1024)S(1)} %copy-done.16, bf16[7168,256]{1,0:T(8,128)(2,1)} %param.14), kind=kLoop, calls=%fused_computation.2 | loop fusion | flops 11010048 | bytes 14708736 | tf_op jit(solution)/shard_map/convert_element_type | solution.py:242
  53.5 6.6 %pad_maximum_fusion = bf16[7168,512]{1,0:T(8,128)(2,1)} fusion(bf16[7168,256]{1,0:T(8,128)(2,1)} %get-tuple-element.78, bf16[7168,256]{1,0:T(8,128)(2,1)} %get-tuple-element.77), kind=kLoop, calls=%fused_computation | loop fusion | flops 14680064 | bytes 14680064 | tf_op jit(solution)/shard_map/concatenate | solution.py:241
  63.6 2.2 collective-permute-start.9
  67.3 6.0 %copy.32 = bf16[7168,256]{1,0:T(8,128)(2,1)} copy(bf16[7168,256]{0,1:T(8,128)(2,1)} %bitcast.67) | data formatting | bytes 7340032 | tf_op jit(solution)/shard_map/transpose | solution.py:247
  79.1 1.9 collective-permute-start.13
  87.0 2.9 %collective-permute-done.14 = bf16[8,112,128]{2,1,0:T(8,128)(2,1)S(1)} collective-permute-done((bf16[8,112,128]{2,1,0:T(8,128)(2,1)S(1)}, bf16[8,112,128]{2,1,0:T(8,128)(2,1)S(1)}, u32[]{:S(2)}, u32[]{:S(2)}) %collective-permute-start.14) | collective-permute-done | bytes 229408 | tf_op jit(solution)/shard_map/ppermute | solution.py:21
  91.1 3.8 %collective-permute-done.12 = bf16[8,112,128]{2,1,0:T(8,128)(2,1)S(1)} collective-permute-done((bf16[8,112,128]{2,1,0:T(8,128)(2,1)S(1)}, bf16[8,112,128]{2,1,0:T(8,128)(2,1)S(1)}, u32[]{:S(2)}, u32[]{:S(2)}) %collective-permute-start.12) | collective-permute-done | bytes 229408 | tf_op jit(solution)/shard_map/ppermute | solution.py:21
  95.0 2.0 copy-done.3
  97.1 2.2 copy-done.4
  99.3 7.7 %shard_map.109.hidden_ref = bf16[256,128]{1,0:T(8,128)(2,1)S(1)} custom-call(s32[16]{0:T(128)S(1)} %dynamic-slice_bitcast_fusion.at_ref.slice_ref, bf16[16,112,128]{2,1,0:T(8,128)(2,1)S(1)} %constant_dynamic-update-slice_fusion.x0, bf16[16,112,128]{2,1,0:T(8,128)(2,1)S(1)} %constant_dynamic-update-slice_fusion.5.x1, ...), custom_call_target="tpu_custom_call" | custom-call | flops 939524096 | bytes 9175040 | tf_op jit(solution)/shard_map/pallas_call | solution.py:147
  107.0 3.1 %shard_map.110 = bf16[7168,128]{1,0:T(8,128)(2,1)} custom-call(bf16[1,256,7168]{2,1,0:T(8,128)(2,1)S(1)} %copy-done.5, bf16[256,128]{1,0:T(8,128)(2,1)S(1)} %shard_map.109.hidden_ref), custom_call_target="tpu_custom_call" | custom-call | flops 469762048 | bytes 5505024 | tf_op jit(solution)/shard_map/pallas_call | solution.py:179
  110.1 10.7 %all-gather.2.cloned.1.call-done = bf16[7168,1024]{1,0:T(8,128)(2,1)} async-done(((bf16[448,1024]{1,0:T(8,128)(2,1)}), bf16[7168,1024]{1,0:T(8,128)(2,1)}) %all-gather.2.cloned.1.call-update) | async-done | bytes 14680080 | tf_op jit(solution)/shard_map/all_gather | solution.py:216
  120.7 13.3 %fusion.10.gate_up_ref = f32[512,1024]{1,0:T(8,128)S(1)} fusion(bf16[7168,512]{1,0:T(8,128)(2,1)} %pad_maximum_fusion, bf16[7168,1024]{1,0:T(8,128)(2,1)} %all-gather.2.cloned.1.call-done), kind=kOutput, calls=%fused_computation.84 | convolution fusion | flops 7516192768 | bytes 24117248 | tf_op jit(solution)/shard_map/dot_general | solution.py:36
  134.1 3.2 %shard_map.111 = (bf16[256,512]{1,0:T(8,128)(2,1)S(1)}, bf16[8,448,256]{2,1,0:T(8,128)(2,1)}, bf16[8,448,256]{2,1,0:T(8,128)(2,1)}) custom-call(s32[16]{0:T(128)S(1)} %dynamic-slice_bitcast_fusion.at_ref.slice_ref, f32[512,1024]{1,0:T(8,128)S(1)} %fusion.10.gate_up_ref, f32[1,1024]{1,0:T(1,128)S(1)} %add_rsqrt_fusion.scale_ref, ...), custom_call_target="tpu_custom_call" | custom-call | flops 939524096 | bytes 7340032 | tf_op jit(solution)/shard_map/pallas_call | solution.py:66
  138.7 2.1 collective-permute-start.24
  140.8 3.0 %shard_map.112 = (bf16[256,512]{1,0:T(8,128)(2,1)S(1)}, bf16[8,448,256]{2,1,0:T(8,128)(2,1)}, bf16[8,448,256]{2,1,0:T(8,128)(2,1)}) custom-call(s32[16]{0:T(128)S(1)} %dynamic-slice_bitcast_fusion.at_ref.slice_ref, f32[512,1024]{1,0:T(8,128)S(1)} %fusion.10.gate_up_ref, f32[1,1024]{1,0:T(1,128)S(1)} %add_rsqrt_fusion.scale_ref, ...), custom_call_target="tpu_custom_call" | custom-call | flops 939524096 | bytes 7340032 | tf_op jit(solution)/shard_map/pallas_call | solution.py:66
  144.0 1.9 collective-permute-start.32
  145.9 2.0 copy-done.1
  147.9 3.8 %shard_map.113 = (bf16[8,448,256]{2,1,0:T(8,128)(2,1)S(1)}, bf16[8,448,256]{2,1,0:T(8,128)(2,1)S(1)}, bf16[8,448,256]{2,1,0:T(8,128)(2,1)S(1)}, bf16[8,448,256]{2,1,0:T(8,128)(2,1)S(1)}) custom-call(s32[16]{0:T(128)S(1)} %dynamic-slice_bitcast_fusion.at_ref.slice_ref, bf16[16,448,256]{2,1,0:T(8,128)(2,1)S(1)} %bitcast.62, ...), custom_call_target="tpu_custom_call" | custom-call | flops 1879048192 | bytes 14680064 | tf_op jit(solution)/shard_map/pallas_call | solution.py:96
  151.7 32.7 %collective-permute-done.20 = bf16[8,448,256]{2,1,0:T(8,128)(2,1)} collective-permute-done((bf16[8,448,256]{2,1,0:T(8,128)(2,1)}, bf16[8,448,256]{2,1,0:T(8,128)(2,1)}, u32[]{:S(2)}, u32[]{:S(2)}) %collective-permute-start.20) | collective-permute-done | bytes 1835040 | tf_op jit(solution)/shard_map/ppermute | solution.py:21
  185.8 2.9 %collective-permute-start.21 = (bf16[4,448,256]{2,1,0:T(8,128)(2,1)S(1)}, bf16[4,448,256]{2,1,0:T(8,128)(2,1)S(1)}, u32[]{:S(2)}, u32[]{:S(2)}) collective-permute-start(bf16[4,448,256]{2,1,0:T(8,128)(2,1)S(1)} %add_convert_fusion.3), channel_id=1, source_target_pairs={{0,3},{1,2},{2,1},{3,0},{4,7},{5,6},{6,5},{7,4},{8,11},{9,10},{10,... | collective-permute-start | bytes 2752520 | tf_op jit(solution)/shard_map/ppermute | solution.py:21
  190.4 1.6 collective-permute-done.28
  193.4 1.8 collective-permute-start.29
  196.7 12.9 %collective-permute-done.21 = bf16[4,448,256]{2,1,0:T(8,128)(2,1)S(1)} collective-permute-done((bf16[4,448,256]{2,1,0:T(8,128)(2,1)S(1)}, bf16[4,448,256]{2,1,0:T(8,128)(2,1)S(1)}, u32[]{:S(2)}, u32[]{:S(2)}) %collective-permute-start.21) | collective-permute-done | bytes 917536 | tf_op jit(solution)/shard_map/ppermute | solution.py:21
  218.1 5.8 %collective-permute-done.22 = bf16[2,448,256]{2,1,0:T(8,128)(2,1)S(1)} collective-permute-done((bf16[2,448,256]{2,1,0:T(8,128)(2,1)S(1)}, bf16[2,448,256]{2,1,0:T(8,128)(2,1)S(1)}, u32[]{:S(2)}, u32[]{:S(2)}) %collective-permute-start.22) | collective-permute-done | bytes 458784 | tf_op jit(solution)/shard_map/ppermute | solution.py:21
  225.0 2.2 collective-permute-start.23
  227.2 1.9 add_convert_fusion.10
  229.6 1.9 add_convert_fusion.9
  233.0 1.9 add_bitcast_fusion.3
  234.9 1.7 copy.34
  236.6 4.2 %all-to-all-start.1 = ((bf16[8,16,448]{2,1,0:T(8,128)(2,1)}), bf16[8,16,448]{2,1,0:T(8,128)(2,1)S(1)}, u32[]{:S(2)}, u32[]{:S(2)}) async-start(bf16[8,16,448]{2,1,0:T(8,128)(2,1)} %bitcast.18), calls=%async_computation.2 | async-start | bytes 262144 | tf_op jit(solution)/shard_map/all_to_all | solution.py:274
  240.8 2.2 add_convert_fusion.4
  243.0 1.8 collective-permute-start.34
  244.8 2.1 add_bitcast_fusion.2
  247.0 10.4 %collective-permute-done.34 = bf16[2,448,256]{2,1,0:T(8,128)(2,1)} collective-permute-done((bf16[2,448,256]{2,1,0:T(8,128)(2,1)}, bf16[2,448,256]{2,1,0:T(8,128)(2,1)}, u32[]{:S(2)}, u32[]{:S(2)}) %collective-permute-start.34) | collective-permute-done | bytes 458784 | tf_op jit(solution)/shard_map/ppermute | solution.py:21
  261.5 4.6 %collective-permute-done.35 = bf16[1,448,256]{2,1,0:T(8,128)(2,1)S(1)} collective-permute-done((bf16[1,448,256]{2,1,0:T(8,128)(2,1)S(1)}, bf16[1,448,256]{2,1,0:T(8,128)(2,1)S(1)}, u32[]{:S(2)}, u32[]{:S(2)}) %collective-permute-start.35) | collective-permute-done | bytes 229408 | tf_op jit(solution)/shard_map/ppermute | solution.py:21
  (155 shorter events, 55.1 us)
Async XLA Ops:
  6.5 114.2 %all-gather.2.cloned.1.call-start = ((), (), s32[]{:S(2)}) async-start(), calls=%async_computation.3 | async-start | bytes 15597568 | tf_op jit(solution)/shard_map/all_gather | solution.py:216
  8.7 7.1 %collective-permute-start.16 = (f32[1,1024]{1,0:T(1,128)S(1)}, f32[1,1024]{1,0:T(1,128)S(1)}, u32[]{:S(2)}, u32[]{:S(2)}) collective-permute-start(f32[1,1024]{1,0:T(1,128)S(1)} %bitcast.73), channel_id=1, source_target_pairs={{0,1},{1,0},{2,3},{3,2},{4,5},{5,4},{6,7},{7,6},{8,9},{9,8},{10,11... | collective-permute-start | bytes 12296 | tf_op jit(solution)/shard_map/ppermute | solution.py:21
  15.4 16.0 %copy-start.16 = (f32[7168]{0:T(1024)S(1)}, f32[7168]{0:T(1024)}, u32[]{:S(2)}) copy-start(f32[7168]{0:T(1024)} %param.12) | copy-start | bytes 86020
  15.7 4.9 %collective-permute-start.17 = (f32[1,1024]{1,0:T(1,128)S(1)}, f32[1,1024]{1,0:T(1,128)S(1)}, u32[]{:S(2)}, u32[]{:S(2)}) collective-permute-start(f32[1,1024]{1,0:T(1,128)S(1)} %add.156), channel_id=1, source_target_pairs={{0,3},{1,2},{2,1},{3,0},{4,7},{5,6},{6,5},{7,4},{8,11},{9,10},{10,... | collective-permute-start | bytes 12296 | tf_op jit(solution)/shard_map/ppermute | solution.py:21
  20.6 7.5 %collective-permute-start.18 = (f32[1,1024]{1,0:T(1,128)S(1)}, f32[1,1024]{1,0:T(1,128)S(1)}, u32[]{:S(2)}, u32[]{:S(2)}) collective-permute-start(f32[1,1024]{1,0:T(1,128)S(1)} %add.157), channel_id=1, source_target_pairs={{0,4},{1,5},{2,6},{3,7},{4,0},{5,1},{6,2},{7,3},{8,12},{9,13},{10,... | collective-permute-start | bytes 12296 | tf_op jit(solution)/shard_map/ppermute | solution.py:21
  23.7 10.4 %all-to-all-start = ((bf16[8,16,448]{2,1,0:T(8,128)(2,1)}), bf16[8,16,448]{2,1,0:T(8,128)(2,1)S(1)}, u32[]{:S(2)}, u32[]{:S(2)}) async-start(bf16[8,16,448]{2,1,0:T(8,128)(2,1)} %bitcast.3), calls=%async_computation | async-start | bytes 262144 | tf_op jit(solution)/shard_map/all_to_all | solution.py:226
  28.0 206.9 %reduce-scatter.2.cloned.1.call-start = ((), (), s32[]{:S(2)}) async-start(), calls=%async_computation.4 | async-start | bytes 1949696 | tf_op jit(solution)/shard_map/reduce_scatter | solution.py:255
  28.1 5.8 %collective-permute-start.19 = (f32[1,1024]{1,0:T(1,128)S(1)}, f32[1,1024]{1,0:T(1,128)S(1)}, u32[]{:S(2)}, u32[]{:S(2)}) collective-permute-start(f32[1,1024]{1,0:T(1,128)S(1)} %add.158), channel_id=1, source_target_pairs={{0,12},{1,13},{2,14},{3,15},{4,8},{5,9},{6,10},{7,11},{8,4},{9,5},... | collective-permute-start | bytes 12296 | tf_op jit(solution)/shard_map/ppermute | solution.py:21
  34.3 5.9 %collective-permute-start.6 = (bf16[1,112,128]{2,1,0:T(8,128)(2,1)S(1)}, bf16[1,112,128]{2,1,0:T(8,128)(2,1)S(1)}, u32[]{:S(2)}, u32[]{:S(2)}) collective-permute-start(bf16[1,112,128]{2,1,0:T(8,128)(2,1)S(1)} %get-tuple-element.73), channel_id=1, source_target_pairs={{0,12},{1,13},{2,14},{3,15},{4,8},{5,9},{6,10},{7,11},{8,4},{9,5},... | collective-permute-start | bytes 86024 | tf_op jit(solution)/shard_map/ppermute | solution.py:21
  36.9 5.4 %collective-permute-start.4 = (bf16[1,112,128]{2,1,0:T(8,128)(2,1)S(1)}, bf16[1,112,128]{2,1,0:T(8,128)(2,1)S(1)}, u32[]{:S(2)}, u32[]{:S(2)}) collective-permute-start(bf16[1,112,128]{2,1,0:T(8,128)(2,1)S(1)} %get-tuple-element.74), channel_id=1, source_target_pairs={{0,4},{1,5},{2,6},{3,7},{4,0},{5,1},{6,2},{7,3},{8,12},{9,13},{10,... | collective-permute-start | bytes 86024 | tf_op jit(solution)/shard_map/ppermute | solution.py:21
  38.0 5.1 %collective-permute-start.2 = (bf16[1,112,128]{2,1,0:T(8,128)(2,1)S(1)}, bf16[1,112,128]{2,1,0:T(8,128)(2,1)S(1)}, u32[]{:S(2)}, u32[]{:S(2)}) collective-permute-start(bf16[1,112,128]{2,1,0:T(8,128)(2,1)S(1)} %get-tuple-element.75), channel_id=1, source_target_pairs={{0,3},{1,2},{2,1},{3,0},{4,7},{5,6},{6,5},{7,4},{8,11},{9,10},{10,... | collective-permute-start | bytes 86024 | tf_op jit(solution)/shard_map/ppermute | solution.py:21
  40.2 4.0 %collective-permute-start = (bf16[1,112,128]{2,1,0:T(8,128)(2,1)S(1)}, bf16[1,112,128]{2,1,0:T(8,128)(2,1)S(1)}, u32[]{:S(2)}, u32[]{:S(2)}) collective-permute-start(bf16[1,112,128]{2,1,0:T(8,128)(2,1)S(1)} %get-tuple-element.76), channel_id=1, source_target_pairs={{0,1},{1,0},{2,3},{3,2},{4,5},{5,4},{6,7},{7,6},{8,9},{9,8},{10,11... | collective-permute-start | bytes 86024 | tf_op jit(solution)/shard_map/ppermute | solution.py:21
  40.2 20.0 %collective-permute-start.7 = (bf16[2,112,128]{2,1,0:T(8,128)(2,1)S(1)}, bf16[2,112,128]{2,1,0:T(8,128)(2,1)S(1)}, u32[]{:S(2)}, u32[]{:S(2)}) collective-permute-start(bf16[2,112,128]{2,1,0:T(8,128)(2,1)S(1)} %pad_maximum_fusion.12), channel_id=1, source_target_pairs={{0,1},{1,0},{2,3},{3,2},{4,5},{5,4},{6,7},{7,6},{8,9},{9,8},{10,11... | collective-permute-start | bytes 172040 | tf_op jit(solution)/shard_map/ppermute | solution.py:21
  42.3 17.9 %collective-permute-start.5 = (bf16[2,112,128]{2,1,0:T(8,128)(2,1)S(1)}, bf16[2,112,128]{2,1,0:T(8,128)(2,1)S(1)}, u32[]{:S(2)}, u32[]{:S(2)}) collective-permute-start(bf16[2,112,128]{2,1,0:T(8,128)(2,1)S(1)} %pad_maximum_fusion.11), channel_id=1, source_target_pairs={{0,12},{1,13},{2,14},{3,15},{4,8},{5,9},{6,10},{7,11},{8,4},{9,5},... | collective-permute-start | bytes 172040 | tf_op jit(solution)/shard_map/ppermute | solution.py:21
  43.1 17.1 %collective-permute-start.3 = (bf16[2,112,128]{2,1,0:T(8,128)(2,1)S(1)}, bf16[2,112,128]{2,1,0:T(8,128)(2,1)S(1)}, u32[]{:S(2)}, u32[]{:S(2)}) collective-permute-start(bf16[2,112,128]{2,1,0:T(8,128)(2,1)S(1)} %pad_maximum_fusion.10), channel_id=1, source_target_pairs={{0,4},{1,5},{2,6},{3,7},{4,0},{5,1},{6,2},{7,3},{8,12},{9,13},{10,... | collective-permute-start | bytes 172040 | tf_op jit(solution)/shard_map/ppermute | solution.py:21
  44.2 16.0 %collective-permute-start.1 = (bf16[2,112,128]{2,1,0:T(8,128)(2,1)S(1)}, bf16[2,112,128]{2,1,0:T(8,128)(2,1)S(1)}, u32[]{:S(2)}, u32[]{:S(2)}) collective-permute-start(bf16[2,112,128]{2,1,0:T(8,128)(2,1)S(1)} %pad_maximum_fusion.9), channel_id=1, source_target_pairs={{0,3},{1,2},{2,1},{3,0},{4,7},{5,6},{6,5},{7,4},{8,11},{9,10},{10,... | collective-permute-start | bytes 172040 | tf_op jit(solution)/shard_map/ppermute | solution.py:21
  60.9 12.4 %collective-permute-start.11 = (bf16[4,112,128]{2,1,0:T(8,128)(2,1)}, bf16[4,112,128]{2,1,0:T(8,128)(2,1)}, u32[]{:S(2)}, u32[]{:S(2)}) collective-permute-start(bf16[4,112,128]{2,1,0:T(8,128)(2,1)} %pad_maximum_fusion.8), channel_id=1, source_target_pairs={{0,3},{1,2},{2,1},{3,0},{4,7},{5,6},{6,5},{7,4},{8,11},{9,10},{10,... | collective-permute-start | bytes 344072 | tf_op jit(solution)/shard_map/ppermute | solution.py:21
  63.0 10.3 %collective-permute-start.10 = (bf16[4,112,128]{2,1,0:T(8,128)(2,1)}, bf16[4,112,128]{2,1,0:T(8,128)(2,1)}, u32[]{:S(2)}, u32[]{:S(2)}) collective-permute-start(bf16[4,112,128]{2,1,0:T(8,128)(2,1)} %pad_maximum_fusion.7), channel_id=1, source_target_pairs={{0,1},{1,0},{2,3},{3,2},{4,5},{5,4},{6,7},{7,6},{8,9},{9,8},{10,11... | collective-permute-start | bytes 344072 | tf_op jit(solution)/shard_map/ppermute | solution.py:21
  63.6 9.7 %collective-permute-start.9 = (bf16[4,112,128]{2,1,0:T(8,128)(2,1)}, bf16[4,112,128]{2,1,0:T(8,128)(2,1)}, u32[]{:S(2)}, u32[]{:S(2)}) collective-permute-start(bf16[4,112,128]{2,1,0:T(8,128)(2,1)} %pad_maximum_fusion.6), channel_id=1, source_target_pairs={{0,12},{1,13},{2,14},{3,15},{4,8},{5,9},{6,10},{7,11},{8,4},{9,5},... | collective-permute-start | bytes 344072 | tf_op jit(solution)/shard_map/ppermute | solution.py:21
  66.5 7.5 %collective-permute-start.8 = (bf16[4,112,128]{2,1,0:T(8,128)(2,1)}, bf16[4,112,128]{2,1,0:T(8,128)(2,1)}, u32[]{:S(2)}, u32[]{:S(2)}) collective-permute-start(bf16[4,112,128]{2,1,0:T(8,128)(2,1)} %pad_maximum_fusion.5), channel_id=1, source_target_pairs={{0,4},{1,5},{2,6},{3,7},{4,0},{5,1},{6,2},{7,3},{8,12},{9,13},{10,... | collective-permute-start | bytes 344072 | tf_op jit(solution)/shard_map/ppermute | solution.py:21
  75.0 12.0 %collective-permute-start.15 = (bf16[8,112,128]{2,1,0:T(8,128)(2,1)S(1)}, bf16[8,112,128]{2,1,0:T(8,128)(2,1)S(1)}, u32[]{:S(2)}, u32[]{:S(2)}) collective-permute-start(bf16[8,112,128]{2,1,0:T(8,128)(2,1)S(1)} %pad_maximum_fusion.4), channel_id=1, source_target_pairs={{0,4},{1,5},{2,6},{3,7},{4,0},{5,1},{6,2},{7,3},{8,12},{9,13},{10,... | collective-permute-start | bytes 688136 | tf_op jit(solution)/shard_map/ppermute | solution.py:21
  76.8 18.2 %copy-start.2 = (f32[7168,1]{1,0:T(8,128)S(1)}, f32[7168,1]{1,0:T(8,128)}, u32[]{:S(2)}) copy-start(f32[7168,1]{1,0:T(8,128)} %copy.33.gain_ref) | copy-start | bytes 86020
  76.8 13.1 %collective-permute-start.14 = (bf16[8,112,128]{2,1,0:T(8,128)(2,1)S(1)}, bf16[8,112,128]{2,1,0:T(8,128)(2,1)S(1)}, u32[]{:S(2)}, u32[]{:S(2)}) collective-permute-start(bf16[8,112,128]{2,1,0:T(8,128)(2,1)S(1)} %pad_maximum_fusion.3), channel_id=1, source_target_pairs={{0,3},{1,2},{2,1},{3,0},{4,7},{5,6},{6,5},{7,4},{8,11},{9,10},{10,... | collective-permute-start | bytes 688136 | tf_op jit(solution)/shard_map/ppermute | solution.py:21
  79.1 12.0 %collective-permute-start.13 = (bf16[8,112,128]{2,1,0:T(8,128)(2,1)S(1)}, bf16[8,112,128]{2,1,0:T(8,128)(2,1)S(1)}, u32[]{:S(2)}, u32[]{:S(2)}) collective-permute-start(bf16[8,112,128]{2,1,0:T(8,128)(2,1)S(1)} %pad_maximum_fusion.2), channel_id=1, source_target_pairs={{0,1},{1,0},{2,3},{3,2},{4,5},{5,4},{6,7},{7,6},{8,9},{9,8},{10,11... | collective-permute-start | bytes 688136 | tf_op jit(solution)/shard_map/ppermute | solution.py:21
  81.9 13.1 %collective-permute-start.12 = (bf16[8,112,128]{2,1,0:T(8,128)(2,1)S(1)}, bf16[8,112,128]{2,1,0:T(8,128)(2,1)S(1)}, u32[]{:S(2)}, u32[]{:S(2)}) collective-permute-start(bf16[8,112,128]{2,1,0:T(8,128)(2,1)S(1)} %pad_maximum_fusion.1), channel_id=1, source_target_pairs={{0,12},{1,13},{2,14},{3,15},{4,8},{5,9},{6,10},{7,11},{8,4},{9,5},... | collective-permute-start | bytes 688136 | tf_op jit(solution)/shard_map/ppermute | solution.py:21
  120.7 13.3 %copy-start = (bf16[7168,256]{1,0:T(8,128)(2,1)S(1)}, bf16[7168,256]{1,0:T(8,128)(2,1)}, u32[]{:S(2)}) copy-start(bf16[7168,256]{1,0:T(8,128)(2,1)} %copy.32) | copy-start | bytes 11010052
  137.2 47.2 %collective-permute-start.20 = (bf16[8,448,256]{2,1,0:T(8,128)(2,1)}, bf16[8,448,256]{2,1,0:T(8,128)(2,1)}, u32[]{:S(2)}, u32[]{:S(2)}) collective-permute-start(bf16[8,448,256]{2,1,0:T(8,128)(2,1)} %get-tuple-element.53), channel_id=1, source_target_pairs={{0,1},{1,0},{2,3},{3,2},{4,5},{5,4},{6,7},{7,6},{8,9},{9,8},{10,11... | collective-permute-start | bytes 5505032 | tf_op jit(solution)/shard_map/ppermute | solution.py:21
  138.7 50.1 %collective-permute-start.24 = (bf16[8,448,256]{2,1,0:T(8,128)(2,1)}, bf16[8,448,256]{2,1,0:T(8,128)(2,1)}, u32[]{:S(2)}, u32[]{:S(2)}) collective-permute-start(bf16[8,448,256]{2,1,0:T(8,128)(2,1)} %get-tuple-element.55), channel_id=1, source_target_pairs={{0,3},{1,2},{2,1},{3,0},{4,7},{5,6},{6,5},{7,4},{8,11},{9,10},{10,... | collective-permute-start | bytes 5505032 | tf_op jit(solution)/shard_map/ppermute | solution.py:21
  143.8 48.2 %collective-permute-start.28 = (bf16[8,448,256]{2,1,0:T(8,128)(2,1)}, bf16[8,448,256]{2,1,0:T(8,128)(2,1)}, u32[]{:S(2)}, u32[]{:S(2)}) collective-permute-start(bf16[8,448,256]{2,1,0:T(8,128)(2,1)} %get-tuple-element.57), channel_id=1, source_target_pairs={{0,4},{1,5},{2,6},{3,7},{4,0},{5,1},{6,2},{7,3},{8,12},{9,13},{10,... | collective-permute-start | bytes 5505032 | tf_op jit(solution)/shard_map/ppermute | solution.py:21
  144.0 51.2 %collective-permute-start.32 = (bf16[8,448,256]{2,1,0:T(8,128)(2,1)}, bf16[8,448,256]{2,1,0:T(8,128)(2,1)}, u32[]{:S(2)}, u32[]{:S(2)}) collective-permute-start(bf16[8,448,256]{2,1,0:T(8,128)(2,1)} %get-tuple-element.59), channel_id=1, source_target_pairs={{0,12},{1,13},{2,14},{3,15},{4,8},{5,9},{6,10},{7,11},{8,4},{9,5},... | collective-permute-start | bytes 5505032 | tf_op jit(solution)/shard_map/ppermute | solution.py:21
  151.7 75.4 %copy-start.7 = (bf16[8,448,256]{2,1,0:T(8,128)(2,1)}, bf16[8,448,256]{2,1,0:T(8,128)(2,1)S(1)}, u32[]{:S(2)}) copy-start(bf16[8,448,256]{2,1,0:T(8,128)(2,1)S(1)} %get-tuple-element.54) | copy-start | bytes 5505028
  151.7 77.9 %copy-start.6 = (bf16[8,448,256]{2,1,0:T(8,128)(2,1)}, bf16[8,448,256]{2,1,0:T(8,128)(2,1)S(1)}, u32[]{:S(2)}) copy-start(bf16[8,448,256]{2,1,0:T(8,128)(2,1)S(1)} %get-tuple-element.56) | copy-start | bytes 5505028
  185.8 23.8 %collective-permute-start.21 = (bf16[4,448,256]{2,1,0:T(8,128)(2,1)S(1)}, bf16[4,448,256]{2,1,0:T(8,128)(2,1)S(1)}, u32[]{:S(2)}, u32[]{:S(2)}) collective-permute-start(bf16[4,448,256]{2,1,0:T(8,128)(2,1)S(1)} %add_convert_fusion.3), channel_id=1, source_target_pairs={{0,3},{1,2},{2,1},{3,0},{4,7},{5,6},{6,5},{7,4},{8,11},{9,10},{10,... | collective-permute-start | bytes 2752520 | tf_op jit(solution)/shard_map/ppermute | solution.py:21
  190.2 23.7 %collective-permute-start.25 = (bf16[4,448,256]{2,1,0:T(8,128)(2,1)S(1)}, bf16[4,448,256]{2,1,0:T(8,128)(2,1)S(1)}, u32[]{:S(2)}, u32[]{:S(2)}) collective-permute-start(bf16[4,448,256]{2,1,0:T(8,128)(2,1)S(1)} %add_convert_fusion.2), channel_id=1, source_target_pairs={{0,4},{1,5},{2,6},{3,7},{4,0},{5,1},{6,2},{7,3},{8,12},{9,13},{10,... | collective-permute-start | bytes 2752520 | tf_op jit(solution)/shard_map/ppermute | solution.py:21
  193.4 22.8 %collective-permute-start.29 = (bf16[4,448,256]{2,1,0:T(8,128)(2,1)S(1)}, bf16[4,448,256]{2,1,0:T(8,128)(2,1)S(1)}, u32[]{:S(2)}, u32[]{:S(2)}) collective-permute-start(bf16[4,448,256]{2,1,0:T(8,128)(2,1)S(1)} %add_convert_fusion.1), channel_id=1, source_target_pairs={{0,12},{1,13},{2,14},{3,15},{4,8},{5,9},{6,10},{7,11},{8,4},{9,5},... | collective-permute-start | bytes 2752520 | tf_op jit(solution)/shard_map/ppermute | solution.py:21
  196.6 38.3 %collective-permute-start.33 = (bf16[4,448,256]{2,1,0:T(8,128)(2,1)S(1)}, bf16[4,448,256]{2,1,0:T(8,128)(2,1)}, u32[]{:S(2)}, u32[]{:S(2)}) collective-permute-start(bf16[4,448,256]{2,1,0:T(8,128)(2,1)S(1)} %add_convert_fusion), channel_id=1, source_target_pairs={{0,1},{1,0},{2,3},{3,2},{4,5},{5,4},{6,7},{7,6},{8,9},{9,8},{10,11... | collective-permute-start | bytes 2752520 | tf_op jit(solution)/shard_map/ppermute | solution.py:21
  210.8 13.1 %collective-permute-start.22 = (bf16[2,448,256]{2,1,0:T(8,128)(2,1)S(1)}, bf16[2,448,256]{2,1,0:T(8,128)(2,1)S(1)}, u32[]{:S(2)}, u32[]{:S(2)}) collective-permute-start(bf16[2,448,256]{2,1,0:T(8,128)(2,1)S(1)} %add_convert_fusion.7), channel_id=1, source_target_pairs={{0,4},{1,5},{2,6},{3,7},{4,0},{5,1},{6,2},{7,3},{8,12},{9,13},{10,... | collective-permute-start | bytes 1376264 | tf_op jit(solution)/shard_map/ppermute | solution.py:21
  213.8 13.3 %copy-start.10 = (bf16[4,448,256]{2,1,0:T(8,128)(2,1)}, bf16[4,448,256]{2,1,0:T(8,128)(2,1)S(1)}, u32[]{:S(2)}) copy-start(bf16[4,448,256]{2,1,0:T(8,128)(2,1)S(1)} %collective-permute-done.25) | copy-start | bytes 2752516
  215.4 11.8 %collective-permute-start.26 = (bf16[2,448,256]{2,1,0:T(8,128)(2,1)S(1)}, bf16[2,448,256]{2,1,0:T(8,128)(2,1)S(1)}, u32[]{:S(2)}, u32[]{:S(2)}) collective-permute-start(bf16[2,448,256]{2,1,0:T(8,128)(2,1)S(1)} %add_convert_fusion.6), channel_id=1, source_target_pairs={{0,12},{1,13},{2,14},{3,15},{4,8},{5,9},{6,10},{7,11},{8,4},{9,5},... | collective-permute-start | bytes 1376264 | tf_op jit(solution)/shard_map/ppermute | solution.py:21
  216.1 13.5 %copy-start.9 = (bf16[4,448,256]{2,1,0:T(8,128)(2,1)}, bf16[4,448,256]{2,1,0:T(8,128)(2,1)S(1)}, u32[]{:S(2)}) copy-start(bf16[4,448,256]{2,1,0:T(8,128)(2,1)S(1)} %collective-permute-done.29) | copy-start | bytes 2752516
  217.7 11.9 %collective-permute-start.30 = (bf16[2,448,256]{2,1,0:T(8,128)(2,1)S(1)}, bf16[2,448,256]{2,1,0:T(8,128)(2,1)S(1)}, u32[]{:S(2)}, u32[]{:S(2)}) collective-permute-start(bf16[2,448,256]{2,1,0:T(8,128)(2,1)S(1)} %add_convert_fusion.5), channel_id=1, source_target_pairs={{0,1},{1,0},{2,3},{3,2},{4,5},{5,4},{6,7},{7,6},{8,9},{9,8},{10,11... | collective-permute-start | bytes 1376264 | tf_op jit(solution)/shard_map/ppermute | solution.py:21
  225.0 8.1 %collective-permute-start.23 = (bf16[1,448,256]{2,1,0:T(8,128)(2,1)S(1)}, bf16[1,448,256]{2,1,0:T(8,128)(2,1)S(1)}, u32[]{:S(2)}, u32[]{:S(2)}) collective-permute-start(bf16[1,448,256]{2,1,0:T(8,128)(2,1)S(1)} %add_convert_fusion.11), channel_id=1, source_target_pairs={{0,12},{1,13},{2,14},{3,15},{4,8},{5,9},{6,10},{7,11},{8,4},{9,5},... | collective-permute-start | bytes 688136 | tf_op jit(solution)/shard_map/ppermute | solution.py:21
  229.1 15.7 %collective-permute-start.27 = (bf16[1,448,256]{2,1,0:T(8,128)(2,1)}, bf16[1,448,256]{2,1,0:T(8,128)(2,1)S(1)}, u32[]{:S(2)}, u32[]{:S(2)}) collective-permute-start(bf16[1,448,256]{2,1,0:T(8,128)(2,1)} %add_convert_fusion.10), channel_id=1, source_target_pairs={{0,1},{1,0},{2,3},{3,2},{4,5},{5,4},{6,7},{7,6},{8,9},{9,8},{10,11... | collective-permute-start | bytes 688136 | tf_op jit(solution)/shard_map/ppermute | solution.py:21
  231.6 28.5 %collective-permute-start.31 = (bf16[1,448,256]{2,1,0:T(8,128)(2,1)}, bf16[1,448,256]{2,1,0:T(8,128)(2,1)}, u32[]{:S(2)}, u32[]{:S(2)}) collective-permute-start(bf16[1,448,256]{2,1,0:T(8,128)(2,1)} %add_convert_fusion.9), channel_id=1, source_target_pairs={{0,3},{1,2},{2,1},{3,0},{4,7},{5,6},{6,5},{7,4},{8,11},{9,10},{10,... | collective-permute-start | bytes 688136 | tf_op jit(solution)/shard_map/ppermute | solution.py:21
  236.6 10.4 %all-to-all-start.1 = ((bf16[8,16,448]{2,1,0:T(8,128)(2,1)}), bf16[8,16,448]{2,1,0:T(8,128)(2,1)S(1)}, u32[]{:S(2)}, u32[]{:S(2)}) async-start(bf16[8,16,448]{2,1,0:T(8,128)(2,1)} %bitcast.18), calls=%async_computation.2 | async-start | bytes 262144 | tf_op jit(solution)/shard_map/all_to_all | solution.py:274
  243.0 14.5 %collective-permute-start.34 = (bf16[2,448,256]{2,1,0:T(8,128)(2,1)}, bf16[2,448,256]{2,1,0:T(8,128)(2,1)}, u32[]{:S(2)}, u32[]{:S(2)}) collective-permute-start(bf16[2,448,256]{2,1,0:T(8,128)(2,1)} %add_convert_fusion.4), channel_id=1, source_target_pairs={{0,3},{1,2},{2,1},{3,0},{4,7},{5,6},{6,5},{7,4},{8,11},{9,10},{10,... | collective-permute-start | bytes 1376264 | tf_op jit(solution)/shard_map/ppermute | solution.py:21
  258.8 8.6 %copy-start.12 = (f32[448,256]{1,0:T(8,128)S(1)}, f32[448,256]{1,0:T(8,128)}, u32[]{:S(2)}) copy-start(f32[448,256]{1,0:T(8,128)} %add_bitcast_fusion.3) | copy-start | bytes 1376260
  258.8 7.3 %collective-permute-start.35 = (bf16[1,448,256]{2,1,0:T(8,128)(2,1)S(1)}, bf16[1,448,256]{2,1,0:T(8,128)(2,1)S(1)}, u32[]{:S(2)}, u32[]{:S(2)}) collective-permute-start(bf16[1,448,256]{2,1,0:T(8,128)(2,1)S(1)} %add_convert_fusion.8), channel_id=1, source_target_pairs={{0,4},{1,5},{2,6},{3,7},{4,0},{5,1},{6,2},{7,3},{8,12},{9,13},{10,... | collective-permute-start | bytes 688136 | tf_op jit(solution)/shard_map/ppermute | solution.py:21
  (11 other events, 55.9 us)
Sparse Core Ops, SparseCore 0:
  9.5 111.1 all-gather.1
  146.0 75.5 reduce-scatter.1

commit v8 on v7

--- a/solution.py
+++ b/solution.py
@@ -190,6 +190,10 @@
             flops=2 * features * deep * columns, bytes_accessed=2 * features * (deep + columns), transcendentals=0
         ),
     )(weight, hidden)
+
+
+def add_pair(kept, got):
+    return (kept.astype(jnp.float32) + got.astype(jnp.float32)).astype(jnp.bfloat16)
 
 
 def shards(
@@ -251,15 +255,25 @@
 
     expert_hidden = expert_gate_up(slice_of, pooled, expert_gate, expert_up, gain_column)
     expert_partial = expert_down_parts(expert_down, expert_hidden)
-    expert_partial, scale, whole_columns = lax.optimization_barrier((expert_partial, scale, whole_columns))
-    expert_out = lax.psum_scatter(expert_partial, "local", scatter_dimension=0, tiled=True)
+    expert_partial, scale = lax.optimization_barrier((expert_partial, scale))
+    def halve(array, bit):
+        half = 1 << bit
+        upper = (local_index >> bit) & 1
+        keep = lax.dynamic_slice_in_dim(array, upper * half, half, 0)
+        return keep, lax.dynamic_slice_in_dim(array, (1 - upper) * half, half, 0)
+
+    expert_keep, expert_send = halve(expert_partial.reshape(16, slice_width, slot_count), 3)
+    expert_keep, expert_send, whole_columns = lax.optimization_barrier((expert_keep, expert_send, whole_columns))
+    expert_got = flip_local(expert_send, 3)
 
     gate_up = transposed_dot(weight, whole_columns)
     low_hidden, *sent = sent_parts(0, slice_of, gate_up, scale, turned)
     high_hidden, *more = sent_parts(2, slice_of, gate_up, scale, turned)
     sent += more
+    sent[3], expert_got = lax.optimization_barrier((sent[3], expert_got))
     arrived = [flip_local(sent[s], STREAMS[s][0]) for s in range(4)]
     sums = kept_parts(slice_of, turned, (low_hidden, high_hidden))
+    arrived[3], expert_got = lax.optimization_barrier((arrived[3], expert_got))
     terms = [[sums[s], arrived[s]] for s in range(4)]
 
     def added(s, low, high):
@@ -269,14 +283,22 @@
         half = 8 >> step
         for s in range(4):
             terms[s].append(flip_local(added(s, half, 2 * half).astype(jnp.bfloat16), STREAMS[s][step]))
+        if step < 3:
+            expert_keep, expert_send = halve(add_pair(expert_keep, expert_got), (3, 2, 0)[step])
+            expert_got = flip_local(expert_send, (3, 2, 0)[step])
+            if step == 1:
+                terms[0][-1], expert_got = lax.optimization_barrier((terms[0][-1], expert_got))
         if step == 1:
-            terms[3][-1], expert_out = lax.optimization_barrier((terms[3][-1], expert_out))
+            expert_keep, expert_send = halve(add_pair(expert_keep, expert_got), 1)
+            expert_got = flip_local(expert_send, 1)
+            terms[3][-1], expert_got = lax.optimization_barrier((terms[3][-1], expert_got))
+        if step == 2:
+            expert_out = add_pair(expert_keep, expert_got)[0]
+            terms[1][-1], expert_out = lax.optimization_barrier((terms[1][-1], expert_out))
             returned = lax.all_to_all(
                 expert_out.T.reshape(node_count, NODE_CAP, slice_width), "node", split_axis=0, concat_axis=0, tiled=True
             ).reshape(slot_count, slice_width)
             route_term = (slot_gate[:, None] * returned.astype(jnp.float32)).astype(jnp.bfloat16)
-        if step == 2:
-            terms[3][-1], route_term = lax.optimization_barrier((terms[3][-1], route_term))
     expert_part = lax.dot_general(
         route_term, chosen, (((0,), (1,)), ((), ())), preferred_element_type=jnp.float32
     )

time: 277 us -> 283 us (1.022)
  waiting for transfers between devices: 91.8 us -> 82.6 us
  other arithmetic: 50.1 us -> 56.9 us
  local copies, waits for them, and re-layouts: 24.5 us -> 28.3 us
  starting transfers between devices: 59.5 us -> 62.7 us
    ppermute x36 -> x40, waiting for transfers between devices: 80.2 us -> 72.5 us  [flip_local(): lax.ppermute(array, 'local', [(i, LOCAL_AT[LOCAL_LABEL[i] ^ 1 << bit]) fo...]
    optimization_barrier x0 -> x2, local copies, waits for them, and re-layouts: none -> 3.58 us  [the longest x1 2.26 us: shards(): arrived[3], expert_got = lax.optimization_barrier((arrived[3], expert_got))]
    ppermute x36 -> x40, starting transfers between devices: 50.9 us -> 54.2 us  [flip_local(): lax.ppermute(array, 'local', [(i, LOCAL_AT[LOCAL_LABEL[i] ^ 1 << bit]) fo...]
    convert_element_type x12, other arithmetic: 18.3 us -> 21.4 us  [shards(): added(s, half, 2 * half).astype(jnp.bfloat16)]
  transfers between devices with their start and end apart: 40 -> 43, of which waited for: 16 -> 17; matrix products, arithmetic and copies ran while one was open for 24% -> 33% of each run, Pallas kernels for 6% -> 7%
where the time goes in v8:
time: 283 us; the launch traced here: 281 us
  waiting for transfers between devices  82.6 us (29%)
  starting transfers between devices  62.7 us (22%)
  other arithmetic  56.9 us (20%)
  local copies, waits for them, and re-layouts  28.3 us (10%)
  Pallas kernels  19.8 us (7%)
  matrix products  16.5 us (6%)
  between operations  13.9 us (5%)
    ppermute x40, waiting for transfers between devices, flip_local(): lax.ppermute(array, 'local', [(i, LOCAL_AT[LOCAL_LABEL[i] ^ 1 << bit]) fo...  72.5 us
    ppermute x40, starting transfers between devices, flip_local(): lax.ppermute(array, 'local', [(i, LOCAL_AT[LOCAL_LABEL[i] ^ 1 << bit]) fo...  54.2 us
    convert_element_type x12, other arithmetic, shards(): added(s, half, 2 * half).astype(jnp.bfloat16)  21.4 us
    dot_general x1, matrix products, transposed_dot(): lax.dot_general(weight, rows, (((0,), (0,)), ((), ())), preferred_element...  13.3 us
    unnamed x50, local copies, waits for them, and re-layouts  11.1 us
    all_gather x1, waiting for transfers between devices, shards(): whole_columns = lax.all_gather(columns, 'local', axis=0, tiled=True)  9.19 us
    squeeze x4, other arithmetic, shards(): dense_part = jnp.concatenate([added(s, 0, 1)[0] for s in range(4)], axis=1)  7.77 us
    pallas_call x1, Pallas kernels, expert_gate_up(): pl.pallas_call(functools.partial(expert_kernel, blocks, blocks * rows), g...  7.67 us
  transfers between devices with their start and end apart: 43, of which 17 were waited for; matrix products, arithmetic and copies ran while one was open for 33% of the time, Pallas kernels for 7%

profile of v8, /device:TPU:0, one launch (start us, length us, event | category | flops | bytes accessed | tf_op | source)
XLA Modules:
  0.0 280.7 jit_solution(1458739394444902482)
XLA Ops:
  11.2 2.3 reduce-window.6
  15.7 2.3 collective-permute-start.17
  20.6 1.9 collective-permute-start.18
  23.7 4.3 %all-to-all-start = ((bf16[8,16,448]{2,1,0:T(8,128)(2,1)}), bf16[8,16,448]{2,1,0:T(8,128)(2,1)S(1)}, u32[]{:S(2)}, u32[]{:S(2)}) async-start(bf16[8,16,448]{2,1,0:T(8,128)(2,1)} %bitcast.3), calls=%async_computation | async-start | bytes 262144 | tf_op jit(solution)/shard_map/all_to_all | solution.py:230
  28.0 2.6 collective-permute-start.19
  31.3 2.5 copy.45.gain_ref
  34.3 2.6 collective-permute-start.6
  38.0 2.2 collective-permute-start.2
  40.2 2.1 collective-permute-start.7
  44.2 2.3 collective-permute-start.1
  46.5 7.0 %multiply_convert_fusion.1 = (bf16[7168,256]{1,0:T(8,128)(2,1)}, bf16[7168,256]{1,0:T(8,128)(2,1)}) fusion(bf16[7168,256]{1,0:T(8,128)(2,1)} %param.13, f32[7168]{0:T(1024)S(1)} %copy-done.16, bf16[7168,256]{1,0:T(8,128)(2,1)} %param.14), kind=kLoop, calls=%fused_computation.2 | loop fusion | flops 11010048 | bytes 14708736 | tf_op jit(solution)/shard_map/convert_element_type | solution.py:246
  53.5 6.6 %pad_maximum_fusion = bf16[7168,512]{1,0:T(8,128)(2,1)} fusion(bf16[7168,256]{1,0:T(8,128)(2,1)} %get-tuple-element.96, bf16[7168,256]{1,0:T(8,128)(2,1)} %get-tuple-element.95), kind=kLoop, calls=%fused_computation | loop fusion | flops 14680064 | bytes 14680064 | tf_op jit(solution)/shard_map/concatenate | solution.py:245
  63.7 2.3 collective-permute-start.9
  67.3 5.9 %copy.44 = bf16[7168,256]{1,0:T(8,128)(2,1)} copy(bf16[7168,256]{0,1:T(8,128)(2,1)} %bitcast.70) | data formatting | bytes 7340032 | tf_op jit(solution)/shard_map/transpose | solution.py:251
  87.1 2.9 %collective-permute-done.14 = bf16[8,112,128]{2,1,0:T(8,128)(2,1)S(1)} collective-permute-done((bf16[8,112,128]{2,1,0:T(8,128)(2,1)S(1)}, bf16[8,112,128]{2,1,0:T(8,128)(2,1)S(1)}, u32[]{:S(2)}, u32[]{:S(2)}) %collective-permute-start.14) | collective-permute-done | bytes 229408 | tf_op jit(solution)/shard_map/ppermute | solution.py:21
  91.2 3.9 %collective-permute-done.12 = bf16[8,112,128]{2,1,0:T(8,128)(2,1)S(1)} collective-permute-done((bf16[8,112,128]{2,1,0:T(8,128)(2,1)S(1)}, bf16[8,112,128]{2,1,0:T(8,128)(2,1)S(1)}, u32[]{:S(2)}, u32[]{:S(2)}) %collective-permute-start.12) | collective-permute-done | bytes 229408 | tf_op jit(solution)/shard_map/ppermute | solution.py:21
  95.1 2.0 copy-done.3
  97.2 2.2 copy-done.4
  99.4 7.7 %shard_map.109.hidden_ref = bf16[256,128]{1,0:T(8,128)(2,1)S(1)} custom-call(s32[16]{0:T(128)S(1)} %fusion.13.at_ref.slice_ref, bf16[16,112,128]{2,1,0:T(8,128)(2,1)S(1)} %constant_dynamic-update-slice_fusion.x0, bf16[16,112,128]{2,1,0:T(8,128)(2,1)S(1)} %constant_dynamic-update-slice_fusion.5.x1, ...), custom_call_target="tpu_custom_call" | custom-call | flops 939524096 | bytes 9175040 | tf_op jit(solution)/shard_map/pallas_call | solution.py:147
  107.0 2.1 shard_map.110
  111.5 9.2 %all-gather.2.cloned.1.call-done = bf16[7168,1024]{1,0:T(8,128)(2,1)} async-done(((bf16[448,1024]{1,0:T(8,128)(2,1)}), bf16[7168,1024]{1,0:T(8,128)(2,1)}) %all-gather.2.cloned.1.call-update) | async-done | bytes 14680080 | tf_op jit(solution)/shard_map/all_gather | solution.py:220
  120.7 2.7 collective-permute-start.22
  123.5 13.3 %fusion.14.gate_up_ref = f32[512,1024]{1,0:T(8,128)S(1)} fusion(bf16[7168,512]{1,0:T(8,128)(2,1)} %pad_maximum_fusion, bf16[7168,1024]{1,0:T(8,128)(2,1)} %all-gather.2.cloned.1.call-done), kind=kOutput, calls=%fused_computation.96 | convolution fusion | flops 7516192768 | bytes 24117248 | tf_op jit(solution)/shard_map/dot_general | solution.py:36
  136.8 3.0 %shard_map.111 = (bf16[256,512]{1,0:T(8,128)(2,1)S(1)}, bf16[8,448,256]{2,1,0:T(8,128)(2,1)}, bf16[8,448,256]{2,1,0:T(8,128)(2,1)}) custom-call(s32[16]{0:T(128)S(1)} %fusion.13.at_ref.slice_ref, f32[512,1024]{1,0:T(8,128)S(1)} %fusion.14.gate_up_ref, f32[1,1024]{1,0:T(1,128)S(1)} %add_rsqrt_fusion.scale_ref, bf16[16,448,256]{2,1,0:T(8,128)(2,1)S(1)} %bitcast.62), custom_call_target="tpu_custom_call" | custom-call | flops 939524096 | bytes 7340032 | tf_op jit(solution)/shard_map/pallas_call | solution.py:66
  140.0 3.2 %shard_map.112 = (bf16[256,512]{1,0:T(8,128)(2,1)S(1)}, bf16[8,448,256]{2,1,0:T(8,128)(2,1)}, bf16[8,448,256]{2,1,0:T(8,128)(2,1)}) custom-call(s32[16]{0:T(128)S(1)} %fusion.13.at_ref.slice_ref, f32[512,1024]{1,0:T(8,128)S(1)} %fusion.14.gate_up_ref, f32[1,1024]{1,0:T(1,128)S(1)} %add_rsqrt_fusion.scale_ref, bf16[16,448,256]{2,1,0:T(8,128)(2,1)S(1)} %bitcast.63), custom_call_target="tpu_custom_call" | custom-call | flops 939524096 | bytes 7340032 | tf_op jit(solution)/shard_map/pallas_call | solution.py:66
  147.1 2.0 copy-done.1
  149.1 3.8 %shard_map.113 = (bf16[8,448,256]{2,1,0:T(8,128)(2,1)S(1)}, bf16[8,448,256]{2,1,0:T(8,128)(2,1)S(1)}, bf16[8,448,256]{2,1,0:T(8,128)(2,1)S(1)}, bf16[8,448,256]{2,1,0:T(8,128)(2,1)S(1)}) custom-call(s32[16]{0:T(128)S(1)} %fusion.13.at_ref.slice_ref, bf16[16,448,256]{2,1,0:T(8,128)(2,1)S(1)} %bitcast.64, bf16[16,448,256]{2,1,0:T(8,128)(2,1)S(1)} %bitcast.65, ...), custom_call_target="tpu_custom_call" | custom-call | flops 1879048192 | bytes 14680064 | tf_op jit(solution)/shard_map/pallas_call | solution.py:96
  153.0 28.7 %collective-permute-done.20 = bf16[8,448,256]{2,1,0:T(8,128)(2,1)} collective-permute-done((bf16[8,448,256]{2,1,0:T(8,128)(2,1)}, bf16[8,448,256]{2,1,0:T(8,128)(2,1)}, u32[]{:S(2)}, u32[]{:S(2)}) %collective-permute-start.20) | collective-permute-done | bytes 1835040 | tf_op jit(solution)/shard_map/ppermute | solution.py:21
  181.6 2.3 add_convert_fusion.4
  184.8 2.3 add_convert_fusion.1
  187.1 2.3 collective-permute-start.35
  189.5 2.3 add_convert_fusion.3
  191.8 2.3 copy.47
  196.0 2.1 collective-permute-start.24
  199.8 9.5 %collective-permute-done.35 = bf16[4,448,256]{2,1,0:T(8,128)(2,1)} collective-permute-done((bf16[4,448,256]{2,1,0:T(8,128)(2,1)}, bf16[4,448,256]{2,1,0:T(8,128)(2,1)}, u32[]{:S(2)}, u32[]{:S(2)}) %collective-permute-start.35) | collective-permute-done | bytes 917536 | tf_op jit(solution)/shard_map/ppermute | solution.py:21
  212.5 2.9 %collective-permute-done.28 = bf16[4,448,256]{2,1,0:T(8,128)(2,1)} collective-permute-done((bf16[4,448,256]{2,1,0:T(8,128)(2,1)}, bf16[4,448,256]{2,1,0:T(8,128)(2,1)}, u32[]{:S(2)}, u32[]{:S(2)}) %collective-permute-start.28) | collective-permute-done | bytes 917536 | tf_op jit(solution)/shard_map/ppermute | solution.py:21
  218.1 5.5 %collective-permute-done.24 = bf16[4,448,128]{1,2,0:T(8,128)(2,1)S(1)} collective-permute-done((bf16[4,448,128]{1,2,0:T(8,128)(2,1)S(1)}, bf16[4,448,128]{1,2,0:T(8,128)(2,1)S(1)}, u32[]{:S(2)}, u32[]{:S(2)}) %collective-permute-start.24) | collective-permute-done | bytes 458784 | tf_op jit(solution)/shard_map/ppermute | solution.py:21
  225.4 3.8 %collective-permute-done.36 = bf16[2,448,256]{2,1,0:T(8,128)(2,1)S(1)} collective-permute-done((bf16[2,448,256]{2,1,0:T(8,128)(2,1)S(1)}, bf16[2,448,256]{2,1,0:T(8,128)(2,1)S(1)}, u32[]{:S(2)}, u32[]{:S(2)}) %collective-permute-start.36) | collective-permute-done | bytes 458784 | tf_op jit(solution)/shard_map/ppermute | solution.py:21
  233.9 4.6 %collective-permute-done.37 = bf16[1,448,256]{2,1,0:T(8,128)(2,1)S(1)} collective-permute-done((bf16[1,448,256]{2,1,0:T(8,128)(2,1)S(1)}, bf16[1,448,256]{2,1,0:T(8,128)(2,1)S(1)}, u32[]{:S(2)}, u32[]{:S(2)}) %collective-permute-start.37) | collective-permute-done | bytes 229408 | tf_op jit(solution)/shard_map/ppermute | solution.py:21
  238.6 2.0 add_bitcast_fusion.1
  241.6 2.1 add_convert_fusion.6
  245.1 2.1 add_convert_fusion.14
  250.6 2.0 add_convert_fusion.13
  253.8 4.2 %all-to-all-start.1 = ((bf16[8,16,448]{2,1,0:T(8,128)(2,1)}), bf16[8,16,448]{2,1,0:T(8,128)(2,1)}, u32[]{:S(2)}, u32[]{:S(2)}) async-start(bf16[8,16,448]{2,1,0:T(8,128)(2,1)} %bitcast.21), calls=%async_computation.1 | async-start | bytes 262144 | tf_op jit(solution)/shard_map/all_to_all | solution.py:298
  258.1 2.3 add_bitcast_fusion.3
  261.8 2.2 add_bitcast_fusion.2
  264.0 5.8 %collective-permute-done.39 = bf16[1,448,256]{2,1,0:T(8,128)(2,1)S(1)} collective-permute-done((bf16[1,448,256]{2,1,0:T(8,128)(2,1)S(1)}, bf16[1,448,256]{2,1,0:T(8,128)(2,1)S(1)}, u32[]{:S(2)}, u32[]{:S(2)}) %collective-permute-start.39) | collective-permute-done | bytes 229408 | tf_op jit(solution)/shard_map/ppermute | solution.py:21
  271.1 2.8 fusion.3
  (168 shorter events, 67.6 us)
Async XLA Ops:
  6.5 114.2 %all-gather.2.cloned.1.call-start = ((), (), s32[]{:S(2)}) async-start(), calls=%async_computation.2 | async-start | bytes 15597568 | tf_op jit(solution)/shard_map/all_gather | solution.py:220
  8.7 7.1 %collective-permute-start.16 = (f32[1,1024]{1,0:T(1,128)S(1)}, f32[1,1024]{1,0:T(1,128)S(1)}, u32[]{:S(2)}, u32[]{:S(2)}) collective-permute-start(f32[1,1024]{1,0:T(1,128)S(1)} %bitcast.75), channel_id=1, source_target_pairs={{0,1},{1,0},{2,3},{3,2},{4,5},{5,4},{6,7},{7,6},{8,9},{9,8},{10,11... | collective-permute-start | bytes 12296 | tf_op jit(solution)/shard_map/ppermute | solution.py:21
  15.4 16.0 %copy-start.16 = (f32[7168]{0:T(1024)S(1)}, f32[7168]{0:T(1024)}, u32[]{:S(2)}) copy-start(f32[7168]{0:T(1024)} %param.12) | copy-start | bytes 86020
  15.7 4.9 %collective-permute-start.17 = (f32[1,1024]{1,0:T(1,128)S(1)}, f32[1,1024]{1,0:T(1,128)S(1)}, u32[]{:S(2)}, u32[]{:S(2)}) collective-permute-start(f32[1,1024]{1,0:T(1,128)S(1)} %add.191), channel_id=1, source_target_pairs={{0,3},{1,2},{2,1},{3,0},{4,7},{5,6},{6,5},{7,4},{8,11},{9,10},{10,... | collective-permute-start | bytes 12296 | tf_op jit(solution)/shard_map/ppermute | solution.py:21
  20.6 7.4 %collective-permute-start.18 = (f32[1,1024]{1,0:T(1,128)S(1)}, f32[1,1024]{1,0:T(1,128)S(1)}, u32[]{:S(2)}, u32[]{:S(2)}) collective-permute-start(f32[1,1024]{1,0:T(1,128)S(1)} %add.192), channel_id=1, source_target_pairs={{0,4},{1,5},{2,6},{3,7},{4,0},{5,1},{6,2},{7,3},{8,12},{9,13},{10,... | collective-permute-start | bytes 12296 | tf_op jit(solution)/shard_map/ppermute | solution.py:21
  23.7 10.4 %all-to-all-start = ((bf16[8,16,448]{2,1,0:T(8,128)(2,1)}), bf16[8,16,448]{2,1,0:T(8,128)(2,1)S(1)}, u32[]{:S(2)}, u32[]{:S(2)}) async-start(bf16[8,16,448]{2,1,0:T(8,128)(2,1)} %bitcast.3), calls=%async_computation | async-start | bytes 262144 | tf_op jit(solution)/shard_map/all_to_all | solution.py:230
  28.0 5.8 %collective-permute-start.19 = (f32[1,1024]{1,0:T(1,128)S(1)}, f32[1,1024]{1,0:T(1,128)S(1)}, u32[]{:S(2)}, u32[]{:S(2)}) collective-permute-start(f32[1,1024]{1,0:T(1,128)S(1)} %add.193), channel_id=1, source_target_pairs={{0,12},{1,13},{2,14},{3,15},{4,8},{5,9},{6,10},{7,11},{8,4},{9,5},... | collective-permute-start | bytes 12296 | tf_op jit(solution)/shard_map/ppermute | solution.py:21
  34.3 5.9 %collective-permute-start.6 = (bf16[1,112,128]{2,1,0:T(8,128)(2,1)S(1)}, bf16[1,112,128]{2,1,0:T(8,128)(2,1)S(1)}, u32[]{:S(2)}, u32[]{:S(2)}) collective-permute-start(bf16[1,112,128]{2,1,0:T(8,128)(2,1)S(1)} %get-tuple-element.91), channel_id=1, source_target_pairs={{0,12},{1,13},{2,14},{3,15},{4,8},{5,9},{6,10},{7,11},{8,4},{9,5},... | collective-permute-start | bytes 86024 | tf_op jit(solution)/shard_map/ppermute | solution.py:21
  36.9 5.4 %collective-permute-start.4 = (bf16[1,112,128]{2,1,0:T(8,128)(2,1)S(1)}, bf16[1,112,128]{2,1,0:T(8,128)(2,1)S(1)}, u32[]{:S(2)}, u32[]{:S(2)}) collective-permute-start(bf16[1,112,128]{2,1,0:T(8,128)(2,1)S(1)} %get-tuple-element.92), channel_id=1, source_target_pairs={{0,4},{1,5},{2,6},{3,7},{4,0},{5,1},{6,2},{7,3},{8,12},{9,13},{10,... | collective-permute-start | bytes 86024 | tf_op jit(solution)/shard_map/ppermute | solution.py:21
  38.0 5.1 %collective-permute-start.2 = (bf16[1,112,128]{2,1,0:T(8,128)(2,1)S(1)}, bf16[1,112,128]{2,1,0:T(8,128)(2,1)S(1)}, u32[]{:S(2)}, u32[]{:S(2)}) collective-permute-start(bf16[1,112,128]{2,1,0:T(8,128)(2,1)S(1)} %get-tuple-element.93), channel_id=1, source_target_pairs={{0,3},{1,2},{2,1},{3,0},{4,7},{5,6},{6,5},{7,4},{8,11},{9,10},{10,... | collective-permute-start | bytes 86024 | tf_op jit(solution)/shard_map/ppermute | solution.py:21
  40.2 4.0 %collective-permute-start = (bf16[1,112,128]{2,1,0:T(8,128)(2,1)S(1)}, bf16[1,112,128]{2,1,0:T(8,128)(2,1)S(1)}, u32[]{:S(2)}, u32[]{:S(2)}) collective-permute-start(bf16[1,112,128]{2,1,0:T(8,128)(2,1)S(1)} %get-tuple-element.94), channel_id=1, source_target_pairs={{0,1},{1,0},{2,3},{3,2},{4,5},{5,4},{6,7},{7,6},{8,9},{9,8},{10,11... | collective-permute-start | bytes 86024 | tf_op jit(solution)/shard_map/ppermute | solution.py:21
  40.2 20.0 %collective-permute-start.7 = (bf16[2,112,128]{2,1,0:T(8,128)(2,1)S(1)}, bf16[2,112,128]{2,1,0:T(8,128)(2,1)S(1)}, u32[]{:S(2)}, u32[]{:S(2)}) collective-permute-start(bf16[2,112,128]{2,1,0:T(8,128)(2,1)S(1)} %pad_maximum_fusion.12), channel_id=1, source_target_pairs={{0,1},{1,0},{2,3},{3,2},{4,5},{5,4},{6,7},{7,6},{8,9},{9,8},{10,11... | collective-permute-start | bytes 172040 | tf_op jit(solution)/shard_map/ppermute | solution.py:21
  42.3 17.9 %collective-permute-start.5 = (bf16[2,112,128]{2,1,0:T(8,128)(2,1)S(1)}, bf16[2,112,128]{2,1,0:T(8,128)(2,1)S(1)}, u32[]{:S(2)}, u32[]{:S(2)}) collective-permute-start(bf16[2,112,128]{2,1,0:T(8,128)(2,1)S(1)} %pad_maximum_fusion.11), channel_id=1, source_target_pairs={{0,12},{1,13},{2,14},{3,15},{4,8},{5,9},{6,10},{7,11},{8,4},{9,5},... | collective-permute-start | bytes 172040 | tf_op jit(solution)/shard_map/ppermute | solution.py:21
  43.1 17.1 %collective-permute-start.3 = (bf16[2,112,128]{2,1,0:T(8,128)(2,1)S(1)}, bf16[2,112,128]{2,1,0:T(8,128)(2,1)S(1)}, u32[]{:S(2)}, u32[]{:S(2)}) collective-permute-start(bf16[2,112,128]{2,1,0:T(8,128)(2,1)S(1)} %pad_maximum_fusion.10), channel_id=1, source_target_pairs={{0,4},{1,5},{2,6},{3,7},{4,0},{5,1},{6,2},{7,3},{8,12},{9,13},{10,... | collective-permute-start | bytes 172040 | tf_op jit(solution)/shard_map/ppermute | solution.py:21
  44.2 16.0 %collective-permute-start.1 = (bf16[2,112,128]{2,1,0:T(8,128)(2,1)S(1)}, bf16[2,112,128]{2,1,0:T(8,128)(2,1)S(1)}, u32[]{:S(2)}, u32[]{:S(2)}) collective-permute-start(bf16[2,112,128]{2,1,0:T(8,128)(2,1)S(1)} %pad_maximum_fusion.9), channel_id=1, source_target_pairs={{0,3},{1,2},{2,1},{3,0},{4,7},{5,6},{6,5},{7,4},{8,11},{9,10},{10,... | collective-permute-start | bytes 172040 | tf_op jit(solution)/shard_map/ppermute | solution.py:21
  60.9 12.4 %collective-permute-start.11 = (bf16[4,112,128]{2,1,0:T(8,128)(2,1)}, bf16[4,112,128]{2,1,0:T(8,128)(2,1)}, u32[]{:S(2)}, u32[]{:S(2)}) collective-permute-start(bf16[4,112,128]{2,1,0:T(8,128)(2,1)} %pad_maximum_fusion.8), channel_id=1, source_target_pairs={{0,3},{1,2},{2,1},{3,0},{4,7},{5,6},{6,5},{7,4},{8,11},{9,10},{10,... | collective-permute-start | bytes 344072 | tf_op jit(solution)/shard_map/ppermute | solution.py:21
  63.0 10.3 %collective-permute-start.10 = (bf16[4,112,128]{2,1,0:T(8,128)(2,1)}, bf16[4,112,128]{2,1,0:T(8,128)(2,1)}, u32[]{:S(2)}, u32[]{:S(2)}) collective-permute-start(bf16[4,112,128]{2,1,0:T(8,128)(2,1)} %pad_maximum_fusion.7), channel_id=1, source_target_pairs={{0,1},{1,0},{2,3},{3,2},{4,5},{5,4},{6,7},{7,6},{8,9},{9,8},{10,11... | collective-permute-start | bytes 344072 | tf_op jit(solution)/shard_map/ppermute | solution.py:21
  63.7 9.6 %collective-permute-start.9 = (bf16[4,112,128]{2,1,0:T(8,128)(2,1)}, bf16[4,112,128]{2,1,0:T(8,128)(2,1)}, u32[]{:S(2)}, u32[]{:S(2)}) collective-permute-start(bf16[4,112,128]{2,1,0:T(8,128)(2,1)} %pad_maximum_fusion.6), channel_id=1, source_target_pairs={{0,12},{1,13},{2,14},{3,15},{4,8},{5,9},{6,10},{7,11},{8,4},{9,5},... | collective-permute-start | bytes 344072 | tf_op jit(solution)/shard_map/ppermute | solution.py:21
  66.6 7.5 %collective-permute-start.8 = (bf16[4,112,128]{2,1,0:T(8,128)(2,1)}, bf16[4,112,128]{2,1,0:T(8,128)(2,1)}, u32[]{:S(2)}, u32[]{:S(2)}) collective-permute-start(bf16[4,112,128]{2,1,0:T(8,128)(2,1)} %pad_maximum_fusion.5), channel_id=1, source_target_pairs={{0,4},{1,5},{2,6},{3,7},{4,0},{5,1},{6,2},{7,3},{8,12},{9,13},{10,... | collective-permute-start | bytes 344072 | tf_op jit(solution)/shard_map/ppermute | solution.py:21
  75.1 12.0 %collective-permute-start.15 = (bf16[8,112,128]{2,1,0:T(8,128)(2,1)S(1)}, bf16[8,112,128]{2,1,0:T(8,128)(2,1)S(1)}, u32[]{:S(2)}, u32[]{:S(2)}) collective-permute-start(bf16[8,112,128]{2,1,0:T(8,128)(2,1)S(1)} %pad_maximum_fusion.4), channel_id=1, source_target_pairs={{0,4},{1,5},{2,6},{3,7},{4,0},{5,1},{6,2},{7,3},{8,12},{9,13},{10,... | collective-permute-start | bytes 688136 | tf_op jit(solution)/shard_map/ppermute | solution.py:21
  76.9 18.2 %copy-start.2 = (f32[7168,1]{1,0:T(8,128)S(1)}, f32[7168,1]{1,0:T(8,128)}, u32[]{:S(2)}) copy-start(f32[7168,1]{1,0:T(8,128)} %copy.45.gain_ref) | copy-start | bytes 86020
  76.9 13.1 %collective-permute-start.14 = (bf16[8,112,128]{2,1,0:T(8,128)(2,1)S(1)}, bf16[8,112,128]{2,1,0:T(8,128)(2,1)S(1)}, u32[]{:S(2)}, u32[]{:S(2)}) collective-permute-start(bf16[8,112,128]{2,1,0:T(8,128)(2,1)S(1)} %pad_maximum_fusion.3), channel_id=1, source_target_pairs={{0,3},{1,2},{2,1},{3,0},{4,7},{5,6},{6,5},{7,4},{8,11},{9,10},{10,... | collective-permute-start | bytes 688136 | tf_op jit(solution)/shard_map/ppermute | solution.py:21
  79.1 12.1 %collective-permute-start.13 = (bf16[8,112,128]{2,1,0:T(8,128)(2,1)S(1)}, bf16[8,112,128]{2,1,0:T(8,128)(2,1)S(1)}, u32[]{:S(2)}, u32[]{:S(2)}) collective-permute-start(bf16[8,112,128]{2,1,0:T(8,128)(2,1)S(1)} %pad_maximum_fusion.2), channel_id=1, source_target_pairs={{0,1},{1,0},{2,3},{3,2},{4,5},{5,4},{6,7},{7,6},{8,9},{9,8},{10,11... | collective-permute-start | bytes 688136 | tf_op jit(solution)/shard_map/ppermute | solution.py:21
  81.9 13.1 %collective-permute-start.12 = (bf16[8,112,128]{2,1,0:T(8,128)(2,1)S(1)}, bf16[8,112,128]{2,1,0:T(8,128)(2,1)S(1)}, u32[]{:S(2)}, u32[]{:S(2)}) collective-permute-start(bf16[8,112,128]{2,1,0:T(8,128)(2,1)S(1)} %pad_maximum_fusion.1), channel_id=1, source_target_pairs={{0,12},{1,13},{2,14},{3,15},{4,8},{5,9},{6,10},{7,11},{8,4},{9,5},... | collective-permute-start | bytes 688136 | tf_op jit(solution)/shard_map/ppermute | solution.py:21
  120.7 24.6 %collective-permute-start.22 = (bf16[8,448,128]{2,1,0:T(8,128)(2,1)}, bf16[8,448,128]{2,1,0:T(8,128)(2,1)S(1)}, u32[]{:S(2)}, u32[]{:S(2)}) collective-permute-start(bf16[8,448,128]{2,1,0:T(8,128)(2,1)} %get-tuple-element.65), channel_id=1, source_target_pairs={{0,12},{1,13},{2,14},{3,15},{4,8},{5,9},{6,10},{7,11},{8,4},{9,5},... | collective-permute-start | bytes 2752520 | tf_op jit(solution)/shard_map/ppermute | solution.py:21
  139.8 41.8 %collective-permute-start.20 = (bf16[8,448,256]{2,1,0:T(8,128)(2,1)}, bf16[8,448,256]{2,1,0:T(8,128)(2,1)}, u32[]{:S(2)}, u32[]{:S(2)}) collective-permute-start(bf16[8,448,256]{2,1,0:T(8,128)(2,1)} %get-tuple-element.62), channel_id=1, source_target_pairs={{0,1},{1,0},{2,3},{3,2},{4,5},{5,4},{6,7},{7,6},{8,9},{9,8},{10,11... | collective-permute-start | bytes 5505032 | tf_op jit(solution)/shard_map/ppermute | solution.py:21
  143.3 41.6 %collective-permute-start.34 = (bf16[8,448,256]{2,1,0:T(8,128)(2,1)}, bf16[8,448,256]{2,1,0:T(8,128)(2,1)}, u32[]{:S(2)}, u32[]{:S(2)}) collective-permute-start(bf16[8,448,256]{2,1,0:T(8,128)(2,1)} %get-tuple-element.78), channel_id=1, source_target_pairs={{0,4},{1,5},{2,6},{3,7},{4,0},{5,1},{6,2},{7,3},{8,12},{9,13},{10,... | collective-permute-start | bytes 5505032 | tf_op jit(solution)/shard_map/ppermute | solution.py:21
  143.4 46.0 %collective-permute-start.27 = (bf16[8,448,256]{2,1,0:T(8,128)(2,1)}, bf16[8,448,256]{2,1,0:T(8,128)(2,1)}, u32[]{:S(2)}, u32[]{:S(2)}) collective-permute-start(bf16[8,448,256]{2,1,0:T(8,128)(2,1)} %get-tuple-element.71), channel_id=1, source_target_pairs={{0,3},{1,2},{2,1},{3,0},{4,7},{5,6},{6,5},{7,4},{8,11},{9,10},{10,... | collective-permute-start | bytes 5505032 | tf_op jit(solution)/shard_map/ppermute | solution.py:21
  145.3 46.5 %collective-permute-start.23 = (bf16[8,448,256]{2,1,0:T(8,128)(2,1)}, bf16[8,448,256]{2,1,0:T(8,128)(2,1)}, u32[]{:S(2)}, u32[]{:S(2)}) collective-permute-start(bf16[8,448,256]{2,1,0:T(8,128)(2,1)} %get-tuple-element.66), channel_id=1, source_target_pairs={{0,12},{1,13},{2,14},{3,15},{4,8},{5,9},{6,10},{7,11},{8,4},{9,5},... | collective-permute-start | bytes 5505032 | tf_op jit(solution)/shard_map/ppermute | solution.py:21
  152.9 34.2 %copy-start.7 = (bf16[8,448,256]{2,1,0:T(8,128)(2,1)}, bf16[8,448,256]{2,1,0:T(8,128)(2,1)S(1)}, u32[]{:S(2)}) copy-start(bf16[8,448,256]{2,1,0:T(8,128)(2,1)S(1)} %get-tuple-element.61) | copy-start | bytes 5505028
  152.9 34.2 %copy-start.8 = (bf16[8,448,256]{2,1,0:T(8,128)(2,1)}, bf16[8,448,256]{2,1,0:T(8,128)(2,1)S(1)}, u32[]{:S(2)}) copy-start(bf16[8,448,256]{2,1,0:T(8,128)(2,1)S(1)} %get-tuple-element.77) | copy-start | bytes 5505028
  152.9 36.5 %copy-start.6 = (bf16[8,448,256]{2,1,0:T(8,128)(2,1)}, bf16[8,448,256]{2,1,0:T(8,128)(2,1)S(1)}, u32[]{:S(2)}) copy-start(bf16[8,448,256]{2,1,0:T(8,128)(2,1)S(1)} %get-tuple-element.70) | copy-start | bytes 5505028
  184.0 34.1 %collective-permute-start.21 = (bf16[4,448,256]{2,1,0:T(8,128)(2,1)}, bf16[4,448,256]{2,1,0:T(8,128)(2,1)}, u32[]{:S(2)}, u32[]{:S(2)}) collective-permute-start(bf16[4,448,256]{2,1,0:T(8,128)(2,1)} %add_convert_fusion.4), channel_id=1, source_target_pairs={{0,3},{1,2},{2,1},{3,0},{4,7},{5,6},{6,5},{7,4},{8,11},{9,10},{10,... | collective-permute-start | bytes 2752520 | tf_op jit(solution)/shard_map/ppermute | solution.py:21
  187.1 22.2 %collective-permute-start.35 = (bf16[4,448,256]{2,1,0:T(8,128)(2,1)}, bf16[4,448,256]{2,1,0:T(8,128)(2,1)}, u32[]{:S(2)}, u32[]{:S(2)}) collective-permute-start(bf16[4,448,256]{2,1,0:T(8,128)(2,1)} %add_convert_fusion.1), channel_id=1, source_target_pairs={{0,12},{1,13},{2,14},{3,15},{4,8},{5,9},{6,10},{7,11},{8,4},{9,5},... | collective-permute-start | bytes 2752520 | tf_op jit(solution)/shard_map/ppermute | solution.py:21
  191.8 23.6 %collective-permute-start.28 = (bf16[4,448,256]{2,1,0:T(8,128)(2,1)}, bf16[4,448,256]{2,1,0:T(8,128)(2,1)}, u32[]{:S(2)}, u32[]{:S(2)}) collective-permute-start(bf16[4,448,256]{2,1,0:T(8,128)(2,1)} %add_convert_fusion.3), channel_id=1, source_target_pairs={{0,4},{1,5},{2,6},{3,7},{4,0},{5,1},{6,2},{7,3},{8,12},{9,13},{10,... | collective-permute-start | bytes 2752520 | tf_op jit(solution)/shard_map/ppermute | solution.py:21
  196.0 27.6 %collective-permute-start.24 = (bf16[4,448,128]{1,2,0:T(8,128)(2,1)S(1)}, bf16[4,448,128]{1,2,0:T(8,128)(2,1)S(1)}, u32[]{:S(2)}, u32[]{:S(2)}) collective-permute-start(bf16[4,448,128]{1,2,0:T(8,128)(2,1)S(1)} %constant_dynamic-slice_fusion.2), channel_id=1, source_target_pairs={{0,4},{1,5},{2,6},{3,7},{4,0},{5,1},{6,2},{7,3},{8,12},{9,13},{10,... | collective-permute-start | bytes 1376264 | tf_op jit(solution)/shard_map/ppermute | solution.py:21
  199.5 41.9 %collective-permute-start.30 = (bf16[4,448,256]{2,1,0:T(8,128)(2,1)S(1)}, bf16[4,448,256]{2,1,0:T(8,128)(2,1)S(1)}, u32[]{:S(2)}, u32[]{:S(2)}) collective-permute-start(bf16[4,448,256]{2,1,0:T(8,128)(2,1)S(1)} %add_convert_fusion.2), channel_id=1, source_target_pairs={{0,1},{1,0},{2,3},{3,2},{4,5},{5,4},{6,7},{7,6},{8,9},{9,8},{10,11... | collective-permute-start | bytes 2752520 | tf_op jit(solution)/shard_map/ppermute | solution.py:21
  210.7 18.5 %collective-permute-start.36 = (bf16[2,448,256]{2,1,0:T(8,128)(2,1)S(1)}, bf16[2,448,256]{2,1,0:T(8,128)(2,1)S(1)}, u32[]{:S(2)}, u32[]{:S(2)}) collective-permute-start(bf16[2,448,256]{2,1,0:T(8,128)(2,1)S(1)} %add_convert_fusion.7), channel_id=1, source_target_pairs={{0,1},{1,0},{2,3},{3,2},{4,5},{5,4},{6,7},{7,6},{8,9},{9,8},{10,11... | collective-permute-start | bytes 1376264 | tf_op jit(solution)/shard_map/ppermute | solution.py:21
  216.9 33.0 %collective-permute-start.29 = (bf16[2,448,256]{2,1,0:T(8,128)(2,1)S(1)}, bf16[2,448,256]{2,1,0:T(8,128)(2,1)S(1)}, u32[]{:S(2)}, u32[]{:S(2)}) collective-permute-start(bf16[2,448,256]{2,1,0:T(8,128)(2,1)S(1)} %add_convert_fusion.8), channel_id=1, source_target_pairs={{0,12},{1,13},{2,14},{3,15},{4,8},{5,9},{6,10},{7,11},{8,4},{9,5},... | collective-permute-start | bytes 1376264 | tf_op jit(solution)/shard_map/ppermute | solution.py:21
  225.1 20.1 %collective-permute-start.25 = (bf16[2,448,256]{2,1,0:T(8,128)(2,1)S(1)}, bf16[2,448,256]{2,1,0:T(8,128)(2,1)S(1)}, u32[]{:S(2)}, u32[]{:S(2)}) collective-permute-start(bf16[2,448,256]{2,1,0:T(8,128)(2,1)S(1)} %add_convert_fusion.9), channel_id=1, source_target_pairs={{0,4},{1,5},{2,6},{3,7},{4,0},{5,1},{6,2},{7,3},{8,12},{9,13},{10,... | collective-permute-start | bytes 1376264 | tf_op jit(solution)/shard_map/ppermute | solution.py:21
  230.4 8.2 %collective-permute-start.37 = (bf16[1,448,256]{2,1,0:T(8,128)(2,1)S(1)}, bf16[1,448,256]{2,1,0:T(8,128)(2,1)S(1)}, u32[]{:S(2)}, u32[]{:S(2)}) collective-permute-start(bf16[1,448,256]{2,1,0:T(8,128)(2,1)S(1)} %add_convert_fusion.12), channel_id=1, source_target_pairs={{0,3},{1,2},{2,1},{3,0},{4,7},{5,6},{6,5},{7,4},{8,11},{9,10},{10,... | collective-permute-start | bytes 688136 | tf_op jit(solution)/shard_map/ppermute | solution.py:21
  232.0 9.3 %collective-permute-start.31 = (bf16[2,448,128]{1,2,0:T(8,128)(2,1)S(1)}, bf16[2,448,128]{1,2,0:T(8,128)(2,1)S(1)}, u32[]{:S(2)}, u32[]{:S(2)}) collective-permute-start(bf16[2,448,128]{1,2,0:T(8,128)(2,1)S(1)} %constant_dynamic-slice_fusion.1), channel_id=1, source_target_pairs={{0,3},{1,2},{2,1},{3,0},{4,7},{5,6},{6,5},{7,4},{8,11},{9,10},{10,... | collective-permute-start | bytes 688136 | tf_op jit(solution)/shard_map/ppermute | solution.py:21
  241.5 7.7 %collective-permute-start.32 = (bf16[1,448,128]{1,2,0:T(8,128)(2,1)S(1)}, bf16[1,448,128]{1,2,0:T(8,128)(2,1)S(1)}, u32[]{:S(2)}, u32[]{:S(2)}) collective-permute-start(bf16[1,448,128]{1,2,0:T(8,128)(2,1)S(1)} %constant_dynamic-slice_fusion), channel_id=1, source_target_pairs={{0,1},{1,0},{2,3},{3,2},{4,5},{5,4},{6,7},{7,6},{8,9},{9,8},{10,11... | collective-permute-start | bytes 344072 | tf_op jit(solution)/shard_map/ppermute | solution.py:21
  243.7 16.7 %collective-permute-start.38 = (bf16[2,448,256]{2,1,0:T(8,128)(2,1)}, bf16[2,448,256]{2,1,0:T(8,128)(2,1)}, u32[]{:S(2)}, u32[]{:S(2)}) collective-permute-start(bf16[2,448,256]{2,1,0:T(8,128)(2,1)} %add_convert_fusion.6), channel_id=1, source_target_pairs={{0,3},{1,2},{2,1},{3,0},{4,7},{5,6},{6,5},{7,4},{8,11},{9,10},{10,... | collective-permute-start | bytes 1376264 | tf_op jit(solution)/shard_map/ppermute | solution.py:21
  247.3 10.8 %collective-permute-start.26 = (bf16[1,448,256]{2,1,0:T(8,128)(2,1)}, bf16[1,448,256]{2,1,0:T(8,128)(2,1)}, u32[]{:S(2)}, u32[]{:S(2)}) collective-permute-start(bf16[1,448,256]{2,1,0:T(8,128)(2,1)} %add_convert_fusion.14), channel_id=1, source_target_pairs={{0,12},{1,13},{2,14},{3,15},{4,8},{5,9},{6,10},{7,11},{8,4},{9,5},... | collective-permute-start | bytes 688136 | tf_op jit(solution)/shard_map/ppermute | solution.py:21
  252.6 9.2 %collective-permute-start.33 = (bf16[1,448,256]{2,1,0:T(8,128)(2,1)}, bf16[1,448,256]{2,1,0:T(8,128)(2,1)}, u32[]{:S(2)}, u32[]{:S(2)}) collective-permute-start(bf16[1,448,256]{2,1,0:T(8,128)(2,1)} %add_convert_fusion.13), channel_id=1, source_target_pairs={{0,1},{1,0},{2,3},{3,2},{4,5},{5,4},{6,7},{7,6},{8,9},{9,8},{10,11... | collective-permute-start | bytes 688136 | tf_op jit(solution)/shard_map/ppermute | solution.py:21
  253.8 17.2 %all-to-all-start.1 = ((bf16[8,16,448]{2,1,0:T(8,128)(2,1)}), bf16[8,16,448]{2,1,0:T(8,128)(2,1)}, u32[]{:S(2)}, u32[]{:S(2)}) async-start(bf16[8,16,448]{2,1,0:T(8,128)(2,1)} %bitcast.21), calls=%async_computation.1 | async-start | bytes 262144 | tf_op jit(solution)/shard_map/all_to_all | solution.py:298
  261.7 8.1 %collective-permute-start.39 = (bf16[1,448,256]{2,1,0:T(8,128)(2,1)S(1)}, bf16[1,448,256]{2,1,0:T(8,128)(2,1)S(1)}, u32[]{:S(2)}, u32[]{:S(2)}) collective-permute-start(bf16[1,448,256]{2,1,0:T(8,128)(2,1)S(1)} %add_convert_fusion.11), channel_id=1, source_target_pairs={{0,4},{1,5},{2,6},{3,7},{4,0},{5,1},{6,2},{7,3},{8,12},{9,13},{10,... | collective-permute-start | bytes 688136 | tf_op jit(solution)/shard_map/ppermute | solution.py:21
  (14 other events, 82.2 us)
Sparse Core Ops, SparseCore 0:
  9.5 111.1 all-gather.1

commit v9 on v7

--- a/solution.py
+++ b/solution.py
@@ -270,7 +270,7 @@
         for s in range(4):
             terms[s].append(flip_local(added(s, half, 2 * half).astype(jnp.bfloat16), STREAMS[s][step]))
         if step == 1:
-            terms[3][-1], expert_out = lax.optimization_barrier((terms[3][-1], expert_out))
+            terms[0][-1], expert_out = lax.optimization_barrier((terms[0][-1], expert_out))
             returned = lax.all_to_all(
                 expert_out.T.reshape(node_count, NODE_CAP, slice_width), "node", split_axis=0, concat_axis=0, tiled=True
             ).reshape(slot_count, slice_width)

time: 277 us -> 281 us (1.014)
  waiting for transfers between devices: 91.8 us -> 99.7 us
  starting transfers between devices: 59.5 us -> 56.5 us
    all_to_all x1, waiting for transfers between devices: 0.01 us -> 4 us  [shards(): lax.all_to_all(expert_out.T.reshape(node_count, NODE_CAP, slice_width), '...]
    ppermute x36, waiting for transfers between devices: 80.2 us -> 84 us  [flip_local(): lax.ppermute(array, 'local', [(i, LOCAL_AT[LOCAL_LABEL[i] ^ 1 << bit]) fo...]
    ppermute x36, starting transfers between devices: 50.9 us -> 47.9 us  [flip_local(): lax.ppermute(array, 'local', [(i, LOCAL_AT[LOCAL_LABEL[i] ^ 1 << bit]) fo...]
    unnamed x50 -> x40, local copies, waits for them, and re-layouts: 10.3 us -> 10.3 us
  transfers between devices with their start and end apart: 40 -> 40, of which waited for: 16 -> 20; matrix products, arithmetic and copies ran while one was open for 24% -> 24% of each run, Pallas kernels for 6% -> 6%
where the time goes in v9:
time: 281 us; the launch traced here: 279 us
  waiting for transfers between devices  99.7 us (35%)
  starting transfers between devices  56.5 us (20%)
  other arithmetic  48.8 us (17%)
  local copies, waits for them, and re-layouts  24.4 us (9%)
  Pallas kernels  20.9 us (7%)
  matrix products  15.1 us (5%)
  between operations  13.9 us (5%)
    ppermute x36, waiting for transfers between devices, flip_local(): lax.ppermute(array, 'local', [(i, LOCAL_AT[LOCAL_LABEL[i] ^ 1 << bit]) fo...  84 us
    ppermute x36, starting transfers between devices, flip_local(): lax.ppermute(array, 'local', [(i, LOCAL_AT[LOCAL_LABEL[i] ^ 1 << bit]) fo...  47.9 us
    convert_element_type x12, other arithmetic, shards(): added(s, half, 2 * half).astype(jnp.bfloat16)  17.3 us
    dot_general x1, matrix products, transposed_dot(): lax.dot_general(weight, rows, (((0,), (0,)), ((), ())), preferred_element...  13.3 us
    all_gather x1, waiting for transfers between devices, shards(): whole_columns = lax.all_gather(columns, 'local', axis=0, tiled=True)  10.7 us
    unnamed x40, local copies, waits for them, and re-layouts  10.3 us
    pallas_call x1, Pallas kernels, expert_gate_up(): pl.pallas_call(functools.partial(expert_kernel, blocks, blocks * rows), g...  7.67 us
    convert_element_type x1, other arithmetic, shards(): (w.astype(jnp.float32) * gain_column).astype(jnp.bfloat16)  7.04 us
  transfers between devices with their start and end apart: 40, of which 20 were waited for; matrix products, arithmetic and copies ran while one was open for 24% of the time, Pallas kernels for 6%

profile of v9, /device:TPU:0, one launch (start us, length us, event | category | flops | bytes accessed | tf_op | source)
XLA Modules:
  0.0 279.2 jit_solution(4241255067299877319)
XLA Ops:
  8.7 1.7 collective-permute-start.16
  11.2 2.3 reduce-window.6
  15.7 2.3 collective-permute-start.17
  18.8 1.9 collective-permute-done.17
  20.6 1.9 collective-permute-start.18
  23.7 4.3 %all-to-all-start = ((bf16[8,16,448]{2,1,0:T(8,128)(2,1)}), bf16[8,16,448]{2,1,0:T(8,128)(2,1)S(1)}, u32[]{:S(2)}, u32[]{:S(2)}) async-start(bf16[8,16,448]{2,1,0:T(8,128)(2,1)} %bitcast.3), calls=%async_computation | async-start | bytes 262144 | tf_op jit(solution)/shard_map/all_to_all | solution.py:226
  28.1 2.6 collective-permute-start.19
  31.4 2.5 copy.33.gain_ref
  34.3 2.6 collective-permute-start.6
  38.0 2.2 collective-permute-start.2
  40.2 2.1 collective-permute-start.7
  44.2 2.3 collective-permute-start.1
  46.5 7.0 %multiply_convert_fusion.1 = (bf16[7168,256]{1,0:T(8,128)(2,1)}, bf16[7168,256]{1,0:T(8,128)(2,1)}) fusion(bf16[7168,256]{1,0:T(8,128)(2,1)} %param.13, f32[7168]{0:T(1024)S(1)} %copy-done.11, bf16[7168,256]{1,0:T(8,128)(2,1)} %param.14), kind=kLoop, calls=%fused_computation.2 | loop fusion | flops 11010048 | bytes 14708736 | tf_op jit(solution)/shard_map/convert_element_type | solution.py:242
  53.5 6.6 %pad_maximum_fusion = bf16[7168,512]{1,0:T(8,128)(2,1)} fusion(bf16[7168,256]{1,0:T(8,128)(2,1)} %get-tuple-element.78, bf16[7168,256]{1,0:T(8,128)(2,1)} %get-tuple-element.77), kind=kLoop, calls=%fused_computation | loop fusion | flops 14680064 | bytes 14680064 | tf_op jit(solution)/shard_map/concatenate | solution.py:241
  63.6 2.2 collective-permute-start.9
  67.3 5.9 %copy.32 = bf16[7168,256]{1,0:T(8,128)(2,1)} copy(bf16[7168,256]{0,1:T(8,128)(2,1)} %bitcast.67) | data formatting | bytes 7340032 | tf_op jit(solution)/shard_map/transpose | solution.py:247
  79.1 1.9 collective-permute-start.13
  87.0 2.9 %collective-permute-done.14 = bf16[8,112,128]{2,1,0:T(8,128)(2,1)S(1)} collective-permute-done((bf16[8,112,128]{2,1,0:T(8,128)(2,1)S(1)}, bf16[8,112,128]{2,1,0:T(8,128)(2,1)S(1)}, u32[]{:S(2)}, u32[]{:S(2)}) %collective-permute-start.14) | collective-permute-done | bytes 229408 | tf_op jit(solution)/shard_map/ppermute | solution.py:21
  91.1 3.8 %collective-permute-done.12 = bf16[8,112,128]{2,1,0:T(8,128)(2,1)S(1)} collective-permute-done((bf16[8,112,128]{2,1,0:T(8,128)(2,1)S(1)}, bf16[8,112,128]{2,1,0:T(8,128)(2,1)S(1)}, u32[]{:S(2)}, u32[]{:S(2)}) %collective-permute-start.12) | collective-permute-done | bytes 229408 | tf_op jit(solution)/shard_map/ppermute | solution.py:21
  95.0 2.0 copy-done.3
  97.0 2.2 copy-done.4
  99.2 7.7 %shard_map.109.hidden_ref = bf16[256,128]{1,0:T(8,128)(2,1)S(1)} custom-call(s32[16]{0:T(128)S(1)} %dynamic-slice_bitcast_fusion.at_ref.slice_ref, bf16[16,112,128]{2,1,0:T(8,128)(2,1)S(1)} %constant_dynamic-update-slice_fusion.x0, bf16[16,112,128]{2,1,0:T(8,128)(2,1)S(1)} %constant_dynamic-update-slice_fusion.5.x1, ...), custom_call_target="tpu_custom_call" | custom-call | flops 939524096 | bytes 9175040 | tf_op jit(solution)/shard_map/pallas_call | solution.py:147
  106.9 3.1 %shard_map.110 = bf16[7168,128]{1,0:T(8,128)(2,1)} custom-call(bf16[1,256,7168]{2,1,0:T(8,128)(2,1)S(1)} %copy-done.5, bf16[256,128]{1,0:T(8,128)(2,1)S(1)} %shard_map.109.hidden_ref), custom_call_target="tpu_custom_call" | custom-call | flops 469762048 | bytes 5505024 | tf_op jit(solution)/shard_map/pallas_call | solution.py:179
  110.0 10.7 %all-gather.2.cloned.1.call-done = bf16[7168,1024]{1,0:T(8,128)(2,1)} async-done(((bf16[448,1024]{1,0:T(8,128)(2,1)}), bf16[7168,1024]{1,0:T(8,128)(2,1)}) %all-gather.2.cloned.1.call-update) | async-done | bytes 14680080 | tf_op jit(solution)/shard_map/all_gather | solution.py:216
  120.7 13.3 %fusion.10.gate_up_ref = f32[512,1024]{1,0:T(8,128)S(1)} fusion(bf16[7168,512]{1,0:T(8,128)(2,1)} %pad_maximum_fusion, bf16[7168,1024]{1,0:T(8,128)(2,1)} %all-gather.2.cloned.1.call-done), kind=kOutput, calls=%fused_computation.84 | convolution fusion | flops 7516192768 | bytes 24117248 | tf_op jit(solution)/shard_map/dot_general | solution.py:36
  134.1 3.2 %shard_map.111 = (bf16[256,512]{1,0:T(8,128)(2,1)S(1)}, bf16[8,448,256]{2,1,0:T(8,128)(2,1)}, bf16[8,448,256]{2,1,0:T(8,128)(2,1)}) custom-call(s32[16]{0:T(128)S(1)} %dynamic-slice_bitcast_fusion.at_ref.slice_ref, f32[512,1024]{1,0:T(8,128)S(1)} %fusion.10.gate_up_ref, f32[1,1024]{1,0:T(1,128)S(1)} %add_rsqrt_fusion.scale_ref, ...), custom_call_target="tpu_custom_call" | custom-call | flops 939524096 | bytes 7340032 | tf_op jit(solution)/shard_map/pallas_call | solution.py:66
  137.2 2.7 collective-permute-start.24
  139.9 3.1 %shard_map.112 = (bf16[256,512]{1,0:T(8,128)(2,1)S(1)}, bf16[8,448,256]{2,1,0:T(8,128)(2,1)}, bf16[8,448,256]{2,1,0:T(8,128)(2,1)}) custom-call(s32[16]{0:T(128)S(1)} %dynamic-slice_bitcast_fusion.at_ref.slice_ref, f32[512,1024]{1,0:T(8,128)S(1)} %fusion.10.gate_up_ref, f32[1,1024]{1,0:T(1,128)S(1)} %add_rsqrt_fusion.scale_ref, ...), custom_call_target="tpu_custom_call" | custom-call | flops 939524096 | bytes 7340032 | tf_op jit(solution)/shard_map/pallas_call | solution.py:66
  143.2 1.9 collective-permute-start.32
  145.4 2.0 copy-done.1
  147.4 3.8 %shard_map.113 = (bf16[8,448,256]{2,1,0:T(8,128)(2,1)S(1)}, bf16[8,448,256]{2,1,0:T(8,128)(2,1)S(1)}, bf16[8,448,256]{2,1,0:T(8,128)(2,1)S(1)}, bf16[8,448,256]{2,1,0:T(8,128)(2,1)S(1)}) custom-call(s32[16]{0:T(128)S(1)} %dynamic-slice_bitcast_fusion.at_ref.slice_ref, bf16[16,448,256]{2,1,0:T(8,128)(2,1)S(1)} %bitcast.62, ...), custom_call_target="tpu_custom_call" | custom-call | flops 1879048192 | bytes 14680064 | tf_op jit(solution)/shard_map/pallas_call | solution.py:96
  151.2 34.3 %collective-permute-done.24 = bf16[8,448,256]{2,1,0:T(8,128)(2,1)} collective-permute-done((bf16[8,448,256]{2,1,0:T(8,128)(2,1)}, bf16[8,448,256]{2,1,0:T(8,128)(2,1)}, u32[]{:S(2)}, u32[]{:S(2)}) %collective-permute-start.24) | collective-permute-done | bytes 1835040 | tf_op jit(solution)/shard_map/ppermute | solution.py:21
  188.5 4.2 %collective-permute-done.28 = bf16[8,448,256]{2,1,0:T(8,128)(2,1)} collective-permute-done((bf16[8,448,256]{2,1,0:T(8,128)(2,1)}, bf16[8,448,256]{2,1,0:T(8,128)(2,1)}, u32[]{:S(2)}, u32[]{:S(2)}) %collective-permute-start.28) | collective-permute-done | bytes 1835040 | tf_op jit(solution)/shard_map/ppermute | solution.py:21
  198.4 2.2 collective-permute-start.21
  200.6 11.8 %collective-permute-done.25 = bf16[4,448,256]{2,1,0:T(8,128)(2,1)S(1)} collective-permute-done((bf16[4,448,256]{2,1,0:T(8,128)(2,1)S(1)}, bf16[4,448,256]{2,1,0:T(8,128)(2,1)S(1)}, u32[]{:S(2)}, u32[]{:S(2)}) %collective-permute-start.25) | collective-permute-done | bytes 917536 | tf_op jit(solution)/shard_map/ppermute | solution.py:21
  213.9 1.7 collective-permute-done.29
  217.0 2.3 add_convert_fusion.4
  219.3 2.6 collective-permute-start.34
  221.9 4.8 %collective-permute-done.26 = bf16[2,448,256]{2,1,0:T(8,128)(2,1)S(1)} collective-permute-done((bf16[2,448,256]{2,1,0:T(8,128)(2,1)S(1)}, bf16[2,448,256]{2,1,0:T(8,128)(2,1)S(1)}, u32[]{:S(2)}, u32[]{:S(2)}) %collective-permute-start.26) | collective-permute-done | bytes 458784 | tf_op jit(solution)/shard_map/ppermute | solution.py:21
  229.2 2.3 collective-permute-start.31
  231.4 2.5 collective-permute-done.27
  233.9 1.9 add_bitcast_fusion.2
  236.7 1.9 add_bitcast_fusion.1
  240.2 4.3 %all-to-all-start.1 = ((bf16[8,16,448]{2,1,0:T(8,128)(2,1)}), bf16[8,16,448]{2,1,0:T(8,128)(2,1)S(1)}, u32[]{:S(2)}, u32[]{:S(2)}) async-start(bf16[8,16,448]{2,1,0:T(8,128)(2,1)} %bitcast.18), calls=%async_computation.2 | async-start | bytes 262144 | tf_op jit(solution)/shard_map/all_to_all | solution.py:274
  244.5 2.1 add_convert_fusion.7
  246.6 4.0 %all-to-all-done.1 = bf16[8,16,448]{2,1,0:T(8,128)(2,1)S(1)} async-done(((bf16[8,16,448]{2,1,0:T(8,128)(2,1)}), bf16[8,16,448]{2,1,0:T(8,128)(2,1)S(1)}, u32[]{:S(2)}, u32[]{:S(2)}) %all-to-all-start.1) | async-done | bytes 114720 | tf_op jit(solution)/shard_map/all_to_all | solution.py:274
  252.2 8.0 %collective-permute-done.22 = bf16[2,448,256]{2,1,0:T(8,128)(2,1)} collective-permute-done((bf16[2,448,256]{2,1,0:T(8,128)(2,1)}, bf16[2,448,256]{2,1,0:T(8,128)(2,1)}, u32[]{:S(2)}, u32[]{:S(2)}) %collective-permute-start.22) | collective-permute-done | bytes 458784 | tf_op jit(solution)/shard_map/ppermute | solution.py:21
  266.1 3.6 %collective-permute-done.23 = bf16[1,448,256]{2,1,0:T(8,128)(2,1)S(1)} collective-permute-done((bf16[1,448,256]{2,1,0:T(8,128)(2,1)S(1)}, bf16[1,448,256]{2,1,0:T(8,128)(2,1)S(1)}, u32[]{:S(2)}, u32[]{:S(2)}) %collective-permute-start.23) | collective-permute-done | bytes 229408 | tf_op jit(solution)/shard_map/ppermute | solution.py:21
  (145 shorter events, 56.3 us)
Async XLA Ops:
  6.5 114.2 %all-gather.2.cloned.1.call-start = ((), (), s32[]{:S(2)}) async-start(), calls=%async_computation.3 | async-start | bytes 15597568 | tf_op jit(solution)/shard_map/all_gather | solution.py:216
  8.7 7.1 %collective-permute-start.16 = (f32[1,1024]{1,0:T(1,128)S(1)}, f32[1,1024]{1,0:T(1,128)S(1)}, u32[]{:S(2)}, u32[]{:S(2)}) collective-permute-start(f32[1,1024]{1,0:T(1,128)S(1)} %bitcast.73), channel_id=1, source_target_pairs={{0,1},{1,0},{2,3},{3,2},{4,5},{5,4},{6,7},{7,6},{8,9},{9,8},{10,11... | collective-permute-start | bytes 12296 | tf_op jit(solution)/shard_map/ppermute | solution.py:21
  14.1 8.5 %copy-start.7 = (bf16[1024,448]{0,1:T(8,128)(2,1)S(1)}, bf16[1024,448]{0,1:T(8,128)(2,1)}, u32[]{:S(2)}) copy-start(bf16[1024,448]{0,1:T(8,128)(2,1)} %param.11) | copy-start | bytes 2752516
  15.4 16.0 %copy-start.11 = (f32[7168]{0:T(1024)S(1)}, f32[7168]{0:T(1024)}, u32[]{:S(2)}) copy-start(f32[7168]{0:T(1024)} %param.12) | copy-start | bytes 86020
  15.7 4.9 %collective-permute-start.17 = (f32[1,1024]{1,0:T(1,128)S(1)}, f32[1,1024]{1,0:T(1,128)S(1)}, u32[]{:S(2)}, u32[]{:S(2)}) collective-permute-start(f32[1,1024]{1,0:T(1,128)S(1)} %add.156), channel_id=1, source_target_pairs={{0,3},{1,2},{2,1},{3,0},{4,7},{5,6},{6,5},{7,4},{8,11},{9,10},{10,... | collective-permute-start | bytes 12296 | tf_op jit(solution)/shard_map/ppermute | solution.py:21
  20.6 7.5 %collective-permute-start.18 = (f32[1,1024]{1,0:T(1,128)S(1)}, f32[1,1024]{1,0:T(1,128)S(1)}, u32[]{:S(2)}, u32[]{:S(2)}) collective-permute-start(f32[1,1024]{1,0:T(1,128)S(1)} %add.157), channel_id=1, source_target_pairs={{0,4},{1,5},{2,6},{3,7},{4,0},{5,1},{6,2},{7,3},{8,12},{9,13},{10,... | collective-permute-start | bytes 12296 | tf_op jit(solution)/shard_map/ppermute | solution.py:21
  23.7 10.4 %all-to-all-start = ((bf16[8,16,448]{2,1,0:T(8,128)(2,1)}), bf16[8,16,448]{2,1,0:T(8,128)(2,1)S(1)}, u32[]{:S(2)}, u32[]{:S(2)}) async-start(bf16[8,16,448]{2,1,0:T(8,128)(2,1)} %bitcast.3), calls=%async_computation | async-start | bytes 262144 | tf_op jit(solution)/shard_map/all_to_all | solution.py:226
  28.0 210.5 %reduce-scatter.2.cloned.1.call-start = ((), (), s32[]{:S(2)}) async-start(), calls=%async_computation.4 | async-start | bytes 1949696 | tf_op jit(solution)/shard_map/reduce_scatter | solution.py:255
  28.1 5.8 %collective-permute-start.19 = (f32[1,1024]{1,0:T(1,128)S(1)}, f32[1,1024]{1,0:T(1,128)S(1)}, u32[]{:S(2)}, u32[]{:S(2)}) collective-permute-start(f32[1,1024]{1,0:T(1,128)S(1)} %add.158), channel_id=1, source_target_pairs={{0,12},{1,13},{2,14},{3,15},{4,8},{5,9},{6,10},{7,11},{8,4},{9,5},... | collective-permute-start | bytes 12296 | tf_op jit(solution)/shard_map/ppermute | solution.py:21
  34.3 5.9 %collective-permute-start.6 = (bf16[1,112,128]{2,1,0:T(8,128)(2,1)S(1)}, bf16[1,112,128]{2,1,0:T(8,128)(2,1)S(1)}, u32[]{:S(2)}, u32[]{:S(2)}) collective-permute-start(bf16[1,112,128]{2,1,0:T(8,128)(2,1)S(1)} %get-tuple-element.73), channel_id=1, source_target_pairs={{0,12},{1,13},{2,14},{3,15},{4,8},{5,9},{6,10},{7,11},{8,4},{9,5},... | collective-permute-start | bytes 86024 | tf_op jit(solution)/shard_map/ppermute | solution.py:21
  36.9 5.4 %collective-permute-start.4 = (bf16[1,112,128]{2,1,0:T(8,128)(2,1)S(1)}, bf16[1,112,128]{2,1,0:T(8,128)(2,1)S(1)}, u32[]{:S(2)}, u32[]{:S(2)}) collective-permute-start(bf16[1,112,128]{2,1,0:T(8,128)(2,1)S(1)} %get-tuple-element.74), channel_id=1, source_target_pairs={{0,4},{1,5},{2,6},{3,7},{4,0},{5,1},{6,2},{7,3},{8,12},{9,13},{10,... | collective-permute-start | bytes 86024 | tf_op jit(solution)/shard_map/ppermute | solution.py:21
  38.0 5.1 %collective-permute-start.2 = (bf16[1,112,128]{2,1,0:T(8,128)(2,1)S(1)}, bf16[1,112,128]{2,1,0:T(8,128)(2,1)S(1)}, u32[]{:S(2)}, u32[]{:S(2)}) collective-permute-start(bf16[1,112,128]{2,1,0:T(8,128)(2,1)S(1)} %get-tuple-element.75), channel_id=1, source_target_pairs={{0,3},{1,2},{2,1},{3,0},{4,7},{5,6},{6,5},{7,4},{8,11},{9,10},{10,... | collective-permute-start | bytes 86024 | tf_op jit(solution)/shard_map/ppermute | solution.py:21
  40.2 4.0 %collective-permute-start = (bf16[1,112,128]{2,1,0:T(8,128)(2,1)S(1)}, bf16[1,112,128]{2,1,0:T(8,128)(2,1)S(1)}, u32[]{:S(2)}, u32[]{:S(2)}) collective-permute-start(bf16[1,112,128]{2,1,0:T(8,128)(2,1)S(1)} %get-tuple-element.76), channel_id=1, source_target_pairs={{0,1},{1,0},{2,3},{3,2},{4,5},{5,4},{6,7},{7,6},{8,9},{9,8},{10,11... | collective-permute-start | bytes 86024 | tf_op jit(solution)/shard_map/ppermute | solution.py:21
  40.2 20.0 %collective-permute-start.7 = (bf16[2,112,128]{2,1,0:T(8,128)(2,1)S(1)}, bf16[2,112,128]{2,1,0:T(8,128)(2,1)S(1)}, u32[]{:S(2)}, u32[]{:S(2)}) collective-permute-start(bf16[2,112,128]{2,1,0:T(8,128)(2,1)S(1)} %pad_maximum_fusion.12), channel_id=1, source_target_pairs={{0,1},{1,0},{2,3},{3,2},{4,5},{5,4},{6,7},{7,6},{8,9},{9,8},{10,11... | collective-permute-start | bytes 172040 | tf_op jit(solution)/shard_map/ppermute | solution.py:21
  42.3 17.8 %collective-permute-start.5 = (bf16[2,112,128]{2,1,0:T(8,128)(2,1)S(1)}, bf16[2,112,128]{2,1,0:T(8,128)(2,1)S(1)}, u32[]{:S(2)}, u32[]{:S(2)}) collective-permute-start(bf16[2,112,128]{2,1,0:T(8,128)(2,1)S(1)} %pad_maximum_fusion.11), channel_id=1, source_target_pairs={{0,12},{1,13},{2,14},{3,15},{4,8},{5,9},{6,10},{7,11},{8,4},{9,5},... | collective-permute-start | bytes 172040 | tf_op jit(solution)/shard_map/ppermute | solution.py:21
  43.1 17.1 %collective-permute-start.3 = (bf16[2,112,128]{2,1,0:T(8,128)(2,1)S(1)}, bf16[2,112,128]{2,1,0:T(8,128)(2,1)S(1)}, u32[]{:S(2)}, u32[]{:S(2)}) collective-permute-start(bf16[2,112,128]{2,1,0:T(8,128)(2,1)S(1)} %pad_maximum_fusion.10), channel_id=1, source_target_pairs={{0,4},{1,5},{2,6},{3,7},{4,0},{5,1},{6,2},{7,3},{8,12},{9,13},{10,... | collective-permute-start | bytes 172040 | tf_op jit(solution)/shard_map/ppermute | solution.py:21
  44.2 16.0 %collective-permute-start.1 = (bf16[2,112,128]{2,1,0:T(8,128)(2,1)S(1)}, bf16[2,112,128]{2,1,0:T(8,128)(2,1)S(1)}, u32[]{:S(2)}, u32[]{:S(2)}) collective-permute-start(bf16[2,112,128]{2,1,0:T(8,128)(2,1)S(1)} %pad_maximum_fusion.9), channel_id=1, source_target_pairs={{0,3},{1,2},{2,1},{3,0},{4,7},{5,6},{6,5},{7,4},{8,11},{9,10},{10,... | collective-permute-start | bytes 172040 | tf_op jit(solution)/shard_map/ppermute | solution.py:21
  60.9 12.4 %collective-permute-start.11 = (bf16[4,112,128]{2,1,0:T(8,128)(2,1)}, bf16[4,112,128]{2,1,0:T(8,128)(2,1)}, u32[]{:S(2)}, u32[]{:S(2)}) collective-permute-start(bf16[4,112,128]{2,1,0:T(8,128)(2,1)} %pad_maximum_fusion.8), channel_id=1, source_target_pairs={{0,3},{1,2},{2,1},{3,0},{4,7},{5,6},{6,5},{7,4},{8,11},{9,10},{10,... | collective-permute-start | bytes 344072 | tf_op jit(solution)/shard_map/ppermute | solution.py:21
  63.0 10.3 %collective-permute-start.10 = (bf16[4,112,128]{2,1,0:T(8,128)(2,1)}, bf16[4,112,128]{2,1,0:T(8,128)(2,1)}, u32[]{:S(2)}, u32[]{:S(2)}) collective-permute-start(bf16[4,112,128]{2,1,0:T(8,128)(2,1)} %pad_maximum_fusion.7), channel_id=1, source_target_pairs={{0,1},{1,0},{2,3},{3,2},{4,5},{5,4},{6,7},{7,6},{8,9},{9,8},{10,11... | collective-permute-start | bytes 344072 | tf_op jit(solution)/shard_map/ppermute | solution.py:21
  63.6 9.6 %collective-permute-start.9 = (bf16[4,112,128]{2,1,0:T(8,128)(2,1)}, bf16[4,112,128]{2,1,0:T(8,128)(2,1)}, u32[]{:S(2)}, u32[]{:S(2)}) collective-permute-start(bf16[4,112,128]{2,1,0:T(8,128)(2,1)} %pad_maximum_fusion.6), channel_id=1, source_target_pairs={{0,12},{1,13},{2,14},{3,15},{4,8},{5,9},{6,10},{7,11},{8,4},{9,5},... | collective-permute-start | bytes 344072 | tf_op jit(solution)/shard_map/ppermute | solution.py:21
  66.5 7.5 %collective-permute-start.8 = (bf16[4,112,128]{2,1,0:T(8,128)(2,1)}, bf16[4,112,128]{2,1,0:T(8,128)(2,1)}, u32[]{:S(2)}, u32[]{:S(2)}) collective-permute-start(bf16[4,112,128]{2,1,0:T(8,128)(2,1)} %pad_maximum_fusion.5), channel_id=1, source_target_pairs={{0,4},{1,5},{2,6},{3,7},{4,0},{5,1},{6,2},{7,3},{8,12},{9,13},{10,... | collective-permute-start | bytes 344072 | tf_op jit(solution)/shard_map/ppermute | solution.py:21
  75.0 12.0 %collective-permute-start.15 = (bf16[8,112,128]{2,1,0:T(8,128)(2,1)S(1)}, bf16[8,112,128]{2,1,0:T(8,128)(2,1)S(1)}, u32[]{:S(2)}, u32[]{:S(2)}) collective-permute-start(bf16[8,112,128]{2,1,0:T(8,128)(2,1)S(1)} %pad_maximum_fusion.4), channel_id=1, source_target_pairs={{0,4},{1,5},{2,6},{3,7},{4,0},{5,1},{6,2},{7,3},{8,12},{9,13},{10,... | collective-permute-start | bytes 688136 | tf_op jit(solution)/shard_map/ppermute | solution.py:21
  76.7 18.2 %copy-start.2 = (f32[7168,1]{1,0:T(8,128)S(1)}, f32[7168,1]{1,0:T(8,128)}, u32[]{:S(2)}) copy-start(f32[7168,1]{1,0:T(8,128)} %copy.33.gain_ref) | copy-start | bytes 86020
  76.8 13.1 %collective-permute-start.14 = (bf16[8,112,128]{2,1,0:T(8,128)(2,1)S(1)}, bf16[8,112,128]{2,1,0:T(8,128)(2,1)S(1)}, u32[]{:S(2)}, u32[]{:S(2)}) collective-permute-start(bf16[8,112,128]{2,1,0:T(8,128)(2,1)S(1)} %pad_maximum_fusion.3), channel_id=1, source_target_pairs={{0,3},{1,2},{2,1},{3,0},{4,7},{5,6},{6,5},{7,4},{8,11},{9,10},{10,... | collective-permute-start | bytes 688136 | tf_op jit(solution)/shard_map/ppermute | solution.py:21
  79.1 12.0 %collective-permute-start.13 = (bf16[8,112,128]{2,1,0:T(8,128)(2,1)S(1)}, bf16[8,112,128]{2,1,0:T(8,128)(2,1)S(1)}, u32[]{:S(2)}, u32[]{:S(2)}) collective-permute-start(bf16[8,112,128]{2,1,0:T(8,128)(2,1)S(1)} %pad_maximum_fusion.2), channel_id=1, source_target_pairs={{0,1},{1,0},{2,3},{3,2},{4,5},{5,4},{6,7},{7,6},{8,9},{9,8},{10,11... | collective-permute-start | bytes 688136 | tf_op jit(solution)/shard_map/ppermute | solution.py:21
  81.8 13.1 %collective-permute-start.12 = (bf16[8,112,128]{2,1,0:T(8,128)(2,1)S(1)}, bf16[8,112,128]{2,1,0:T(8,128)(2,1)S(1)}, u32[]{:S(2)}, u32[]{:S(2)}) collective-permute-start(bf16[8,112,128]{2,1,0:T(8,128)(2,1)S(1)} %pad_maximum_fusion.1), channel_id=1, source_target_pairs={{0,12},{1,13},{2,14},{3,15},{4,8},{5,9},{6,10},{7,11},{8,4},{9,5},... | collective-permute-start | bytes 688136 | tf_op jit(solution)/shard_map/ppermute | solution.py:21
  120.7 13.3 %copy-start = (bf16[7168,256]{1,0:T(8,128)(2,1)S(1)}, bf16[7168,256]{1,0:T(8,128)(2,1)}, u32[]{:S(2)}) copy-start(bf16[7168,256]{1,0:T(8,128)(2,1)} %copy.32) | copy-start | bytes 11010052
  137.2 48.3 %collective-permute-start.24 = (bf16[8,448,256]{2,1,0:T(8,128)(2,1)}, bf16[8,448,256]{2,1,0:T(8,128)(2,1)}, u32[]{:S(2)}, u32[]{:S(2)}) collective-permute-start(bf16[8,448,256]{2,1,0:T(8,128)(2,1)} %get-tuple-element.57), channel_id=1, source_target_pairs={{0,3},{1,2},{2,1},{3,0},{4,7},{5,6},{6,5},{7,4},{8,11},{9,10},{10,... | collective-permute-start | bytes 5505032 | tf_op jit(solution)/shard_map/ppermute | solution.py:21
  143.1 49.7 %collective-permute-start.28 = (bf16[8,448,256]{2,1,0:T(8,128)(2,1)}, bf16[8,448,256]{2,1,0:T(8,128)(2,1)}, u32[]{:S(2)}, u32[]{:S(2)}) collective-permute-start(bf16[8,448,256]{2,1,0:T(8,128)(2,1)} %get-tuple-element.59), channel_id=1, source_target_pairs={{0,4},{1,5},{2,6},{3,7},{4,0},{5,1},{6,2},{7,3},{8,12},{9,13},{10,... | collective-permute-start | bytes 5505032 | tf_op jit(solution)/shard_map/ppermute | solution.py:21
  143.2 51.0 %collective-permute-start.32 = (bf16[8,448,256]{2,1,0:T(8,128)(2,1)}, bf16[8,448,256]{2,1,0:T(8,128)(2,1)}, u32[]{:S(2)}, u32[]{:S(2)}) collective-permute-start(bf16[8,448,256]{2,1,0:T(8,128)(2,1)} %get-tuple-element.61), channel_id=1, source_target_pairs={{0,12},{1,13},{2,14},{3,15},{4,8},{5,9},{6,10},{7,11},{8,4},{9,5},... | collective-permute-start | bytes 5505032 | tf_op jit(solution)/shard_map/ppermute | solution.py:21
  145.1 51.9 %collective-permute-start.20 = (bf16[8,448,256]{2,1,0:T(8,128)(2,1)}, bf16[8,448,256]{2,1,0:T(8,128)(2,1)}, u32[]{:S(2)}, u32[]{:S(2)}) collective-permute-start(bf16[8,448,256]{2,1,0:T(8,128)(2,1)} %get-tuple-element.53), channel_id=1, source_target_pairs={{0,1},{1,0},{2,3},{3,2},{4,5},{5,4},{6,7},{7,6},{8,9},{9,8},{10,11... | collective-permute-start | bytes 5505032 | tf_op jit(solution)/shard_map/ppermute | solution.py:21
  151.2 65.8 %copy-start.6 = (bf16[8,448,256]{2,1,0:T(8,128)(2,1)}, bf16[8,448,256]{2,1,0:T(8,128)(2,1)S(1)}, u32[]{:S(2)}) copy-start(bf16[8,448,256]{2,1,0:T(8,128)(2,1)S(1)} %get-tuple-element.60) | copy-start | bytes 5505028
  186.9 25.5 %collective-permute-start.25 = (bf16[4,448,256]{2,1,0:T(8,128)(2,1)S(1)}, bf16[4,448,256]{2,1,0:T(8,128)(2,1)S(1)}, u32[]{:S(2)}, u32[]{:S(2)}) collective-permute-start(bf16[4,448,256]{2,1,0:T(8,128)(2,1)S(1)} %add_convert_fusion.2), channel_id=1, source_target_pairs={{0,4},{1,5},{2,6},{3,7},{4,0},{5,1},{6,2},{7,3},{8,12},{9,13},{10,... | collective-permute-start | bytes 2752520 | tf_op jit(solution)/shard_map/ppermute | solution.py:21
  194.2 21.5 %collective-permute-start.29 = (bf16[4,448,256]{2,1,0:T(8,128)(2,1)S(1)}, bf16[4,448,256]{2,1,0:T(8,128)(2,1)S(1)}, u32[]{:S(2)}, u32[]{:S(2)}) collective-permute-start(bf16[4,448,256]{2,1,0:T(8,128)(2,1)S(1)} %add_convert_fusion.1), channel_id=1, source_target_pairs={{0,12},{1,13},{2,14},{3,15},{4,8},{5,9},{6,10},{7,11},{8,4},{9,5},... | collective-permute-start | bytes 2752520 | tf_op jit(solution)/shard_map/ppermute | solution.py:21
  195.7 21.4 %collective-permute-start.33 = (bf16[4,448,256]{2,1,0:T(8,128)(2,1)S(1)}, bf16[4,448,256]{2,1,0:T(8,128)(2,1)S(1)}, u32[]{:S(2)}, u32[]{:S(2)}) collective-permute-start(bf16[4,448,256]{2,1,0:T(8,128)(2,1)S(1)} %add_convert_fusion), channel_id=1, source_target_pairs={{0,1},{1,0},{2,3},{3,2},{4,5},{5,4},{6,7},{7,6},{8,9},{9,8},{10,11... | collective-permute-start | bytes 2752520 | tf_op jit(solution)/shard_map/ppermute | solution.py:21
  198.4 40.1 %collective-permute-start.21 = (bf16[4,448,256]{2,1,0:T(8,128)(2,1)S(1)}, bf16[4,448,256]{2,1,0:T(8,128)(2,1)}, u32[]{:S(2)}, u32[]{:S(2)}) collective-permute-start(bf16[4,448,256]{2,1,0:T(8,128)(2,1)S(1)} %add_convert_fusion.3), channel_id=1, source_target_pairs={{0,3},{1,2},{2,1},{3,0},{4,7},{5,6},{6,5},{7,4},{8,11},{9,10},{10,... | collective-permute-start | bytes 2752520 | tf_op jit(solution)/shard_map/ppermute | solution.py:21
  213.6 13.1 %collective-permute-start.26 = (bf16[2,448,256]{2,1,0:T(8,128)(2,1)S(1)}, bf16[2,448,256]{2,1,0:T(8,128)(2,1)S(1)}, u32[]{:S(2)}, u32[]{:S(2)}) collective-permute-start(bf16[2,448,256]{2,1,0:T(8,128)(2,1)S(1)} %add_convert_fusion.6), channel_id=1, source_target_pairs={{0,12},{1,13},{2,14},{3,15},{4,8},{5,9},{6,10},{7,11},{8,4},{9,5},... | collective-permute-start | bytes 1376264 | tf_op jit(solution)/shard_map/ppermute | solution.py:21
  216.9 11.2 %collective-permute-start.30 = (bf16[2,448,256]{2,1,0:T(8,128)(2,1)S(1)}, bf16[2,448,256]{2,1,0:T(8,128)(2,1)S(1)}, u32[]{:S(2)}, u32[]{:S(2)}) collective-permute-start(bf16[2,448,256]{2,1,0:T(8,128)(2,1)S(1)} %add_convert_fusion.5), channel_id=1, source_target_pairs={{0,1},{1,0},{2,3},{3,2},{4,5},{5,4},{6,7},{7,6},{8,9},{9,8},{10,11... | collective-permute-start | bytes 1376264 | tf_op jit(solution)/shard_map/ppermute | solution.py:21
  217.0 12.1 %copy-start.8 = (bf16[4,448,256]{2,1,0:T(8,128)(2,1)}, bf16[4,448,256]{2,1,0:T(8,128)(2,1)S(1)}, u32[]{:S(2)}) copy-start(bf16[4,448,256]{2,1,0:T(8,128)(2,1)S(1)} %collective-permute-done.33) | copy-start | bytes 2752516
  219.3 31.4 %collective-permute-start.34 = (bf16[2,448,256]{2,1,0:T(8,128)(2,1)}, bf16[2,448,256]{2,1,0:T(8,128)(2,1)}, u32[]{:S(2)}, u32[]{:S(2)}) collective-permute-start(bf16[2,448,256]{2,1,0:T(8,128)(2,1)} %add_convert_fusion.4), channel_id=1, source_target_pairs={{0,3},{1,2},{2,1},{3,0},{4,7},{5,6},{6,5},{7,4},{8,11},{9,10},{10,... | collective-permute-start | bytes 1376264 | tf_op jit(solution)/shard_map/ppermute | solution.py:21
  227.8 6.1 %collective-permute-start.27 = (bf16[1,448,256]{2,1,0:T(8,128)(2,1)S(1)}, bf16[1,448,256]{2,1,0:T(8,128)(2,1)S(1)}, u32[]{:S(2)}, u32[]{:S(2)}) collective-permute-start(bf16[1,448,256]{2,1,0:T(8,128)(2,1)S(1)} %add_convert_fusion.10), channel_id=1, source_target_pairs={{0,1},{1,0},{2,3},{3,2},{4,5},{5,4},{6,7},{7,6},{8,9},{9,8},{10,11... | collective-permute-start | bytes 688136 | tf_op jit(solution)/shard_map/ppermute | solution.py:21
  229.2 7.5 %collective-permute-start.31 = (bf16[1,448,256]{2,1,0:T(8,128)(2,1)S(1)}, bf16[1,448,256]{2,1,0:T(8,128)(2,1)S(1)}, u32[]{:S(2)}, u32[]{:S(2)}) collective-permute-start(bf16[1,448,256]{2,1,0:T(8,128)(2,1)S(1)} %add_convert_fusion.9), channel_id=1, source_target_pairs={{0,3},{1,2},{2,1},{3,0},{4,7},{5,6},{6,5},{7,4},{8,11},{9,10},{10,... | collective-permute-start | bytes 688136 | tf_op jit(solution)/shard_map/ppermute | solution.py:21
  240.2 10.4 %all-to-all-start.1 = ((bf16[8,16,448]{2,1,0:T(8,128)(2,1)}), bf16[8,16,448]{2,1,0:T(8,128)(2,1)S(1)}, u32[]{:S(2)}, u32[]{:S(2)}) async-start(bf16[8,16,448]{2,1,0:T(8,128)(2,1)} %bitcast.18), calls=%async_computation.2 | async-start | bytes 262144 | tf_op jit(solution)/shard_map/all_to_all | solution.py:274
  246.6 13.6 %collective-permute-start.22 = (bf16[2,448,256]{2,1,0:T(8,128)(2,1)}, bf16[2,448,256]{2,1,0:T(8,128)(2,1)}, u32[]{:S(2)}, u32[]{:S(2)}) collective-permute-start(bf16[2,448,256]{2,1,0:T(8,128)(2,1)} %add_convert_fusion.7), channel_id=1, source_target_pairs={{0,4},{1,5},{2,6},{3,7},{4,0},{5,1},{6,2},{7,3},{8,12},{9,13},{10,... | collective-permute-start | bytes 1376264 | tf_op jit(solution)/shard_map/ppermute | solution.py:21
  252.1 12.5 %collective-permute-start.35 = (bf16[1,448,256]{2,1,0:T(8,128)(2,1)S(1)}, bf16[1,448,256]{2,1,0:T(8,128)(2,1)S(1)}, u32[]{:S(2)}, u32[]{:S(2)}) collective-permute-start(bf16[1,448,256]{2,1,0:T(8,128)(2,1)S(1)} %add_convert_fusion.8), channel_id=1, source_target_pairs={{0,4},{1,5},{2,6},{3,7},{4,0},{5,1},{6,2},{7,3},{8,12},{9,13},{10,... | collective-permute-start | bytes 688136 | tf_op jit(solution)/shard_map/ppermute | solution.py:21
  261.5 9.5 %copy-start.9 = (f32[448,256]{1,0:T(8,128)S(1)}, f32[448,256]{1,0:T(8,128)}, u32[]{:S(2)}) copy-start(f32[448,256]{1,0:T(8,128)} %add_bitcast_fusion.2) | copy-start | bytes 1376260
  261.5 9.5 %copy-start.10 = (f32[448,256]{1,0:T(8,128)S(1)}, f32[448,256]{1,0:T(8,128)}, u32[]{:S(2)}) copy-start(f32[448,256]{1,0:T(8,128)} %add_bitcast_fusion.1) | copy-start | bytes 1376260
  261.5 8.1 %collective-permute-start.23 = (bf16[1,448,256]{2,1,0:T(8,128)(2,1)S(1)}, bf16[1,448,256]{2,1,0:T(8,128)(2,1)S(1)}, u32[]{:S(2)}, u32[]{:S(2)}) collective-permute-start(bf16[1,448,256]{2,1,0:T(8,128)(2,1)S(1)} %add_convert_fusion.11), channel_id=1, source_target_pairs={{0,12},{1,13},{2,14},{3,15},{4,8},{5,9},{6,10},{7,11},{8,4},{9,5},... | collective-permute-start | bytes 688136 | tf_op jit(solution)/shard_map/ppermute | solution.py:21
  (6 other events, 21.9 us)
Sparse Core Ops, SparseCore 0:
  9.5 111.1 all-gather.1
  145.5 76.4 reduce-scatter.1

commit v10 on v9

--- a/solution.py
+++ b/solution.py
@@ -252,14 +252,23 @@
     expert_hidden = expert_gate_up(slice_of, pooled, expert_gate, expert_up, gain_column)
     expert_partial = expert_down_parts(expert_down, expert_hidden)
     expert_partial, scale, whole_columns = lax.optimization_barrier((expert_partial, scale, whole_columns))
-    expert_out = lax.psum_scatter(expert_partial, "local", scatter_dimension=0, tiled=True)
+    expert_parts = lax.all_to_all(
+        expert_partial.reshape(16, slice_width, slot_count), "local", split_axis=0, concat_axis=0, tiled=True
+    )
 
     gate_up = transposed_dot(weight, whole_columns)
     low_hidden, *sent = sent_parts(0, slice_of, gate_up, scale, turned)
     high_hidden, *more = sent_parts(2, slice_of, gate_up, scale, turned)
     sent += more
     arrived = [flip_local(sent[s], STREAMS[s][0]) for s in range(4)]
+    low_hidden, expert_parts = lax.optimization_barrier((low_hidden, expert_parts))
     sums = kept_parts(slice_of, turned, (low_hidden, high_hidden))
+    expert_out = jnp.sum(expert_parts.astype(jnp.float32), axis=0).astype(jnp.bfloat16)
+    returned = lax.all_to_all(
+        expert_out.T.reshape(node_count, NODE_CAP, slice_width), "node", split_axis=0, concat_axis=0, tiled=True
+    ).reshape(slot_count, slice_width)
+    route_term = (slot_gate[:, None] * returned.astype(jnp.float32)).astype(jnp.bfloat16)
+    arrived, route_term = lax.optimization_barrier((arrived, route_term))
     terms = [[sums[s], arrived[s]] for s in range(4)]
 
     def added(s, low, high):
@@ -269,14 +278,6 @@
         half = 8 >> step
         for s in range(4):
             terms[s].append(flip_local(added(s, half, 2 * half).astype(jnp.bfloat16), STREAMS[s][step]))
-        if step == 1:
-            terms[0][-1], expert_out = lax.optimization_barrier((terms[0][-1], expert_out))
-            returned = lax.all_to_all(
-                expert_out.T.reshape(node_count, NODE_CAP, slice_width), "node", split_axis=0, concat_axis=0, tiled=True
-            ).reshape(slot_count, slice_width)
-            route_term = (slot_gate[:, None] * returned.astype(jnp.float32)).astype(jnp.bfloat16)
-        if step == 2:
-            terms[3][-1], route_term = lax.optimization_barrier((terms[3][-1], route_term))
     expert_part = lax.dot_general(
         route_term, chosen, (((0,), (1,)), ((), ())), preferred_element_type=jnp.float32
     )

time: 281 us -> 257 us (0.915)
  waiting for transfers between devices: 99.7 us -> 64.8 us
  starting transfers between devices: 56.5 us -> 66.1 us
    ppermute x36, waiting for transfers between devices: 84 us -> 52.1 us  [flip_local(): lax.ppermute(array, 'local', [(i, LOCAL_AT[LOCAL_LABEL[i] ^ 1 << bit]) fo...]
    all_to_all x0 -> x1, starting transfers between devices: none -> 5.33 us  [shards(): lax.all_to_all(expert_partial.reshape(16, slice_width, slot_count), 'loca...]
    ppermute x36, starting transfers between devices: 47.9 us -> 52.2 us  [flip_local(): lax.ppermute(array, 'local', [(i, LOCAL_AT[LOCAL_LABEL[i] ^ 1 << bit]) fo...]
    all_to_all x1, waiting for transfers between devices: 4 us -> 0.01 us  [shards(): lax.all_to_all(expert_out.T.reshape(node_count, NODE_CAP, slice_width), '...]
    unnamed x40 -> x44, local copies, waits for them, and re-layouts: 10.3 us -> 14 us
  transfers between devices with their start and end apart: 40 -> 40, of which waited for: 20 -> 20; matrix products, arithmetic and copies ran while one was open for 24% -> 30% of each run, Pallas kernels for 6% -> 8%
where the time goes in v10:
time: 257 us; the launch traced here: 255 us
  starting transfers between devices  66.1 us (26%)
  waiting for transfers between devices  64.8 us (25%)
  other arithmetic  47.2 us (18%)
  local copies, waits for them, and re-layouts  27.2 us (11%)
  Pallas kernels  20.9 us (8%)
  matrix products  15.1 us (6%)
  between operations  13.9 us (5%)
    ppermute x36, starting transfers between devices, flip_local(): lax.ppermute(array, 'local', [(i, LOCAL_AT[LOCAL_LABEL[i] ^ 1 << bit]) fo...  52.2 us
    ppermute x36, waiting for transfers between devices, flip_local(): lax.ppermute(array, 'local', [(i, LOCAL_AT[LOCAL_LABEL[i] ^ 1 << bit]) fo...  52.1 us
    convert_element_type x12, other arithmetic, shards(): added(s, half, 2 * half).astype(jnp.bfloat16)  15.1 us
    unnamed x44, local copies, waits for them, and re-layouts  14 us
    dot_general x1, matrix products, transposed_dot(): lax.dot_general(weight, rows, (((0,), (0,)), ((), ())), preferred_element...  13.3 us
    all_gather x1, waiting for transfers between devices, shards(): whole_columns = lax.all_gather(columns, 'local', axis=0, tiled=True)  10.6 us
    pallas_call x1, Pallas kernels, expert_gate_up(): pl.pallas_call(functools.partial(expert_kernel, blocks, blocks * rows), g...  7.66 us
    convert_element_type x1, other arithmetic, shards(): (w.astype(jnp.float32) * gain_column).astype(jnp.bfloat16)  7.04 us
  transfers between devices with their start and end apart: 40, of which 20 were waited for; matrix products, arithmetic and copies ran while one was open for 30% of the time, Pallas kernels for 8%

profile of v10, /device:TPU:0, one launch (start us, length us, event | category | flops | bytes accessed | tf_op | source)
XLA Modules:
  0.0 255.2 jit_solution(13123370478089551007)
XLA Ops:
  8.7 1.7 collective-permute-start.16
  11.2 2.3 reduce-window.6
  15.7 2.3 collective-permute-start.17
  18.8 1.9 collective-permute-done.17
  20.6 1.9 collective-permute-start.18
  23.7 4.3 %all-to-all-start = ((bf16[8,16,448]{2,1,0:T(8,128)(2,1)}), bf16[8,16,448]{2,1,0:T(8,128)(2,1)S(1)}, u32[]{:S(2)}, u32[]{:S(2)}) async-start(bf16[8,16,448]{2,1,0:T(8,128)(2,1)} %bitcast.3), calls=%async_computation | async-start | bytes 262144 | tf_op jit(solution)/shard_map/all_to_all | solution.py:226
  28.0 2.6 %collective-permute-start.19 = (f32[1,1024]{1,0:T(1,128)S(1)}, f32[1,1024]{1,0:T(1,128)S(1)}, u32[]{:S(2)}, u32[]{:S(2)}) collective-permute-start(f32[1,1024]{1,0:T(1,128)S(1)} %add.156), channel_id=1, source_target_pairs={{0,12},{1,13},{2,14},{3,15},{4,8},{5,9},{6,10},{7,11},{8,4},{9,5},... | collective-permute-start | bytes 12296 | tf_op jit(solution)/shard_map/ppermute | solution.py:21
  31.3 2.5 copy.51.gain_ref
  34.3 2.6 %collective-permute-start.6 = (bf16[1,112,128]{2,1,0:T(8,128)(2,1)S(1)}, bf16[1,112,128]{2,1,0:T(8,128)(2,1)S(1)}, u32[]{:S(2)}, u32[]{:S(2)}) collective-permute-start(bf16[1,112,128]{2,1,0:T(8,128)(2,1)S(1)} %get-tuple-element.79), channel_id=1, source_target_pairs={{0,12},{1,13},{2,14},{3,15},{4,8},{5,9},{6,10},{7,11},{8,4},{9,5},... | collective-permute-start | bytes 86024 | tf_op jit(solution)/shard_map/ppermute | solution.py:21
  38.0 2.2 collective-permute-start.2
  40.2 2.1 collective-permute-start.7
  44.2 2.3 collective-permute-start.1
  46.5 7.0 %multiply_convert_fusion.1 = (bf16[7168,256]{1,0:T(8,128)(2,1)}, bf16[7168,256]{1,0:T(8,128)(2,1)}) fusion(bf16[7168,256]{1,0:T(8,128)(2,1)} %param.13, f32[7168]{0:T(1024)S(1)} %copy-done.13, bf16[7168,256]{1,0:T(8,128)(2,1)} %param.14), kind=kLoop, calls=%fused_computation.2 | loop fusion | flops 11010048 | bytes 14708736 | tf_op jit(solution)/shard_map/convert_element_type | solution.py:242
  53.5 6.6 %pad_maximum_fusion = bf16[7168,512]{1,0:T(8,128)(2,1)} fusion(bf16[7168,256]{1,0:T(8,128)(2,1)} %get-tuple-element.84, bf16[7168,256]{1,0:T(8,128)(2,1)} %get-tuple-element.83), kind=kLoop, calls=%fused_computation | loop fusion | flops 14680064 | bytes 14680064 | tf_op jit(solution)/shard_map/concatenate | solution.py:241
  60.9 1.5 collective-permute-start.11
  63.6 2.3 collective-permute-start.9
  67.3 6.0 %copy.50 = bf16[7168,256]{1,0:T(8,128)(2,1)} copy(bf16[7168,256]{0,1:T(8,128)(2,1)} %bitcast.68) | data formatting | bytes 7340032 | tf_op jit(solution)/shard_map/transpose | solution.py:247
  79.1 1.9 collective-permute-start.13
  87.0 2.9 %collective-permute-done.14 = bf16[8,112,128]{2,1,0:T(8,128)(2,1)S(1)} collective-permute-done((bf16[8,112,128]{2,1,0:T(8,128)(2,1)S(1)}, bf16[8,112,128]{2,1,0:T(8,128)(2,1)S(1)}, u32[]{:S(2)}, u32[]{:S(2)}) %collective-permute-start.14) | collective-permute-done | bytes 229408 | tf_op jit(solution)/shard_map/ppermute | solution.py:21
  91.2 3.9 %collective-permute-done.12 = bf16[8,112,128]{2,1,0:T(8,128)(2,1)S(1)} collective-permute-done((bf16[8,112,128]{2,1,0:T(8,128)(2,1)S(1)}, bf16[8,112,128]{2,1,0:T(8,128)(2,1)S(1)}, u32[]{:S(2)}, u32[]{:S(2)}) %collective-permute-start.12) | collective-permute-done | bytes 229408 | tf_op jit(solution)/shard_map/ppermute | solution.py:21
  95.1 2.0 copy-done.3
  97.1 2.2 copy-done.4
  99.3 7.7 %shard_map.109.hidden_ref = bf16[256,128]{1,0:T(8,128)(2,1)S(1)} custom-call(s32[16]{0:T(128)S(1)} %dynamic-slice_bitcast_fusion.at_ref.slice_ref, bf16[16,112,128]{2,1,0:T(8,128)(2,1)S(1)} %constant_dynamic-update-slice_fusion.x0, bf16[16,112,128]{2,1,0:T(8,128)(2,1)S(1)} %constant_dynamic-update-slice_fusion.5.x1, ...), custom_call_target="tpu_custom_call" | custom-call | flops 939524096 | bytes 9175040 | tf_op jit(solution)/shard_map/pallas_call | solution.py:147
  107.0 3.1 %shard_map.110 = bf16[7168,128]{1,0:T(8,128)(2,1)} custom-call(bf16[1,256,7168]{2,1,0:T(8,128)(2,1)S(1)} %copy-done.5, bf16[256,128]{1,0:T(8,128)(2,1)S(1)} %shard_map.109.hidden_ref), custom_call_target="tpu_custom_call" | custom-call | flops 469762048 | bytes 5505024 | tf_op jit(solution)/shard_map/pallas_call | solution.py:179
  110.1 10.6 %all-gather.2.cloned.1.call-done = bf16[7168,1024]{1,0:T(8,128)(2,1)} async-done(((bf16[448,1024]{1,0:T(8,128)(2,1)}), bf16[7168,1024]{1,0:T(8,128)(2,1)}) %all-gather.2.cloned.1.call-update) | async-done | bytes 14680080 | tf_op jit(solution)/shard_map/all_gather | solution.py:216
  120.7 5.3 %all-to-all-start.1 = ((bf16[16,448,128]{2,1,0:T(8,128)(2,1)}), bf16[16,448,128]{2,1,0:T(8,128)(2,1)}, u32[]{:S(2)}, u32[]{:S(2)}) async-start(bf16[16,448,128]{2,1,0:T(8,128)(2,1)} %bitcast.14), calls=%async_computation.1 | async-start | bytes 3670016 | tf_op jit(solution)/shard_map/all_to_all | solution.py:255
  126.1 13.3 %fusion.10.gate_up_ref = f32[512,1024]{1,0:T(8,128)S(1)} fusion(bf16[7168,512]{1,0:T(8,128)(2,1)} %pad_maximum_fusion, bf16[7168,1024]{1,0:T(8,128)(2,1)} %all-gather.2.cloned.1.call-done), kind=kOutput, calls=%fused_computation.84 | convolution fusion | flops 7516192768 | bytes 24117248 | tf_op jit(solution)/shard_map/dot_general | solution.py:36
  139.4 3.2 %shard_map.112 = (bf16[256,512]{1,0:T(8,128)(2,1)S(1)}, bf16[8,448,256]{2,1,0:T(8,128)(2,1)}, bf16[8,448,256]{2,1,0:T(8,128)(2,1)}) custom-call(s32[16]{0:T(128)S(1)} %dynamic-slice_bitcast_fusion.at_ref.slice_ref, f32[512,1024]{1,0:T(8,128)S(1)} %fusion.10.gate_up_ref, f32[1,1024]{1,0:T(1,128)S(1)} %add_rsqrt_fusion.scale_ref, ...), custom_call_target="tpu_custom_call" | custom-call | flops 939524096 | bytes 7340032 | tf_op jit(solution)/shard_map/pallas_call | solution.py:66
  142.6 1.9 collective-permute-start.22
  144.4 2.1 collective-permute-start.23
  146.5 3.1 %shard_map.111 = (bf16[256,512]{1,0:T(8,128)(2,1)S(1)}, bf16[8,448,256]{2,1,0:T(8,128)(2,1)}, bf16[8,448,256]{2,1,0:T(8,128)(2,1)}) custom-call(s32[16]{0:T(128)S(1)} %dynamic-slice_bitcast_fusion.at_ref.slice_ref, f32[512,1024]{1,0:T(8,128)S(1)} %fusion.10.gate_up_ref, f32[1,1024]{1,0:T(1,128)S(1)} %add_rsqrt_fusion.scale_ref, ...), custom_call_target="tpu_custom_call" | custom-call | flops 939524096 | bytes 7340032 | tf_op jit(solution)/shard_map/pallas_call | solution.py:66
  149.6 1.5 collective-permute-start.20
  151.1 2.1 collective-permute-start.21
  154.3 1.8 reduce_sum.65
  156.8 4.3 %all-to-all-start.2 = ((bf16[8,16,448]{2,1,0:T(8,128)(2,1)}), bf16[8,16,448]{2,1,0:T(8,128)(2,1)}, u32[]{:S(2)}, u32[]{:S(2)}) async-start(bf16[8,16,448]{2,1,0:T(8,128)(2,1)} %bitcast.16), calls=%async_computation.2 | async-start | bytes 262144 | tf_op jit(solution)/shard_map/all_to_all | solution.py:267
  161.1 2.0 copy-done.1
  163.1 3.8 %shard_map.113 = (bf16[8,448,256]{2,1,0:T(8,128)(2,1)S(1)}, bf16[8,448,256]{2,1,0:T(8,128)(2,1)S(1)}, bf16[8,448,256]{2,1,0:T(8,128)(2,1)S(1)}, bf16[8,448,256]{2,1,0:T(8,128)(2,1)S(1)}) custom-call(s32[16]{0:T(128)S(1)} %dynamic-slice_bitcast_fusion.at_ref.slice_ref, bf16[16,448,256]{2,1,0:T(8,128)(2,1)S(1)} %bitcast.63, ...), custom_call_target="tpu_custom_call" | custom-call | flops 1879048192 | bytes 14680064 | tf_op jit(solution)/shard_map/pallas_call | solution.py:96
  171.7 16.2 %collective-permute-done.22 = bf16[8,448,256]{2,1,0:T(8,128)(2,1)} collective-permute-done((bf16[8,448,256]{2,1,0:T(8,128)(2,1)}, bf16[8,448,256]{2,1,0:T(8,128)(2,1)}, u32[]{:S(2)}, u32[]{:S(2)}) %collective-permute-start.22) | collective-permute-done | bytes 1835040 | tf_op jit(solution)/shard_map/ppermute | solution.py:21
  190.6 2.4 collective-permute-done.21
  193.0 1.7 add_convert_fusion.3
  194.7 2.1 collective-permute-start.24
  196.8 1.4 add_convert_fusion.2
  203.1 12.7 %collective-permute-done.24 = bf16[4,448,256]{2,1,0:T(8,128)(2,1)S(1)} collective-permute-done((bf16[4,448,256]{2,1,0:T(8,128)(2,1)S(1)}, bf16[4,448,256]{2,1,0:T(8,128)(2,1)S(1)}, u32[]{:S(2)}, u32[]{:S(2)}) %collective-permute-start.24) | collective-permute-done | bytes 917536 | tf_op jit(solution)/shard_map/ppermute | solution.py:21
  217.6 1.8 collective-permute-done.27
  220.6 1.5 collective-permute-start.28
  225.1 3.5 %collective-permute-start.34 = (bf16[2,448,256]{2,1,0:T(8,128)(2,1)S(1)}, bf16[2,448,256]{2,1,0:T(8,128)(2,1)S(1)}, u32[]{:S(2)}, u32[]{:S(2)}) collective-permute-start(bf16[2,448,256]{2,1,0:T(8,128)(2,1)S(1)} %add_convert_fusion.4), channel_id=1, source_target_pairs={{0,3},{1,2},{2,1},{3,0},{4,7},{5,6},{6,5},{7,4},{8,11},{9,10},{10,... | collective-permute-start | bytes 1376264 | tf_op jit(solution)/shard_map/ppermute | solution.py:21
  233.4 1.6 collective-permute-done.31
  236.1 2.6 %collective-permute-start.32 = (bf16[1,448,256]{2,1,0:T(8,128)(2,1)S(1)}, bf16[1,448,256]{2,1,0:T(8,128)(2,1)S(1)}, u32[]{:S(2)}, u32[]{:S(2)}) collective-permute-start(bf16[1,448,256]{2,1,0:T(8,128)(2,1)S(1)} %add_convert_fusion.9), channel_id=1, source_target_pairs={{0,3},{1,2},{2,1},{3,0},{4,7},{5,6},{6,5},{7,4},{8,11},{9,10},{10,... | collective-permute-start | bytes 688136 | tf_op jit(solution)/shard_map/ppermute | solution.py:21
  (149 shorter events, 63.2 us)
Async XLA Ops:
  6.5 114.2 %all-gather.2.cloned.1.call-start = ((), (), s32[]{:S(2)}) async-start(), calls=%async_computation.3 | async-start | bytes 15597568 | tf_op jit(solution)/shard_map/all_gather | solution.py:216
  8.7 7.1 %collective-permute-start.16 = (f32[1,1024]{1,0:T(1,128)S(1)}, f32[1,1024]{1,0:T(1,128)S(1)}, u32[]{:S(2)}, u32[]{:S(2)}) collective-permute-start(f32[1,1024]{1,0:T(1,128)S(1)} %bitcast.74), channel_id=1, source_target_pairs={{0,1},{1,0},{2,3},{3,2},{4,5},{5,4},{6,7},{7,6},{8,9},{9,8},{10,11... | collective-permute-start | bytes 12296 | tf_op jit(solution)/shard_map/ppermute | solution.py:21
  14.1 8.5 %copy-start.12 = (bf16[1024,448]{0,1:T(8,128)(2,1)S(1)}, bf16[1024,448]{0,1:T(8,128)(2,1)}, u32[]{:S(2)}) copy-start(bf16[1024,448]{0,1:T(8,128)(2,1)} %param.11) | copy-start | bytes 2752516
  15.4 16.0 %copy-start.13 = (f32[7168]{0:T(1024)S(1)}, f32[7168]{0:T(1024)}, u32[]{:S(2)}) copy-start(f32[7168]{0:T(1024)} %param.12) | copy-start | bytes 86020
  15.7 4.9 %collective-permute-start.17 = (f32[1,1024]{1,0:T(1,128)S(1)}, f32[1,1024]{1,0:T(1,128)S(1)}, u32[]{:S(2)}, u32[]{:S(2)}) collective-permute-start(f32[1,1024]{1,0:T(1,128)S(1)} %add.154), channel_id=1, source_target_pairs={{0,3},{1,2},{2,1},{3,0},{4,7},{5,6},{6,5},{7,4},{8,11},{9,10},{10,... | collective-permute-start | bytes 12296 | tf_op jit(solution)/shard_map/ppermute | solution.py:21
  20.6 7.4 %collective-permute-start.18 = (f32[1,1024]{1,0:T(1,128)S(1)}, f32[1,1024]{1,0:T(1,128)S(1)}, u32[]{:S(2)}, u32[]{:S(2)}) collective-permute-start(f32[1,1024]{1,0:T(1,128)S(1)} %add.155), channel_id=1, source_target_pairs={{0,4},{1,5},{2,6},{3,7},{4,0},{5,1},{6,2},{7,3},{8,12},{9,13},{10,... | collective-permute-start | bytes 12296 | tf_op jit(solution)/shard_map/ppermute | solution.py:21
  23.7 10.4 %all-to-all-start = ((bf16[8,16,448]{2,1,0:T(8,128)(2,1)}), bf16[8,16,448]{2,1,0:T(8,128)(2,1)S(1)}, u32[]{:S(2)}, u32[]{:S(2)}) async-start(bf16[8,16,448]{2,1,0:T(8,128)(2,1)} %bitcast.3), calls=%async_computation | async-start | bytes 262144 | tf_op jit(solution)/shard_map/all_to_all | solution.py:226
  28.0 5.8 %collective-permute-start.19 = (f32[1,1024]{1,0:T(1,128)S(1)}, f32[1,1024]{1,0:T(1,128)S(1)}, u32[]{:S(2)}, u32[]{:S(2)}) collective-permute-start(f32[1,1024]{1,0:T(1,128)S(1)} %add.156), channel_id=1, source_target_pairs={{0,12},{1,13},{2,14},{3,15},{4,8},{5,9},{6,10},{7,11},{8,4},{9,5},... | collective-permute-start | bytes 12296 | tf_op jit(solution)/shard_map/ppermute | solution.py:21
  34.3 5.9 %collective-permute-start.6 = (bf16[1,112,128]{2,1,0:T(8,128)(2,1)S(1)}, bf16[1,112,128]{2,1,0:T(8,128)(2,1)S(1)}, u32[]{:S(2)}, u32[]{:S(2)}) collective-permute-start(bf16[1,112,128]{2,1,0:T(8,128)(2,1)S(1)} %get-tuple-element.79), channel_id=1, source_target_pairs={{0,12},{1,13},{2,14},{3,15},{4,8},{5,9},{6,10},{7,11},{8,4},{9,5},... | collective-permute-start | bytes 86024 | tf_op jit(solution)/shard_map/ppermute | solution.py:21
  36.9 5.4 %collective-permute-start.4 = (bf16[1,112,128]{2,1,0:T(8,128)(2,1)S(1)}, bf16[1,112,128]{2,1,0:T(8,128)(2,1)S(1)}, u32[]{:S(2)}, u32[]{:S(2)}) collective-permute-start(bf16[1,112,128]{2,1,0:T(8,128)(2,1)S(1)} %get-tuple-element.80), channel_id=1, source_target_pairs={{0,4},{1,5},{2,6},{3,7},{4,0},{5,1},{6,2},{7,3},{8,12},{9,13},{10,... | collective-permute-start | bytes 86024 | tf_op jit(solution)/shard_map/ppermute | solution.py:21
  38.0 5.1 %collective-permute-start.2 = (bf16[1,112,128]{2,1,0:T(8,128)(2,1)S(1)}, bf16[1,112,128]{2,1,0:T(8,128)(2,1)S(1)}, u32[]{:S(2)}, u32[]{:S(2)}) collective-permute-start(bf16[1,112,128]{2,1,0:T(8,128)(2,1)S(1)} %get-tuple-element.81), channel_id=1, source_target_pairs={{0,3},{1,2},{2,1},{3,0},{4,7},{5,6},{6,5},{7,4},{8,11},{9,10},{10,... | collective-permute-start | bytes 86024 | tf_op jit(solution)/shard_map/ppermute | solution.py:21
  40.2 4.0 %collective-permute-start = (bf16[1,112,128]{2,1,0:T(8,128)(2,1)S(1)}, bf16[1,112,128]{2,1,0:T(8,128)(2,1)S(1)}, u32[]{:S(2)}, u32[]{:S(2)}) collective-permute-start(bf16[1,112,128]{2,1,0:T(8,128)(2,1)S(1)} %get-tuple-element.82), channel_id=1, source_target_pairs={{0,1},{1,0},{2,3},{3,2},{4,5},{5,4},{6,7},{7,6},{8,9},{9,8},{10,11... | collective-permute-start | bytes 86024 | tf_op jit(solution)/shard_map/ppermute | solution.py:21
  40.2 19.9 %collective-permute-start.7 = (bf16[2,112,128]{2,1,0:T(8,128)(2,1)S(1)}, bf16[2,112,128]{2,1,0:T(8,128)(2,1)S(1)}, u32[]{:S(2)}, u32[]{:S(2)}) collective-permute-start(bf16[2,112,128]{2,1,0:T(8,128)(2,1)S(1)} %pad_maximum_fusion.12), channel_id=1, source_target_pairs={{0,1},{1,0},{2,3},{3,2},{4,5},{5,4},{6,7},{7,6},{8,9},{9,8},{10,11... | collective-permute-start | bytes 172040 | tf_op jit(solution)/shard_map/ppermute | solution.py:21
  42.3 17.8 %collective-permute-start.5 = (bf16[2,112,128]{2,1,0:T(8,128)(2,1)S(1)}, bf16[2,112,128]{2,1,0:T(8,128)(2,1)S(1)}, u32[]{:S(2)}, u32[]{:S(2)}) collective-permute-start(bf16[2,112,128]{2,1,0:T(8,128)(2,1)S(1)} %pad_maximum_fusion.11), channel_id=1, source_target_pairs={{0,12},{1,13},{2,14},{3,15},{4,8},{5,9},{6,10},{7,11},{8,4},{9,5},... | collective-permute-start | bytes 172040 | tf_op jit(solution)/shard_map/ppermute | solution.py:21
  43.1 17.1 %collective-permute-start.3 = (bf16[2,112,128]{2,1,0:T(8,128)(2,1)S(1)}, bf16[2,112,128]{2,1,0:T(8,128)(2,1)S(1)}, u32[]{:S(2)}, u32[]{:S(2)}) collective-permute-start(bf16[2,112,128]{2,1,0:T(8,128)(2,1)S(1)} %pad_maximum_fusion.10), channel_id=1, source_target_pairs={{0,4},{1,5},{2,6},{3,7},{4,0},{5,1},{6,2},{7,3},{8,12},{9,13},{10,... | collective-permute-start | bytes 172040 | tf_op jit(solution)/shard_map/ppermute | solution.py:21
  44.2 16.0 %collective-permute-start.1 = (bf16[2,112,128]{2,1,0:T(8,128)(2,1)S(1)}, bf16[2,112,128]{2,1,0:T(8,128)(2,1)S(1)}, u32[]{:S(2)}, u32[]{:S(2)}) collective-permute-start(bf16[2,112,128]{2,1,0:T(8,128)(2,1)S(1)} %pad_maximum_fusion.9), channel_id=1, source_target_pairs={{0,3},{1,2},{2,1},{3,0},{4,7},{5,6},{6,5},{7,4},{8,11},{9,10},{10,... | collective-permute-start | bytes 172040 | tf_op jit(solution)/shard_map/ppermute | solution.py:21
  60.9 12.4 %collective-permute-start.11 = (bf16[4,112,128]{2,1,0:T(8,128)(2,1)}, bf16[4,112,128]{2,1,0:T(8,128)(2,1)}, u32[]{:S(2)}, u32[]{:S(2)}) collective-permute-start(bf16[4,112,128]{2,1,0:T(8,128)(2,1)} %pad_maximum_fusion.8), channel_id=1, source_target_pairs={{0,3},{1,2},{2,1},{3,0},{4,7},{5,6},{6,5},{7,4},{8,11},{9,10},{10,... | collective-permute-start | bytes 344072 | tf_op jit(solution)/shard_map/ppermute | solution.py:21
  63.0 10.3 %collective-permute-start.10 = (bf16[4,112,128]{2,1,0:T(8,128)(2,1)}, bf16[4,112,128]{2,1,0:T(8,128)(2,1)}, u32[]{:S(2)}, u32[]{:S(2)}) collective-permute-start(bf16[4,112,128]{2,1,0:T(8,128)(2,1)} %pad_maximum_fusion.7), channel_id=1, source_target_pairs={{0,1},{1,0},{2,3},{3,2},{4,5},{5,4},{6,7},{7,6},{8,9},{9,8},{10,11... | collective-permute-start | bytes 344072 | tf_op jit(solution)/shard_map/ppermute | solution.py:21
  63.6 9.7 %collective-permute-start.9 = (bf16[4,112,128]{2,1,0:T(8,128)(2,1)}, bf16[4,112,128]{2,1,0:T(8,128)(2,1)}, u32[]{:S(2)}, u32[]{:S(2)}) collective-permute-start(bf16[4,112,128]{2,1,0:T(8,128)(2,1)} %pad_maximum_fusion.6), channel_id=1, source_target_pairs={{0,12},{1,13},{2,14},{3,15},{4,8},{5,9},{6,10},{7,11},{8,4},{9,5},... | collective-permute-start | bytes 344072 | tf_op jit(solution)/shard_map/ppermute | solution.py:21
  66.5 7.5 %collective-permute-start.8 = (bf16[4,112,128]{2,1,0:T(8,128)(2,1)}, bf16[4,112,128]{2,1,0:T(8,128)(2,1)}, u32[]{:S(2)}, u32[]{:S(2)}) collective-permute-start(bf16[4,112,128]{2,1,0:T(8,128)(2,1)} %pad_maximum_fusion.5), channel_id=1, source_target_pairs={{0,4},{1,5},{2,6},{3,7},{4,0},{5,1},{6,2},{7,3},{8,12},{9,13},{10,... | collective-permute-start | bytes 344072 | tf_op jit(solution)/shard_map/ppermute | solution.py:21
  75.0 12.0 %collective-permute-start.15 = (bf16[8,112,128]{2,1,0:T(8,128)(2,1)S(1)}, bf16[8,112,128]{2,1,0:T(8,128)(2,1)S(1)}, u32[]{:S(2)}, u32[]{:S(2)}) collective-permute-start(bf16[8,112,128]{2,1,0:T(8,128)(2,1)S(1)} %pad_maximum_fusion.4), channel_id=1, source_target_pairs={{0,4},{1,5},{2,6},{3,7},{4,0},{5,1},{6,2},{7,3},{8,12},{9,13},{10,... | collective-permute-start | bytes 688136 | tf_op jit(solution)/shard_map/ppermute | solution.py:21
  76.8 18.3 %copy-start.2 = (f32[7168,1]{1,0:T(8,128)S(1)}, f32[7168,1]{1,0:T(8,128)}, u32[]{:S(2)}) copy-start(f32[7168,1]{1,0:T(8,128)} %copy.51.gain_ref) | copy-start | bytes 86020
  76.8 13.1 %collective-permute-start.14 = (bf16[8,112,128]{2,1,0:T(8,128)(2,1)S(1)}, bf16[8,112,128]{2,1,0:T(8,128)(2,1)S(1)}, u32[]{:S(2)}, u32[]{:S(2)}) collective-permute-start(bf16[8,112,128]{2,1,0:T(8,128)(2,1)S(1)} %pad_maximum_fusion.3), channel_id=1, source_target_pairs={{0,3},{1,2},{2,1},{3,0},{4,7},{5,6},{6,5},{7,4},{8,11},{9,10},{10,... | collective-permute-start | bytes 688136 | tf_op jit(solution)/shard_map/ppermute | solution.py:21
  79.1 12.0 %collective-permute-start.13 = (bf16[8,112,128]{2,1,0:T(8,128)(2,1)S(1)}, bf16[8,112,128]{2,1,0:T(8,128)(2,1)S(1)}, u32[]{:S(2)}, u32[]{:S(2)}) collective-permute-start(bf16[8,112,128]{2,1,0:T(8,128)(2,1)S(1)} %pad_maximum_fusion.2), channel_id=1, source_target_pairs={{0,1},{1,0},{2,3},{3,2},{4,5},{5,4},{6,7},{7,6},{8,9},{9,8},{10,11... | collective-permute-start | bytes 688136 | tf_op jit(solution)/shard_map/ppermute | solution.py:21
  81.9 13.1 %collective-permute-start.12 = (bf16[8,112,128]{2,1,0:T(8,128)(2,1)S(1)}, bf16[8,112,128]{2,1,0:T(8,128)(2,1)S(1)}, u32[]{:S(2)}, u32[]{:S(2)}) collective-permute-start(bf16[8,112,128]{2,1,0:T(8,128)(2,1)S(1)} %pad_maximum_fusion.1), channel_id=1, source_target_pairs={{0,12},{1,13},{2,14},{3,15},{4,8},{5,9},{6,10},{7,11},{8,4},{9,5},... | collective-permute-start | bytes 688136 | tf_op jit(solution)/shard_map/ppermute | solution.py:21
  99.3 7.7 %copy-start.5 = (bf16[1,256,7168]{2,1,0:T(8,128)(2,1)S(1)}, bf16[1,256,7168]{2,1,0:T(8,128)(2,1)}, u32[]{:S(2)}) copy-start(bf16[1,256,7168]{2,1,0:T(8,128)(2,1)} %weight_ref.1) | copy-start | bytes 11010052
  120.7 33.5 %all-to-all-start.1 = ((bf16[16,448,128]{2,1,0:T(8,128)(2,1)}), bf16[16,448,128]{2,1,0:T(8,128)(2,1)}, u32[]{:S(2)}, u32[]{:S(2)}) async-start(bf16[16,448,128]{2,1,0:T(8,128)(2,1)} %bitcast.14), calls=%async_computation.1 | async-start | bytes 3670016 | tf_op jit(solution)/shard_map/all_to_all | solution.py:255
  126.1 13.3 %copy-start = (bf16[7168,256]{1,0:T(8,128)(2,1)S(1)}, bf16[7168,256]{1,0:T(8,128)(2,1)}, u32[]{:S(2)}) copy-start(bf16[7168,256]{1,0:T(8,128)(2,1)} %copy.50) | copy-start | bytes 11010052
  142.6 45.4 %collective-permute-start.22 = (bf16[8,448,256]{2,1,0:T(8,128)(2,1)}, bf16[8,448,256]{2,1,0:T(8,128)(2,1)}, u32[]{:S(2)}, u32[]{:S(2)}) collective-permute-start(bf16[8,448,256]{2,1,0:T(8,128)(2,1)} %get-tuple-element.60), channel_id=1, source_target_pairs={{0,4},{1,5},{2,6},{3,7},{4,0},{5,1},{6,2},{7,3},{8,12},{9,13},{10,... | collective-permute-start | bytes 5505032 | tf_op jit(solution)/shard_map/ppermute | solution.py:21
  144.4 44.9 %collective-permute-start.23 = (bf16[8,448,256]{2,1,0:T(8,128)(2,1)}, bf16[8,448,256]{2,1,0:T(8,128)(2,1)}, u32[]{:S(2)}, u32[]{:S(2)}) collective-permute-start(bf16[8,448,256]{2,1,0:T(8,128)(2,1)} %get-tuple-element.61), channel_id=1, source_target_pairs={{0,12},{1,13},{2,14},{3,15},{4,8},{5,9},{6,10},{7,11},{8,4},{9,5},... | collective-permute-start | bytes 5505032 | tf_op jit(solution)/shard_map/ppermute | solution.py:21
  149.6 40.9 %collective-permute-start.20 = (bf16[8,448,256]{2,1,0:T(8,128)(2,1)}, bf16[8,448,256]{2,1,0:T(8,128)(2,1)}, u32[]{:S(2)}, u32[]{:S(2)}) collective-permute-start(bf16[8,448,256]{2,1,0:T(8,128)(2,1)} %get-tuple-element.58), channel_id=1, source_target_pairs={{0,1},{1,0},{2,3},{3,2},{4,5},{5,4},{6,7},{7,6},{8,9},{9,8},{10,11... | collective-permute-start | bytes 5505032 | tf_op jit(solution)/shard_map/ppermute | solution.py:21
  151.1 41.9 %collective-permute-start.21 = (bf16[8,448,256]{2,1,0:T(8,128)(2,1)}, bf16[8,448,256]{2,1,0:T(8,128)(2,1)}, u32[]{:S(2)}, u32[]{:S(2)}) collective-permute-start(bf16[8,448,256]{2,1,0:T(8,128)(2,1)} %get-tuple-element.59), channel_id=1, source_target_pairs={{0,3},{1,2},{2,1},{3,0},{4,7},{5,6},{6,5},{7,4},{8,11},{9,10},{10,... | collective-permute-start | bytes 5505032 | tf_op jit(solution)/shard_map/ppermute | solution.py:21
  156.8 13.8 %all-to-all-start.2 = ((bf16[8,16,448]{2,1,0:T(8,128)(2,1)}), bf16[8,16,448]{2,1,0:T(8,128)(2,1)}, u32[]{:S(2)}, u32[]{:S(2)}) async-start(bf16[8,16,448]{2,1,0:T(8,128)(2,1)} %bitcast.16), calls=%async_computation.2 | async-start | bytes 262144 | tf_op jit(solution)/shard_map/all_to_all | solution.py:267
  170.6 26.2 %copy-start.9 = (bf16[8,448,256]{2,1,0:T(8,128)(2,1)S(1)}, bf16[8,448,256]{2,1,0:T(8,128)(2,1)}, u32[]{:S(2)}) copy-start(bf16[8,448,256]{2,1,0:T(8,128)(2,1)} %copy-done.8) | copy-start | bytes 5505028
  194.7 4.2 %copy-start.7 = (bf16[8,448,256]{2,1,0:T(8,128)(2,1)S(1)}, bf16[8,448,256]{2,1,0:T(8,128)(2,1)}, u32[]{:S(2)}) copy-start(bf16[8,448,256]{2,1,0:T(8,128)(2,1)} %copy-done.6) | copy-start | bytes 5505028
  194.7 21.1 %collective-permute-start.24 = (bf16[4,448,256]{2,1,0:T(8,128)(2,1)S(1)}, bf16[4,448,256]{2,1,0:T(8,128)(2,1)S(1)}, u32[]{:S(2)}, u32[]{:S(2)}) collective-permute-start(bf16[4,448,256]{2,1,0:T(8,128)(2,1)S(1)} %add_convert_fusion.3), channel_id=1, source_target_pairs={{0,3},{1,2},{2,1},{3,0},{4,7},{5,6},{6,5},{7,4},{8,11},{9,10},{10,... | collective-permute-start | bytes 2752520 | tf_op jit(solution)/shard_map/ppermute | solution.py:21
  198.3 21.1 %collective-permute-start.27 = (bf16[4,448,256]{2,1,0:T(8,128)(2,1)S(1)}, bf16[4,448,256]{2,1,0:T(8,128)(2,1)S(1)}, u32[]{:S(2)}, u32[]{:S(2)}) collective-permute-start(bf16[4,448,256]{2,1,0:T(8,128)(2,1)S(1)} %add_convert_fusion.2), channel_id=1, source_target_pairs={{0,4},{1,5},{2,6},{3,7},{4,0},{5,1},{6,2},{7,3},{8,12},{9,13},{10,... | collective-permute-start | bytes 2752520 | tf_op jit(solution)/shard_map/ppermute | solution.py:21
  200.3 15.4 %copy-start.11 = (bf16[8,448,256]{2,1,0:T(8,128)(2,1)S(1)}, bf16[8,448,256]{2,1,0:T(8,128)(2,1)}, u32[]{:S(2)}) copy-start(bf16[8,448,256]{2,1,0:T(8,128)(2,1)} %copy-done.10) | copy-start | bytes 5505028
  200.3 21.8 %collective-permute-start.30 = (bf16[4,448,256]{2,1,0:T(8,128)(2,1)S(1)}, bf16[4,448,256]{2,1,0:T(8,128)(2,1)S(1)}, u32[]{:S(2)}, u32[]{:S(2)}) collective-permute-start(bf16[4,448,256]{2,1,0:T(8,128)(2,1)S(1)} %add_convert_fusion.1), channel_id=1, source_target_pairs={{0,12},{1,13},{2,14},{3,15},{4,8},{5,9},{6,10},{7,11},{8,4},{9,5},... | collective-permute-start | bytes 2752520 | tf_op jit(solution)/shard_map/ppermute | solution.py:21
  203.0 20.9 %collective-permute-start.33 = (bf16[4,448,256]{2,1,0:T(8,128)(2,1)S(1)}, bf16[4,448,256]{2,1,0:T(8,128)(2,1)S(1)}, u32[]{:S(2)}, u32[]{:S(2)}) collective-permute-start(bf16[4,448,256]{2,1,0:T(8,128)(2,1)S(1)} %add_convert_fusion), channel_id=1, source_target_pairs={{0,1},{1,0},{2,3},{3,2},{4,5},{5,4},{6,7},{7,6},{8,9},{9,8},{10,11... | collective-permute-start | bytes 2752520 | tf_op jit(solution)/shard_map/ppermute | solution.py:21
  216.9 11.7 %collective-permute-start.25 = (bf16[2,448,256]{2,1,0:T(8,128)(2,1)S(1)}, bf16[2,448,256]{2,1,0:T(8,128)(2,1)S(1)}, u32[]{:S(2)}, u32[]{:S(2)}) collective-permute-start(bf16[2,448,256]{2,1,0:T(8,128)(2,1)S(1)} %add_convert_fusion.7), channel_id=1, source_target_pairs={{0,4},{1,5},{2,6},{3,7},{4,0},{5,1},{6,2},{7,3},{8,12},{9,13},{10,... | collective-permute-start | bytes 1376264 | tf_op jit(solution)/shard_map/ppermute | solution.py:21
  220.6 11.6 %collective-permute-start.28 = (bf16[2,448,256]{2,1,0:T(8,128)(2,1)S(1)}, bf16[2,448,256]{2,1,0:T(8,128)(2,1)S(1)}, u32[]{:S(2)}, u32[]{:S(2)}) collective-permute-start(bf16[2,448,256]{2,1,0:T(8,128)(2,1)S(1)} %add_convert_fusion.6), channel_id=1, source_target_pairs={{0,12},{1,13},{2,14},{3,15},{4,8},{5,9},{6,10},{7,11},{8,4},{9,5},... | collective-permute-start | bytes 1376264 | tf_op jit(solution)/shard_map/ppermute | solution.py:21
  223.3 11.7 %collective-permute-start.31 = (bf16[2,448,256]{2,1,0:T(8,128)(2,1)S(1)}, bf16[2,448,256]{2,1,0:T(8,128)(2,1)S(1)}, u32[]{:S(2)}, u32[]{:S(2)}) collective-permute-start(bf16[2,448,256]{2,1,0:T(8,128)(2,1)S(1)} %add_convert_fusion.5), channel_id=1, source_target_pairs={{0,1},{1,0},{2,3},{3,2},{4,5},{5,4},{6,7},{7,6},{8,9},{9,8},{10,11... | collective-permute-start | bytes 1376264 | tf_op jit(solution)/shard_map/ppermute | solution.py:21
  225.1 13.6 %collective-permute-start.34 = (bf16[2,448,256]{2,1,0:T(8,128)(2,1)S(1)}, bf16[2,448,256]{2,1,0:T(8,128)(2,1)S(1)}, u32[]{:S(2)}, u32[]{:S(2)}) collective-permute-start(bf16[2,448,256]{2,1,0:T(8,128)(2,1)S(1)} %add_convert_fusion.4), channel_id=1, source_target_pairs={{0,3},{1,2},{2,1},{3,0},{4,7},{5,6},{6,5},{7,4},{8,11},{9,10},{10,... | collective-permute-start | bytes 1376264 | tf_op jit(solution)/shard_map/ppermute | solution.py:21
  229.7 10.1 %collective-permute-start.26 = (bf16[1,448,256]{2,1,0:T(8,128)(2,1)S(1)}, bf16[1,448,256]{2,1,0:T(8,128)(2,1)S(1)}, u32[]{:S(2)}, u32[]{:S(2)}) collective-permute-start(bf16[1,448,256]{2,1,0:T(8,128)(2,1)S(1)} %add_convert_fusion.11), channel_id=1, source_target_pairs={{0,12},{1,13},{2,14},{3,15},{4,8},{5,9},{6,10},{7,11},{8,4},{9,5},... | collective-permute-start | bytes 688136 | tf_op jit(solution)/shard_map/ppermute | solution.py:21
  233.3 7.7 %collective-permute-start.29 = (bf16[1,448,256]{2,1,0:T(8,128)(2,1)S(1)}, bf16[1,448,256]{2,1,0:T(8,128)(2,1)S(1)}, u32[]{:S(2)}, u32[]{:S(2)}) collective-permute-start(bf16[1,448,256]{2,1,0:T(8,128)(2,1)S(1)} %add_convert_fusion.10), channel_id=1, source_target_pairs={{0,1},{1,0},{2,3},{3,2},{4,5},{5,4},{6,7},{7,6},{8,9},{9,8},{10,11... | collective-permute-start | bytes 688136 | tf_op jit(solution)/shard_map/ppermute | solution.py:21
  236.1 7.3 %collective-permute-start.32 = (bf16[1,448,256]{2,1,0:T(8,128)(2,1)S(1)}, bf16[1,448,256]{2,1,0:T(8,128)(2,1)S(1)}, u32[]{:S(2)}, u32[]{:S(2)}) collective-permute-start(bf16[1,448,256]{2,1,0:T(8,128)(2,1)S(1)} %add_convert_fusion.9), channel_id=1, source_target_pairs={{0,3},{1,2},{2,1},{3,0},{4,7},{5,6},{6,5},{7,4},{8,11},{9,10},{10,... | collective-permute-start | bytes 688136 | tf_op jit(solution)/shard_map/ppermute | solution.py:21
  239.8 6.1 %collective-permute-start.35 = (bf16[1,448,256]{2,1,0:T(8,128)(2,1)S(1)}, bf16[1,448,256]{2,1,0:T(8,128)(2,1)S(1)}, u32[]{:S(2)}, u32[]{:S(2)}) collective-permute-start(bf16[1,448,256]{2,1,0:T(8,128)(2,1)S(1)} %add_convert_fusion.8), channel_id=1, source_target_pairs={{0,4},{1,5},{2,6},{3,7},{4,0},{5,1},{6,2},{7,3},{8,12},{9,13},{10,... | collective-permute-start | bytes 688136 | tf_op jit(solution)/shard_map/ppermute | solution.py:21
  (8 other events, 17.9 us)
Sparse Core Ops, SparseCore 0:
  9.5 111.1 all-gather.1

commit v11 on v10

--- a/solution.py
+++ b/solution.py
@@ -251,7 +251,7 @@
 
     expert_hidden = expert_gate_up(slice_of, pooled, expert_gate, expert_up, gain_column)
     expert_partial = expert_down_parts(expert_down, expert_hidden)
-    expert_partial, scale, whole_columns = lax.optimization_barrier((expert_partial, scale, whole_columns))
+    _, scale, whole_columns = lax.optimization_barrier((expert_partial, scale, whole_columns))
     expert_parts = lax.all_to_all(
         expert_partial.reshape(16, slice_width, slot_count), "local", split_axis=0, concat_axis=0, tiled=True
     )
@@ -268,7 +268,7 @@
         expert_out.T.reshape(node_count, NODE_CAP, slice_width), "node", split_axis=0, concat_axis=0, tiled=True
     ).reshape(slot_count, slice_width)
     route_term = (slot_gate[:, None] * returned.astype(jnp.float32)).astype(jnp.bfloat16)
-    arrived, route_term = lax.optimization_barrier((arrived, route_term))
+    arrived[1], route_term = lax.optimization_barrier((arrived[1], route_term))
     terms = [[sums[s], arrived[s]] for s in range(4)]
 
     def added(s, low, high):

time: 257 us -> 260 us (1.012)
  waiting for transfers between devices: 64.8 us -> 68.1 us
    all_gather x1, waiting for transfers between devices: 10.6 us -> 22.8 us  [shards(): whole_columns = lax.all_gather(columns, 'local', axis=0, tiled=True)]
    ppermute x36, waiting for transfers between devices: 52.1 us -> 44.3 us  [flip_local(): lax.ppermute(array, 'local', [(i, LOCAL_AT[LOCAL_LABEL[i] ^ 1 << bit]) fo...]
  transfers between devices with their start and end apart: 40 -> 40, of which waited for: 20 -> 19; matrix products, arithmetic and copies ran while one was open for 30% -> 30% of each run, Pallas kernels for 8% -> 8%
where the time goes in v11:
time: 260 us; the launch traced here: 259 us
  waiting for transfers between devices  68.1 us (26%)
  starting transfers between devices  66.5 us (26%)
  other arithmetic  47.2 us (18%)
  local copies, waits for them, and re-layouts  27.2 us (10%)
  Pallas kernels  20.9 us (8%)
  matrix products  15.1 us (6%)
  between operations  13.8 us (5%)
    ppermute x36, starting transfers between devices, flip_local(): lax.ppermute(array, 'local', [(i, LOCAL_AT[LOCAL_LABEL[i] ^ 1 << bit]) fo...  53.6 us
    ppermute x36, waiting for transfers between devices, flip_local(): lax.ppermute(array, 'local', [(i, LOCAL_AT[LOCAL_LABEL[i] ^ 1 << bit]) fo...  44.3 us
    all_gather x1, waiting for transfers between devices, shards(): whole_columns = lax.all_gather(columns, 'local', axis=0, tiled=True)  22.8 us
    convert_element_type x12, other arithmetic, shards(): added(s, half, 2 * half).astype(jnp.bfloat16)  15.1 us
    unnamed x44, local copies, waits for them, and re-layouts  14 us
    dot_general x1, matrix products, transposed_dot(): lax.dot_general(weight, rows, (((0,), (0,)), ((), ())), preferred_element...  13.3 us
    pallas_call x1, Pallas kernels, expert_gate_up(): pl.pallas_call(functools.partial(expert_kernel, blocks, blocks * rows), g...  7.66 us
    convert_element_type x1, other arithmetic, shards(): (w.astype(jnp.float32) * gain_column).astype(jnp.bfloat16)  7.04 us
  transfers between devices with their start and end apart: 40, of which 19 were waited for; matrix products, arithmetic and copies ran while one was open for 30% of the time, Pallas kernels for 8%

profile of v11, /device:TPU:0, one launch (start us, length us, event | category | flops | bytes accessed | tf_op | source)
XLA Modules:
  0.0 258.9 jit_solution(9700507174760048829)
XLA Ops:
  7.3 1.4 fusion
  8.7 1.7 collective-permute-start.16
  11.2 2.3 reduce-window.6
  15.7 2.3 collective-permute-start.17
  18.8 1.9 collective-permute-done.17
  20.6 1.9 collective-permute-start.18
  23.7 4.3 %all-to-all-start = ((bf16[8,16,448]{2,1,0:T(8,128)(2,1)}), bf16[8,16,448]{2,1,0:T(8,128)(2,1)S(1)}, u32[]{:S(2)}, u32[]{:S(2)}) async-start(bf16[8,16,448]{2,1,0:T(8,128)(2,1)} %bitcast.3), calls=%async_computation | async-start | bytes 262144 | tf_op jit(solution)/shard_map/all_to_all | solution.py:226
  28.0 2.6 %collective-permute-start.19 = (f32[1,1024]{1,0:T(1,128)S(1)}, f32[1,1024]{1,0:T(1,128)S(1)}, u32[]{:S(2)}, u32[]{:S(2)}) collective-permute-start(f32[1,1024]{1,0:T(1,128)S(1)} %add.156), channel_id=1, source_target_pairs={{0,12},{1,13},{2,14},{3,15},{4,8},{5,9},{6,10},{7,11},{8,4},{9,5},... | collective-permute-start | bytes 12296 | tf_op jit(solution)/shard_map/ppermute | solution.py:21
  31.3 2.5 copy.51.gain_ref
  34.3 2.6 %collective-permute-start.6 = (bf16[1,112,128]{2,1,0:T(8,128)(2,1)S(1)}, bf16[1,112,128]{2,1,0:T(8,128)(2,1)S(1)}, u32[]{:S(2)}, u32[]{:S(2)}) collective-permute-start(bf16[1,112,128]{2,1,0:T(8,128)(2,1)S(1)} %get-tuple-element.71), channel_id=1, source_target_pairs={{0,12},{1,13},{2,14},{3,15},{4,8},{5,9},{6,10},{7,11},{8,4},{9,5},... | collective-permute-start | bytes 86024 | tf_op jit(solution)/shard_map/ppermute | solution.py:21
  38.0 2.2 collective-permute-start.2
  40.2 2.1 collective-permute-start.7
  44.2 2.3 collective-permute-start.1
  46.5 7.0 %multiply_convert_fusion.1 = (bf16[7168,256]{1,0:T(8,128)(2,1)}, bf16[7168,256]{1,0:T(8,128)(2,1)}) fusion(bf16[7168,256]{1,0:T(8,128)(2,1)} %param.13, f32[7168]{0:T(1024)S(1)} %copy-done.13, bf16[7168,256]{1,0:T(8,128)(2,1)} %param.14), kind=kLoop, calls=%fused_computation.2 | loop fusion | flops 11010048 | bytes 14708736 | tf_op jit(solution)/shard_map/convert_element_type | solution.py:242
  53.5 6.6 %pad_maximum_fusion = bf16[7168,512]{1,0:T(8,128)(2,1)} fusion(bf16[7168,256]{1,0:T(8,128)(2,1)} %get-tuple-element.76, bf16[7168,256]{1,0:T(8,128)(2,1)} %get-tuple-element.75), kind=kLoop, calls=%fused_computation | loop fusion | flops 14680064 | bytes 14680064 | tf_op jit(solution)/shard_map/concatenate | solution.py:241
  60.9 1.5 collective-permute-start.11
  63.6 2.3 collective-permute-start.9
  67.3 6.0 %copy.50 = bf16[7168,256]{1,0:T(8,128)(2,1)} copy(bf16[7168,256]{0,1:T(8,128)(2,1)} %bitcast.68) | data formatting | bytes 7340032 | tf_op jit(solution)/shard_map/transpose | solution.py:247
  79.1 1.9 collective-permute-start.13
  87.0 2.9 %collective-permute-done.14 = bf16[8,112,128]{2,1,0:T(8,128)(2,1)S(1)} collective-permute-done((bf16[8,112,128]{2,1,0:T(8,128)(2,1)S(1)}, bf16[8,112,128]{2,1,0:T(8,128)(2,1)S(1)}, u32[]{:S(2)}, u32[]{:S(2)}) %collective-permute-start.14) | collective-permute-done | bytes 229408 | tf_op jit(solution)/shard_map/ppermute | solution.py:21
  91.2 3.9 %collective-permute-done.12 = bf16[8,112,128]{2,1,0:T(8,128)(2,1)S(1)} collective-permute-done((bf16[8,112,128]{2,1,0:T(8,128)(2,1)S(1)}, bf16[8,112,128]{2,1,0:T(8,128)(2,1)S(1)}, u32[]{:S(2)}, u32[]{:S(2)}) %collective-permute-start.12) | collective-permute-done | bytes 229408 | tf_op jit(solution)/shard_map/ppermute | solution.py:21
  95.1 2.0 copy-done.3
  97.1 2.2 copy-done.4
  99.3 7.7 %shard_map.109.hidden_ref = bf16[256,128]{1,0:T(8,128)(2,1)S(1)} custom-call(s32[16]{0:T(128)S(1)} %dynamic-slice_bitcast_fusion.at_ref.slice_ref, bf16[16,112,128]{2,1,0:T(8,128)(2,1)S(1)} %constant_dynamic-update-slice_fusion.x0, bf16[16,112,128]{2,1,0:T(8,128)(2,1)S(1)} %constant_dynamic-update-slice_fusion.5.x1, ...), custom_call_target="tpu_custom_call" | custom-call | flops 939524096 | bytes 9175040 | tf_op jit(solution)/shard_map/pallas_call | solution.py:147
  107.0 3.1 %shard_map.110 = bf16[7168,128]{1,0:T(8,128)(2,1)} custom-call(bf16[1,256,7168]{2,1,0:T(8,128)(2,1)S(1)} %copy-done.5, bf16[256,128]{1,0:T(8,128)(2,1)S(1)} %shard_map.109.hidden_ref), custom_call_target="tpu_custom_call" | custom-call | flops 469762048 | bytes 5505024 | tf_op jit(solution)/shard_map/pallas_call | solution.py:179
  110.1 4.4 %all-to-all-start.1 = ((bf16[16,448,128]{2,1,0:T(8,128)(2,1)}), bf16[16,448,128]{2,1,0:T(8,128)(2,1)}, u32[]{:S(2)}, u32[]{:S(2)}) async-start(bf16[16,448,128]{2,1,0:T(8,128)(2,1)} %bitcast.14), calls=%async_computation.1 | async-start | bytes 3670016 | tf_op jit(solution)/shard_map/all_to_all | solution.py:255
  114.5 22.8 %all-gather.2.cloned.1.call-done = bf16[7168,1024]{1,0:T(8,128)(2,1)} async-done(((bf16[448,1024]{1,0:T(8,128)(2,1)}), bf16[7168,1024]{1,0:T(8,128)(2,1)}) %all-gather.2.cloned.1.call-update) | async-done | bytes 14680080 | tf_op jit(solution)/shard_map/all_gather | solution.py:216
  137.3 13.3 %fusion.10.gate_up_ref = f32[512,1024]{1,0:T(8,128)S(1)} fusion(bf16[7168,512]{1,0:T(8,128)(2,1)} %pad_maximum_fusion, bf16[7168,1024]{1,0:T(8,128)(2,1)} %all-gather.2.cloned.1.call-done), kind=kOutput, calls=%fused_computation.84 | convolution fusion | flops 7516192768 | bytes 24117248 | tf_op jit(solution)/shard_map/dot_general | solution.py:36
  150.6 3.2 %shard_map.111 = (bf16[256,512]{1,0:T(8,128)(2,1)S(1)}, bf16[8,448,256]{2,1,0:T(8,128)(2,1)}, bf16[8,448,256]{2,1,0:T(8,128)(2,1)}) custom-call(s32[16]{0:T(128)S(1)} %dynamic-slice_bitcast_fusion.at_ref.slice_ref, f32[512,1024]{1,0:T(8,128)S(1)} %fusion.10.gate_up_ref, f32[1,1024]{1,0:T(1,128)S(1)} %add_rsqrt_fusion.scale_ref, ...), custom_call_target="tpu_custom_call" | custom-call | flops 939524096 | bytes 7340032 | tf_op jit(solution)/shard_map/pallas_call | solution.py:66
  153.8 1.6 collective-permute-start.20
  155.4 4.4 %collective-permute-start.24 = (bf16[8,448,256]{2,1,0:T(8,128)(2,1)}, bf16[8,448,256]{2,1,0:T(8,128)(2,1)}, u32[]{:S(2)}, u32[]{:S(2)}) collective-permute-start(bf16[8,448,256]{2,1,0:T(8,128)(2,1)} %get-tuple-element.55), channel_id=1, source_target_pairs={{0,3},{1,2},{2,1},{3,0},{4,7},{5,6},{6,5},{7,4},{8,11},{9,10},{10,... | collective-permute-start | bytes 5505032 | tf_op jit(solution)/shard_map/ppermute | solution.py:21
  159.8 3.1 %shard_map.112 = (bf16[256,512]{1,0:T(8,128)(2,1)S(1)}, bf16[8,448,256]{2,1,0:T(8,128)(2,1)}, bf16[8,448,256]{2,1,0:T(8,128)(2,1)}) custom-call(s32[16]{0:T(128)S(1)} %dynamic-slice_bitcast_fusion.at_ref.slice_ref, f32[512,1024]{1,0:T(8,128)S(1)} %fusion.10.gate_up_ref, f32[1,1024]{1,0:T(1,128)S(1)} %add_rsqrt_fusion.scale_ref, ...), custom_call_target="tpu_custom_call" | custom-call | flops 939524096 | bytes 7340032 | tf_op jit(solution)/shard_map/pallas_call | solution.py:66
  163.0 1.8 collective-permute-start.32
  164.8 1.8 reduce_sum.65
  167.3 4.3 %all-to-all-start.2 = ((bf16[8,16,448]{2,1,0:T(8,128)(2,1)}), bf16[8,16,448]{2,1,0:T(8,128)(2,1)}, u32[]{:S(2)}, u32[]{:S(2)}) async-start(bf16[8,16,448]{2,1,0:T(8,128)(2,1)} %bitcast.17), calls=%async_computation.2 | async-start | bytes 262144 | tf_op jit(solution)/shard_map/all_to_all | solution.py:267
  171.6 2.0 copy-done.1
  173.6 3.8 %shard_map.113 = (bf16[8,448,256]{2,1,0:T(8,128)(2,1)S(1)}, bf16[8,448,256]{2,1,0:T(8,128)(2,1)S(1)}, bf16[8,448,256]{2,1,0:T(8,128)(2,1)S(1)}, bf16[8,448,256]{2,1,0:T(8,128)(2,1)S(1)}) custom-call(s32[16]{0:T(128)S(1)} %dynamic-slice_bitcast_fusion.at_ref.slice_ref, bf16[16,448,256]{2,1,0:T(8,128)(2,1)S(1)} %bitcast.63, ...), custom_call_target="tpu_custom_call" | custom-call | flops 1879048192 | bytes 14680064 | tf_op jit(solution)/shard_map/pallas_call | solution.py:96
  182.3 13.5 %collective-permute-done.20 = bf16[8,448,256]{2,1,0:T(8,128)(2,1)} collective-permute-done((bf16[8,448,256]{2,1,0:T(8,128)(2,1)}, bf16[8,448,256]{2,1,0:T(8,128)(2,1)}, u32[]{:S(2)}, u32[]{:S(2)}) %collective-permute-start.20) | collective-permute-done | bytes 1835040 | tf_op jit(solution)/shard_map/ppermute | solution.py:21
  195.7 1.7 add_convert_fusion.3
  197.4 5.2 %collective-permute-start.21 = (bf16[4,448,256]{2,1,0:T(8,128)(2,1)S(1)}, bf16[4,448,256]{2,1,0:T(8,128)(2,1)S(1)}, u32[]{:S(2)}, u32[]{:S(2)}) collective-permute-start(bf16[4,448,256]{2,1,0:T(8,128)(2,1)S(1)} %add_convert_fusion.3), channel_id=1, source_target_pairs={{0,3},{1,2},{2,1},{3,0},{4,7},{5,6},{6,5},{7,4},{8,11},{9,10},{10,... | collective-permute-start | bytes 2752520 | tf_op jit(solution)/shard_map/ppermute | solution.py:21
  202.6 1.4 add_convert_fusion.2
  204.3 1.4 add_convert_fusion.1
  206.9 1.4 add_convert_fusion
  208.9 13.1 %collective-permute-done.21 = bf16[4,448,256]{2,1,0:T(8,128)(2,1)S(1)} collective-permute-done((bf16[4,448,256]{2,1,0:T(8,128)(2,1)S(1)}, bf16[4,448,256]{2,1,0:T(8,128)(2,1)S(1)}, u32[]{:S(2)}, u32[]{:S(2)}) %collective-permute-start.21) | collective-permute-done | bytes 917536 | tf_op jit(solution)/shard_map/ppermute | solution.py:21
  223.2 1.4 collective-permute-start.22
  232.1 2.7 %collective-permute-done.22 = bf16[2,448,256]{2,1,0:T(8,128)(2,1)S(1)} collective-permute-done((bf16[2,448,256]{2,1,0:T(8,128)(2,1)S(1)}, bf16[2,448,256]{2,1,0:T(8,128)(2,1)S(1)}, u32[]{:S(2)}, u32[]{:S(2)}) %collective-permute-start.22) | collective-permute-done | bytes 458784 | tf_op jit(solution)/shard_map/ppermute | solution.py:21
  240.4 1.9 collective-permute-start.31
  250.7 1.4 fusion.3
  (149 shorter events, 56.5 us)
Async XLA Ops:
  6.5 130.8 %all-gather.2.cloned.1.call-start = ((), (), s32[]{:S(2)}) async-start(), calls=%async_computation.3 | async-start | bytes 15597568 | tf_op jit(solution)/shard_map/all_gather | solution.py:216
  8.7 7.1 %collective-permute-start.16 = (f32[1,1024]{1,0:T(1,128)S(1)}, f32[1,1024]{1,0:T(1,128)S(1)}, u32[]{:S(2)}, u32[]{:S(2)}) collective-permute-start(f32[1,1024]{1,0:T(1,128)S(1)} %bitcast.74), channel_id=1, source_target_pairs={{0,1},{1,0},{2,3},{3,2},{4,5},{5,4},{6,7},{7,6},{8,9},{9,8},{10,11... | collective-permute-start | bytes 12296 | tf_op jit(solution)/shard_map/ppermute | solution.py:21
  14.1 8.5 %copy-start.12 = (bf16[1024,448]{0,1:T(8,128)(2,1)S(1)}, bf16[1024,448]{0,1:T(8,128)(2,1)}, u32[]{:S(2)}) copy-start(bf16[1024,448]{0,1:T(8,128)(2,1)} %param.11) | copy-start | bytes 2752516
  15.4 16.0 %copy-start.13 = (f32[7168]{0:T(1024)S(1)}, f32[7168]{0:T(1024)}, u32[]{:S(2)}) copy-start(f32[7168]{0:T(1024)} %param.12) | copy-start | bytes 86020
  15.7 4.9 %collective-permute-start.17 = (f32[1,1024]{1,0:T(1,128)S(1)}, f32[1,1024]{1,0:T(1,128)S(1)}, u32[]{:S(2)}, u32[]{:S(2)}) collective-permute-start(f32[1,1024]{1,0:T(1,128)S(1)} %add.154), channel_id=1, source_target_pairs={{0,3},{1,2},{2,1},{3,0},{4,7},{5,6},{6,5},{7,4},{8,11},{9,10},{10,... | collective-permute-start | bytes 12296 | tf_op jit(solution)/shard_map/ppermute | solution.py:21
  20.6 7.4 %collective-permute-start.18 = (f32[1,1024]{1,0:T(1,128)S(1)}, f32[1,1024]{1,0:T(1,128)S(1)}, u32[]{:S(2)}, u32[]{:S(2)}) collective-permute-start(f32[1,1024]{1,0:T(1,128)S(1)} %add.155), channel_id=1, source_target_pairs={{0,4},{1,5},{2,6},{3,7},{4,0},{5,1},{6,2},{7,3},{8,12},{9,13},{10,... | collective-permute-start | bytes 12296 | tf_op jit(solution)/shard_map/ppermute | solution.py:21
  23.7 10.4 %all-to-all-start = ((bf16[8,16,448]{2,1,0:T(8,128)(2,1)}), bf16[8,16,448]{2,1,0:T(8,128)(2,1)S(1)}, u32[]{:S(2)}, u32[]{:S(2)}) async-start(bf16[8,16,448]{2,1,0:T(8,128)(2,1)} %bitcast.3), calls=%async_computation | async-start | bytes 262144 | tf_op jit(solution)/shard_map/all_to_all | solution.py:226
  28.0 5.8 %collective-permute-start.19 = (f32[1,1024]{1,0:T(1,128)S(1)}, f32[1,1024]{1,0:T(1,128)S(1)}, u32[]{:S(2)}, u32[]{:S(2)}) collective-permute-start(f32[1,1024]{1,0:T(1,128)S(1)} %add.156), channel_id=1, source_target_pairs={{0,12},{1,13},{2,14},{3,15},{4,8},{5,9},{6,10},{7,11},{8,4},{9,5},... | collective-permute-start | bytes 12296 | tf_op jit(solution)/shard_map/ppermute | solution.py:21
  34.3 5.9 %collective-permute-start.6 = (bf16[1,112,128]{2,1,0:T(8,128)(2,1)S(1)}, bf16[1,112,128]{2,1,0:T(8,128)(2,1)S(1)}, u32[]{:S(2)}, u32[]{:S(2)}) collective-permute-start(bf16[1,112,128]{2,1,0:T(8,128)(2,1)S(1)} %get-tuple-element.71), channel_id=1, source_target_pairs={{0,12},{1,13},{2,14},{3,15},{4,8},{5,9},{6,10},{7,11},{8,4},{9,5},... | collective-permute-start | bytes 86024 | tf_op jit(solution)/shard_map/ppermute | solution.py:21
  36.9 5.4 %collective-permute-start.4 = (bf16[1,112,128]{2,1,0:T(8,128)(2,1)S(1)}, bf16[1,112,128]{2,1,0:T(8,128)(2,1)S(1)}, u32[]{:S(2)}, u32[]{:S(2)}) collective-permute-start(bf16[1,112,128]{2,1,0:T(8,128)(2,1)S(1)} %get-tuple-element.72), channel_id=1, source_target_pairs={{0,4},{1,5},{2,6},{3,7},{4,0},{5,1},{6,2},{7,3},{8,12},{9,13},{10,... | collective-permute-start | bytes 86024 | tf_op jit(solution)/shard_map/ppermute | solution.py:21
  38.0 5.1 %collective-permute-start.2 = (bf16[1,112,128]{2,1,0:T(8,128)(2,1)S(1)}, bf16[1,112,128]{2,1,0:T(8,128)(2,1)S(1)}, u32[]{:S(2)}, u32[]{:S(2)}) collective-permute-start(bf16[1,112,128]{2,1,0:T(8,128)(2,1)S(1)} %get-tuple-element.73), channel_id=1, source_target_pairs={{0,3},{1,2},{2,1},{3,0},{4,7},{5,6},{6,5},{7,4},{8,11},{9,10},{10,... | collective-permute-start | bytes 86024 | tf_op jit(solution)/shard_map/ppermute | solution.py:21
  40.2 4.0 %collective-permute-start = (bf16[1,112,128]{2,1,0:T(8,128)(2,1)S(1)}, bf16[1,112,128]{2,1,0:T(8,128)(2,1)S(1)}, u32[]{:S(2)}, u32[]{:S(2)}) collective-permute-start(bf16[1,112,128]{2,1,0:T(8,128)(2,1)S(1)} %get-tuple-element.74), channel_id=1, source_target_pairs={{0,1},{1,0},{2,3},{3,2},{4,5},{5,4},{6,7},{7,6},{8,9},{9,8},{10,11... | collective-permute-start | bytes 86024 | tf_op jit(solution)/shard_map/ppermute | solution.py:21
  40.2 19.9 %collective-permute-start.7 = (bf16[2,112,128]{2,1,0:T(8,128)(2,1)S(1)}, bf16[2,112,128]{2,1,0:T(8,128)(2,1)S(1)}, u32[]{:S(2)}, u32[]{:S(2)}) collective-permute-start(bf16[2,112,128]{2,1,0:T(8,128)(2,1)S(1)} %pad_maximum_fusion.12), channel_id=1, source_target_pairs={{0,1},{1,0},{2,3},{3,2},{4,5},{5,4},{6,7},{7,6},{8,9},{9,8},{10,11... | collective-permute-start | bytes 172040 | tf_op jit(solution)/shard_map/ppermute | solution.py:21
  42.3 17.8 %collective-permute-start.5 = (bf16[2,112,128]{2,1,0:T(8,128)(2,1)S(1)}, bf16[2,112,128]{2,1,0:T(8,128)(2,1)S(1)}, u32[]{:S(2)}, u32[]{:S(2)}) collective-permute-start(bf16[2,112,128]{2,1,0:T(8,128)(2,1)S(1)} %pad_maximum_fusion.11), channel_id=1, source_target_pairs={{0,12},{1,13},{2,14},{3,15},{4,8},{5,9},{6,10},{7,11},{8,4},{9,5},... | collective-permute-start | bytes 172040 | tf_op jit(solution)/shard_map/ppermute | solution.py:21
  43.1 17.1 %collective-permute-start.3 = (bf16[2,112,128]{2,1,0:T(8,128)(2,1)S(1)}, bf16[2,112,128]{2,1,0:T(8,128)(2,1)S(1)}, u32[]{:S(2)}, u32[]{:S(2)}) collective-permute-start(bf16[2,112,128]{2,1,0:T(8,128)(2,1)S(1)} %pad_maximum_fusion.10), channel_id=1, source_target_pairs={{0,4},{1,5},{2,6},{3,7},{4,0},{5,1},{6,2},{7,3},{8,12},{9,13},{10,... | collective-permute-start | bytes 172040 | tf_op jit(solution)/shard_map/ppermute | solution.py:21
  44.2 16.0 %collective-permute-start.1 = (bf16[2,112,128]{2,1,0:T(8,128)(2,1)S(1)}, bf16[2,112,128]{2,1,0:T(8,128)(2,1)S(1)}, u32[]{:S(2)}, u32[]{:S(2)}) collective-permute-start(bf16[2,112,128]{2,1,0:T(8,128)(2,1)S(1)} %pad_maximum_fusion.9), channel_id=1, source_target_pairs={{0,3},{1,2},{2,1},{3,0},{4,7},{5,6},{6,5},{7,4},{8,11},{9,10},{10,... | collective-permute-start | bytes 172040 | tf_op jit(solution)/shard_map/ppermute | solution.py:21
  60.9 12.4 %collective-permute-start.11 = (bf16[4,112,128]{2,1,0:T(8,128)(2,1)}, bf16[4,112,128]{2,1,0:T(8,128)(2,1)}, u32[]{:S(2)}, u32[]{:S(2)}) collective-permute-start(bf16[4,112,128]{2,1,0:T(8,128)(2,1)} %pad_maximum_fusion.8), channel_id=1, source_target_pairs={{0,3},{1,2},{2,1},{3,0},{4,7},{5,6},{6,5},{7,4},{8,11},{9,10},{10,... | collective-permute-start | bytes 344072 | tf_op jit(solution)/shard_map/ppermute | solution.py:21
  63.0 10.3 %collective-permute-start.10 = (bf16[4,112,128]{2,1,0:T(8,128)(2,1)}, bf16[4,112,128]{2,1,0:T(8,128)(2,1)}, u32[]{:S(2)}, u32[]{:S(2)}) collective-permute-start(bf16[4,112,128]{2,1,0:T(8,128)(2,1)} %pad_maximum_fusion.7), channel_id=1, source_target_pairs={{0,1},{1,0},{2,3},{3,2},{4,5},{5,4},{6,7},{7,6},{8,9},{9,8},{10,11... | collective-permute-start | bytes 344072 | tf_op jit(solution)/shard_map/ppermute | solution.py:21
  63.6 9.7 %collective-permute-start.9 = (bf16[4,112,128]{2,1,0:T(8,128)(2,1)}, bf16[4,112,128]{2,1,0:T(8,128)(2,1)}, u32[]{:S(2)}, u32[]{:S(2)}) collective-permute-start(bf16[4,112,128]{2,1,0:T(8,128)(2,1)} %pad_maximum_fusion.6), channel_id=1, source_target_pairs={{0,12},{1,13},{2,14},{3,15},{4,8},{5,9},{6,10},{7,11},{8,4},{9,5},... | collective-permute-start | bytes 344072 | tf_op jit(solution)/shard_map/ppermute | solution.py:21
  66.5 7.5 %collective-permute-start.8 = (bf16[4,112,128]{2,1,0:T(8,128)(2,1)}, bf16[4,112,128]{2,1,0:T(8,128)(2,1)}, u32[]{:S(2)}, u32[]{:S(2)}) collective-permute-start(bf16[4,112,128]{2,1,0:T(8,128)(2,1)} %pad_maximum_fusion.5), channel_id=1, source_target_pairs={{0,4},{1,5},{2,6},{3,7},{4,0},{5,1},{6,2},{7,3},{8,12},{9,13},{10,... | collective-permute-start | bytes 344072 | tf_op jit(solution)/shard_map/ppermute | solution.py:21
  75.0 12.0 %collective-permute-start.15 = (bf16[8,112,128]{2,1,0:T(8,128)(2,1)S(1)}, bf16[8,112,128]{2,1,0:T(8,128)(2,1)S(1)}, u32[]{:S(2)}, u32[]{:S(2)}) collective-permute-start(bf16[8,112,128]{2,1,0:T(8,128)(2,1)S(1)} %pad_maximum_fusion.4), channel_id=1, source_target_pairs={{0,4},{1,5},{2,6},{3,7},{4,0},{5,1},{6,2},{7,3},{8,12},{9,13},{10,... | collective-permute-start | bytes 688136 | tf_op jit(solution)/shard_map/ppermute | solution.py:21
  76.8 18.3 %copy-start.2 = (f32[7168,1]{1,0:T(8,128)S(1)}, f32[7168,1]{1,0:T(8,128)}, u32[]{:S(2)}) copy-start(f32[7168,1]{1,0:T(8,128)} %copy.51.gain_ref) | copy-start | bytes 86020
  76.8 13.1 %collective-permute-start.14 = (bf16[8,112,128]{2,1,0:T(8,128)(2,1)S(1)}, bf16[8,112,128]{2,1,0:T(8,128)(2,1)S(1)}, u32[]{:S(2)}, u32[]{:S(2)}) collective-permute-start(bf16[8,112,128]{2,1,0:T(8,128)(2,1)S(1)} %pad_maximum_fusion.3), channel_id=1, source_target_pairs={{0,3},{1,2},{2,1},{3,0},{4,7},{5,6},{6,5},{7,4},{8,11},{9,10},{10,... | collective-permute-start | bytes 688136 | tf_op jit(solution)/shard_map/ppermute | solution.py:21
  79.1 12.0 %collective-permute-start.13 = (bf16[8,112,128]{2,1,0:T(8,128)(2,1)S(1)}, bf16[8,112,128]{2,1,0:T(8,128)(2,1)S(1)}, u32[]{:S(2)}, u32[]{:S(2)}) collective-permute-start(bf16[8,112,128]{2,1,0:T(8,128)(2,1)S(1)} %pad_maximum_fusion.2), channel_id=1, source_target_pairs={{0,1},{1,0},{2,3},{3,2},{4,5},{5,4},{6,7},{7,6},{8,9},{9,8},{10,11... | collective-permute-start | bytes 688136 | tf_op jit(solution)/shard_map/ppermute | solution.py:21
  81.9 13.1 %collective-permute-start.12 = (bf16[8,112,128]{2,1,0:T(8,128)(2,1)S(1)}, bf16[8,112,128]{2,1,0:T(8,128)(2,1)S(1)}, u32[]{:S(2)}, u32[]{:S(2)}) collective-permute-start(bf16[8,112,128]{2,1,0:T(8,128)(2,1)S(1)} %pad_maximum_fusion.1), channel_id=1, source_target_pairs={{0,12},{1,13},{2,14},{3,15},{4,8},{5,9},{6,10},{7,11},{8,4},{9,5},... | collective-permute-start | bytes 688136 | tf_op jit(solution)/shard_map/ppermute | solution.py:21
  99.3 7.7 %copy-start.5 = (bf16[1,256,7168]{2,1,0:T(8,128)(2,1)S(1)}, bf16[1,256,7168]{2,1,0:T(8,128)(2,1)}, u32[]{:S(2)}) copy-start(bf16[1,256,7168]{2,1,0:T(8,128)(2,1)} %weight_ref.1) | copy-start | bytes 11010052
  110.1 54.7 %all-to-all-start.1 = ((bf16[16,448,128]{2,1,0:T(8,128)(2,1)}), bf16[16,448,128]{2,1,0:T(8,128)(2,1)}, u32[]{:S(2)}, u32[]{:S(2)}) async-start(bf16[16,448,128]{2,1,0:T(8,128)(2,1)} %bitcast.14), calls=%async_computation.1 | async-start | bytes 3670016 | tf_op jit(solution)/shard_map/all_to_all | solution.py:255
  137.3 13.3 %copy-start = (bf16[7168,256]{1,0:T(8,128)(2,1)S(1)}, bf16[7168,256]{1,0:T(8,128)(2,1)}, u32[]{:S(2)}) copy-start(bf16[7168,256]{1,0:T(8,128)(2,1)} %copy.50) | copy-start | bytes 11010052
  153.8 41.9 %collective-permute-start.20 = (bf16[8,448,256]{2,1,0:T(8,128)(2,1)}, bf16[8,448,256]{2,1,0:T(8,128)(2,1)}, u32[]{:S(2)}, u32[]{:S(2)}) collective-permute-start(bf16[8,448,256]{2,1,0:T(8,128)(2,1)} %get-tuple-element.53), channel_id=1, source_target_pairs={{0,1},{1,0},{2,3},{3,2},{4,5},{5,4},{6,7},{7,6},{8,9},{9,8},{10,11... | collective-permute-start | bytes 5505032 | tf_op jit(solution)/shard_map/ppermute | solution.py:21
  155.4 47.2 %collective-permute-start.24 = (bf16[8,448,256]{2,1,0:T(8,128)(2,1)}, bf16[8,448,256]{2,1,0:T(8,128)(2,1)}, u32[]{:S(2)}, u32[]{:S(2)}) collective-permute-start(bf16[8,448,256]{2,1,0:T(8,128)(2,1)} %get-tuple-element.55), channel_id=1, source_target_pairs={{0,3},{1,2},{2,1},{3,0},{4,7},{5,6},{6,5},{7,4},{8,11},{9,10},{10,... | collective-permute-start | bytes 5505032 | tf_op jit(solution)/shard_map/ppermute | solution.py:21
  163.0 41.4 %collective-permute-start.28 = (bf16[8,448,256]{2,1,0:T(8,128)(2,1)}, bf16[8,448,256]{2,1,0:T(8,128)(2,1)}, u32[]{:S(2)}, u32[]{:S(2)}) collective-permute-start(bf16[8,448,256]{2,1,0:T(8,128)(2,1)} %get-tuple-element.59), channel_id=1, source_target_pairs={{0,4},{1,5},{2,6},{3,7},{4,0},{5,1},{6,2},{7,3},{8,12},{9,13},{10,... | collective-permute-start | bytes 5505032 | tf_op jit(solution)/shard_map/ppermute | solution.py:21
  163.0 44.0 %collective-permute-start.32 = (bf16[8,448,256]{2,1,0:T(8,128)(2,1)}, bf16[8,448,256]{2,1,0:T(8,128)(2,1)}, u32[]{:S(2)}, u32[]{:S(2)}) collective-permute-start(bf16[8,448,256]{2,1,0:T(8,128)(2,1)} %get-tuple-element.61), channel_id=1, source_target_pairs={{0,12},{1,13},{2,14},{3,15},{4,8},{5,9},{6,10},{7,11},{8,4},{9,5},... | collective-permute-start | bytes 5505032 | tf_op jit(solution)/shard_map/ppermute | solution.py:21
  167.3 13.8 %all-to-all-start.2 = ((bf16[8,16,448]{2,1,0:T(8,128)(2,1)}), bf16[8,16,448]{2,1,0:T(8,128)(2,1)}, u32[]{:S(2)}, u32[]{:S(2)}) async-start(bf16[8,16,448]{2,1,0:T(8,128)(2,1)} %bitcast.17), calls=%async_computation.2 | async-start | bytes 262144 | tf_op jit(solution)/shard_map/all_to_all | solution.py:267
  181.1 21.5 %copy-start.9 = (bf16[8,448,256]{2,1,0:T(8,128)(2,1)S(1)}, bf16[8,448,256]{2,1,0:T(8,128)(2,1)}, u32[]{:S(2)}) copy-start(bf16[8,448,256]{2,1,0:T(8,128)(2,1)} %copy-done.8) | copy-start | bytes 5505028
  197.4 6.9 %copy-start.7 = (bf16[8,448,256]{2,1,0:T(8,128)(2,1)S(1)}, bf16[8,448,256]{2,1,0:T(8,128)(2,1)}, u32[]{:S(2)}) copy-start(bf16[8,448,256]{2,1,0:T(8,128)(2,1)} %copy-done.6) | copy-start | bytes 5505028
  197.4 24.5 %collective-permute-start.21 = (bf16[4,448,256]{2,1,0:T(8,128)(2,1)S(1)}, bf16[4,448,256]{2,1,0:T(8,128)(2,1)S(1)}, u32[]{:S(2)}, u32[]{:S(2)}) collective-permute-start(bf16[4,448,256]{2,1,0:T(8,128)(2,1)S(1)} %add_convert_fusion.3), channel_id=1, source_target_pairs={{0,3},{1,2},{2,1},{3,0},{4,7},{5,6},{6,5},{7,4},{8,11},{9,10},{10,... | collective-permute-start | bytes 2752520 | tf_op jit(solution)/shard_map/ppermute | solution.py:21
  204.1 21.7 %collective-permute-start.25 = (bf16[4,448,256]{2,1,0:T(8,128)(2,1)S(1)}, bf16[4,448,256]{2,1,0:T(8,128)(2,1)S(1)}, u32[]{:S(2)}, u32[]{:S(2)}) collective-permute-start(bf16[4,448,256]{2,1,0:T(8,128)(2,1)S(1)} %add_convert_fusion.2), channel_id=1, source_target_pairs={{0,4},{1,5},{2,6},{3,7},{4,0},{5,1},{6,2},{7,3},{8,12},{9,13},{10,... | collective-permute-start | bytes 2752520 | tf_op jit(solution)/shard_map/ppermute | solution.py:21
  205.8 16.2 %copy-start.11 = (bf16[8,448,256]{2,1,0:T(8,128)(2,1)S(1)}, bf16[8,448,256]{2,1,0:T(8,128)(2,1)}, u32[]{:S(2)}) copy-start(bf16[8,448,256]{2,1,0:T(8,128)(2,1)} %copy-done.10) | copy-start | bytes 5505028
  205.8 22.2 %collective-permute-start.29 = (bf16[4,448,256]{2,1,0:T(8,128)(2,1)S(1)}, bf16[4,448,256]{2,1,0:T(8,128)(2,1)S(1)}, u32[]{:S(2)}, u32[]{:S(2)}) collective-permute-start(bf16[4,448,256]{2,1,0:T(8,128)(2,1)S(1)} %add_convert_fusion.1), channel_id=1, source_target_pairs={{0,12},{1,13},{2,14},{3,15},{4,8},{5,9},{6,10},{7,11},{8,4},{9,5},... | collective-permute-start | bytes 2752520 | tf_op jit(solution)/shard_map/ppermute | solution.py:21
  208.4 21.2 %collective-permute-start.33 = (bf16[4,448,256]{2,1,0:T(8,128)(2,1)S(1)}, bf16[4,448,256]{2,1,0:T(8,128)(2,1)S(1)}, u32[]{:S(2)}, u32[]{:S(2)}) collective-permute-start(bf16[4,448,256]{2,1,0:T(8,128)(2,1)S(1)} %add_convert_fusion), channel_id=1, source_target_pairs={{0,1},{1,0},{2,3},{3,2},{4,5},{5,4},{6,7},{7,6},{8,9},{9,8},{10,11... | collective-permute-start | bytes 2752520 | tf_op jit(solution)/shard_map/ppermute | solution.py:21
  223.2 11.6 %collective-permute-start.22 = (bf16[2,448,256]{2,1,0:T(8,128)(2,1)S(1)}, bf16[2,448,256]{2,1,0:T(8,128)(2,1)S(1)}, u32[]{:S(2)}, u32[]{:S(2)}) collective-permute-start(bf16[2,448,256]{2,1,0:T(8,128)(2,1)S(1)} %add_convert_fusion.7), channel_id=1, source_target_pairs={{0,4},{1,5},{2,6},{3,7},{4,0},{5,1},{6,2},{7,3},{8,12},{9,13},{10,... | collective-permute-start | bytes 1376264 | tf_op jit(solution)/shard_map/ppermute | solution.py:21
  227.0 10.5 %collective-permute-start.26 = (bf16[2,448,256]{2,1,0:T(8,128)(2,1)S(1)}, bf16[2,448,256]{2,1,0:T(8,128)(2,1)S(1)}, u32[]{:S(2)}, u32[]{:S(2)}) collective-permute-start(bf16[2,448,256]{2,1,0:T(8,128)(2,1)S(1)} %add_convert_fusion.6), channel_id=1, source_target_pairs={{0,12},{1,13},{2,14},{3,15},{4,8},{5,9},{6,10},{7,11},{8,4},{9,5},... | collective-permute-start | bytes 1376264 | tf_op jit(solution)/shard_map/ppermute | solution.py:21
  229.2 10.2 %collective-permute-start.30 = (bf16[2,448,256]{2,1,0:T(8,128)(2,1)S(1)}, bf16[2,448,256]{2,1,0:T(8,128)(2,1)S(1)}, u32[]{:S(2)}, u32[]{:S(2)}) collective-permute-start(bf16[2,448,256]{2,1,0:T(8,128)(2,1)S(1)} %add_convert_fusion.5), channel_id=1, source_target_pairs={{0,1},{1,0},{2,3},{3,2},{4,5},{5,4},{6,7},{7,6},{8,9},{9,8},{10,11... | collective-permute-start | bytes 1376264 | tf_op jit(solution)/shard_map/ppermute | solution.py:21
  230.8 11.7 %collective-permute-start.34 = (bf16[2,448,256]{2,1,0:T(8,128)(2,1)S(1)}, bf16[2,448,256]{2,1,0:T(8,128)(2,1)S(1)}, u32[]{:S(2)}, u32[]{:S(2)}) collective-permute-start(bf16[2,448,256]{2,1,0:T(8,128)(2,1)S(1)} %add_convert_fusion.4), channel_id=1, source_target_pairs={{0,3},{1,2},{2,1},{3,0},{4,7},{5,6},{6,5},{7,4},{8,11},{9,10},{10,... | collective-permute-start | bytes 1376264 | tf_op jit(solution)/shard_map/ppermute | solution.py:21
  235.8 8.9 %collective-permute-start.23 = (bf16[1,448,256]{2,1,0:T(8,128)(2,1)S(1)}, bf16[1,448,256]{2,1,0:T(8,128)(2,1)S(1)}, u32[]{:S(2)}, u32[]{:S(2)}) collective-permute-start(bf16[1,448,256]{2,1,0:T(8,128)(2,1)S(1)} %add_convert_fusion.11), channel_id=1, source_target_pairs={{0,12},{1,13},{2,14},{3,15},{4,8},{5,9},{6,10},{7,11},{8,4},{9,5},... | collective-permute-start | bytes 688136 | tf_op jit(solution)/shard_map/ppermute | solution.py:21
  238.6 7.2 %collective-permute-start.27 = (bf16[1,448,256]{2,1,0:T(8,128)(2,1)S(1)}, bf16[1,448,256]{2,1,0:T(8,128)(2,1)S(1)}, u32[]{:S(2)}, u32[]{:S(2)}) collective-permute-start(bf16[1,448,256]{2,1,0:T(8,128)(2,1)S(1)} %add_convert_fusion.10), channel_id=1, source_target_pairs={{0,1},{1,0},{2,3},{3,2},{4,5},{5,4},{6,7},{7,6},{8,9},{9,8},{10,11... | collective-permute-start | bytes 688136 | tf_op jit(solution)/shard_map/ppermute | solution.py:21
  240.4 7.3 %collective-permute-start.31 = (bf16[1,448,256]{2,1,0:T(8,128)(2,1)S(1)}, bf16[1,448,256]{2,1,0:T(8,128)(2,1)S(1)}, u32[]{:S(2)}, u32[]{:S(2)}) collective-permute-start(bf16[1,448,256]{2,1,0:T(8,128)(2,1)S(1)} %add_convert_fusion.9), channel_id=1, source_target_pairs={{0,3},{1,2},{2,1},{3,0},{4,7},{5,6},{6,5},{7,4},{8,11},{9,10},{10,... | collective-permute-start | bytes 688136 | tf_op jit(solution)/shard_map/ppermute | solution.py:21
  243.5 6.1 %collective-permute-start.35 = (bf16[1,448,256]{2,1,0:T(8,128)(2,1)S(1)}, bf16[1,448,256]{2,1,0:T(8,128)(2,1)S(1)}, u32[]{:S(2)}, u32[]{:S(2)}) collective-permute-start(bf16[1,448,256]{2,1,0:T(8,128)(2,1)S(1)} %add_convert_fusion.8), channel_id=1, source_target_pairs={{0,4},{1,5},{2,6},{3,7},{4,0},{5,1},{6,2},{7,3},{8,12},{9,13},{10,... | collective-permute-start | bytes 688136 | tf_op jit(solution)/shard_map/ppermute | solution.py:21
  (8 other events, 17.9 us)
Sparse Core Ops, SparseCore 0:
  9.5 127.7 all-gather.1

commit v12 on v11

--- a/solution.py
+++ b/solution.py
@@ -251,7 +251,7 @@
 
     expert_hidden = expert_gate_up(slice_of, pooled, expert_gate, expert_up, gain_column)
     expert_partial = expert_down_parts(expert_down, expert_hidden)
-    _, scale, whole_columns = lax.optimization_barrier((expert_partial, scale, whole_columns))
+    expert_partial, scale, whole_columns = lax.optimization_barrier((expert_partial, scale, whole_columns))
     expert_parts = lax.all_to_all(
         expert_partial.reshape(16, slice_width, slot_count), "local", split_axis=0, concat_axis=0, tiled=True
     )

time: 260 us -> 254 us (0.977)
  waiting for transfers between devices: 68.1 us -> 63.1 us
    all_gather x1, waiting for transfers between devices: 22.8 us -> 10.6 us  [shards(): whole_columns = lax.all_gather(columns, 'local', axis=0, tiled=True)]
    ppermute x36, waiting for transfers between devices: 44.3 us -> 49.1 us  [flip_local(): lax.ppermute(array, 'local', [(i, LOCAL_AT[LOCAL_LABEL[i] ^ 1 << bit]) fo...]
where the time goes in v12:
time: 254 us; the launch traced here: 253 us
  starting transfers between devices  65.4 us (26%)
  waiting for transfers between devices  63.1 us (25%)
  other arithmetic  47.2 us (19%)
  local copies, waits for them, and re-layouts  27.2 us (11%)
  Pallas kernels  20.9 us (8%)
  matrix products  15.1 us (6%)
  between operations  13.9 us (5%)
    ppermute x36, starting transfers between devices, flip_local(): lax.ppermute(array, 'local', [(i, LOCAL_AT[LOCAL_LABEL[i] ^ 1 << bit]) fo...  51.5 us
    ppermute x36, waiting for transfers between devices, flip_local(): lax.ppermute(array, 'local', [(i, LOCAL_AT[LOCAL_LABEL[i] ^ 1 << bit]) fo...  49.1 us
    convert_element_type x12, other arithmetic, shards(): added(s, half, 2 * half).astype(jnp.bfloat16)  15.1 us
    unnamed x44, local copies, waits for them, and re-layouts  14 us
    dot_general x1, matrix products, transposed_dot(): lax.dot_general(weight, rows, (((0,), (0,)), ((), ())), preferred_element...  13.3 us
    all_gather x1, waiting for transfers between devices, shards(): whole_columns = lax.all_gather(columns, 'local', axis=0, tiled=True)  10.6 us
    pallas_call x1, Pallas kernels, expert_gate_up(): pl.pallas_call(functools.partial(expert_kernel, blocks, blocks * rows), g...  7.66 us
    convert_element_type x1, other arithmetic, shards(): (w.astype(jnp.float32) * gain_column).astype(jnp.bfloat16)  7.04 us
  transfers between devices with their start and end apart: 40, of which 19 were waited for; matrix products, arithmetic and copies ran while one was open for 30% of the time, Pallas kernels for 8%

profile of v12, /device:TPU:0, one launch (start us, length us, event | category | flops | bytes accessed | tf_op | source)
XLA Modules:
  0.0 252.8 jit_solution(976621716166451524)
XLA Ops:
  8.7 1.7 collective-permute-start.16
  11.2 2.3 reduce-window.6
  15.7 2.3 collective-permute-start.17
  18.8 1.9 collective-permute-done.17
  20.6 1.9 collective-permute-start.18
  23.7 4.3 %all-to-all-start = ((bf16[8,16,448]{2,1,0:T(8,128)(2,1)}), bf16[8,16,448]{2,1,0:T(8,128)(2,1)S(1)}, u32[]{:S(2)}, u32[]{:S(2)}) async-start(bf16[8,16,448]{2,1,0:T(8,128)(2,1)} %bitcast.3), calls=%async_computation | async-start | bytes 262144 | tf_op jit(solution)/shard_map/all_to_all | solution.py:226
  28.0 2.6 %collective-permute-start.19 = (f32[1,1024]{1,0:T(1,128)S(1)}, f32[1,1024]{1,0:T(1,128)S(1)}, u32[]{:S(2)}, u32[]{:S(2)}) collective-permute-start(f32[1,1024]{1,0:T(1,128)S(1)} %add.156), channel_id=1, source_target_pairs={{0,12},{1,13},{2,14},{3,15},{4,8},{5,9},{6,10},{7,11},{8,4},{9,5},... | collective-permute-start | bytes 12296 | tf_op jit(solution)/shard_map/ppermute | solution.py:21
  31.3 2.5 copy.51.gain_ref
  34.3 2.6 %collective-permute-start.6 = (bf16[1,112,128]{2,1,0:T(8,128)(2,1)S(1)}, bf16[1,112,128]{2,1,0:T(8,128)(2,1)S(1)}, u32[]{:S(2)}, u32[]{:S(2)}) collective-permute-start(bf16[1,112,128]{2,1,0:T(8,128)(2,1)S(1)} %get-tuple-element.73), channel_id=1, source_target_pairs={{0,12},{1,13},{2,14},{3,15},{4,8},{5,9},{6,10},{7,11},{8,4},{9,5},... | collective-permute-start | bytes 86024 | tf_op jit(solution)/shard_map/ppermute | solution.py:21
  38.0 2.2 collective-permute-start.2
  40.2 2.1 collective-permute-start.7
  44.2 2.3 collective-permute-start.1
  46.5 7.0 %multiply_convert_fusion.1 = (bf16[7168,256]{1,0:T(8,128)(2,1)}, bf16[7168,256]{1,0:T(8,128)(2,1)}) fusion(bf16[7168,256]{1,0:T(8,128)(2,1)} %param.13, f32[7168]{0:T(1024)S(1)} %copy-done.13, bf16[7168,256]{1,0:T(8,128)(2,1)} %param.14), kind=kLoop, calls=%fused_computation.2 | loop fusion | flops 11010048 | bytes 14708736 | tf_op jit(solution)/shard_map/convert_element_type | solution.py:242
  53.5 6.6 %pad_maximum_fusion = bf16[7168,512]{1,0:T(8,128)(2,1)} fusion(bf16[7168,256]{1,0:T(8,128)(2,1)} %get-tuple-element.78, bf16[7168,256]{1,0:T(8,128)(2,1)} %get-tuple-element.77), kind=kLoop, calls=%fused_computation | loop fusion | flops 14680064 | bytes 14680064 | tf_op jit(solution)/shard_map/concatenate | solution.py:241
  63.6 2.3 collective-permute-start.9
  67.3 6.0 %copy.50 = bf16[7168,256]{1,0:T(8,128)(2,1)} copy(bf16[7168,256]{0,1:T(8,128)(2,1)} %bitcast.68) | data formatting | bytes 7340032 | tf_op jit(solution)/shard_map/transpose | solution.py:247
  79.1 1.9 collective-permute-start.13
  87.0 2.9 %collective-permute-done.14 = bf16[8,112,128]{2,1,0:T(8,128)(2,1)S(1)} collective-permute-done((bf16[8,112,128]{2,1,0:T(8,128)(2,1)S(1)}, bf16[8,112,128]{2,1,0:T(8,128)(2,1)S(1)}, u32[]{:S(2)}, u32[]{:S(2)}) %collective-permute-start.14) | collective-permute-done | bytes 229408 | tf_op jit(solution)/shard_map/ppermute | solution.py:21
  91.2 3.9 %collective-permute-done.12 = bf16[8,112,128]{2,1,0:T(8,128)(2,1)S(1)} collective-permute-done((bf16[8,112,128]{2,1,0:T(8,128)(2,1)S(1)}, bf16[8,112,128]{2,1,0:T(8,128)(2,1)S(1)}, u32[]{:S(2)}, u32[]{:S(2)}) %collective-permute-start.12) | collective-permute-done | bytes 229408 | tf_op jit(solution)/shard_map/ppermute | solution.py:21
  95.1 2.0 copy-done.3
  97.1 2.2 copy-done.4
  99.3 7.7 %shard_map.109.hidden_ref = bf16[256,128]{1,0:T(8,128)(2,1)S(1)} custom-call(s32[16]{0:T(128)S(1)} %dynamic-slice_bitcast_fusion.at_ref.slice_ref, bf16[16,112,128]{2,1,0:T(8,128)(2,1)S(1)} %constant_dynamic-update-slice_fusion.x0, bf16[16,112,128]{2,1,0:T(8,128)(2,1)S(1)} %constant_dynamic-update-slice_fusion.5.x1, ...), custom_call_target="tpu_custom_call" | custom-call | flops 939524096 | bytes 9175040 | tf_op jit(solution)/shard_map/pallas_call | solution.py:147
  107.0 3.1 %shard_map.110 = bf16[7168,128]{1,0:T(8,128)(2,1)} custom-call(bf16[1,256,7168]{2,1,0:T(8,128)(2,1)S(1)} %copy-done.5, bf16[256,128]{1,0:T(8,128)(2,1)S(1)} %shard_map.109.hidden_ref), custom_call_target="tpu_custom_call" | custom-call | flops 469762048 | bytes 5505024 | tf_op jit(solution)/shard_map/pallas_call | solution.py:179
  110.1 10.6 %all-gather.2.cloned.1.call-done = bf16[7168,1024]{1,0:T(8,128)(2,1)} async-done(((bf16[448,1024]{1,0:T(8,128)(2,1)}), bf16[7168,1024]{1,0:T(8,128)(2,1)}) %all-gather.2.cloned.1.call-update) | async-done | bytes 14680080 | tf_op jit(solution)/shard_map/all_gather | solution.py:216
  120.7 5.3 %all-to-all-start.1 = ((bf16[16,448,128]{2,1,0:T(8,128)(2,1)}), bf16[16,448,128]{2,1,0:T(8,128)(2,1)}, u32[]{:S(2)}, u32[]{:S(2)}) async-start(bf16[16,448,128]{2,1,0:T(8,128)(2,1)} %bitcast.14), calls=%async_computation.1 | async-start | bytes 3670016 | tf_op jit(solution)/shard_map/all_to_all | solution.py:255
  126.1 13.3 %fusion.10.gate_up_ref = f32[512,1024]{1,0:T(8,128)S(1)} fusion(bf16[7168,512]{1,0:T(8,128)(2,1)} %pad_maximum_fusion, bf16[7168,1024]{1,0:T(8,128)(2,1)} %all-gather.2.cloned.1.call-done), kind=kOutput, calls=%fused_computation.84 | convolution fusion | flops 7516192768 | bytes 24117248 | tf_op jit(solution)/shard_map/dot_general | solution.py:36
  139.4 3.2 %shard_map.111 = (bf16[256,512]{1,0:T(8,128)(2,1)S(1)}, bf16[8,448,256]{2,1,0:T(8,128)(2,1)}, bf16[8,448,256]{2,1,0:T(8,128)(2,1)}) custom-call(s32[16]{0:T(128)S(1)} %dynamic-slice_bitcast_fusion.at_ref.slice_ref, f32[512,1024]{1,0:T(8,128)S(1)} %fusion.10.gate_up_ref, f32[1,1024]{1,0:T(1,128)S(1)} %add_rsqrt_fusion.scale_ref, ...), custom_call_target="tpu_custom_call" | custom-call | flops 939524096 | bytes 7340032 | tf_op jit(solution)/shard_map/pallas_call | solution.py:66
  142.6 1.9 collective-permute-start.20
  144.5 2.1 collective-permute-start.24
  146.5 3.1 %shard_map.112 = (bf16[256,512]{1,0:T(8,128)(2,1)S(1)}, bf16[8,448,256]{2,1,0:T(8,128)(2,1)}, bf16[8,448,256]{2,1,0:T(8,128)(2,1)}) custom-call(s32[16]{0:T(128)S(1)} %dynamic-slice_bitcast_fusion.at_ref.slice_ref, f32[512,1024]{1,0:T(8,128)S(1)} %fusion.10.gate_up_ref, f32[1,1024]{1,0:T(1,128)S(1)} %add_rsqrt_fusion.scale_ref, ...), custom_call_target="tpu_custom_call" | custom-call | flops 939524096 | bytes 7340032 | tf_op jit(solution)/shard_map/pallas_call | solution.py:66
  151.1 2.1 collective-permute-start.32
  153.2 2.3 all-to-all-done.1
  155.5 1.8 reduce_sum.65
  158.0 4.2 %all-to-all-start.2 = ((bf16[8,16,448]{2,1,0:T(8,128)(2,1)}), bf16[8,16,448]{2,1,0:T(8,128)(2,1)}, u32[]{:S(2)}, u32[]{:S(2)}) async-start(bf16[8,16,448]{2,1,0:T(8,128)(2,1)} %bitcast.17), calls=%async_computation.2 | async-start | bytes 262144 | tf_op jit(solution)/shard_map/all_to_all | solution.py:267
  162.3 2.0 copy-done.1
  164.3 3.8 %shard_map.113 = (bf16[8,448,256]{2,1,0:T(8,128)(2,1)S(1)}, bf16[8,448,256]{2,1,0:T(8,128)(2,1)S(1)}, bf16[8,448,256]{2,1,0:T(8,128)(2,1)S(1)}, bf16[8,448,256]{2,1,0:T(8,128)(2,1)S(1)}) custom-call(s32[16]{0:T(128)S(1)} %dynamic-slice_bitcast_fusion.at_ref.slice_ref, bf16[16,448,256]{2,1,0:T(8,128)(2,1)S(1)} %bitcast.63, ...), custom_call_target="tpu_custom_call" | custom-call | flops 1879048192 | bytes 14680064 | tf_op jit(solution)/shard_map/pallas_call | solution.py:96
  172.9 16.6 %collective-permute-done.20 = bf16[8,448,256]{2,1,0:T(8,128)(2,1)} collective-permute-done((bf16[8,448,256]{2,1,0:T(8,128)(2,1)}, bf16[8,448,256]{2,1,0:T(8,128)(2,1)}, u32[]{:S(2)}, u32[]{:S(2)}) %collective-permute-start.20) | collective-permute-done | bytes 1835040 | tf_op jit(solution)/shard_map/ppermute | solution.py:21
  189.6 1.7 add_convert_fusion.3
  191.2 3.1 %collective-permute-start.21 = (bf16[4,448,256]{2,1,0:T(8,128)(2,1)S(1)}, bf16[4,448,256]{2,1,0:T(8,128)(2,1)S(1)}, u32[]{:S(2)}, u32[]{:S(2)}) collective-permute-start(bf16[4,448,256]{2,1,0:T(8,128)(2,1)S(1)} %add_convert_fusion.3), channel_id=1, source_target_pairs={{0,3},{1,2},{2,1},{3,0},{4,7},{5,6},{6,5},{7,4},{8,11},{9,10},{10,... | collective-permute-start | bytes 2752520 | tf_op jit(solution)/shard_map/ppermute | solution.py:21
  198.1 2.6 %collective-permute-start.29 = (bf16[4,448,256]{2,1,0:T(8,128)(2,1)S(1)}, bf16[4,448,256]{2,1,0:T(8,128)(2,1)S(1)}, u32[]{:S(2)}, u32[]{:S(2)}) collective-permute-start(bf16[4,448,256]{2,1,0:T(8,128)(2,1)S(1)} %add_convert_fusion.1), channel_id=1, source_target_pairs={{0,12},{1,13},{2,14},{3,15},{4,8},{5,9},{6,10},{7,11},{8,4},{9,5},... | collective-permute-start | bytes 2752520 | tf_op jit(solution)/shard_map/ppermute | solution.py:21
  202.2 11.4 %collective-permute-done.21 = bf16[4,448,256]{2,1,0:T(8,128)(2,1)S(1)} collective-permute-done((bf16[4,448,256]{2,1,0:T(8,128)(2,1)S(1)}, bf16[4,448,256]{2,1,0:T(8,128)(2,1)S(1)}, u32[]{:S(2)}, u32[]{:S(2)}) %collective-permute-start.21) | collective-permute-done | bytes 917536 | tf_op jit(solution)/shard_map/ppermute | solution.py:21
  215.9 1.8 collective-permute-done.25
  218.9 1.7 collective-permute-start.26
  221.9 1.8 collective-permute-done.33
  227.4 2.0 collective-permute-start.23
  230.7 2.8 %collective-permute-done.30 = bf16[2,448,256]{2,1,0:T(8,128)(2,1)S(1)} collective-permute-done((bf16[2,448,256]{2,1,0:T(8,128)(2,1)S(1)}, bf16[2,448,256]{2,1,0:T(8,128)(2,1)S(1)}, u32[]{:S(2)}, u32[]{:S(2)}) %collective-permute-start.30) | collective-permute-done | bytes 458784 | tf_op jit(solution)/shard_map/ppermute | solution.py:21
  234.6 1.7 collective-permute-start.31
  239.6 2.2 collective-permute-done.31
  (149 shorter events, 59.8 us)
Async XLA Ops:
  6.5 114.2 %all-gather.2.cloned.1.call-start = ((), (), s32[]{:S(2)}) async-start(), calls=%async_computation.3 | async-start | bytes 15597568 | tf_op jit(solution)/shard_map/all_gather | solution.py:216
  8.7 7.1 %collective-permute-start.16 = (f32[1,1024]{1,0:T(1,128)S(1)}, f32[1,1024]{1,0:T(1,128)S(1)}, u32[]{:S(2)}, u32[]{:S(2)}) collective-permute-start(f32[1,1024]{1,0:T(1,128)S(1)} %bitcast.74), channel_id=1, source_target_pairs={{0,1},{1,0},{2,3},{3,2},{4,5},{5,4},{6,7},{7,6},{8,9},{9,8},{10,11... | collective-permute-start | bytes 12296 | tf_op jit(solution)/shard_map/ppermute | solution.py:21
  14.1 8.5 %copy-start.12 = (bf16[1024,448]{0,1:T(8,128)(2,1)S(1)}, bf16[1024,448]{0,1:T(8,128)(2,1)}, u32[]{:S(2)}) copy-start(bf16[1024,448]{0,1:T(8,128)(2,1)} %param.11) | copy-start | bytes 2752516
  15.4 16.0 %copy-start.13 = (f32[7168]{0:T(1024)S(1)}, f32[7168]{0:T(1024)}, u32[]{:S(2)}) copy-start(f32[7168]{0:T(1024)} %param.12) | copy-start | bytes 86020
  15.7 4.9 %collective-permute-start.17 = (f32[1,1024]{1,0:T(1,128)S(1)}, f32[1,1024]{1,0:T(1,128)S(1)}, u32[]{:S(2)}, u32[]{:S(2)}) collective-permute-start(f32[1,1024]{1,0:T(1,128)S(1)} %add.154), channel_id=1, source_target_pairs={{0,3},{1,2},{2,1},{3,0},{4,7},{5,6},{6,5},{7,4},{8,11},{9,10},{10,... | collective-permute-start | bytes 12296 | tf_op jit(solution)/shard_map/ppermute | solution.py:21
  20.6 7.4 %collective-permute-start.18 = (f32[1,1024]{1,0:T(1,128)S(1)}, f32[1,1024]{1,0:T(1,128)S(1)}, u32[]{:S(2)}, u32[]{:S(2)}) collective-permute-start(f32[1,1024]{1,0:T(1,128)S(1)} %add.155), channel_id=1, source_target_pairs={{0,4},{1,5},{2,6},{3,7},{4,0},{5,1},{6,2},{7,3},{8,12},{9,13},{10,... | collective-permute-start | bytes 12296 | tf_op jit(solution)/shard_map/ppermute | solution.py:21
  23.7 10.4 %all-to-all-start = ((bf16[8,16,448]{2,1,0:T(8,128)(2,1)}), bf16[8,16,448]{2,1,0:T(8,128)(2,1)S(1)}, u32[]{:S(2)}, u32[]{:S(2)}) async-start(bf16[8,16,448]{2,1,0:T(8,128)(2,1)} %bitcast.3), calls=%async_computation | async-start | bytes 262144 | tf_op jit(solution)/shard_map/all_to_all | solution.py:226
  28.0 5.8 %collective-permute-start.19 = (f32[1,1024]{1,0:T(1,128)S(1)}, f32[1,1024]{1,0:T(1,128)S(1)}, u32[]{:S(2)}, u32[]{:S(2)}) collective-permute-start(f32[1,1024]{1,0:T(1,128)S(1)} %add.156), channel_id=1, source_target_pairs={{0,12},{1,13},{2,14},{3,15},{4,8},{5,9},{6,10},{7,11},{8,4},{9,5},... | collective-permute-start | bytes 12296 | tf_op jit(solution)/shard_map/ppermute | solution.py:21
  34.3 5.9 %collective-permute-start.6 = (bf16[1,112,128]{2,1,0:T(8,128)(2,1)S(1)}, bf16[1,112,128]{2,1,0:T(8,128)(2,1)S(1)}, u32[]{:S(2)}, u32[]{:S(2)}) collective-permute-start(bf16[1,112,128]{2,1,0:T(8,128)(2,1)S(1)} %get-tuple-element.73), channel_id=1, source_target_pairs={{0,12},{1,13},{2,14},{3,15},{4,8},{5,9},{6,10},{7,11},{8,4},{9,5},... | collective-permute-start | bytes 86024 | tf_op jit(solution)/shard_map/ppermute | solution.py:21
  36.9 5.4 %collective-permute-start.4 = (bf16[1,112,128]{2,1,0:T(8,128)(2,1)S(1)}, bf16[1,112,128]{2,1,0:T(8,128)(2,1)S(1)}, u32[]{:S(2)}, u32[]{:S(2)}) collective-permute-start(bf16[1,112,128]{2,1,0:T(8,128)(2,1)S(1)} %get-tuple-element.74), channel_id=1, source_target_pairs={{0,4},{1,5},{2,6},{3,7},{4,0},{5,1},{6,2},{7,3},{8,12},{9,13},{10,... | collective-permute-start | bytes 86024 | tf_op jit(solution)/shard_map/ppermute | solution.py:21
  38.0 5.1 %collective-permute-start.2 = (bf16[1,112,128]{2,1,0:T(8,128)(2,1)S(1)}, bf16[1,112,128]{2,1,0:T(8,128)(2,1)S(1)}, u32[]{:S(2)}, u32[]{:S(2)}) collective-permute-start(bf16[1,112,128]{2,1,0:T(8,128)(2,1)S(1)} %get-tuple-element.75), channel_id=1, source_target_pairs={{0,3},{1,2},{2,1},{3,0},{4,7},{5,6},{6,5},{7,4},{8,11},{9,10},{10,... | collective-permute-start | bytes 86024 | tf_op jit(solution)/shard_map/ppermute | solution.py:21
  40.2 4.0 %collective-permute-start = (bf16[1,112,128]{2,1,0:T(8,128)(2,1)S(1)}, bf16[1,112,128]{2,1,0:T(8,128)(2,1)S(1)}, u32[]{:S(2)}, u32[]{:S(2)}) collective-permute-start(bf16[1,112,128]{2,1,0:T(8,128)(2,1)S(1)} %get-tuple-element.76), channel_id=1, source_target_pairs={{0,1},{1,0},{2,3},{3,2},{4,5},{5,4},{6,7},{7,6},{8,9},{9,8},{10,11... | collective-permute-start | bytes 86024 | tf_op jit(solution)/shard_map/ppermute | solution.py:21
  40.2 19.9 %collective-permute-start.7 = (bf16[2,112,128]{2,1,0:T(8,128)(2,1)S(1)}, bf16[2,112,128]{2,1,0:T(8,128)(2,1)S(1)}, u32[]{:S(2)}, u32[]{:S(2)}) collective-permute-start(bf16[2,112,128]{2,1,0:T(8,128)(2,1)S(1)} %pad_maximum_fusion.12), channel_id=1, source_target_pairs={{0,1},{1,0},{2,3},{3,2},{4,5},{5,4},{6,7},{7,6},{8,9},{9,8},{10,11... | collective-permute-start | bytes 172040 | tf_op jit(solution)/shard_map/ppermute | solution.py:21
  42.3 17.8 %collective-permute-start.5 = (bf16[2,112,128]{2,1,0:T(8,128)(2,1)S(1)}, bf16[2,112,128]{2,1,0:T(8,128)(2,1)S(1)}, u32[]{:S(2)}, u32[]{:S(2)}) collective-permute-start(bf16[2,112,128]{2,1,0:T(8,128)(2,1)S(1)} %pad_maximum_fusion.11), channel_id=1, source_target_pairs={{0,12},{1,13},{2,14},{3,15},{4,8},{5,9},{6,10},{7,11},{8,4},{9,5},... | collective-permute-start | bytes 172040 | tf_op jit(solution)/shard_map/ppermute | solution.py:21
  43.1 17.1 %collective-permute-start.3 = (bf16[2,112,128]{2,1,0:T(8,128)(2,1)S(1)}, bf16[2,112,128]{2,1,0:T(8,128)(2,1)S(1)}, u32[]{:S(2)}, u32[]{:S(2)}) collective-permute-start(bf16[2,112,128]{2,1,0:T(8,128)(2,1)S(1)} %pad_maximum_fusion.10), channel_id=1, source_target_pairs={{0,4},{1,5},{2,6},{3,7},{4,0},{5,1},{6,2},{7,3},{8,12},{9,13},{10,... | collective-permute-start | bytes 172040 | tf_op jit(solution)/shard_map/ppermute | solution.py:21
  44.2 16.0 %collective-permute-start.1 = (bf16[2,112,128]{2,1,0:T(8,128)(2,1)S(1)}, bf16[2,112,128]{2,1,0:T(8,128)(2,1)S(1)}, u32[]{:S(2)}, u32[]{:S(2)}) collective-permute-start(bf16[2,112,128]{2,1,0:T(8,128)(2,1)S(1)} %pad_maximum_fusion.9), channel_id=1, source_target_pairs={{0,3},{1,2},{2,1},{3,0},{4,7},{5,6},{6,5},{7,4},{8,11},{9,10},{10,... | collective-permute-start | bytes 172040 | tf_op jit(solution)/shard_map/ppermute | solution.py:21
  60.9 12.4 %collective-permute-start.11 = (bf16[4,112,128]{2,1,0:T(8,128)(2,1)}, bf16[4,112,128]{2,1,0:T(8,128)(2,1)}, u32[]{:S(2)}, u32[]{:S(2)}) collective-permute-start(bf16[4,112,128]{2,1,0:T(8,128)(2,1)} %pad_maximum_fusion.8), channel_id=1, source_target_pairs={{0,3},{1,2},{2,1},{3,0},{4,7},{5,6},{6,5},{7,4},{8,11},{9,10},{10,... | collective-permute-start | bytes 344072 | tf_op jit(solution)/shard_map/ppermute | solution.py:21
  63.0 10.3 %collective-permute-start.10 = (bf16[4,112,128]{2,1,0:T(8,128)(2,1)}, bf16[4,112,128]{2,1,0:T(8,128)(2,1)}, u32[]{:S(2)}, u32[]{:S(2)}) collective-permute-start(bf16[4,112,128]{2,1,0:T(8,128)(2,1)} %pad_maximum_fusion.7), channel_id=1, source_target_pairs={{0,1},{1,0},{2,3},{3,2},{4,5},{5,4},{6,7},{7,6},{8,9},{9,8},{10,11... | collective-permute-start | bytes 344072 | tf_op jit(solution)/shard_map/ppermute | solution.py:21
  63.6 9.7 %collective-permute-start.9 = (bf16[4,112,128]{2,1,0:T(8,128)(2,1)}, bf16[4,112,128]{2,1,0:T(8,128)(2,1)}, u32[]{:S(2)}, u32[]{:S(2)}) collective-permute-start(bf16[4,112,128]{2,1,0:T(8,128)(2,1)} %pad_maximum_fusion.6), channel_id=1, source_target_pairs={{0,12},{1,13},{2,14},{3,15},{4,8},{5,9},{6,10},{7,11},{8,4},{9,5},... | collective-permute-start | bytes 344072 | tf_op jit(solution)/shard_map/ppermute | solution.py:21
  66.5 7.5 %collective-permute-start.8 = (bf16[4,112,128]{2,1,0:T(8,128)(2,1)}, bf16[4,112,128]{2,1,0:T(8,128)(2,1)}, u32[]{:S(2)}, u32[]{:S(2)}) collective-permute-start(bf16[4,112,128]{2,1,0:T(8,128)(2,1)} %pad_maximum_fusion.5), channel_id=1, source_target_pairs={{0,4},{1,5},{2,6},{3,7},{4,0},{5,1},{6,2},{7,3},{8,12},{9,13},{10,... | collective-permute-start | bytes 344072 | tf_op jit(solution)/shard_map/ppermute | solution.py:21
  75.0 12.0 %collective-permute-start.15 = (bf16[8,112,128]{2,1,0:T(8,128)(2,1)S(1)}, bf16[8,112,128]{2,1,0:T(8,128)(2,1)S(1)}, u32[]{:S(2)}, u32[]{:S(2)}) collective-permute-start(bf16[8,112,128]{2,1,0:T(8,128)(2,1)S(1)} %pad_maximum_fusion.4), channel_id=1, source_target_pairs={{0,4},{1,5},{2,6},{3,7},{4,0},{5,1},{6,2},{7,3},{8,12},{9,13},{10,... | collective-permute-start | bytes 688136 | tf_op jit(solution)/shard_map/ppermute | solution.py:21
  76.8 18.3 %copy-start.2 = (f32[7168,1]{1,0:T(8,128)S(1)}, f32[7168,1]{1,0:T(8,128)}, u32[]{:S(2)}) copy-start(f32[7168,1]{1,0:T(8,128)} %copy.51.gain_ref) | copy-start | bytes 86020
  76.8 13.1 %collective-permute-start.14 = (bf16[8,112,128]{2,1,0:T(8,128)(2,1)S(1)}, bf16[8,112,128]{2,1,0:T(8,128)(2,1)S(1)}, u32[]{:S(2)}, u32[]{:S(2)}) collective-permute-start(bf16[8,112,128]{2,1,0:T(8,128)(2,1)S(1)} %pad_maximum_fusion.3), channel_id=1, source_target_pairs={{0,3},{1,2},{2,1},{3,0},{4,7},{5,6},{6,5},{7,4},{8,11},{9,10},{10,... | collective-permute-start | bytes 688136 | tf_op jit(solution)/shard_map/ppermute | solution.py:21
  79.1 12.0 %collective-permute-start.13 = (bf16[8,112,128]{2,1,0:T(8,128)(2,1)S(1)}, bf16[8,112,128]{2,1,0:T(8,128)(2,1)S(1)}, u32[]{:S(2)}, u32[]{:S(2)}) collective-permute-start(bf16[8,112,128]{2,1,0:T(8,128)(2,1)S(1)} %pad_maximum_fusion.2), channel_id=1, source_target_pairs={{0,1},{1,0},{2,3},{3,2},{4,5},{5,4},{6,7},{7,6},{8,9},{9,8},{10,11... | collective-permute-start | bytes 688136 | tf_op jit(solution)/shard_map/ppermute | solution.py:21
  81.9 13.1 %collective-permute-start.12 = (bf16[8,112,128]{2,1,0:T(8,128)(2,1)S(1)}, bf16[8,112,128]{2,1,0:T(8,128)(2,1)S(1)}, u32[]{:S(2)}, u32[]{:S(2)}) collective-permute-start(bf16[8,112,128]{2,1,0:T(8,128)(2,1)S(1)} %pad_maximum_fusion.1), channel_id=1, source_target_pairs={{0,12},{1,13},{2,14},{3,15},{4,8},{5,9},{6,10},{7,11},{8,4},{9,5},... | collective-permute-start | bytes 688136 | tf_op jit(solution)/shard_map/ppermute | solution.py:21
  99.3 7.7 %copy-start.5 = (bf16[1,256,7168]{2,1,0:T(8,128)(2,1)S(1)}, bf16[1,256,7168]{2,1,0:T(8,128)(2,1)}, u32[]{:S(2)}) copy-start(bf16[1,256,7168]{2,1,0:T(8,128)(2,1)} %weight_ref.1) | copy-start | bytes 11010052
  120.7 34.7 %all-to-all-start.1 = ((bf16[16,448,128]{2,1,0:T(8,128)(2,1)}), bf16[16,448,128]{2,1,0:T(8,128)(2,1)}, u32[]{:S(2)}, u32[]{:S(2)}) async-start(bf16[16,448,128]{2,1,0:T(8,128)(2,1)} %bitcast.14), calls=%async_computation.1 | async-start | bytes 3670016 | tf_op jit(solution)/shard_map/all_to_all | solution.py:255
  126.1 13.3 %copy-start = (bf16[7168,256]{1,0:T(8,128)(2,1)S(1)}, bf16[7168,256]{1,0:T(8,128)(2,1)}, u32[]{:S(2)}) copy-start(bf16[7168,256]{1,0:T(8,128)(2,1)} %copy.50) | copy-start | bytes 11010052
  142.6 47.0 %collective-permute-start.20 = (bf16[8,448,256]{2,1,0:T(8,128)(2,1)}, bf16[8,448,256]{2,1,0:T(8,128)(2,1)}, u32[]{:S(2)}, u32[]{:S(2)}) collective-permute-start(bf16[8,448,256]{2,1,0:T(8,128)(2,1)} %get-tuple-element.55), channel_id=1, source_target_pairs={{0,1},{1,0},{2,3},{3,2},{4,5},{5,4},{6,7},{7,6},{8,9},{9,8},{10,11... | collective-permute-start | bytes 5505032 | tf_op jit(solution)/shard_map/ppermute | solution.py:21
  144.5 49.9 %collective-permute-start.24 = (bf16[8,448,256]{2,1,0:T(8,128)(2,1)}, bf16[8,448,256]{2,1,0:T(8,128)(2,1)}, u32[]{:S(2)}, u32[]{:S(2)}) collective-permute-start(bf16[8,448,256]{2,1,0:T(8,128)(2,1)} %get-tuple-element.57), channel_id=1, source_target_pairs={{0,3},{1,2},{2,1},{3,0},{4,7},{5,6},{6,5},{7,4},{8,11},{9,10},{10,... | collective-permute-start | bytes 5505032 | tf_op jit(solution)/shard_map/ppermute | solution.py:21
  149.7 46.9 %collective-permute-start.28 = (bf16[8,448,256]{2,1,0:T(8,128)(2,1)}, bf16[8,448,256]{2,1,0:T(8,128)(2,1)}, u32[]{:S(2)}, u32[]{:S(2)}) collective-permute-start(bf16[8,448,256]{2,1,0:T(8,128)(2,1)} %get-tuple-element.61), channel_id=1, source_target_pairs={{0,4},{1,5},{2,6},{3,7},{4,0},{5,1},{6,2},{7,3},{8,12},{9,13},{10,... | collective-permute-start | bytes 5505032 | tf_op jit(solution)/shard_map/ppermute | solution.py:21
  151.1 49.5 %collective-permute-start.32 = (bf16[8,448,256]{2,1,0:T(8,128)(2,1)}, bf16[8,448,256]{2,1,0:T(8,128)(2,1)}, u32[]{:S(2)}, u32[]{:S(2)}) collective-permute-start(bf16[8,448,256]{2,1,0:T(8,128)(2,1)} %get-tuple-element.63), channel_id=1, source_target_pairs={{0,12},{1,13},{2,14},{3,15},{4,8},{5,9},{6,10},{7,11},{8,4},{9,5},... | collective-permute-start | bytes 5505032 | tf_op jit(solution)/shard_map/ppermute | solution.py:21
  158.0 13.8 %all-to-all-start.2 = ((bf16[8,16,448]{2,1,0:T(8,128)(2,1)}), bf16[8,16,448]{2,1,0:T(8,128)(2,1)}, u32[]{:S(2)}, u32[]{:S(2)}) async-start(bf16[8,16,448]{2,1,0:T(8,128)(2,1)} %bitcast.17), calls=%async_computation.2 | async-start | bytes 262144 | tf_op jit(solution)/shard_map/all_to_all | solution.py:267
  171.8 22.6 %copy-start.9 = (bf16[8,448,256]{2,1,0:T(8,128)(2,1)S(1)}, bf16[8,448,256]{2,1,0:T(8,128)(2,1)}, u32[]{:S(2)}) copy-start(bf16[8,448,256]{2,1,0:T(8,128)(2,1)} %copy-done.8) | copy-start | bytes 5505028
  191.2 5.4 %copy-start.7 = (bf16[8,448,256]{2,1,0:T(8,128)(2,1)S(1)}, bf16[8,448,256]{2,1,0:T(8,128)(2,1)}, u32[]{:S(2)}) copy-start(bf16[8,448,256]{2,1,0:T(8,128)(2,1)} %copy-done.6) | copy-start | bytes 5505028
  191.2 22.3 %collective-permute-start.21 = (bf16[4,448,256]{2,1,0:T(8,128)(2,1)S(1)}, bf16[4,448,256]{2,1,0:T(8,128)(2,1)S(1)}, u32[]{:S(2)}, u32[]{:S(2)}) collective-permute-start(bf16[4,448,256]{2,1,0:T(8,128)(2,1)S(1)} %add_convert_fusion.3), channel_id=1, source_target_pairs={{0,3},{1,2},{2,1},{3,0},{4,7},{5,6},{6,5},{7,4},{8,11},{9,10},{10,... | collective-permute-start | bytes 2752520 | tf_op jit(solution)/shard_map/ppermute | solution.py:21
  195.8 21.9 %collective-permute-start.25 = (bf16[4,448,256]{2,1,0:T(8,128)(2,1)S(1)}, bf16[4,448,256]{2,1,0:T(8,128)(2,1)S(1)}, u32[]{:S(2)}, u32[]{:S(2)}) collective-permute-start(bf16[4,448,256]{2,1,0:T(8,128)(2,1)S(1)} %add_convert_fusion.2), channel_id=1, source_target_pairs={{0,4},{1,5},{2,6},{3,7},{4,0},{5,1},{6,2},{7,3},{8,12},{9,13},{10,... | collective-permute-start | bytes 2752520 | tf_op jit(solution)/shard_map/ppermute | solution.py:21
  198.0 15.5 %copy-start.11 = (bf16[8,448,256]{2,1,0:T(8,128)(2,1)S(1)}, bf16[8,448,256]{2,1,0:T(8,128)(2,1)}, u32[]{:S(2)}) copy-start(bf16[8,448,256]{2,1,0:T(8,128)(2,1)} %copy-done.10) | copy-start | bytes 5505028
  198.1 22.5 %collective-permute-start.29 = (bf16[4,448,256]{2,1,0:T(8,128)(2,1)S(1)}, bf16[4,448,256]{2,1,0:T(8,128)(2,1)S(1)}, u32[]{:S(2)}, u32[]{:S(2)}) collective-permute-start(bf16[4,448,256]{2,1,0:T(8,128)(2,1)S(1)} %add_convert_fusion.1), channel_id=1, source_target_pairs={{0,12},{1,13},{2,14},{3,15},{4,8},{5,9},{6,10},{7,11},{8,4},{9,5},... | collective-permute-start | bytes 2752520 | tf_op jit(solution)/shard_map/ppermute | solution.py:21
  202.1 21.6 %collective-permute-start.33 = (bf16[4,448,256]{2,1,0:T(8,128)(2,1)S(1)}, bf16[4,448,256]{2,1,0:T(8,128)(2,1)S(1)}, u32[]{:S(2)}, u32[]{:S(2)}) collective-permute-start(bf16[4,448,256]{2,1,0:T(8,128)(2,1)S(1)} %add_convert_fusion), channel_id=1, source_target_pairs={{0,1},{1,0},{2,3},{3,2},{4,5},{5,4},{6,7},{7,6},{8,9},{9,8},{10,11... | collective-permute-start | bytes 2752520 | tf_op jit(solution)/shard_map/ppermute | solution.py:21
  214.8 11.6 %collective-permute-start.22 = (bf16[2,448,256]{2,1,0:T(8,128)(2,1)S(1)}, bf16[2,448,256]{2,1,0:T(8,128)(2,1)S(1)}, u32[]{:S(2)}, u32[]{:S(2)}) collective-permute-start(bf16[2,448,256]{2,1,0:T(8,128)(2,1)S(1)} %add_convert_fusion.7), channel_id=1, source_target_pairs={{0,4},{1,5},{2,6},{3,7},{4,0},{5,1},{6,2},{7,3},{8,12},{9,13},{10,... | collective-permute-start | bytes 1376264 | tf_op jit(solution)/shard_map/ppermute | solution.py:21
  218.9 10.6 %collective-permute-start.26 = (bf16[2,448,256]{2,1,0:T(8,128)(2,1)S(1)}, bf16[2,448,256]{2,1,0:T(8,128)(2,1)S(1)}, u32[]{:S(2)}, u32[]{:S(2)}) collective-permute-start(bf16[2,448,256]{2,1,0:T(8,128)(2,1)S(1)} %add_convert_fusion.6), channel_id=1, source_target_pairs={{0,12},{1,13},{2,14},{3,15},{4,8},{5,9},{6,10},{7,11},{8,4},{9,5},... | collective-permute-start | bytes 1376264 | tf_op jit(solution)/shard_map/ppermute | solution.py:21
  221.8 11.7 %collective-permute-start.30 = (bf16[2,448,256]{2,1,0:T(8,128)(2,1)S(1)}, bf16[2,448,256]{2,1,0:T(8,128)(2,1)S(1)}, u32[]{:S(2)}, u32[]{:S(2)}) collective-permute-start(bf16[2,448,256]{2,1,0:T(8,128)(2,1)S(1)} %add_convert_fusion.5), channel_id=1, source_target_pairs={{0,1},{1,0},{2,3},{3,2},{4,5},{5,4},{6,7},{7,6},{8,9},{9,8},{10,11... | collective-permute-start | bytes 1376264 | tf_op jit(solution)/shard_map/ppermute | solution.py:21
  224.9 11.4 %collective-permute-start.34 = (bf16[2,448,256]{2,1,0:T(8,128)(2,1)S(1)}, bf16[2,448,256]{2,1,0:T(8,128)(2,1)S(1)}, u32[]{:S(2)}, u32[]{:S(2)}) collective-permute-start(bf16[2,448,256]{2,1,0:T(8,128)(2,1)S(1)} %add_convert_fusion.4), channel_id=1, source_target_pairs={{0,3},{1,2},{2,1},{3,0},{4,7},{5,6},{6,5},{7,4},{8,11},{9,10},{10,... | collective-permute-start | bytes 1376264 | tf_op jit(solution)/shard_map/ppermute | solution.py:21
  227.4 10.0 %collective-permute-start.23 = (bf16[1,448,256]{2,1,0:T(8,128)(2,1)S(1)}, bf16[1,448,256]{2,1,0:T(8,128)(2,1)S(1)}, u32[]{:S(2)}, u32[]{:S(2)}) collective-permute-start(bf16[1,448,256]{2,1,0:T(8,128)(2,1)S(1)} %add_convert_fusion.11), channel_id=1, source_target_pairs={{0,12},{1,13},{2,14},{3,15},{4,8},{5,9},{6,10},{7,11},{8,4},{9,5},... | collective-permute-start | bytes 688136 | tf_op jit(solution)/shard_map/ppermute | solution.py:21
  230.6 7.9 %collective-permute-start.27 = (bf16[1,448,256]{2,1,0:T(8,128)(2,1)S(1)}, bf16[1,448,256]{2,1,0:T(8,128)(2,1)S(1)}, u32[]{:S(2)}, u32[]{:S(2)}) collective-permute-start(bf16[1,448,256]{2,1,0:T(8,128)(2,1)S(1)} %add_convert_fusion.10), channel_id=1, source_target_pairs={{0,1},{1,0},{2,3},{3,2},{4,5},{5,4},{6,7},{7,6},{8,9},{9,8},{10,11... | collective-permute-start | bytes 688136 | tf_op jit(solution)/shard_map/ppermute | solution.py:21
  234.6 7.3 %collective-permute-start.31 = (bf16[1,448,256]{2,1,0:T(8,128)(2,1)S(1)}, bf16[1,448,256]{2,1,0:T(8,128)(2,1)S(1)}, u32[]{:S(2)}, u32[]{:S(2)}) collective-permute-start(bf16[1,448,256]{2,1,0:T(8,128)(2,1)S(1)} %add_convert_fusion.9), channel_id=1, source_target_pairs={{0,3},{1,2},{2,1},{3,0},{4,7},{5,6},{6,5},{7,4},{8,11},{9,10},{10,... | collective-permute-start | bytes 688136 | tf_op jit(solution)/shard_map/ppermute | solution.py:21
  237.3 6.1 %collective-permute-start.35 = (bf16[1,448,256]{2,1,0:T(8,128)(2,1)S(1)}, bf16[1,448,256]{2,1,0:T(8,128)(2,1)S(1)}, u32[]{:S(2)}, u32[]{:S(2)}) collective-permute-start(bf16[1,448,256]{2,1,0:T(8,128)(2,1)S(1)} %add_convert_fusion.8), channel_id=1, source_target_pairs={{0,4},{1,5},{2,6},{3,7},{4,0},{5,1},{6,2},{7,3},{8,12},{9,13},{10,... | collective-permute-start | bytes 688136 | tf_op jit(solution)/shard_map/ppermute | solution.py:21
  (8 other events, 17.9 us)
Sparse Core Ops, SparseCore 0:
  9.5 111.1 all-gather.1

commit v13 on v12

--- a/solution.py
+++ b/solution.py
@@ -238,10 +238,8 @@
         square_sum = square_sum + flip_local(square_sum, step)
         if step == 1:
             dense_gate, dense_up, _ = lax.optimization_barrier((dense_gate, dense_up, pooled))
-            weight = jnp.concatenate(
-                [(w.astype(jnp.float32) * gain_column).astype(jnp.bfloat16) for w in (dense_gate, dense_up)], axis=1
-            )
-            got, weight = lax.optimization_barrier((got, weight))
+            folded = [(w.astype(jnp.float32) * gain_column).astype(jnp.bfloat16) for w in (dense_gate, dense_up)]
+            got, folded = lax.optimization_barrier((got, folded))
         if step == 2:
             dense_down, _ = lax.optimization_barrier((dense_down, pooled))
             turned = dense_down.T.reshape(16, slice_width, dense_down.shape[0])
@@ -251,12 +249,14 @@
 
     expert_hidden = expert_gate_up(slice_of, pooled, expert_gate, expert_up, gain_column)
     expert_partial = expert_down_parts(expert_down, expert_hidden)
-    expert_partial, scale, whole_columns = lax.optimization_barrier((expert_partial, scale, whole_columns))
+    expert_partial, scale, whole_columns, folded = lax.optimization_barrier(
+        (expert_partial, scale, whole_columns, folded)
+    )
     expert_parts = lax.all_to_all(
         expert_partial.reshape(16, slice_width, slot_count), "local", split_axis=0, concat_axis=0, tiled=True
     )
 
-    gate_up = transposed_dot(weight, whole_columns)
+    gate_up = transposed_dot(jnp.concatenate(folded, axis=1), whole_columns)
     low_hidden, *sent = sent_parts(0, slice_of, gate_up, scale, turned)
     high_hidden, *more = sent_parts(2, slice_of, gate_up, scale, turned)
     sent += more

time: 254 us -> 254 us (level)
  other arithmetic: 47.2 us -> 39.7 us
  waiting for transfers between devices: 63.1 us -> 69.2 us
    all_gather x1, waiting for transfers between devices: 10.6 us -> 17.9 us  [shards(): whole_columns = lax.all_gather(columns, 'local', axis=0, tiled=True)]
    concatenate x1 -> x0, other arithmetic: 6.62 us -> none  [shards(): jnp.concatenate([(w.astype(jnp.float32) * gain_column).astype(jnp.bfloat1...]
  transfers between devices with their start and end apart: 40 -> 40, of which waited for: 19 -> 18; matrix products, arithmetic and copies ran while one was open for 30% -> 28% of each run, Pallas kernels for 8% -> 8%
where the time goes in v13:
time: 254 us; the launch traced here: 253 us
  waiting for transfers between devices  69.2 us (27%)
  starting transfers between devices  65.9 us (26%)
  other arithmetic  39.7 us (16%)
  local copies, waits for them, and re-layouts  28 us (11%)
  Pallas kernels  20.9 us (8%)
  matrix products  15.1 us (6%)
  between operations  13.9 us (5%)
    ppermute x36, starting transfers between devices, flip_local(): lax.ppermute(array, 'local', [(i, LOCAL_AT[LOCAL_LABEL[i] ^ 1 << bit]) fo...  52.1 us
    ppermute x36, waiting for transfers between devices, flip_local(): lax.ppermute(array, 'local', [(i, LOCAL_AT[LOCAL_LABEL[i] ^ 1 << bit]) fo...  48.2 us
    all_gather x1, waiting for transfers between devices, shards(): whole_columns = lax.all_gather(columns, 'local', axis=0, tiled=True)  17.9 us
    convert_element_type x12, other arithmetic, shards(): added(s, half, 2 * half).astype(jnp.bfloat16)  15 us
    unnamed x44, local copies, waits for them, and re-layouts  13.9 us
    dot_general x1, matrix products, transposed_dot(): lax.dot_general(weight, rows, (((0,), (0,)), ((), ())), preferred_element...  13.3 us
    pallas_call x1, Pallas kernels, expert_gate_up(): pl.pallas_call(functools.partial(expert_kernel, blocks, blocks * rows), g...  7.67 us
    convert_element_type x1, other arithmetic, shards(): (w.astype(jnp.float32) * gain_column).astype(jnp.bfloat16)  7.04 us
  transfers between devices with their start and end apart: 40, of which 18 were waited for; matrix products, arithmetic and copies ran while one was open for 28% of the time, Pallas kernels for 8%

profile of v13, /device:TPU:0, one launch (start us, length us, event | category | flops | bytes accessed | tf_op | source)
XLA Modules:
  0.0 252.7 jit_solution(9394663306820619562)
XLA Ops:
  8.7 1.7 collective-permute-start.16
  11.2 2.3 reduce-window.6
  15.7 2.3 collective-permute-start.17
  18.8 1.9 collective-permute-done.17
  20.6 1.9 collective-permute-start.18
  23.7 4.3 %all-to-all-start = ((bf16[8,16,448]{2,1,0:T(8,128)(2,1)}), bf16[8,16,448]{2,1,0:T(8,128)(2,1)S(1)}, u32[]{:S(2)}, u32[]{:S(2)}) async-start(bf16[8,16,448]{2,1,0:T(8,128)(2,1)} %bitcast.3), calls=%async_computation | async-start | bytes 262144 | tf_op jit(solution)/shard_map/all_to_all | solution.py:226
  28.0 2.6 %collective-permute-start.19 = (f32[1,1024]{1,0:T(1,128)S(1)}, f32[1,1024]{1,0:T(1,128)S(1)}, u32[]{:S(2)}, u32[]{:S(2)}) collective-permute-start(f32[1,1024]{1,0:T(1,128)S(1)} %add.156), channel_id=1, source_target_pairs={{0,12},{1,13},{2,14},{3,15},{4,8},{5,9},{6,10},{7,11},{8,4},{9,5},... | collective-permute-start | bytes 12296 | tf_op jit(solution)/shard_map/ppermute | solution.py:21
  31.3 2.5 copy.51.gain_ref
  34.3 2.6 %collective-permute-start.6 = (bf16[1,112,128]{2,1,0:T(8,128)(2,1)S(1)}, bf16[1,112,128]{2,1,0:T(8,128)(2,1)S(1)}, u32[]{:S(2)}, u32[]{:S(2)}) collective-permute-start(bf16[1,112,128]{2,1,0:T(8,128)(2,1)S(1)} %get-tuple-element.79), channel_id=1, source_target_pairs={{0,12},{1,13},{2,14},{3,15},{4,8},{5,9},{6,10},{7,11},{8,4},{9,5},... | collective-permute-start | bytes 86024 | tf_op jit(solution)/shard_map/ppermute | solution.py:21
  38.0 2.2 collective-permute-start.2
  40.2 2.1 collective-permute-start.7
  44.2 2.3 collective-permute-start.1
  46.5 7.0 %multiply_convert_fusion = (bf16[7168,256]{1,0:T(8,128)(2,1)}, bf16[7168,256]{1,0:T(8,128)(2,1)}) fusion(bf16[7168,256]{1,0:T(8,128)(2,1)} %param.14, f32[7168]{0:T(1024)S(1)} %copy-done.13, bf16[7168,256]{1,0:T(8,128)(2,1)} %param.13), kind=kLoop, calls=%fused_computation.4 | loop fusion | flops 11010048 | bytes 14708736 | tf_op jit(solution)/shard_map/convert_element_type | solution.py:241
  56.9 1.6 collective-permute-start.9
  60.4 6.0 %copy.50 = bf16[7168,256]{1,0:T(8,128)(2,1)} copy(bf16[7168,256]{0,1:T(8,128)(2,1)} %bitcast.67) | data formatting | bytes 7340032 | tf_op jit(solution)/shard_map/transpose | solution.py:245
  72.1 1.8 collective-permute-start.13
  74.9 1.5 collective-permute-start.12
  80.2 2.7 %collective-permute-done.14 = bf16[8,112,128]{2,1,0:T(8,128)(2,1)S(1)} collective-permute-done((bf16[8,112,128]{2,1,0:T(8,128)(2,1)S(1)}, bf16[8,112,128]{2,1,0:T(8,128)(2,1)S(1)}, u32[]{:S(2)}, u32[]{:S(2)}) %collective-permute-start.14) | collective-permute-done | bytes 229408 | tf_op jit(solution)/shard_map/ppermute | solution.py:21
  83.9 3.9 %collective-permute-done.12 = bf16[8,112,128]{2,1,0:T(8,128)(2,1)S(1)} collective-permute-done((bf16[8,112,128]{2,1,0:T(8,128)(2,1)S(1)}, bf16[8,112,128]{2,1,0:T(8,128)(2,1)S(1)}, u32[]{:S(2)}, u32[]{:S(2)}) %collective-permute-start.12) | collective-permute-done | bytes 229408 | tf_op jit(solution)/shard_map/ppermute | solution.py:21
  87.9 2.1 copy-done.3
  90.0 2.0 copy-done.4
  92.0 7.7 %shard_map.109.hidden_ref = bf16[256,128]{1,0:T(8,128)(2,1)S(1)} custom-call(s32[16]{0:T(128)S(1)} %dynamic-slice_bitcast_fusion.at_ref.slice_ref, bf16[16,112,128]{2,1,0:T(8,128)(2,1)S(1)} %constant_dynamic-update-slice_fusion.x0, bf16[16,112,128]{2,1,0:T(8,128)(2,1)S(1)} %constant_dynamic-update-slice_fusion.5.x1, ...), custom_call_target="tpu_custom_call" | custom-call | flops 939524096 | bytes 9175040 | tf_op jit(solution)/shard_map/pallas_call | solution.py:147
  99.7 3.1 %shard_map.110 = bf16[7168,128]{1,0:T(8,128)(2,1)} custom-call(bf16[1,256,7168]{2,1,0:T(8,128)(2,1)S(1)} %copy-done.5, bf16[256,128]{1,0:T(8,128)(2,1)S(1)} %shard_map.109.hidden_ref), custom_call_target="tpu_custom_call" | custom-call | flops 469762048 | bytes 5505024 | tf_op jit(solution)/shard_map/pallas_call | solution.py:179
  102.8 17.9 %all-gather.2.cloned.1.call-done = bf16[7168,1024]{1,0:T(8,128)(2,1)} async-done(((bf16[448,1024]{1,0:T(8,128)(2,1)}), bf16[7168,1024]{1,0:T(8,128)(2,1)}) %all-gather.2.cloned.1.call-update) | async-done | bytes 14680080 | tf_op jit(solution)/shard_map/all_gather | solution.py:216
  120.7 5.3 %all-to-all-start.1 = ((bf16[16,448,128]{2,1,0:T(8,128)(2,1)}), bf16[16,448,128]{2,1,0:T(8,128)(2,1)S(1)}, u32[]{:S(2)}, u32[]{:S(2)}) async-start(bf16[16,448,128]{2,1,0:T(8,128)(2,1)} %bitcast.14), calls=%async_computation.1 | async-start | bytes 3670016 | tf_op jit(solution)/shard_map/all_to_all | solution.py:255
  126.0 13.3 %fusion.gate_up_ref = f32[512,1024]{1,0:T(8,128)S(1)} fusion(bf16[7168,1024]{1,0:T(8,128)(2,1)} %all-gather.2.cloned.1.call-done, bf16[7168,256]{1,0:T(8,128)(2,1)} %get-tuple-element.53, bf16[7168,256]{1,0:T(8,128)(2,1)} %get-tuple-element.52), kind=kOutput, calls=%fused_computation | convolution fusion | flops 7530872832 | bytes 24117248 | tf_op jit(solution)/shard_map/dot_general | solution.py:36
  139.4 3.2 %shard_map.111 = (bf16[256,512]{1,0:T(8,128)(2,1)S(1)}, bf16[8,448,256]{2,1,0:T(8,128)(2,1)}, bf16[8,448,256]{2,1,0:T(8,128)(2,1)}) custom-call(s32[16]{0:T(128)S(1)} %dynamic-slice_bitcast_fusion.at_ref.slice_ref, f32[512,1024]{1,0:T(8,128)S(1)} %fusion.gate_up_ref, f32[1,1024]{1,0:T(1,128)S(1)} %add_rsqrt_fusion.scale_ref, bf16[16,448,256]{2,1,0:T(8,128)(2,1)S(1)} %bitcast.60), custom_call_target="tpu_custom_call" | custom-call | flops 939524096 | bytes 7340032 | tf_op jit(solution)/shard_map/pallas_call | solution.py:66
  142.5 1.9 collective-permute-start.20
  144.5 2.1 collective-permute-start.24
  146.5 3.1 %shard_map.112 = (bf16[256,512]{1,0:T(8,128)(2,1)S(1)}, bf16[8,448,256]{2,1,0:T(8,128)(2,1)}, bf16[8,448,256]{2,1,0:T(8,128)(2,1)}) custom-call(s32[16]{0:T(128)S(1)} %dynamic-slice_bitcast_fusion.at_ref.slice_ref, f32[512,1024]{1,0:T(8,128)S(1)} %fusion.gate_up_ref, f32[1,1024]{1,0:T(1,128)S(1)} %add_rsqrt_fusion.scale_ref, bf16[16,448,256]{2,1,0:T(8,128)(2,1)S(1)} %bitcast.61), custom_call_target="tpu_custom_call" | custom-call | flops 939524096 | bytes 7340032 | tf_op jit(solution)/shard_map/pallas_call | solution.py:66
  151.1 2.1 collective-permute-start.32
  153.2 2.2 all-to-all-done.1
  156.3 1.7 copy.52
  157.9 4.3 %all-to-all-start.2 = ((bf16[8,16,448]{2,1,0:T(8,128)(2,1)}), bf16[8,16,448]{2,1,0:T(8,128)(2,1)}, u32[]{:S(2)}, u32[]{:S(2)}) async-start(bf16[8,16,448]{2,1,0:T(8,128)(2,1)} %bitcast.17), calls=%async_computation.2 | async-start | bytes 262144 | tf_op jit(solution)/shard_map/all_to_all | solution.py:267
  162.2 2.0 copy-done.1
  164.2 3.8 %shard_map.113 = (bf16[8,448,256]{2,1,0:T(8,128)(2,1)S(1)}, bf16[8,448,256]{2,1,0:T(8,128)(2,1)S(1)}, bf16[8,448,256]{2,1,0:T(8,128)(2,1)S(1)}, bf16[8,448,256]{2,1,0:T(8,128)(2,1)S(1)}) custom-call(s32[16]{0:T(128)S(1)} %dynamic-slice_bitcast_fusion.at_ref.slice_ref, bf16[16,448,256]{2,1,0:T(8,128)(2,1)S(1)} %bitcast.62, ...), custom_call_target="tpu_custom_call" | custom-call | flops 1879048192 | bytes 14680064 | tf_op jit(solution)/shard_map/pallas_call | solution.py:96
  172.9 16.7 %collective-permute-done.20 = bf16[8,448,256]{2,1,0:T(8,128)(2,1)} collective-permute-done((bf16[8,448,256]{2,1,0:T(8,128)(2,1)}, bf16[8,448,256]{2,1,0:T(8,128)(2,1)}, u32[]{:S(2)}, u32[]{:S(2)}) %collective-permute-start.20) | collective-permute-done | bytes 1835040 | tf_op jit(solution)/shard_map/ppermute | solution.py:21
  189.5 1.7 add_convert_fusion.3
  191.2 3.1 %collective-permute-start.21 = (bf16[4,448,256]{2,1,0:T(8,128)(2,1)S(1)}, bf16[4,448,256]{2,1,0:T(8,128)(2,1)S(1)}, u32[]{:S(2)}, u32[]{:S(2)}) collective-permute-start(bf16[4,448,256]{2,1,0:T(8,128)(2,1)S(1)} %add_convert_fusion.3), channel_id=1, source_target_pairs={{0,3},{1,2},{2,1},{3,0},{4,7},{5,6},{6,5},{7,4},{8,11},{9,10},{10,... | collective-permute-start | bytes 2752520 | tf_op jit(solution)/shard_map/ppermute | solution.py:21
  198.1 2.6 %collective-permute-start.29 = (bf16[4,448,256]{2,1,0:T(8,128)(2,1)S(1)}, bf16[4,448,256]{2,1,0:T(8,128)(2,1)S(1)}, u32[]{:S(2)}, u32[]{:S(2)}) collective-permute-start(bf16[4,448,256]{2,1,0:T(8,128)(2,1)S(1)} %add_convert_fusion.1), channel_id=1, source_target_pairs={{0,12},{1,13},{2,14},{3,15},{4,8},{5,9},{6,10},{7,11},{8,4},{9,5},... | collective-permute-start | bytes 2752520 | tf_op jit(solution)/shard_map/ppermute | solution.py:21
  202.1 11.4 %collective-permute-done.21 = bf16[4,448,256]{2,1,0:T(8,128)(2,1)S(1)} collective-permute-done((bf16[4,448,256]{2,1,0:T(8,128)(2,1)S(1)}, bf16[4,448,256]{2,1,0:T(8,128)(2,1)S(1)}, u32[]{:S(2)}, u32[]{:S(2)}) %collective-permute-start.21) | collective-permute-done | bytes 917536 | tf_op jit(solution)/shard_map/ppermute | solution.py:21
  215.9 1.7 collective-permute-done.25
  218.9 1.7 collective-permute-start.26
  221.9 1.7 collective-permute-done.33
  227.4 2.0 collective-permute-start.23
  230.8 2.7 %collective-permute-done.30 = bf16[2,448,256]{2,1,0:T(8,128)(2,1)S(1)} collective-permute-done((bf16[2,448,256]{2,1,0:T(8,128)(2,1)S(1)}, bf16[2,448,256]{2,1,0:T(8,128)(2,1)S(1)}, u32[]{:S(2)}, u32[]{:S(2)}) %collective-permute-start.30) | collective-permute-done | bytes 458784 | tf_op jit(solution)/shard_map/ppermute | solution.py:21
  234.5 1.8 collective-permute-start.31
  239.6 2.2 collective-permute-done.31
  (148 shorter events, 58.8 us)
Async XLA Ops:
  6.5 114.2 %all-gather.2.cloned.1.call-start = ((), (), s32[]{:S(2)}) async-start(), calls=%async_computation.3 | async-start | bytes 15597568 | tf_op jit(solution)/shard_map/all_gather | solution.py:216
  8.7 7.1 %collective-permute-start.16 = (f32[1,1024]{1,0:T(1,128)S(1)}, f32[1,1024]{1,0:T(1,128)S(1)}, u32[]{:S(2)}, u32[]{:S(2)}) collective-permute-start(f32[1,1024]{1,0:T(1,128)S(1)} %bitcast.73), channel_id=1, source_target_pairs={{0,1},{1,0},{2,3},{3,2},{4,5},{5,4},{6,7},{7,6},{8,9},{9,8},{10,11... | collective-permute-start | bytes 12296 | tf_op jit(solution)/shard_map/ppermute | solution.py:21
  14.1 8.5 %copy-start.12 = (bf16[1024,448]{0,1:T(8,128)(2,1)S(1)}, bf16[1024,448]{0,1:T(8,128)(2,1)}, u32[]{:S(2)}) copy-start(bf16[1024,448]{0,1:T(8,128)(2,1)} %param.11) | copy-start | bytes 2752516
  15.4 16.0 %copy-start.13 = (f32[7168]{0:T(1024)S(1)}, f32[7168]{0:T(1024)}, u32[]{:S(2)}) copy-start(f32[7168]{0:T(1024)} %param.12) | copy-start | bytes 86020
  15.7 4.9 %collective-permute-start.17 = (f32[1,1024]{1,0:T(1,128)S(1)}, f32[1,1024]{1,0:T(1,128)S(1)}, u32[]{:S(2)}, u32[]{:S(2)}) collective-permute-start(f32[1,1024]{1,0:T(1,128)S(1)} %add.154), channel_id=1, source_target_pairs={{0,3},{1,2},{2,1},{3,0},{4,7},{5,6},{6,5},{7,4},{8,11},{9,10},{10,... | collective-permute-start | bytes 12296 | tf_op jit(solution)/shard_map/ppermute | solution.py:21
  20.6 7.4 %collective-permute-start.18 = (f32[1,1024]{1,0:T(1,128)S(1)}, f32[1,1024]{1,0:T(1,128)S(1)}, u32[]{:S(2)}, u32[]{:S(2)}) collective-permute-start(f32[1,1024]{1,0:T(1,128)S(1)} %add.155), channel_id=1, source_target_pairs={{0,4},{1,5},{2,6},{3,7},{4,0},{5,1},{6,2},{7,3},{8,12},{9,13},{10,... | collective-permute-start | bytes 12296 | tf_op jit(solution)/shard_map/ppermute | solution.py:21
  23.7 10.4 %all-to-all-start = ((bf16[8,16,448]{2,1,0:T(8,128)(2,1)}), bf16[8,16,448]{2,1,0:T(8,128)(2,1)S(1)}, u32[]{:S(2)}, u32[]{:S(2)}) async-start(bf16[8,16,448]{2,1,0:T(8,128)(2,1)} %bitcast.3), calls=%async_computation | async-start | bytes 262144 | tf_op jit(solution)/shard_map/all_to_all | solution.py:226
  28.0 5.8 %collective-permute-start.19 = (f32[1,1024]{1,0:T(1,128)S(1)}, f32[1,1024]{1,0:T(1,128)S(1)}, u32[]{:S(2)}, u32[]{:S(2)}) collective-permute-start(f32[1,1024]{1,0:T(1,128)S(1)} %add.156), channel_id=1, source_target_pairs={{0,12},{1,13},{2,14},{3,15},{4,8},{5,9},{6,10},{7,11},{8,4},{9,5},... | collective-permute-start | bytes 12296 | tf_op jit(solution)/shard_map/ppermute | solution.py:21
  34.3 5.9 %collective-permute-start.6 = (bf16[1,112,128]{2,1,0:T(8,128)(2,1)S(1)}, bf16[1,112,128]{2,1,0:T(8,128)(2,1)S(1)}, u32[]{:S(2)}, u32[]{:S(2)}) collective-permute-start(bf16[1,112,128]{2,1,0:T(8,128)(2,1)S(1)} %get-tuple-element.79), channel_id=1, source_target_pairs={{0,12},{1,13},{2,14},{3,15},{4,8},{5,9},{6,10},{7,11},{8,4},{9,5},... | collective-permute-start | bytes 86024 | tf_op jit(solution)/shard_map/ppermute | solution.py:21
  36.9 5.4 %collective-permute-start.4 = (bf16[1,112,128]{2,1,0:T(8,128)(2,1)S(1)}, bf16[1,112,128]{2,1,0:T(8,128)(2,1)S(1)}, u32[]{:S(2)}, u32[]{:S(2)}) collective-permute-start(bf16[1,112,128]{2,1,0:T(8,128)(2,1)S(1)} %get-tuple-element.80), channel_id=1, source_target_pairs={{0,4},{1,5},{2,6},{3,7},{4,0},{5,1},{6,2},{7,3},{8,12},{9,13},{10,... | collective-permute-start | bytes 86024 | tf_op jit(solution)/shard_map/ppermute | solution.py:21
  38.0 5.1 %collective-permute-start.2 = (bf16[1,112,128]{2,1,0:T(8,128)(2,1)S(1)}, bf16[1,112,128]{2,1,0:T(8,128)(2,1)S(1)}, u32[]{:S(2)}, u32[]{:S(2)}) collective-permute-start(bf16[1,112,128]{2,1,0:T(8,128)(2,1)S(1)} %get-tuple-element.81), channel_id=1, source_target_pairs={{0,3},{1,2},{2,1},{3,0},{4,7},{5,6},{6,5},{7,4},{8,11},{9,10},{10,... | collective-permute-start | bytes 86024 | tf_op jit(solution)/shard_map/ppermute | solution.py:21
  40.2 4.0 %collective-permute-start = (bf16[1,112,128]{2,1,0:T(8,128)(2,1)S(1)}, bf16[1,112,128]{2,1,0:T(8,128)(2,1)S(1)}, u32[]{:S(2)}, u32[]{:S(2)}) collective-permute-start(bf16[1,112,128]{2,1,0:T(8,128)(2,1)S(1)} %get-tuple-element.82), channel_id=1, source_target_pairs={{0,1},{1,0},{2,3},{3,2},{4,5},{5,4},{6,7},{7,6},{8,9},{9,8},{10,11... | collective-permute-start | bytes 86024 | tf_op jit(solution)/shard_map/ppermute | solution.py:21
  40.2 13.3 %collective-permute-start.7 = (bf16[2,112,128]{2,1,0:T(8,128)(2,1)S(1)}, bf16[2,112,128]{2,1,0:T(8,128)(2,1)S(1)}, u32[]{:S(2)}, u32[]{:S(2)}) collective-permute-start(bf16[2,112,128]{2,1,0:T(8,128)(2,1)S(1)} %pad_maximum_fusion.11), channel_id=1, source_target_pairs={{0,1},{1,0},{2,3},{3,2},{4,5},{5,4},{6,7},{7,6},{8,9},{9,8},{10,11... | collective-permute-start | bytes 172040 | tf_op jit(solution)/shard_map/ppermute | solution.py:21
  42.3 11.2 %collective-permute-start.5 = (bf16[2,112,128]{2,1,0:T(8,128)(2,1)S(1)}, bf16[2,112,128]{2,1,0:T(8,128)(2,1)S(1)}, u32[]{:S(2)}, u32[]{:S(2)}) collective-permute-start(bf16[2,112,128]{2,1,0:T(8,128)(2,1)S(1)} %pad_maximum_fusion.10), channel_id=1, source_target_pairs={{0,12},{1,13},{2,14},{3,15},{4,8},{5,9},{6,10},{7,11},{8,4},{9,5},... | collective-permute-start | bytes 172040 | tf_op jit(solution)/shard_map/ppermute | solution.py:21
  43.1 10.5 %collective-permute-start.3 = (bf16[2,112,128]{2,1,0:T(8,128)(2,1)S(1)}, bf16[2,112,128]{2,1,0:T(8,128)(2,1)S(1)}, u32[]{:S(2)}, u32[]{:S(2)}) collective-permute-start(bf16[2,112,128]{2,1,0:T(8,128)(2,1)S(1)} %pad_maximum_fusion.9), channel_id=1, source_target_pairs={{0,4},{1,5},{2,6},{3,7},{4,0},{5,1},{6,2},{7,3},{8,12},{9,13},{10,... | collective-permute-start | bytes 172040 | tf_op jit(solution)/shard_map/ppermute | solution.py:21
  44.2 9.4 %collective-permute-start.1 = (bf16[2,112,128]{2,1,0:T(8,128)(2,1)S(1)}, bf16[2,112,128]{2,1,0:T(8,128)(2,1)S(1)}, u32[]{:S(2)}, u32[]{:S(2)}) collective-permute-start(bf16[2,112,128]{2,1,0:T(8,128)(2,1)S(1)} %pad_maximum_fusion.8), channel_id=1, source_target_pairs={{0,3},{1,2},{2,1},{3,0},{4,7},{5,6},{6,5},{7,4},{8,11},{9,10},{10,... | collective-permute-start | bytes 172040 | tf_op jit(solution)/shard_map/ppermute | solution.py:21
  54.3 12.2 %collective-permute-start.11 = (bf16[4,112,128]{2,1,0:T(8,128)(2,1)}, bf16[4,112,128]{2,1,0:T(8,128)(2,1)}, u32[]{:S(2)}, u32[]{:S(2)}) collective-permute-start(bf16[4,112,128]{2,1,0:T(8,128)(2,1)} %pad_maximum_fusion.7), channel_id=1, source_target_pairs={{0,3},{1,2},{2,1},{3,0},{4,7},{5,6},{6,5},{7,4},{8,11},{9,10},{10,... | collective-permute-start | bytes 344072 | tf_op jit(solution)/shard_map/ppermute | solution.py:21
  56.2 10.2 %collective-permute-start.10 = (bf16[4,112,128]{2,1,0:T(8,128)(2,1)}, bf16[4,112,128]{2,1,0:T(8,128)(2,1)}, u32[]{:S(2)}, u32[]{:S(2)}) collective-permute-start(bf16[4,112,128]{2,1,0:T(8,128)(2,1)} %pad_maximum_fusion.6), channel_id=1, source_target_pairs={{0,1},{1,0},{2,3},{3,2},{4,5},{5,4},{6,7},{7,6},{8,9},{9,8},{10,11... | collective-permute-start | bytes 344072 | tf_op jit(solution)/shard_map/ppermute | solution.py:21
  56.9 9.5 %collective-permute-start.9 = (bf16[4,112,128]{2,1,0:T(8,128)(2,1)}, bf16[4,112,128]{2,1,0:T(8,128)(2,1)}, u32[]{:S(2)}, u32[]{:S(2)}) collective-permute-start(bf16[4,112,128]{2,1,0:T(8,128)(2,1)} %pad_maximum_fusion.5), channel_id=1, source_target_pairs={{0,12},{1,13},{2,14},{3,15},{4,8},{5,9},{6,10},{7,11},{8,4},{9,5},... | collective-permute-start | bytes 344072 | tf_op jit(solution)/shard_map/ppermute | solution.py:21
  59.2 7.6 %collective-permute-start.8 = (bf16[4,112,128]{2,1,0:T(8,128)(2,1)}, bf16[4,112,128]{2,1,0:T(8,128)(2,1)}, u32[]{:S(2)}, u32[]{:S(2)}) collective-permute-start(bf16[4,112,128]{2,1,0:T(8,128)(2,1)} %pad_maximum_fusion.4), channel_id=1, source_target_pairs={{0,4},{1,5},{2,6},{3,7},{4,0},{5,1},{6,2},{7,3},{8,12},{9,13},{10,... | collective-permute-start | bytes 344072 | tf_op jit(solution)/shard_map/ppermute | solution.py:21
  67.7 12.4 %collective-permute-start.15 = (bf16[8,112,128]{2,1,0:T(8,128)(2,1)S(1)}, bf16[8,112,128]{2,1,0:T(8,128)(2,1)S(1)}, u32[]{:S(2)}, u32[]{:S(2)}) collective-permute-start(bf16[8,112,128]{2,1,0:T(8,128)(2,1)S(1)} %pad_maximum_fusion.3), channel_id=1, source_target_pairs={{0,4},{1,5},{2,6},{3,7},{4,0},{5,1},{6,2},{7,3},{8,12},{9,13},{10,... | collective-permute-start | bytes 688136 | tf_op jit(solution)/shard_map/ppermute | solution.py:21
  70.0 17.8 %copy-start.2 = (f32[7168,1]{1,0:T(8,128)S(1)}, f32[7168,1]{1,0:T(8,128)}, u32[]{:S(2)}) copy-start(f32[7168,1]{1,0:T(8,128)} %copy.51.gain_ref) | copy-start | bytes 86020
  70.0 12.8 %collective-permute-start.14 = (bf16[8,112,128]{2,1,0:T(8,128)(2,1)S(1)}, bf16[8,112,128]{2,1,0:T(8,128)(2,1)S(1)}, u32[]{:S(2)}, u32[]{:S(2)}) collective-permute-start(bf16[8,112,128]{2,1,0:T(8,128)(2,1)S(1)} %pad_maximum_fusion.2), channel_id=1, source_target_pairs={{0,3},{1,2},{2,1},{3,0},{4,7},{5,6},{6,5},{7,4},{8,11},{9,10},{10,... | collective-permute-start | bytes 688136 | tf_op jit(solution)/shard_map/ppermute | solution.py:21
  72.1 11.7 %collective-permute-start.13 = (bf16[8,112,128]{2,1,0:T(8,128)(2,1)S(1)}, bf16[8,112,128]{2,1,0:T(8,128)(2,1)S(1)}, u32[]{:S(2)}, u32[]{:S(2)}) collective-permute-start(bf16[8,112,128]{2,1,0:T(8,128)(2,1)S(1)} %pad_maximum_fusion.1), channel_id=1, source_target_pairs={{0,1},{1,0},{2,3},{3,2},{4,5},{5,4},{6,7},{7,6},{8,9},{9,8},{10,11... | collective-permute-start | bytes 688136 | tf_op jit(solution)/shard_map/ppermute | solution.py:21
  74.9 12.9 %collective-permute-start.12 = (bf16[8,112,128]{2,1,0:T(8,128)(2,1)S(1)}, bf16[8,112,128]{2,1,0:T(8,128)(2,1)S(1)}, u32[]{:S(2)}, u32[]{:S(2)}) collective-permute-start(bf16[8,112,128]{2,1,0:T(8,128)(2,1)S(1)} %pad_maximum_fusion), channel_id=1, source_target_pairs={{0,12},{1,13},{2,14},{3,15},{4,8},{5,9},{6,10},{7,11},{8,4},{9,5},... | collective-permute-start | bytes 688136 | tf_op jit(solution)/shard_map/ppermute | solution.py:21
  92.0 7.7 %copy-start.5 = (bf16[1,256,7168]{2,1,0:T(8,128)(2,1)S(1)}, bf16[1,256,7168]{2,1,0:T(8,128)(2,1)}, u32[]{:S(2)}) copy-start(bf16[1,256,7168]{2,1,0:T(8,128)(2,1)} %weight_ref.1) | copy-start | bytes 11010052
  120.7 34.6 %all-to-all-start.1 = ((bf16[16,448,128]{2,1,0:T(8,128)(2,1)}), bf16[16,448,128]{2,1,0:T(8,128)(2,1)S(1)}, u32[]{:S(2)}, u32[]{:S(2)}) async-start(bf16[16,448,128]{2,1,0:T(8,128)(2,1)} %bitcast.14), calls=%async_computation.1 | async-start | bytes 3670016 | tf_op jit(solution)/shard_map/all_to_all | solution.py:255
  126.0 13.3 %copy-start = (bf16[7168,256]{1,0:T(8,128)(2,1)S(1)}, bf16[7168,256]{1,0:T(8,128)(2,1)}, u32[]{:S(2)}) copy-start(bf16[7168,256]{1,0:T(8,128)(2,1)} %copy.50) | copy-start | bytes 11010052
  142.5 47.0 %collective-permute-start.20 = (bf16[8,448,256]{2,1,0:T(8,128)(2,1)}, bf16[8,448,256]{2,1,0:T(8,128)(2,1)}, u32[]{:S(2)}, u32[]{:S(2)}) collective-permute-start(bf16[8,448,256]{2,1,0:T(8,128)(2,1)} %get-tuple-element.61), channel_id=1, source_target_pairs={{0,1},{1,0},{2,3},{3,2},{4,5},{5,4},{6,7},{7,6},{8,9},{9,8},{10,11... | collective-permute-start | bytes 5505032 | tf_op jit(solution)/shard_map/ppermute | solution.py:21
  144.5 49.9 %collective-permute-start.24 = (bf16[8,448,256]{2,1,0:T(8,128)(2,1)}, bf16[8,448,256]{2,1,0:T(8,128)(2,1)}, u32[]{:S(2)}, u32[]{:S(2)}) collective-permute-start(bf16[8,448,256]{2,1,0:T(8,128)(2,1)} %get-tuple-element.63), channel_id=1, source_target_pairs={{0,3},{1,2},{2,1},{3,0},{4,7},{5,6},{6,5},{7,4},{8,11},{9,10},{10,... | collective-permute-start | bytes 5505032 | tf_op jit(solution)/shard_map/ppermute | solution.py:21
  149.7 46.9 %collective-permute-start.28 = (bf16[8,448,256]{2,1,0:T(8,128)(2,1)}, bf16[8,448,256]{2,1,0:T(8,128)(2,1)}, u32[]{:S(2)}, u32[]{:S(2)}) collective-permute-start(bf16[8,448,256]{2,1,0:T(8,128)(2,1)} %get-tuple-element.67), channel_id=1, source_target_pairs={{0,4},{1,5},{2,6},{3,7},{4,0},{5,1},{6,2},{7,3},{8,12},{9,13},{10,... | collective-permute-start | bytes 5505032 | tf_op jit(solution)/shard_map/ppermute | solution.py:21
  151.1 49.5 %collective-permute-start.32 = (bf16[8,448,256]{2,1,0:T(8,128)(2,1)}, bf16[8,448,256]{2,1,0:T(8,128)(2,1)}, u32[]{:S(2)}, u32[]{:S(2)}) collective-permute-start(bf16[8,448,256]{2,1,0:T(8,128)(2,1)} %get-tuple-element.69), channel_id=1, source_target_pairs={{0,12},{1,13},{2,14},{3,15},{4,8},{5,9},{6,10},{7,11},{8,4},{9,5},... | collective-permute-start | bytes 5505032 | tf_op jit(solution)/shard_map/ppermute | solution.py:21
  157.9 13.8 %all-to-all-start.2 = ((bf16[8,16,448]{2,1,0:T(8,128)(2,1)}), bf16[8,16,448]{2,1,0:T(8,128)(2,1)}, u32[]{:S(2)}, u32[]{:S(2)}) async-start(bf16[8,16,448]{2,1,0:T(8,128)(2,1)} %bitcast.17), calls=%async_computation.2 | async-start | bytes 262144 | tf_op jit(solution)/shard_map/all_to_all | solution.py:267
  171.7 22.6 %copy-start.9 = (bf16[8,448,256]{2,1,0:T(8,128)(2,1)S(1)}, bf16[8,448,256]{2,1,0:T(8,128)(2,1)}, u32[]{:S(2)}) copy-start(bf16[8,448,256]{2,1,0:T(8,128)(2,1)} %copy-done.8) | copy-start | bytes 5505028
  191.2 5.4 %copy-start.7 = (bf16[8,448,256]{2,1,0:T(8,128)(2,1)S(1)}, bf16[8,448,256]{2,1,0:T(8,128)(2,1)}, u32[]{:S(2)}) copy-start(bf16[8,448,256]{2,1,0:T(8,128)(2,1)} %copy-done.6) | copy-start | bytes 5505028
  191.2 22.3 %collective-permute-start.21 = (bf16[4,448,256]{2,1,0:T(8,128)(2,1)S(1)}, bf16[4,448,256]{2,1,0:T(8,128)(2,1)S(1)}, u32[]{:S(2)}, u32[]{:S(2)}) collective-permute-start(bf16[4,448,256]{2,1,0:T(8,128)(2,1)S(1)} %add_convert_fusion.3), channel_id=1, source_target_pairs={{0,3},{1,2},{2,1},{3,0},{4,7},{5,6},{6,5},{7,4},{8,11},{9,10},{10,... | collective-permute-start | bytes 2752520 | tf_op jit(solution)/shard_map/ppermute | solution.py:21
  195.8 21.9 %collective-permute-start.25 = (bf16[4,448,256]{2,1,0:T(8,128)(2,1)S(1)}, bf16[4,448,256]{2,1,0:T(8,128)(2,1)S(1)}, u32[]{:S(2)}, u32[]{:S(2)}) collective-permute-start(bf16[4,448,256]{2,1,0:T(8,128)(2,1)S(1)} %add_convert_fusion.2), channel_id=1, source_target_pairs={{0,4},{1,5},{2,6},{3,7},{4,0},{5,1},{6,2},{7,3},{8,12},{9,13},{10,... | collective-permute-start | bytes 2752520 | tf_op jit(solution)/shard_map/ppermute | solution.py:21
  198.1 15.5 %copy-start.11 = (bf16[8,448,256]{2,1,0:T(8,128)(2,1)S(1)}, bf16[8,448,256]{2,1,0:T(8,128)(2,1)}, u32[]{:S(2)}) copy-start(bf16[8,448,256]{2,1,0:T(8,128)(2,1)} %copy-done.10) | copy-start | bytes 5505028
  198.1 22.5 %collective-permute-start.29 = (bf16[4,448,256]{2,1,0:T(8,128)(2,1)S(1)}, bf16[4,448,256]{2,1,0:T(8,128)(2,1)S(1)}, u32[]{:S(2)}, u32[]{:S(2)}) collective-permute-start(bf16[4,448,256]{2,1,0:T(8,128)(2,1)S(1)} %add_convert_fusion.1), channel_id=1, source_target_pairs={{0,12},{1,13},{2,14},{3,15},{4,8},{5,9},{6,10},{7,11},{8,4},{9,5},... | collective-permute-start | bytes 2752520 | tf_op jit(solution)/shard_map/ppermute | solution.py:21
  202.0 21.5 %collective-permute-start.33 = (bf16[4,448,256]{2,1,0:T(8,128)(2,1)S(1)}, bf16[4,448,256]{2,1,0:T(8,128)(2,1)S(1)}, u32[]{:S(2)}, u32[]{:S(2)}) collective-permute-start(bf16[4,448,256]{2,1,0:T(8,128)(2,1)S(1)} %add_convert_fusion), channel_id=1, source_target_pairs={{0,1},{1,0},{2,3},{3,2},{4,5},{5,4},{6,7},{7,6},{8,9},{9,8},{10,11... | collective-permute-start | bytes 2752520 | tf_op jit(solution)/shard_map/ppermute | solution.py:21
  214.8 11.6 %collective-permute-start.22 = (bf16[2,448,256]{2,1,0:T(8,128)(2,1)S(1)}, bf16[2,448,256]{2,1,0:T(8,128)(2,1)S(1)}, u32[]{:S(2)}, u32[]{:S(2)}) collective-permute-start(bf16[2,448,256]{2,1,0:T(8,128)(2,1)S(1)} %add_convert_fusion.7), channel_id=1, source_target_pairs={{0,4},{1,5},{2,6},{3,7},{4,0},{5,1},{6,2},{7,3},{8,12},{9,13},{10,... | collective-permute-start | bytes 1376264 | tf_op jit(solution)/shard_map/ppermute | solution.py:21
  218.9 10.7 %collective-permute-start.26 = (bf16[2,448,256]{2,1,0:T(8,128)(2,1)S(1)}, bf16[2,448,256]{2,1,0:T(8,128)(2,1)S(1)}, u32[]{:S(2)}, u32[]{:S(2)}) collective-permute-start(bf16[2,448,256]{2,1,0:T(8,128)(2,1)S(1)} %add_convert_fusion.6), channel_id=1, source_target_pairs={{0,12},{1,13},{2,14},{3,15},{4,8},{5,9},{6,10},{7,11},{8,4},{9,5},... | collective-permute-start | bytes 1376264 | tf_op jit(solution)/shard_map/ppermute | solution.py:21
  221.8 11.6 %collective-permute-start.30 = (bf16[2,448,256]{2,1,0:T(8,128)(2,1)S(1)}, bf16[2,448,256]{2,1,0:T(8,128)(2,1)S(1)}, u32[]{:S(2)}, u32[]{:S(2)}) collective-permute-start(bf16[2,448,256]{2,1,0:T(8,128)(2,1)S(1)} %add_convert_fusion.5), channel_id=1, source_target_pairs={{0,1},{1,0},{2,3},{3,2},{4,5},{5,4},{6,7},{7,6},{8,9},{9,8},{10,11... | collective-permute-start | bytes 1376264 | tf_op jit(solution)/shard_map/ppermute | solution.py:21
  224.7 11.5 %collective-permute-start.34 = (bf16[2,448,256]{2,1,0:T(8,128)(2,1)S(1)}, bf16[2,448,256]{2,1,0:T(8,128)(2,1)S(1)}, u32[]{:S(2)}, u32[]{:S(2)}) collective-permute-start(bf16[2,448,256]{2,1,0:T(8,128)(2,1)S(1)} %add_convert_fusion.4), channel_id=1, source_target_pairs={{0,3},{1,2},{2,1},{3,0},{4,7},{5,6},{6,5},{7,4},{8,11},{9,10},{10,... | collective-permute-start | bytes 1376264 | tf_op jit(solution)/shard_map/ppermute | solution.py:21
  227.4 10.0 %collective-permute-start.23 = (bf16[1,448,256]{2,1,0:T(8,128)(2,1)S(1)}, bf16[1,448,256]{2,1,0:T(8,128)(2,1)S(1)}, u32[]{:S(2)}, u32[]{:S(2)}) collective-permute-start(bf16[1,448,256]{2,1,0:T(8,128)(2,1)S(1)} %add_convert_fusion.11), channel_id=1, source_target_pairs={{0,12},{1,13},{2,14},{3,15},{4,8},{5,9},{6,10},{7,11},{8,4},{9,5},... | collective-permute-start | bytes 688136 | tf_op jit(solution)/shard_map/ppermute | solution.py:21
  230.7 7.9 %collective-permute-start.27 = (bf16[1,448,256]{2,1,0:T(8,128)(2,1)S(1)}, bf16[1,448,256]{2,1,0:T(8,128)(2,1)S(1)}, u32[]{:S(2)}, u32[]{:S(2)}) collective-permute-start(bf16[1,448,256]{2,1,0:T(8,128)(2,1)S(1)} %add_convert_fusion.10), channel_id=1, source_target_pairs={{0,1},{1,0},{2,3},{3,2},{4,5},{5,4},{6,7},{7,6},{8,9},{9,8},{10,11... | collective-permute-start | bytes 688136 | tf_op jit(solution)/shard_map/ppermute | solution.py:21
  234.5 7.3 %collective-permute-start.31 = (bf16[1,448,256]{2,1,0:T(8,128)(2,1)S(1)}, bf16[1,448,256]{2,1,0:T(8,128)(2,1)S(1)}, u32[]{:S(2)}, u32[]{:S(2)}) collective-permute-start(bf16[1,448,256]{2,1,0:T(8,128)(2,1)S(1)} %add_convert_fusion.9), channel_id=1, source_target_pairs={{0,3},{1,2},{2,1},{3,0},{4,7},{5,6},{6,5},{7,4},{8,11},{9,10},{10,... | collective-permute-start | bytes 688136 | tf_op jit(solution)/shard_map/ppermute | solution.py:21
  237.3 6.1 %collective-permute-start.35 = (bf16[1,448,256]{2,1,0:T(8,128)(2,1)S(1)}, bf16[1,448,256]{2,1,0:T(8,128)(2,1)S(1)}, u32[]{:S(2)}, u32[]{:S(2)}) collective-permute-start(bf16[1,448,256]{2,1,0:T(8,128)(2,1)S(1)} %add_convert_fusion.8), channel_id=1, source_target_pairs={{0,4},{1,5},{2,6},{3,7},{4,0},{5,1},{6,2},{7,3},{8,12},{9,13},{10,... | collective-permute-start | bytes 688136 | tf_op jit(solution)/shard_map/ppermute | solution.py:21
  (8 other events, 17.8 us)
Sparse Core Ops, SparseCore 0:
  9.5 111.1 all-gather.1

commit v14 on v13

--- a/solution.py
+++ b/solution.py
@@ -244,19 +244,21 @@
             dense_down, _ = lax.optimization_barrier((dense_down, pooled))
             turned = dense_down.T.reshape(16, slice_width, dense_down.shape[0])
             got, turned = lax.optimization_barrier((got, turned))
+        if step == 3:
+            folded, _ = lax.optimization_barrier((folded, pooled))
+            weight = jnp.concatenate([w.T for w in folded], axis=0)
+            got, weight = lax.optimization_barrier((got, weight))
         pooled = [jnp.concatenate([pooled[s], got[s]], axis=0) for s in range(4)]
     scale = lax.rsqrt(square_sum / width + EPSILON)
 
     expert_hidden = expert_gate_up(slice_of, pooled, expert_gate, expert_up, gain_column)
     expert_partial = expert_down_parts(expert_down, expert_hidden)
-    expert_partial, scale, whole_columns, folded = lax.optimization_barrier(
-        (expert_partial, scale, whole_columns, folded)
-    )
+    expert_partial, scale, whole_columns = lax.optimization_barrier((expert_partial, scale, whole_columns))
     expert_parts = lax.all_to_all(
         expert_partial.reshape(16, slice_width, slot_count), "local", split_axis=0, concat_axis=0, tiled=True
     )
 
-    gate_up = transposed_dot(jnp.concatenate(folded, axis=1), whole_columns)
+    gate_up = jnp.dot(weight, whole_columns, preferred_element_type=jnp.float32)
     low_hidden, *sent = sent_parts(0, slice_of, gate_up, scale, turned)
     high_hidden, *more = sent_parts(2, slice_of, gate_up, scale, turned)
     sent += more

time: 254 us -> 255 us (level)
  waiting for transfers between devices: 69.2 us -> 59.7 us
  local copies, waits for them, and re-layouts: 28 us -> 32.4 us
  Pallas kernels: 20.9 us -> 24 us
    concatenate x0 -> x1, other arithmetic: none -> 6.79 us  [shards(): weight = jnp.concatenate([w.T for w in folded], axis=0)]
    all_gather x1, waiting for transfers between devices: 17.9 us -> 12.5 us  [shards(): whole_columns = lax.all_gather(columns, 'local', axis=0, tiled=True)]
    concatenate x4, local copies, waits for them, and re-layouts: 0.13 us -> 4.58 us  [shards(): pooled = [jnp.concatenate([pooled[s], got[s]], axis=0) for s in range(4)]]
    ppermute x36, waiting for transfers between devices: 48.2 us -> 44 us  [flip_local(): lax.ppermute(array, 'local', [(i, LOCAL_AT[LOCAL_LABEL[i] ^ 1 << bit]) fo...]
    concatenate x12, other arithmetic: 6.35 us -> 2.95 us  [shards(): pooled = [jnp.concatenate([pooled[s], got[s]], axis=0) for s in range(4)]]
    pallas_call x1, Pallas kernels: 7.67 us -> 10.8 us  [expert_gate_up(): pl.pallas_call(functools.partial(expert_kernel, blocks, blocks * rows), g...]
    unnamed x44 -> x54, local copies, waits for them, and re-layouts: 13.9 us -> 14.7 us
  transfers between devices with their start and end apart: 40 -> 40, of which waited for: 18 -> 15; matrix products, arithmetic and copies ran while one was open for 28% -> 30% of each run, Pallas kernels for 8% -> 9%
where the time goes in v14:
time: 255 us; the launch traced here: 253 us
  starting transfers between devices  66.8 us (26%)
  waiting for transfers between devices  59.7 us (23%)
  other arithmetic  41.2 us (16%)
  local copies, waits for them, and re-layouts  32.4 us (13%)
  Pallas kernels  24 us (9%)
  matrix products  15.1 us (6%)
  between operations  14 us (5%)
    ppermute x36, starting transfers between devices, flip_local(): lax.ppermute(array, 'local', [(i, LOCAL_AT[LOCAL_LABEL[i] ^ 1 << bit]) fo...  53 us
    ppermute x36, waiting for transfers between devices, flip_local(): lax.ppermute(array, 'local', [(i, LOCAL_AT[LOCAL_LABEL[i] ^ 1 << bit]) fo...  44 us
    convert_element_type x12, other arithmetic, shards(): added(s, half, 2 * half).astype(jnp.bfloat16)  15 us
    unnamed x54, local copies, waits for them, and re-layouts  14.7 us
    dot_general x1, matrix products, shards(): gate_up = jnp.dot(weight, whole_columns, preferred_element_type=jnp.float32)  13.3 us
    all_gather x1, waiting for transfers between devices, shards(): whole_columns = lax.all_gather(columns, 'local', axis=0, tiled=True)  12.5 us
    pallas_call x1, Pallas kernels, expert_gate_up(): pl.pallas_call(functools.partial(expert_kernel, blocks, blocks * rows), g...  10.8 us
    convert_element_type x1, other arithmetic, shards(): (w.astype(jnp.float32) * gain_column).astype(jnp.bfloat16)  6.89 us
  transfers between devices with their start and end apart: 40, of which 15 were waited for; matrix products, arithmetic and copies ran while one was open for 30% of the time, Pallas kernels for 9%

profile of v14, /device:TPU:0, one launch (start us, length us, event | category | flops | bytes accessed | tf_op | source)
XLA Modules:
  0.0 253.2 jit_solution(2512706299357089610)
XLA Ops:
  8.7 1.7 collective-permute-start.16
  11.2 2.3 reduce-window.6
  15.7 2.3 collective-permute-start.17
  18.8 1.9 collective-permute-done.17
  20.6 1.9 collective-permute-start.18
  23.7 4.3 %all-to-all-start = ((bf16[8,16,448]{2,1,0:T(8,128)(2,1)}), bf16[8,16,448]{2,1,0:T(8,128)(2,1)S(1)}, u32[]{:S(2)}, u32[]{:S(2)}) async-start(bf16[8,16,448]{2,1,0:T(8,128)(2,1)} %bitcast.3), calls=%async_computation | async-start | bytes 262144 | tf_op jit(solution)/shard_map/all_to_all | solution.py:226
  28.1 2.6 %collective-permute-start.19 = (f32[1,1024]{1,0:T(1,128)S(1)}, f32[1,1024]{1,0:T(1,128)S(1)}, u32[]{:S(2)}, u32[]{:S(2)}) collective-permute-start(f32[1,1024]{1,0:T(1,128)S(1)} %add.156), channel_id=1, source_target_pairs={{0,12},{1,13},{2,14},{3,15},{4,8},{5,9},{6,10},{7,11},{8,4},{9,5},... | collective-permute-start | bytes 12296 | tf_op jit(solution)/shard_map/ppermute | solution.py:21
  31.4 2.5 copy.51.gain_ref
  34.3 2.6 %collective-permute-start.6 = (bf16[1,112,128]{2,1,0:T(8,128)(2,1)S(1)}, bf16[1,112,128]{2,1,0:T(8,128)(2,1)S(1)}, u32[]{:S(2)}, u32[]{:S(2)}) collective-permute-start(bf16[1,112,128]{2,1,0:T(8,128)(2,1)S(1)} %get-tuple-element.89), channel_id=1, source_target_pairs={{0,12},{1,13},{2,14},{3,15},{4,8},{5,9},{6,10},{7,11},{8,4},{9,5},... | collective-permute-start | bytes 86024 | tf_op jit(solution)/shard_map/ppermute | solution.py:21
  38.6 2.2 collective-permute-start.2
  40.8 2.1 collective-permute-start.7
  44.7 2.3 collective-permute-start.1
  47.6 6.9 %multiply_convert_fusion = (bf16[7168,256]{1,0:T(8,128)(2,1)}, bf16[7168,256]{1,0:T(8,128)(2,1)}) fusion(bf16[7168,256]{1,0:T(8,128)(2,1)} %param.14, f32[7168]{0:T(1024)S(1)} %copy-done.18, bf16[7168,256]{1,0:T(8,128)(2,1)} %param.13), kind=kLoop, calls=%fused_computation.1 | loop fusion | flops 11010048 | bytes 14708736 | tf_op jit(solution)/shard_map/convert_element_type | solution.py:241
  56.1 2.3 collective-permute-start.9
  59.3 6.0 %copy.50 = bf16[7168,256]{1,0:T(8,128)(2,1)} copy(bf16[7168,256]{0,1:T(8,128)(2,1)} %bitcast.72) | data formatting | bytes 7340032 | tf_op jit(solution)/shard_map/transpose | solution.py:245
  72.3 2.2 collective-permute-start.12
  75.1 6.8 %pad_maximum_fusion = bf16[512,7168]{0,1:T(8,128)(2,1)} fusion(bf16[256,7168]{0,1:T(8,128)(2,1)} %bitcast.69, bf16[256,7168]{0,1:T(8,128)(2,1)} %bitcast.70), kind=kLoop, calls=%fused_computation | loop fusion | flops 14680064 | bytes 14680064 | tf_op jit(solution)/shard_map/concatenate | solution.py:249
  83.8 1.6 collective-permute-done.12
  86.4 1.7 constant_dynamic-update-slice_fusion.10.x2
  90.0 2.0 copy-done.3
  92.1 2.2 copy-done.4
  94.3 10.8 %shard_map.109.hidden_ref = bf16[256,128]{1,0:T(8,128)(2,1)S(1)} custom-call(s32[16]{0:T(128)S(1)} %dynamic-slice_bitcast_fusion.at_ref.slice_ref, bf16[16,112,128]{2,1,0:T(8,128)(2,1)S(1)} %constant_dynamic-update-slice_fusion.x0, bf16[16,112,128]{2,1,0:T(8,128)(2,1)S(1)} %constant_dynamic-update-slice_fusion.5.x1, ...), custom_call_target="tpu_custom_call" | custom-call | flops 939524096 | bytes 9175040 | tf_op jit(solution)/shard_map/pallas_call | solution.py:147
  105.1 3.1 %shard_map.110 = bf16[7168,128]{1,0:T(8,128)(2,1)} custom-call(bf16[1,256,7168]{2,1,0:T(8,128)(2,1)S(1)} %copy-done.5, bf16[256,128]{1,0:T(8,128)(2,1)S(1)} %shard_map.109.hidden_ref), custom_call_target="tpu_custom_call" | custom-call | flops 469762048 | bytes 5505024 | tf_op jit(solution)/shard_map/pallas_call | solution.py:179
  108.2 12.5 %all-gather.2.cloned.1.call-done = bf16[7168,1024]{1,0:T(8,128)(2,1)} async-done(((bf16[448,1024]{1,0:T(8,128)(2,1)}), bf16[7168,1024]{1,0:T(8,128)(2,1)}) %all-gather.2.cloned.1.call-update) | async-done | bytes 14680080 | tf_op jit(solution)/shard_map/all_gather | solution.py:216
  120.7 5.3 %all-to-all-start.1 = ((bf16[16,448,128]{2,1,0:T(8,128)(2,1)}), bf16[16,448,128]{2,1,0:T(8,128)(2,1)S(1)}, u32[]{:S(2)}, u32[]{:S(2)}) async-start(bf16[16,448,128]{2,1,0:T(8,128)(2,1)} %bitcast.16), calls=%async_computation.1 | async-start | bytes 3670016 | tf_op jit(solution)/shard_map/all_to_all | solution.py:257
  126.0 13.3 %fusion.10.gate_up_ref = f32[512,1024]{1,0:T(8,128)S(1)} fusion(bf16[512,7168]{0,1:T(8,128)(2,1)} %pad_maximum_fusion, bf16[7168,1024]{1,0:T(8,128)(2,1)} %all-gather.2.cloned.1.call-done), kind=kOutput, calls=%fused_computation.84 | convolution fusion | flops 7516192768 | bytes 24117248 | tf_op jit(solution)/shard_map/dot_general | solution.py:261
  139.4 3.2 %shard_map.111 = (bf16[256,512]{1,0:T(8,128)(2,1)S(1)}, bf16[8,448,256]{2,1,0:T(8,128)(2,1)}, bf16[8,448,256]{2,1,0:T(8,128)(2,1)}) custom-call(s32[16]{0:T(128)S(1)} %dynamic-slice_bitcast_fusion.at_ref.slice_ref, f32[512,1024]{1,0:T(8,128)S(1)} %fusion.10.gate_up_ref, f32[1,1024]{1,0:T(1,128)S(1)} %add_rsqrt_fusion.scale_ref, ...), custom_call_target="tpu_custom_call" | custom-call | flops 939524096 | bytes 7340032 | tf_op jit(solution)/shard_map/pallas_call | solution.py:66
  142.5 1.9 collective-permute-start.20
  144.4 2.1 collective-permute-start.24
  146.5 3.1 %shard_map.112 = (bf16[256,512]{1,0:T(8,128)(2,1)S(1)}, bf16[8,448,256]{2,1,0:T(8,128)(2,1)}, bf16[8,448,256]{2,1,0:T(8,128)(2,1)}) custom-call(s32[16]{0:T(128)S(1)} %dynamic-slice_bitcast_fusion.at_ref.slice_ref, f32[512,1024]{1,0:T(8,128)S(1)} %fusion.10.gate_up_ref, f32[1,1024]{1,0:T(1,128)S(1)} %add_rsqrt_fusion.scale_ref, ...), custom_call_target="tpu_custom_call" | custom-call | flops 939524096 | bytes 7340032 | tf_op jit(solution)/shard_map/pallas_call | solution.py:66
  149.6 1.5 collective-permute-start.28
  151.1 2.1 collective-permute-start.32
  153.2 2.2 all-to-all-done.1
  156.4 4.3 %all-to-all-start.2 = ((bf16[8,16,448]{2,1,0:T(8,128)(2,1)}), bf16[8,16,448]{2,1,0:T(8,128)(2,1)S(1)}, u32[]{:S(2)}, u32[]{:S(2)}) async-start(bf16[8,16,448]{2,1,0:T(8,128)(2,1)} %bitcast.19), calls=%async_computation.2 | async-start | bytes 262144 | tf_op jit(solution)/shard_map/all_to_all | solution.py:269
  160.7 2.0 copy-done.1
  162.7 3.8 %shard_map.113 = (bf16[8,448,256]{2,1,0:T(8,128)(2,1)S(1)}, bf16[8,448,256]{2,1,0:T(8,128)(2,1)S(1)}, bf16[8,448,256]{2,1,0:T(8,128)(2,1)S(1)}, bf16[8,448,256]{2,1,0:T(8,128)(2,1)S(1)}) custom-call(s32[16]{0:T(128)S(1)} %dynamic-slice_bitcast_fusion.at_ref.slice_ref, bf16[16,448,256]{2,1,0:T(8,128)(2,1)S(1)} %bitcast.65, ...), custom_call_target="tpu_custom_call" | custom-call | flops 1879048192 | bytes 14680064 | tf_op jit(solution)/shard_map/pallas_call | solution.py:96
  170.3 19.2 %collective-permute-done.20 = bf16[8,448,256]{2,1,0:T(8,128)(2,1)} collective-permute-done((bf16[8,448,256]{2,1,0:T(8,128)(2,1)}, bf16[8,448,256]{2,1,0:T(8,128)(2,1)}, u32[]{:S(2)}, u32[]{:S(2)}) %collective-permute-start.20) | collective-permute-done | bytes 1835040 | tf_op jit(solution)/shard_map/ppermute | solution.py:21
  189.5 1.7 add_convert_fusion.3
  191.2 3.1 %collective-permute-start.21 = (bf16[4,448,256]{2,1,0:T(8,128)(2,1)S(1)}, bf16[4,448,256]{2,1,0:T(8,128)(2,1)S(1)}, u32[]{:S(2)}, u32[]{:S(2)}) collective-permute-start(bf16[4,448,256]{2,1,0:T(8,128)(2,1)S(1)} %add_convert_fusion.3), channel_id=1, source_target_pairs={{0,3},{1,2},{2,1},{3,0},{4,7},{5,6},{6,5},{7,4},{8,11},{9,10},{10,... | collective-permute-start | bytes 2752520 | tf_op jit(solution)/shard_map/ppermute | solution.py:21
  194.4 1.4 add_convert_fusion.2
  198.1 2.6 %collective-permute-start.29 = (bf16[4,448,256]{2,1,0:T(8,128)(2,1)S(1)}, bf16[4,448,256]{2,1,0:T(8,128)(2,1)S(1)}, u32[]{:S(2)}, u32[]{:S(2)}) collective-permute-start(bf16[4,448,256]{2,1,0:T(8,128)(2,1)S(1)} %add_convert_fusion.1), channel_id=1, source_target_pairs={{0,12},{1,13},{2,14},{3,15},{4,8},{5,9},{6,10},{7,11},{8,4},{9,5},... | collective-permute-start | bytes 2752520 | tf_op jit(solution)/shard_map/ppermute | solution.py:21
  202.1 11.4 %collective-permute-done.21 = bf16[4,448,256]{2,1,0:T(8,128)(2,1)S(1)} collective-permute-done((bf16[4,448,256]{2,1,0:T(8,128)(2,1)S(1)}, bf16[4,448,256]{2,1,0:T(8,128)(2,1)S(1)}, u32[]{:S(2)}, u32[]{:S(2)}) %collective-permute-start.21) | collective-permute-done | bytes 917536 | tf_op jit(solution)/shard_map/ppermute | solution.py:21
  215.9 1.7 collective-permute-done.25
  218.9 1.7 collective-permute-start.26
  227.4 2.0 collective-permute-start.23
  230.8 2.7 %collective-permute-done.30 = bf16[2,448,256]{2,1,0:T(8,128)(2,1)S(1)} collective-permute-done((bf16[2,448,256]{2,1,0:T(8,128)(2,1)S(1)}, bf16[2,448,256]{2,1,0:T(8,128)(2,1)S(1)}, u32[]{:S(2)}, u32[]{:S(2)}) %collective-permute-start.30) | collective-permute-done | bytes 458784 | tf_op jit(solution)/shard_map/ppermute | solution.py:21
  234.5 2.2 collective-permute-start.31
  240.1 1.7 collective-permute-done.31
  (159 shorter events, 56.4 us)
Async XLA Ops:
  6.5 114.2 %all-gather.2.cloned.1.call-start = ((), (), s32[]{:S(2)}) async-start(), calls=%async_computation.3 | async-start | bytes 15597568 | tf_op jit(solution)/shard_map/all_gather | solution.py:216
  8.7 7.1 %collective-permute-start.16 = (f32[1,1024]{1,0:T(1,128)S(1)}, f32[1,1024]{1,0:T(1,128)S(1)}, u32[]{:S(2)}, u32[]{:S(2)}) collective-permute-start(f32[1,1024]{1,0:T(1,128)S(1)} %bitcast.78), channel_id=1, source_target_pairs={{0,1},{1,0},{2,3},{3,2},{4,5},{5,4},{6,7},{7,6},{8,9},{9,8},{10,11... | collective-permute-start | bytes 12296 | tf_op jit(solution)/shard_map/ppermute | solution.py:21
  15.4 16.0 %copy-start.18 = (f32[7168]{0:T(1024)S(1)}, f32[7168]{0:T(1024)}, u32[]{:S(2)}) copy-start(f32[7168]{0:T(1024)} %param.12) | copy-start | bytes 86020
  15.7 4.9 %collective-permute-start.17 = (f32[1,1024]{1,0:T(1,128)S(1)}, f32[1,1024]{1,0:T(1,128)S(1)}, u32[]{:S(2)}, u32[]{:S(2)}) collective-permute-start(f32[1,1024]{1,0:T(1,128)S(1)} %add.154), channel_id=1, source_target_pairs={{0,3},{1,2},{2,1},{3,0},{4,7},{5,6},{6,5},{7,4},{8,11},{9,10},{10,... | collective-permute-start | bytes 12296 | tf_op jit(solution)/shard_map/ppermute | solution.py:21
  20.6 7.4 %collective-permute-start.18 = (f32[1,1024]{1,0:T(1,128)S(1)}, f32[1,1024]{1,0:T(1,128)S(1)}, u32[]{:S(2)}, u32[]{:S(2)}) collective-permute-start(f32[1,1024]{1,0:T(1,128)S(1)} %add.155), channel_id=1, source_target_pairs={{0,4},{1,5},{2,6},{3,7},{4,0},{5,1},{6,2},{7,3},{8,12},{9,13},{10,... | collective-permute-start | bytes 12296 | tf_op jit(solution)/shard_map/ppermute | solution.py:21
  23.7 10.4 %all-to-all-start = ((bf16[8,16,448]{2,1,0:T(8,128)(2,1)}), bf16[8,16,448]{2,1,0:T(8,128)(2,1)S(1)}, u32[]{:S(2)}, u32[]{:S(2)}) async-start(bf16[8,16,448]{2,1,0:T(8,128)(2,1)} %bitcast.3), calls=%async_computation | async-start | bytes 262144 | tf_op jit(solution)/shard_map/all_to_all | solution.py:226
  28.1 5.8 %collective-permute-start.19 = (f32[1,1024]{1,0:T(1,128)S(1)}, f32[1,1024]{1,0:T(1,128)S(1)}, u32[]{:S(2)}, u32[]{:S(2)}) collective-permute-start(f32[1,1024]{1,0:T(1,128)S(1)} %add.156), channel_id=1, source_target_pairs={{0,12},{1,13},{2,14},{3,15},{4,8},{5,9},{6,10},{7,11},{8,4},{9,5},... | collective-permute-start | bytes 12296 | tf_op jit(solution)/shard_map/ppermute | solution.py:21
  34.3 6.4 %collective-permute-start.6 = (bf16[1,112,128]{2,1,0:T(8,128)(2,1)S(1)}, bf16[1,112,128]{2,1,0:T(8,128)(2,1)S(1)}, u32[]{:S(2)}, u32[]{:S(2)}) collective-permute-start(bf16[1,112,128]{2,1,0:T(8,128)(2,1)S(1)} %get-tuple-element.89), channel_id=1, source_target_pairs={{0,12},{1,13},{2,14},{3,15},{4,8},{5,9},{6,10},{7,11},{8,4},{9,5},... | collective-permute-start | bytes 86024 | tf_op jit(solution)/shard_map/ppermute | solution.py:21
  37.5 5.3 %collective-permute-start.4 = (bf16[1,112,128]{2,1,0:T(8,128)(2,1)S(1)}, bf16[1,112,128]{2,1,0:T(8,128)(2,1)S(1)}, u32[]{:S(2)}, u32[]{:S(2)}) collective-permute-start(bf16[1,112,128]{2,1,0:T(8,128)(2,1)S(1)} %get-tuple-element.90), channel_id=1, source_target_pairs={{0,4},{1,5},{2,6},{3,7},{4,0},{5,1},{6,2},{7,3},{8,12},{9,13},{10,... | collective-permute-start | bytes 86024 | tf_op jit(solution)/shard_map/ppermute | solution.py:21
  38.6 5.1 %collective-permute-start.2 = (bf16[1,112,128]{2,1,0:T(8,128)(2,1)S(1)}, bf16[1,112,128]{2,1,0:T(8,128)(2,1)S(1)}, u32[]{:S(2)}, u32[]{:S(2)}) collective-permute-start(bf16[1,112,128]{2,1,0:T(8,128)(2,1)S(1)} %get-tuple-element.91), channel_id=1, source_target_pairs={{0,3},{1,2},{2,1},{3,0},{4,7},{5,6},{6,5},{7,4},{8,11},{9,10},{10,... | collective-permute-start | bytes 86024 | tf_op jit(solution)/shard_map/ppermute | solution.py:21
  40.7 4.0 %collective-permute-start = (bf16[1,112,128]{2,1,0:T(8,128)(2,1)S(1)}, bf16[1,112,128]{2,1,0:T(8,128)(2,1)S(1)}, u32[]{:S(2)}, u32[]{:S(2)}) collective-permute-start(bf16[1,112,128]{2,1,0:T(8,128)(2,1)S(1)} %get-tuple-element.92), channel_id=1, source_target_pairs={{0,1},{1,0},{2,3},{3,2},{4,5},{5,4},{6,7},{7,6},{8,9},{9,8},{10,11... | collective-permute-start | bytes 86024 | tf_op jit(solution)/shard_map/ppermute | solution.py:21
  40.8 13.8 %collective-permute-start.7 = (bf16[2,112,128]{2,1,0:T(8,128)(2,1)S(1)}, bf16[2,112,128]{2,1,0:T(8,128)(2,1)S(1)}, u32[]{:S(2)}, u32[]{:S(2)}) collective-permute-start(bf16[2,112,128]{2,1,0:T(8,128)(2,1)S(1)} %pad_maximum_fusion.12), channel_id=1, source_target_pairs={{0,1},{1,0},{2,3},{3,2},{4,5},{5,4},{6,7},{7,6},{8,9},{9,8},{10,11... | collective-permute-start | bytes 172040 | tf_op jit(solution)/shard_map/ppermute | solution.py:21
  42.9 11.7 %collective-permute-start.5 = (bf16[2,112,128]{2,1,0:T(8,128)(2,1)S(1)}, bf16[2,112,128]{2,1,0:T(8,128)(2,1)S(1)}, u32[]{:S(2)}, u32[]{:S(2)}) collective-permute-start(bf16[2,112,128]{2,1,0:T(8,128)(2,1)S(1)} %pad_maximum_fusion.11), channel_id=1, source_target_pairs={{0,12},{1,13},{2,14},{3,15},{4,8},{5,9},{6,10},{7,11},{8,4},{9,5},... | collective-permute-start | bytes 172040 | tf_op jit(solution)/shard_map/ppermute | solution.py:21
  43.7 10.9 %collective-permute-start.3 = (bf16[2,112,128]{2,1,0:T(8,128)(2,1)S(1)}, bf16[2,112,128]{2,1,0:T(8,128)(2,1)S(1)}, u32[]{:S(2)}, u32[]{:S(2)}) collective-permute-start(bf16[2,112,128]{2,1,0:T(8,128)(2,1)S(1)} %pad_maximum_fusion.10), channel_id=1, source_target_pairs={{0,4},{1,5},{2,6},{3,7},{4,0},{5,1},{6,2},{7,3},{8,12},{9,13},{10,... | collective-permute-start | bytes 172040 | tf_op jit(solution)/shard_map/ppermute | solution.py:21
  44.7 9.8 %collective-permute-start.1 = (bf16[2,112,128]{2,1,0:T(8,128)(2,1)S(1)}, bf16[2,112,128]{2,1,0:T(8,128)(2,1)S(1)}, u32[]{:S(2)}, u32[]{:S(2)}) collective-permute-start(bf16[2,112,128]{2,1,0:T(8,128)(2,1)S(1)} %pad_maximum_fusion.9), channel_id=1, source_target_pairs={{0,3},{1,2},{2,1},{3,0},{4,7},{5,6},{6,5},{7,4},{8,11},{9,10},{10,... | collective-permute-start | bytes 172040 | tf_op jit(solution)/shard_map/ppermute | solution.py:21
  54.6 11.3 %collective-permute-start.11 = (bf16[4,112,128]{2,1,0:T(8,128)(2,1)S(1)}, bf16[4,112,128]{2,1,0:T(8,128)(2,1)S(1)}, u32[]{:S(2)}, u32[]{:S(2)}) collective-permute-start(bf16[4,112,128]{2,1,0:T(8,128)(2,1)S(1)} %pad_maximum_fusion.8), channel_id=1, source_target_pairs={{0,3},{1,2},{2,1},{3,0},{4,7},{5,6},{6,5},{7,4},{8,11},{9,10},{10,... | collective-permute-start | bytes 344072 | tf_op jit(solution)/shard_map/ppermute | solution.py:21
  56.0 9.9 %collective-permute-start.10 = (bf16[4,112,128]{2,1,0:T(8,128)(2,1)S(1)}, bf16[4,112,128]{2,1,0:T(8,128)(2,1)S(1)}, u32[]{:S(2)}, u32[]{:S(2)}) collective-permute-start(bf16[4,112,128]{2,1,0:T(8,128)(2,1)S(1)} %pad_maximum_fusion.7), channel_id=1, source_target_pairs={{0,1},{1,0},{2,3},{3,2},{4,5},{5,4},{6,7},{7,6},{8,9},{9,8},{10,11... | collective-permute-start | bytes 344072 | tf_op jit(solution)/shard_map/ppermute | solution.py:21
  56.1 9.8 %collective-permute-start.9 = (bf16[4,112,128]{2,1,0:T(8,128)(2,1)S(1)}, bf16[4,112,128]{2,1,0:T(8,128)(2,1)S(1)}, u32[]{:S(2)}, u32[]{:S(2)}) collective-permute-start(bf16[4,112,128]{2,1,0:T(8,128)(2,1)S(1)} %pad_maximum_fusion.6), channel_id=1, source_target_pairs={{0,12},{1,13},{2,14},{3,15},{4,8},{5,9},{6,10},{7,11},{8,4},{9,5},... | collective-permute-start | bytes 344072 | tf_op jit(solution)/shard_map/ppermute | solution.py:21
  58.4 7.5 %collective-permute-start.8 = (bf16[4,112,128]{2,1,0:T(8,128)(2,1)S(1)}, bf16[4,112,128]{2,1,0:T(8,128)(2,1)S(1)}, u32[]{:S(2)}, u32[]{:S(2)}) collective-permute-start(bf16[4,112,128]{2,1,0:T(8,128)(2,1)S(1)} %pad_maximum_fusion.5), channel_id=1, source_target_pairs={{0,4},{1,5},{2,6},{3,7},{4,0},{5,1},{6,2},{7,3},{8,12},{9,13},{10,... | collective-permute-start | bytes 344072 | tf_op jit(solution)/shard_map/ppermute | solution.py:21
  65.9 9.2 %copy-start.16 = (bf16[4,112,128]{2,1,0:T(8,128)(2,1)}, bf16[4,112,128]{2,1,0:T(8,128)(2,1)S(1)}, u32[]{:S(2)}) copy-start(bf16[4,112,128]{2,1,0:T(8,128)(2,1)S(1)} %collective-permute-done.9) | copy-start | bytes 344068
  66.0 9.2 %copy-start.17 = (bf16[4,112,128]{2,1,0:T(8,128)(2,1)}, bf16[4,112,128]{2,1,0:T(8,128)(2,1)S(1)}, u32[]{:S(2)}) copy-start(bf16[4,112,128]{2,1,0:T(8,128)(2,1)S(1)} %collective-permute-done.8) | copy-start | bytes 344068
  66.7 17.1 %collective-permute-start.15 = (bf16[8,112,128]{2,1,0:T(8,128)(2,1)}, bf16[8,112,128]{2,1,0:T(8,128)(2,1)}, u32[]{:S(2)}, u32[]{:S(2)}) collective-permute-start(bf16[8,112,128]{2,1,0:T(8,128)(2,1)} %pad_maximum_fusion.4), channel_id=1, source_target_pairs={{0,4},{1,5},{2,6},{3,7},{4,0},{5,1},{6,2},{7,3},{8,12},{9,13},{10,... | collective-permute-start | bytes 688136 | tf_op jit(solution)/shard_map/ppermute | solution.py:21
  68.7 15.1 %collective-permute-start.14 = (bf16[8,112,128]{2,1,0:T(8,128)(2,1)}, bf16[8,112,128]{2,1,0:T(8,128)(2,1)}, u32[]{:S(2)}, u32[]{:S(2)}) collective-permute-start(bf16[8,112,128]{2,1,0:T(8,128)(2,1)} %pad_maximum_fusion.3), channel_id=1, source_target_pairs={{0,3},{1,2},{2,1},{3,0},{4,7},{5,6},{6,5},{7,4},{8,11},{9,10},{10,... | collective-permute-start | bytes 688136 | tf_op jit(solution)/shard_map/ppermute | solution.py:21
  70.2 13.6 %collective-permute-start.13 = (bf16[8,112,128]{2,1,0:T(8,128)(2,1)}, bf16[8,112,128]{2,1,0:T(8,128)(2,1)}, u32[]{:S(2)}, u32[]{:S(2)}) collective-permute-start(bf16[8,112,128]{2,1,0:T(8,128)(2,1)} %pad_maximum_fusion.2), channel_id=1, source_target_pairs={{0,1},{1,0},{2,3},{3,2},{4,5},{5,4},{6,7},{7,6},{8,9},{9,8},{10,11... | collective-permute-start | bytes 688136 | tf_op jit(solution)/shard_map/ppermute | solution.py:21
  72.3 13.1 %collective-permute-start.12 = (bf16[8,112,128]{2,1,0:T(8,128)(2,1)}, bf16[8,112,128]{2,1,0:T(8,128)(2,1)}, u32[]{:S(2)}, u32[]{:S(2)}) collective-permute-start(bf16[8,112,128]{2,1,0:T(8,128)(2,1)} %pad_maximum_fusion.1), channel_id=1, source_target_pairs={{0,12},{1,13},{2,14},{3,15},{4,8},{5,9},{6,10},{7,11},{8,4},{9,5},... | collective-permute-start | bytes 688136 | tf_op jit(solution)/shard_map/ppermute | solution.py:21
  75.1 14.9 %copy-start.2 = (f32[7168,1]{1,0:T(8,128)S(1)}, f32[7168,1]{1,0:T(8,128)}, u32[]{:S(2)}) copy-start(f32[7168,1]{1,0:T(8,128)} %copy.51.gain_ref) | copy-start | bytes 86020
  94.3 10.8 %copy-start.5 = (bf16[1,256,7168]{2,1,0:T(8,128)(2,1)S(1)}, bf16[1,256,7168]{2,1,0:T(8,128)(2,1)}, u32[]{:S(2)}) copy-start(bf16[1,256,7168]{2,1,0:T(8,128)(2,1)} %weight_ref.1) | copy-start | bytes 11010052
  120.7 34.6 %all-to-all-start.1 = ((bf16[16,448,128]{2,1,0:T(8,128)(2,1)}), bf16[16,448,128]{2,1,0:T(8,128)(2,1)S(1)}, u32[]{:S(2)}, u32[]{:S(2)}) async-start(bf16[16,448,128]{2,1,0:T(8,128)(2,1)} %bitcast.16), calls=%async_computation.1 | async-start | bytes 3670016 | tf_op jit(solution)/shard_map/all_to_all | solution.py:257
  126.0 13.3 %copy-start = (bf16[7168,256]{1,0:T(8,128)(2,1)S(1)}, bf16[7168,256]{1,0:T(8,128)(2,1)}, u32[]{:S(2)}) copy-start(bf16[7168,256]{1,0:T(8,128)(2,1)} %copy.50) | copy-start | bytes 11010052
  142.5 47.0 %collective-permute-start.20 = (bf16[8,448,256]{2,1,0:T(8,128)(2,1)}, bf16[8,448,256]{2,1,0:T(8,128)(2,1)}, u32[]{:S(2)}, u32[]{:S(2)}) collective-permute-start(bf16[8,448,256]{2,1,0:T(8,128)(2,1)} %get-tuple-element.71), channel_id=1, source_target_pairs={{0,1},{1,0},{2,3},{3,2},{4,5},{5,4},{6,7},{7,6},{8,9},{9,8},{10,11... | collective-permute-start | bytes 5505032 | tf_op jit(solution)/shard_map/ppermute | solution.py:21
  144.4 49.9 %collective-permute-start.24 = (bf16[8,448,256]{2,1,0:T(8,128)(2,1)}, bf16[8,448,256]{2,1,0:T(8,128)(2,1)}, u32[]{:S(2)}, u32[]{:S(2)}) collective-permute-start(bf16[8,448,256]{2,1,0:T(8,128)(2,1)} %get-tuple-element.73), channel_id=1, source_target_pairs={{0,3},{1,2},{2,1},{3,0},{4,7},{5,6},{6,5},{7,4},{8,11},{9,10},{10,... | collective-permute-start | bytes 5505032 | tf_op jit(solution)/shard_map/ppermute | solution.py:21
  149.6 47.0 %collective-permute-start.28 = (bf16[8,448,256]{2,1,0:T(8,128)(2,1)}, bf16[8,448,256]{2,1,0:T(8,128)(2,1)}, u32[]{:S(2)}, u32[]{:S(2)}) collective-permute-start(bf16[8,448,256]{2,1,0:T(8,128)(2,1)} %get-tuple-element.77), channel_id=1, source_target_pairs={{0,4},{1,5},{2,6},{3,7},{4,0},{5,1},{6,2},{7,3},{8,12},{9,13},{10,... | collective-permute-start | bytes 5505032 | tf_op jit(solution)/shard_map/ppermute | solution.py:21
  151.1 49.6 %collective-permute-start.32 = (bf16[8,448,256]{2,1,0:T(8,128)(2,1)}, bf16[8,448,256]{2,1,0:T(8,128)(2,1)}, u32[]{:S(2)}, u32[]{:S(2)}) collective-permute-start(bf16[8,448,256]{2,1,0:T(8,128)(2,1)} %get-tuple-element.79), channel_id=1, source_target_pairs={{0,12},{1,13},{2,14},{3,15},{4,8},{5,9},{6,10},{7,11},{8,4},{9,5},... | collective-permute-start | bytes 5505032 | tf_op jit(solution)/shard_map/ppermute | solution.py:21
  156.4 13.8 %all-to-all-start.2 = ((bf16[8,16,448]{2,1,0:T(8,128)(2,1)}), bf16[8,16,448]{2,1,0:T(8,128)(2,1)S(1)}, u32[]{:S(2)}, u32[]{:S(2)}) async-start(bf16[8,16,448]{2,1,0:T(8,128)(2,1)} %bitcast.19), calls=%async_computation.2 | async-start | bytes 262144 | tf_op jit(solution)/shard_map/all_to_all | solution.py:269
  170.2 24.1 %copy-start.9 = (bf16[8,448,256]{2,1,0:T(8,128)(2,1)S(1)}, bf16[8,448,256]{2,1,0:T(8,128)(2,1)}, u32[]{:S(2)}) copy-start(bf16[8,448,256]{2,1,0:T(8,128)(2,1)} %copy-done.8) | copy-start | bytes 5505028
  191.2 22.3 %collective-permute-start.21 = (bf16[4,448,256]{2,1,0:T(8,128)(2,1)S(1)}, bf16[4,448,256]{2,1,0:T(8,128)(2,1)S(1)}, u32[]{:S(2)}, u32[]{:S(2)}) collective-permute-start(bf16[4,448,256]{2,1,0:T(8,128)(2,1)S(1)} %add_convert_fusion.3), channel_id=1, source_target_pairs={{0,3},{1,2},{2,1},{3,0},{4,7},{5,6},{6,5},{7,4},{8,11},{9,10},{10,... | collective-permute-start | bytes 2752520 | tf_op jit(solution)/shard_map/ppermute | solution.py:21
  195.8 21.9 %collective-permute-start.25 = (bf16[4,448,256]{2,1,0:T(8,128)(2,1)S(1)}, bf16[4,448,256]{2,1,0:T(8,128)(2,1)S(1)}, u32[]{:S(2)}, u32[]{:S(2)}) collective-permute-start(bf16[4,448,256]{2,1,0:T(8,128)(2,1)S(1)} %add_convert_fusion.2), channel_id=1, source_target_pairs={{0,4},{1,5},{2,6},{3,7},{4,0},{5,1},{6,2},{7,3},{8,12},{9,13},{10,... | collective-permute-start | bytes 2752520 | tf_op jit(solution)/shard_map/ppermute | solution.py:21
  198.1 15.5 %copy-start.11 = (bf16[8,448,256]{2,1,0:T(8,128)(2,1)S(1)}, bf16[8,448,256]{2,1,0:T(8,128)(2,1)}, u32[]{:S(2)}) copy-start(bf16[8,448,256]{2,1,0:T(8,128)(2,1)} %copy-done.10) | copy-start | bytes 5505028
  198.1 22.5 %collective-permute-start.29 = (bf16[4,448,256]{2,1,0:T(8,128)(2,1)S(1)}, bf16[4,448,256]{2,1,0:T(8,128)(2,1)S(1)}, u32[]{:S(2)}, u32[]{:S(2)}) collective-permute-start(bf16[4,448,256]{2,1,0:T(8,128)(2,1)S(1)} %add_convert_fusion.1), channel_id=1, source_target_pairs={{0,12},{1,13},{2,14},{3,15},{4,8},{5,9},{6,10},{7,11},{8,4},{9,5},... | collective-permute-start | bytes 2752520 | tf_op jit(solution)/shard_map/ppermute | solution.py:21
  202.0 21.3 %collective-permute-start.33 = (bf16[4,448,256]{2,1,0:T(8,128)(2,1)S(1)}, bf16[4,448,256]{2,1,0:T(8,128)(2,1)S(1)}, u32[]{:S(2)}, u32[]{:S(2)}) collective-permute-start(bf16[4,448,256]{2,1,0:T(8,128)(2,1)S(1)} %add_convert_fusion), channel_id=1, source_target_pairs={{0,1},{1,0},{2,3},{3,2},{4,5},{5,4},{6,7},{7,6},{8,9},{9,8},{10,11... | collective-permute-start | bytes 2752520 | tf_op jit(solution)/shard_map/ppermute | solution.py:21
  214.8 11.6 %collective-permute-start.22 = (bf16[2,448,256]{2,1,0:T(8,128)(2,1)S(1)}, bf16[2,448,256]{2,1,0:T(8,128)(2,1)S(1)}, u32[]{:S(2)}, u32[]{:S(2)}) collective-permute-start(bf16[2,448,256]{2,1,0:T(8,128)(2,1)S(1)} %add_convert_fusion.7), channel_id=1, source_target_pairs={{0,4},{1,5},{2,6},{3,7},{4,0},{5,1},{6,2},{7,3},{8,12},{9,13},{10,... | collective-permute-start | bytes 1376264 | tf_op jit(solution)/shard_map/ppermute | solution.py:21
  218.9 10.7 %collective-permute-start.26 = (bf16[2,448,256]{2,1,0:T(8,128)(2,1)S(1)}, bf16[2,448,256]{2,1,0:T(8,128)(2,1)S(1)}, u32[]{:S(2)}, u32[]{:S(2)}) collective-permute-start(bf16[2,448,256]{2,1,0:T(8,128)(2,1)S(1)} %add_convert_fusion.6), channel_id=1, source_target_pairs={{0,12},{1,13},{2,14},{3,15},{4,8},{5,9},{6,10},{7,11},{8,4},{9,5},... | collective-permute-start | bytes 1376264 | tf_op jit(solution)/shard_map/ppermute | solution.py:21
  221.8 11.6 %collective-permute-start.30 = (bf16[2,448,256]{2,1,0:T(8,128)(2,1)S(1)}, bf16[2,448,256]{2,1,0:T(8,128)(2,1)S(1)}, u32[]{:S(2)}, u32[]{:S(2)}) collective-permute-start(bf16[2,448,256]{2,1,0:T(8,128)(2,1)S(1)} %add_convert_fusion.5), channel_id=1, source_target_pairs={{0,1},{1,0},{2,3},{3,2},{4,5},{5,4},{6,7},{7,6},{8,9},{9,8},{10,11... | collective-permute-start | bytes 1376264 | tf_op jit(solution)/shard_map/ppermute | solution.py:21
  224.5 12.2 %collective-permute-start.34 = (bf16[2,448,256]{2,1,0:T(8,128)(2,1)S(1)}, bf16[2,448,256]{2,1,0:T(8,128)(2,1)S(1)}, u32[]{:S(2)}, u32[]{:S(2)}) collective-permute-start(bf16[2,448,256]{2,1,0:T(8,128)(2,1)S(1)} %add_convert_fusion.4), channel_id=1, source_target_pairs={{0,3},{1,2},{2,1},{3,0},{4,7},{5,6},{6,5},{7,4},{8,11},{9,10},{10,... | collective-permute-start | bytes 1376264 | tf_op jit(solution)/shard_map/ppermute | solution.py:21
  227.4 10.4 %collective-permute-start.23 = (bf16[1,448,256]{2,1,0:T(8,128)(2,1)S(1)}, bf16[1,448,256]{2,1,0:T(8,128)(2,1)S(1)}, u32[]{:S(2)}, u32[]{:S(2)}) collective-permute-start(bf16[1,448,256]{2,1,0:T(8,128)(2,1)S(1)} %add_convert_fusion.11), channel_id=1, source_target_pairs={{0,12},{1,13},{2,14},{3,15},{4,8},{5,9},{6,10},{7,11},{8,4},{9,5},... | collective-permute-start | bytes 688136 | tf_op jit(solution)/shard_map/ppermute | solution.py:21
  230.7 8.3 %collective-permute-start.27 = (bf16[1,448,256]{2,1,0:T(8,128)(2,1)S(1)}, bf16[1,448,256]{2,1,0:T(8,128)(2,1)S(1)}, u32[]{:S(2)}, u32[]{:S(2)}) collective-permute-start(bf16[1,448,256]{2,1,0:T(8,128)(2,1)S(1)} %add_convert_fusion.10), channel_id=1, source_target_pairs={{0,1},{1,0},{2,3},{3,2},{4,5},{5,4},{6,7},{7,6},{8,9},{9,8},{10,11... | collective-permute-start | bytes 688136 | tf_op jit(solution)/shard_map/ppermute | solution.py:21
  234.5 7.3 %collective-permute-start.31 = (bf16[1,448,256]{2,1,0:T(8,128)(2,1)S(1)}, bf16[1,448,256]{2,1,0:T(8,128)(2,1)S(1)}, u32[]{:S(2)}, u32[]{:S(2)}) collective-permute-start(bf16[1,448,256]{2,1,0:T(8,128)(2,1)S(1)} %add_convert_fusion.9), channel_id=1, source_target_pairs={{0,3},{1,2},{2,1},{3,0},{4,7},{5,6},{6,5},{7,4},{8,11},{9,10},{10,... | collective-permute-start | bytes 688136 | tf_op jit(solution)/shard_map/ppermute | solution.py:21
  237.8 6.1 %collective-permute-start.35 = (bf16[1,448,256]{2,1,0:T(8,128)(2,1)S(1)}, bf16[1,448,256]{2,1,0:T(8,128)(2,1)S(1)}, u32[]{:S(2)}, u32[]{:S(2)}) collective-permute-start(bf16[1,448,256]{2,1,0:T(8,128)(2,1)S(1)} %add_convert_fusion.8), channel_id=1, source_target_pairs={{0,4},{1,5},{2,6},{3,7},{4,0},{5,1},{6,2},{7,3},{8,12},{9,13},{10,... | collective-permute-start | bytes 688136 | tf_op jit(solution)/shard_map/ppermute | solution.py:21
  (13 other events, 45.4 us)
Sparse Core Ops, SparseCore 0:
  9.5 111.1 all-gather.1
